TPU v7x, 32 devices: a whole 2x2x4 slice. The times are simulated.
32 devices in a mesh: tensor: 8 (over y, x, core), expert: 4 (over z).
Axes of the slice: x: 2, y: 2, z: 4, core: 2. Of those that a mesh axis runs over, the one named last changes fastest.
Arguments:
- acts: bfloat16 [192, 3072], P('expert', 'tensor'), may hold values from -6 to 6
- grad_out: bfloat16 [192, 3072], P('expert', 'tensor'), may hold values from -6 to 6
- routing: int32 [192, 2], P('expert'), may hold values from 0 to 3, all different within a row; in each aligned block of 48 rows (0 to 47, 48 to 95, ...) at most 48 rows name the same one
- gates: float32 [192, 2], P('expert'), may hold values from 0.1 to 1
- w_gate: bfloat16 [4, 3072, 8192], P('expert', None, 'tensor'), may hold values from -0.109375 to 0.109375
- w_up: bfloat16 [4, 3072, 8192], P('expert', None, 'tensor'), may hold values from -0.109375 to 0.109375
- w_down: bfloat16 [4, 8192, 3072], P('expert', 'tensor'), may hold values from -0.0625 to 0.0625
Outputs:
- grad_gate: bfloat16 [4, 3072, 8192], P('expert', None, 'tensor')
- grad_up: bfloat16 [4, 3072, 8192], P('expert', None, 'tensor')
- grad_down: bfloat16 [4, 8192, 3072], P('expert', 'tensor')
- grad_acts: bfloat16 [192, 3072], P('expert', 'tensor')
Inputs may be any that keep to these rules, and one draw needn't show every extreme that they name: `routing`: within the tokens of one owner group (aligned blocks of 48 rows) no expert is named more than 48 times, a bound that some block reaches; a token's two experts differ.
All inputs are finite; a program needn't handle non-finite values.
Results may differ from a plain program's by a relative error of at most 0.02.
Values may be sent and summed in bfloat16 or wider, within the bound.
No kernel may reach another device: no remote copies, remote signals or barrier semaphores. Data moves between devices by JAX's collectives and lax.ppermute only.
A program may use at most 128 MiB of HBM per device.

v0:
```python
import jax
import jax.numpy as jnp
from jax import lax
from jax.sharding import PartitionSpec as P


def dispatch_table(routing, gates, experts, capacity):
    tok_count = routing.shape[0]
    entries = routing.reshape(-1)
    chosen = (entries[:, None] == jnp.arange(experts, dtype=jnp.int32)[None, :]).astype(jnp.int32)
    earlier = jnp.cumsum(chosen, axis=0) - chosen
    position = jnp.sum(earlier * chosen, axis=1)
    in_slot = (position[:, None] == jnp.arange(capacity, dtype=jnp.int32)[None, :]).astype(
        jnp.float32
    )
    placed = chosen.astype(jnp.float32)[:, :, None] * in_slot[:, None, :]
    placed = placed.reshape(tok_count, 2, experts, capacity)
    table = jnp.sum(placed, axis=1)
    gate_slot = jnp.einsum("tkec,tk->ec", placed, gates)
    return (table, gate_slot)


def contract_rows(left, right):
    return lax.dot_general(
        left, right, (((0,), (0,)), ((), ())), preferred_element_type=jnp.float32
    )


def contract_cols(left, right):
    return lax.dot_general(
        left, right, (((1,), (1,)), ((), ())), preferred_element_type=jnp.float32
    )


def body(acts, grad_out, routing, gates, w_gate, w_up, w_down):
    groups = lax.axis_size("expert")
    tok_count = routing.shape[0]
    capacity = min(tok_count, 4 * tok_count // groups)
    table, gate_slot = dispatch_table(routing, gates, groups, capacity)
    table_half = table.astype(jnp.bfloat16)

    def place_rows(source):
        return jnp.einsum("tec,td->ecd", table_half, source, preferred_element_type=jnp.float32)

    whole_acts, whole_grad = (
        lax.all_gather(acts, "tensor", axis=1, tiled=True),
        lax.all_gather(grad_out, "tensor", axis=1, tiled=True),
    )
    slot_acts = place_rows(whole_acts).astype(jnp.bfloat16)
    slot_grad = (place_rows(whole_grad) * gate_slot[:, :, None]).astype(jnp.bfloat16)
    rows_acts, rows_grad = (
        lax.all_to_all(slot_acts, "expert", split_axis=0, concat_axis=0, tiled=True),
        lax.all_to_all(slot_grad, "expert", split_axis=0, concat_axis=0, tiled=True),
    )
    width = rows_acts.shape[2]
    rows_acts = rows_acts.reshape(-1, width)
    rows_grad = rows_grad.reshape(-1, width)
    gate_shard = w_gate[0]
    up_shard = w_up[0]
    down_shard = w_down[0]
    gate_pre = jnp.dot(rows_acts, gate_shard, preferred_element_type=jnp.float32)
    up_pre = jnp.dot(rows_acts, up_shard, preferred_element_type=jnp.float32)
    gate_sig = jax.nn.sigmoid(gate_pre)
    gate_act = gate_pre * gate_sig
    hidden = (gate_act * up_pre).astype(jnp.bfloat16)
    grad_hidden = contract_cols(rows_grad, down_shard)
    grad_up_pre = (grad_hidden * gate_act).astype(jnp.bfloat16)
    grad_gate_pre = (grad_hidden * up_pre * gate_sig * (1.0 + gate_pre * (1.0 - gate_sig))).astype(
        jnp.bfloat16
    )
    grad_down = contract_rows(hidden, rows_grad).astype(jnp.bfloat16)
    grad_gate = contract_rows(rows_acts, grad_gate_pre).astype(jnp.bfloat16)
    grad_up = contract_rows(rows_acts, grad_up_pre).astype(jnp.bfloat16)
    partial_sum = lax.psum_scatter(
        contract_cols(gate_shard, grad_gate_pre) + contract_cols(up_shard, grad_up_pre),
        "tensor",
        scatter_dimension=0,
        tiled=True,
    )
    feature_count = partial_sum.shape[0]
    slot_back = partial_sum.astype(jnp.bfloat16).reshape(feature_count, groups, capacity)
    returned = lax.all_to_all(slot_back, "expert", split_axis=1, concat_axis=1, tiled=True)
    grad_acts = jnp.einsum(
        "tec,dec->td", table_half, returned, preferred_element_type=jnp.float32
    ).astype(jnp.bfloat16)
    return (grad_gate[None], grad_up[None], grad_down[None], grad_acts)


def solution(mesh):
    return jax.shard_map(
        body,
        mesh=mesh,
        in_specs=(
            P("expert", "tensor"),
            P("expert", "tensor"),
            P("expert", None),
            P("expert", None),
            P("expert", None, "tensor"),
            P("expert", None, "tensor"),
            P("expert", "tensor", None),
        ),
        out_specs=(
            P("expert", None, "tensor"),
            P("expert", None, "tensor"),
            P("expert", "tensor", None),
            P("expert", "tensor"),
        ),
        check_vma=False,
    )
```

profile of v0, /device:TPU:8, one launch (start us, length us, event | category | flops | bytes accessed | tf_op | source)
XLA Modules:
  0.0 165.2 jit_solution(15534556834415958374)
XLA Ops:
  7.2 0.7 convert_convert_fusion
  7.9 0.8 copy.19
  8.7 0.1 eq.47
  8.8 0.1 fusion.26
  8.9 0.1 reduce_window_sum.11
  9.0 0.2 select_reduce_fusion
  9.2 0.1 eq.51
  9.3 0.1 copy.20
  9.4 0.1 fusion.27
  9.5 9.8 %all_gather.6 = bf16[48,3072]{1,0:T(8,128)(2,1)S(1)} all-gather(bf16[48,384]{1,0:T(8,128)(2,1)} %param.7), channel_id=1, replica_groups=mesh['tensor'=8,'expert'=4] {'tensor'}, dimensions={1}, use_global_device_ids=true | all-gather | bytes 331776 | tf_op jit(solution)/shard_map/all_gather | solution.py:46
  19.3 0.1 multiply_reduce_fusion
  19.4 1.5 convolution_convert_fusion
  20.9 5.3 %all-to-all-start = ((bf16[4,48,3072]{2,1,0:T(8,128)(2,1)}), bf16[4,48,3072]{2,1,0:T(8,128)(2,1)S(1)}, u32[]{:S(2)}, u32[]{:S(2)}) async-start(bf16[4,48,3072]{2,1,0:T(8,128)(2,1)} %convolution_convert_fusion), calls=%async_computation | async-start | bytes 2359296 | tf_op jit(solution)/shard_map/all_to_all | solution.py:52
  26.2 9.3 %all_gather.7 = bf16[48,3072]{1,0:T(8,128)(2,1)S(1)} all-gather(bf16[48,384]{1,0:T(8,128)(2,1)S(1)} %copy-done.1), channel_id=1, replica_groups=mesh['tensor'=8,'expert'=4] {'tensor'}, dimensions={1}, use_global_device_ids=true | all-gather | bytes 331776 | tf_op jit(solution)/shard_map/all_gather | solution.py:47
  35.6 0.2 fusion.21
  35.8 1.5 fusion.16
  37.3 14.7 %all-to-all-done = bf16[4,48,3072]{2,1,0:T(8,128)(2,1)S(1)} async-done(((bf16[4,48,3072]{2,1,0:T(8,128)(2,1)}), bf16[4,48,3072]{2,1,0:T(8,128)(2,1)S(1)}, u32[]{:S(2)}, u32[]{:S(2)}) %all-to-all-start) | async-done | bytes 1179680 | tf_op jit(solution)/shard_map/all_to_all | solution.py:52
  52.0 7.6 %all-to-all-start.1 = ((bf16[4,48,3072]{2,1,0:T(8,128)(2,1)}), bf16[4,48,3072]{2,1,0:T(8,128)(2,1)}, u32[]{:S(2)}, u32[]{:S(2)}) async-start(bf16[4,48,3072]{2,1,0:T(8,128)(2,1)} %fusion.16), calls=%async_computation.1 | async-start | bytes 2359296 | tf_op jit(solution)/shard_map/all_to_all | solution.py:53
  59.6 5.3 %fusion.2 = f32[192,1024]{1,0:T(8,128)} fusion(bf16[192,3072]{1,0:T(8,128)(2,1)S(1)} %bitcast.64, bf16[1,3072,1024]{2,1,0:T(8,128)(2,1)} %param.11), kind=kOutput, calls=%fused_computation.2 | convolution fusion | flops 1207959552 | bytes 8257536 | tf_op jit(solution)/shard_map/dot_general | solution.py:61
  64.9 2.4 %fusion.6 = f32[192,1024]{1,0:T(8,128)} fusion(bf16[192,3072]{1,0:T(8,128)(2,1)S(1)} %bitcast.65, bf16[1,3072,1024]{2,1,0:T(8,128)(2,1)S(1)} %bitcast.63), kind=kOutput, calls=%fused_computation.6 | convolution fusion | flops 1207959552 | bytes 8257536 | tf_op jit(solution)/shard_map/dot_general | solution.py:62
  67.3 17.3 %all-to-all-done.1 = bf16[4,48,3072]{2,1,0:T(8,128)(2,1)} async-done(((bf16[4,48,3072]{2,1,0:T(8,128)(2,1)}), bf16[4,48,3072]{2,1,0:T(8,128)(2,1)}, u32[]{:S(2)}, u32[]{:S(2)}) %all-to-all-start.1) | async-done | bytes 1179680 | tf_op jit(solution)/shard_map/all_to_all | solution.py:53
  84.6 5.9 %multiply_convert_fusion.1 = (bf16[192,1024]{1,0:T(8,128)(2,1)S(1)}, bf16[192,1024]{1,0:T(8,128)(2,1)S(1)}) fusion(f32[192,1024]{1,0:T(8,128)} %fusion.2, f32[192,1024]{1,0:T(8,128)} %fusion.6, bf16[192,3072]{1,0:T(8,128)(2,1)} %bitcast.7, bf16[1,1024,3072]{2,1,0:T(8,128)(2,1)} %param.13), kind=kOutput, calls=%fused_computation.21 | convolution fusion | flops 1210515456 | bytes 9830400 | tf_op jit(solution)/shard_map/dot_general | solution.py:30
  90.5 5.0 %fusion = f32[192,3072]{1,0:T(8,128)S(1)} fusion(bf16[192,1024]{1,0:T(8,128)(2,1)S(1)} %get-tuple-element.5, bf16[1,3072,1024]{2,1,0:T(8,128)(2,1)} %param.11), kind=kOutput, calls=%fused_computation | convolution fusion | flops 1207959552 | bytes 9043968 | tf_op jit(solution)/shard_map/dot_general | solution.py:30
  95.5 6.4 %fusion.13 = f32[3072,192]{0,1:T(8,128)} fusion(f32[192,3072]{1,0:T(8,128)S(1)} %fusion, bf16[192,1024]{1,0:T(8,128)(2,1)S(1)} %get-tuple-element.4, bf16[1,3072,1024]{2,1,0:T(8,128)(2,1)} %param.12), kind=kOutput, calls=%fused_computation.15 | convolution fusion | flops 1208549376 | bytes 11403264 | tf_op jit(solution)/shard_map/dot_general | solution.py:30
  102.0 4.6 %convert_bitcast_fusion.1 = bf16[1,3072,1024]{2,1,0:T(8,128)(2,1)} fusion(bf16[192,3072]{1,0:T(8,128)(2,1)S(1)} %bitcast.66, bf16[192,1024]{1,0:T(8,128)(2,1)S(1)} %get-tuple-element.4), kind=kOutput, calls=%fused_computation.11 | convolution fusion | flops 1211105280 | bytes 7864320 | tf_op jit(solution)/shard_map/dot_general | solution.py:24
  106.5 5.8 %convert_bitcast_fusion = bf16[1,1024,3072]{2,1,0:T(8,128)(2,1)} fusion(bf16[192,3072]{1,0:T(8,128)(2,1)} %bitcast.7, f32[192,1024]{1,0:T(8,128)S(1)} %copy-done.3, f32[192,1024]{1,0:T(8,128)S(1)} %copy-done.2), kind=kOutput, calls=%fused_computation.10 | convolution fusion | flops 1212284928 | bytes 9043968 | tf_op jit(solution)/shard_map/dot_general | solution.py:24
  112.4 33.1 %reduce-scatter.2.cloned.1.call-done = f32[384,192]{0,1:T(8,128)} async-done(((f32[3072,192]{0,1:T(8,128)}), f32[384,192]{0,1:T(8,128)}) %reduce-scatter.2.cloned.1.call-update) | async-done | bytes 294928 | tf_op jit(solution)/shard_map/reduce_scatter | solution.py:74
  145.4 1.6 convert_element_type.69
  147.1 5.1 %all-to-all-start.2 = ((bf16[384,4,48]{0,2,1:T(8,128)(2,1)}), bf16[384,4,48]{0,2,1:T(8,128)(2,1)S(1)}, u32[]{:S(2)}, u32[]{:S(2)}) async-start(bf16[384,4,48]{0,2,1:T(8,128)(2,1)} %bitcast.15), calls=%async_computation.3 | async-start | bytes 294912 | tf_op jit(solution)/shard_map/all_to_all | solution.py:82
  152.2 4.6 %convert_bitcast_fusion.2 = bf16[1,3072,1024]{2,1,0:T(8,128)(2,1)} fusion(bf16[192,3072]{1,0:T(8,128)(2,1)S(1)} %bitcast.67, bf16[192,1024]{1,0:T(8,128)(2,1)S(1)} %get-tuple-element.5), kind=kOutput, calls=%fused_computation.12 | convolution fusion | flops 1211105280 | bytes 7864320 | tf_op jit(solution)/shard_map/dot_general | solution.py:24
  156.8 0.7 all-to-all-done.2
  157.5 0.8 fusion.17
  (15 shorter events, 0.1 us)
Async XLA Ops:
  7.2 28.4 %copy-start = (f32[48,2]{0,1:T(2,128)S(1)}, f32[48,2]{0,1:T(2,128)}, u32[]{:S(2)}) copy-start(f32[48,2]{0,1:T(2,128)} %param.10) | copy-start | bytes 1156
  7.2 19.1 %copy-start.1 = (bf16[48,384]{1,0:T(8,128)(2,1)S(1)}, bf16[48,384]{1,0:T(8,128)(2,1)}, u32[]{:S(2)}) copy-start(bf16[48,384]{1,0:T(8,128)(2,1)} %param.8) | copy-start | bytes 110596
  20.9 31.1 %all-to-all-start = ((bf16[4,48,3072]{2,1,0:T(8,128)(2,1)}), bf16[4,48,3072]{2,1,0:T(8,128)(2,1)S(1)}, u32[]{:S(2)}, u32[]{:S(2)}) async-start(bf16[4,48,3072]{2,1,0:T(8,128)(2,1)} %convolution_convert_fusion), calls=%async_computation | async-start | bytes 2359296 | tf_op jit(solution)/shard_map/all_to_all | solution.py:52
  52.0 12.9 %slice-start = ((s8[6291456]{0:T(1024)(128)(4,1)}), s8[2097152]{0:T(1024)(128)(4,1)S(1)}, s32[]{:S(2)}) async-start(s8[6291456]{0:T(1024)(128)(4,1)} %bitcast.62), calls=%async_computation.5 | async-start | bytes 4194304
  52.0 32.6 %all-to-all-start.1 = ((bf16[4,48,3072]{2,1,0:T(8,128)(2,1)}), bf16[4,48,3072]{2,1,0:T(8,128)(2,1)}, u32[]{:S(2)}, u32[]{:S(2)}) async-start(bf16[4,48,3072]{2,1,0:T(8,128)(2,1)} %fusion.16), calls=%async_computation.1 | async-start | bytes 2359296 | tf_op jit(solution)/shard_map/all_to_all | solution.py:53
  59.6 85.8 %reduce-scatter.2.cloned.1.call-start = ((), (), s32[]{:S(2)}) async-start(), calls=%async_computation.4 | async-start | bytes 2654208 | tf_op jit(solution)/shard_map/reduce_scatter | solution.py:74
  59.6 5.3 %slice-start.1 = ((s8[6291456]{0:T(1024)(128)(4,1)}), s8[4194304]{0:T(1024)(128)(4,1)S(1)}, s32[]{:S(2)}) async-start(s8[6291456]{0:T(1024)(128)(4,1)} %bitcast.62), calls=%async_computation.6 | async-start | bytes 8388608
  101.9 4.6 %copy-start.2 = (f32[192,1024]{1,0:T(8,128)S(1)}, f32[192,1024]{1,0:T(8,128)}, u32[]{:S(2)}) copy-start(f32[192,1024]{1,0:T(8,128)} %fusion.2) | copy-start | bytes 2359300
  101.9 4.6 %copy-start.3 = (f32[192,1024]{1,0:T(8,128)S(1)}, f32[192,1024]{1,0:T(8,128)}, u32[]{:S(2)}) copy-start(f32[192,1024]{1,0:T(8,128)} %fusion.6) | copy-start | bytes 2359300
  147.1 10.4 %all-to-all-start.2 = ((bf16[384,4,48]{0,2,1:T(8,128)(2,1)}), bf16[384,4,48]{0,2,1:T(8,128)(2,1)S(1)}, u32[]{:S(2)}, u32[]{:S(2)}) async-start(bf16[384,4,48]{0,2,1:T(8,128)(2,1)} %bitcast.15), calls=%async_computation.3 | async-start | bytes 294912 | tf_op jit(solution)/shard_map/all_to_all | solution.py:82
Sparse Core Ops, SparseCore 0:
  102.1 43.3 reduce-scatter.1
where the time goes:
time: 168 us; the launch traced here: 165 us
  waiting for transfers between devices  65.9 us (39%)
  matrix products  43.9 us (26%)
  blocking collectives  19.1 us (11%)
  starting transfers between devices  18.1 us (11%)
  between operations  14.1 us (8%)
  other arithmetic  2.94 us (2%)
    reduce_scatter x1, waiting for transfers between devices, body(): lax.psum_scatter(contract_cols(gate_shard, grad_gate_pre) + contract_cols...  33.1 us
    dot_general x3, matrix products, contract_cols(): lax.dot_general(left, right, (((1,), (1,)), ((), ())), preferred_element_...  17.3 us
    all_to_all x1, waiting for transfers between devices, body(): lax.all_to_all(slot_grad, 'expert', split_axis=0, concat_axis=0, tiled=True)  17.3 us
    dot_general x3, matrix products, contract_rows(): lax.dot_general(left, right, (((0,), (0,)), ((), ())), preferred_element_...  15 us
    all_to_all x1, waiting for transfers between devices, body(): lax.all_to_all(slot_acts, 'expert', split_axis=0, concat_axis=0, tiled=True)  14.7 us
    all_gather x1, blocking collectives, body(): lax.all_gather(acts, 'tensor', axis=1, tiled=True)  9.8 us
    all_gather x1, blocking collectives, body(): lax.all_gather(grad_out, 'tensor', axis=1, tiled=True)  9.32 us
    all_to_all x1, starting transfers between devices, body(): lax.all_to_all(slot_grad, 'expert', split_axis=0, concat_axis=0, tiled=True)  7.63 us
  transfers between devices with their start and end apart: 4, of which 4 were waited for; matrix products, arithmetic and copies ran while one was open for 15% of the time, Pallas kernels for 0%

commit v1 on v0

v1 whole, which is shorter than its diff:
```python
import functools

import jax
import jax.numpy as jnp
from jax import lax
from jax.experimental import pallas as pl
from jax.experimental.pallas import tpu as pltpu
from jax.sharding import PartitionSpec as P

F32 = jnp.float32
BF16 = jnp.bfloat16
VMEM_LIMIT = 56 * 1024 * 1024


def dot(left, right, left_dim, right_dim):
    return lax.dot_general(
        left, right, (((left_dim,), (right_dim,)), ((), ())), preferred_element_type=F32
    )


def gate_of(routing, gates, expert):
    return jnp.sum(jnp.where(routing == expert, gates, 0.0), axis=1, keepdims=True)


def hidden_grads(gate_pre, up_pre, grad_hidden):
    sig = jax.nn.sigmoid(gate_pre)
    act = gate_pre * sig
    hidden = (act * up_pre).astype(BF16)
    grad_up_pre = (grad_hidden * act).astype(BF16)
    grad_gate_pre = (grad_hidden * up_pre * sig * (1.0 + gate_pre * (1.0 - sig))).astype(BF16)
    return hidden, grad_gate_pre, grad_up_pre


def middle_kernel(place, *refs):
    own, sib = refs[0:4], refs[4:8]
    wg, wu, wd = refs[8:11]
    x_out, g_out, hid, dg, du, keep, send = refs[11:18]
    wgv, wuv, wdv, sems = refs[18:22]
    chip, core = place[0] // 2, place[0] % 2
    width = own[0].shape[2]
    wide = 2 * width
    hidden_count = wgv.shape[1]
    step = 256
    chunks = hidden_count // step
    copies = []
    for f in range(chunks):
        group = []
        cols = pl.ds(f * step, step)
        for p in range(4):
            rows = pl.ds(pl.multiple_of((chip ^ p) * wide, wide), wide)
            here = pl.ds(p * wide, wide)
            group.append(pltpu.make_async_copy(wg.at[rows, cols], wgv.at[here, cols], sems.at[f, p]))
            group.append(pltpu.make_async_copy(wu.at[rows, cols], wuv.at[here, cols], sems.at[f, 4 + p]))
            group.append(pltpu.make_async_copy(wd.at[cols, rows], wdv.at[cols, here], sems.at[f, 8 + p]))
        for copy in group:
            copy.start()
        copies.append(group)
    first = core == 0
    for p in range(4):
        for array, out in ((0, x_out), (1, g_out)):
            mine, other = own[p][array], sib[p][array]
            out[:, p * wide : p * wide + width] = jnp.where(first, mine, other)
            out[:, p * wide + width : (p + 1) * wide] = jnp.where(first, other, mine)
    for f in range(chunks):
        cols = slice(f * step, (f + 1) * step)
        for copy in copies[f]:
            copy.wait()
        gate_pre = dot(x_out[...], wgv[:, cols], 1, 0)
        up_pre = dot(x_out[...], wuv[:, cols], 1, 0)
        grad_hidden = dot(g_out[...], wdv[cols, :], 1, 1)
        hid[:, cols], dg[:, cols], du[:, cols] = hidden_grads(gate_pre, up_pre, grad_hidden)
    for p in (3, 1, 2, 0):
        rows = slice(p * wide, (p + 1) * wide)
        part = dot(dg[...], wgv[rows, :], 1, 1) + dot(du[...], wuv[rows, :], 1, 1)
        low, high = part[:, :width], part[:, width:]
        keep[p] = jnp.where(first, low, high)
        send[p] = jnp.where(first, high, low).astype(BF16)


def middle(place, own, sib, wg, wu, wd):
    rows, width = own[0].shape[1:]
    full, hidden_count = wg.shape
    vmem = pl.BlockSpec(memory_space=pltpu.VMEM)
    hbm = pl.BlockSpec(memory_space=pl.ANY)
    shape = jax.ShapeDtypeStruct
    flops = 2 * rows * full * hidden_count * 5
    return pl.pallas_call(
        middle_kernel,
        out_shape=(
            shape((rows, full), BF16),
            shape((rows, full), BF16),
            shape((rows, hidden_count), BF16),
            shape((rows, hidden_count), BF16),
            shape((rows, hidden_count), BF16),
            shape((4, rows, width), F32),
            shape((4, rows, width), BF16),
        ),
        in_specs=[pl.BlockSpec(memory_space=pltpu.SMEM)] + [vmem] * 8 + [hbm] * 3,
        out_specs=[vmem] * 7,
        scratch_shapes=[
            pltpu.VMEM((full, hidden_count), BF16),
            pltpu.VMEM((full, hidden_count), BF16),
            pltpu.VMEM((hidden_count, full), BF16),
            pltpu.SemaphoreType.DMA((hidden_count // 256, 12)),
        ],
        compiler_params=pltpu.CompilerParams(vmem_limit_bytes=VMEM_LIMIT),
        cost_estimate=pl.CostEstimate(
            flops=flops, bytes_accessed=6 * full * hidden_count, transcendentals=rows * hidden_count
        ),
    )(place, *own, *sib, wg, wu, wd)


def rows_kernel(place, x, d, out):
    out[...] = dot(x[...], d[...], 0, 0).astype(BF16)


def grad_in(place, x, d):
    rows, full = x.shape
    hidden_count = d.shape[1]
    wide = full // 4
    return pl.pallas_call(
        rows_kernel,
        out_shape=jax.ShapeDtypeStruct((full, hidden_count), BF16),
        grid_spec=pltpu.PrefetchScalarGridSpec(
            num_scalar_prefetch=1,
            grid=(4,),
            in_specs=[
                pl.BlockSpec((rows, wide), lambda p, place: (0, p)),
                pl.BlockSpec((rows, hidden_count), lambda p, place: (0, 0)),
            ],
            out_specs=pl.BlockSpec((wide, hidden_count), lambda p, place: ((place[0] // 2) ^ p, 0)),
        ),
        compiler_params=pltpu.CompilerParams(vmem_limit_bytes=VMEM_LIMIT),
        cost_estimate=pl.CostEstimate(
            flops=2 * rows * full * hidden_count, bytes_accessed=2 * full * hidden_count, transcendentals=0
        ),
    )(place, x, d)


def grad_out_of(place, h, g):
    rows, full = g.shape
    hidden_count = h.shape[1]
    wide = full // 4
    return pl.pallas_call(
        rows_kernel,
        out_shape=jax.ShapeDtypeStruct((hidden_count, full), BF16),
        grid_spec=pltpu.PrefetchScalarGridSpec(
            num_scalar_prefetch=1,
            grid=(4,),
            in_specs=[
                pl.BlockSpec((rows, hidden_count), lambda p, place: (0, 0)),
                pl.BlockSpec((rows, wide), lambda p, place: (0, p)),
            ],
            out_specs=pl.BlockSpec((hidden_count, wide), lambda p, place: (0, (place[0] // 2) ^ p)),
        ),
        compiler_params=pltpu.CompilerParams(vmem_limit_bytes=VMEM_LIMIT),
        cost_estimate=pl.CostEstimate(
            flops=2 * rows * full * hidden_count, bytes_accessed=2 * full * hidden_count, transcendentals=0
        ),
    )(place, h, g)


def across(array, mask):
    return lax.ppermute(array, "tensor", [(i, i ^ mask) for i in range(8)])


def along(array, distance, count):
    return lax.ppermute(array, "expert", [(i, (i + distance) % count) for i in range(count)])


def chips_body(acts, grad_out, routing, gates, w_gate, w_up, w_down):
    groups = lax.axis_size("expert")
    z = lax.axis_index("expert")
    place = lax.axis_index("tensor").astype(jnp.int32)[None]
    tok_count, width = acts.shape
    grad_wide = grad_out.astype(F32)

    def for_expert(distance):
        gate = gate_of(routing, gates, (z + distance) % groups)
        return jnp.stack([acts, (grad_wide * gate).astype(BF16)])

    blocks = [for_expert(0)] + [along(for_expert(k), k, groups) for k in range(1, groups)]
    own_piece = jnp.concatenate(blocks, axis=1)
    own = [own_piece] + [across(own_piece, 2 * p) for p in range(1, 4)]
    sib = [across(piece, 1) for piece in own]
    wg, wu, wd = w_gate[0], w_up[0], w_down[0]
    x_all, g_all, hid, dg, du, keep, send = middle(place, own, sib, wg, wu, wd)
    from_core = across(send, 1)
    grad_gate = grad_in(place, x_all, dg)
    grad_up = grad_in(place, x_all, du)
    grad_down = grad_out_of(place, hid, g_all)
    total = keep + from_core.astype(F32)
    parts = total[1:].astype(BF16)
    mine = total[0]
    for p in range(1, 4):
        mine = mine + across(parts[p - 1], 2 * p).astype(F32)
    mine = mine.reshape(groups, tok_count, width)
    back = mine[0]
    sent = mine.astype(BF16)
    for k in range(1, groups):
        back = back + along(sent[k], -k, groups).astype(F32)
    return (grad_gate[None], grad_up[None], grad_down[None], back.astype(BF16))


def any_body(acts, grad_out, routing, gates, w_gate, w_up, w_down):
    expert = lax.axis_index("expert")
    acts_all, grad_all = (
        lax.all_gather(
            lax.all_gather(array, "tensor", axis=1, tiled=True), "expert", axis=0, tiled=True
        )
        for array in (acts, grad_out)
    )
    routing_all = lax.all_gather(routing, "expert", axis=0, tiled=True)
    gates_all = lax.all_gather(gates, "expert", axis=0, tiled=True)
    grad_all = (grad_all.astype(F32) * gate_of(routing_all, gates_all, expert)).astype(BF16)
    wg, wu, wd = w_gate[0], w_up[0], w_down[0]
    hid, dg, du = hidden_grads(dot(acts_all, wg, 1, 0), dot(acts_all, wu, 1, 0), dot(grad_all, wd, 1, 1))
    partial = dot(dg, wg, 1, 1) + dot(du, wu, 1, 1)
    partial = lax.psum_scatter(partial, "tensor", scatter_dimension=1, tiled=True)
    back = lax.psum_scatter(partial, "expert", scatter_dimension=0, tiled=True)
    return (
        dot(acts_all, dg, 0, 0).astype(BF16)[None],
        dot(acts_all, du, 0, 0).astype(BF16)[None],
        dot(hid, grad_all, 0, 0).astype(BF16)[None],
        back.astype(BF16),
    )


def solution(mesh):
    chips = mesh.shape["tensor"] == 8
    return jax.shard_map(
        chips_body if chips else any_body,
        mesh=mesh,
        in_specs=(
            P("expert", "tensor"),
            P("expert", "tensor"),
            P("expert", None),
            P("expert", None),
            P("expert", None, "tensor"),
            P("expert", None, "tensor"),
            P("expert", "tensor", None),
        ),
        out_specs=(
            P("expert", None, "tensor"),
            P("expert", None, "tensor"),
            P("expert", "tensor", None),
            P("expert", "tensor"),
        ),
        check_vma=False,
    )
```

time: 168 us -> 78.3 us (0.47); the launches traced: 165 us -> 77.7 us
  waiting for transfers between devices: 65.9 us -> 21.2 us
  matrix products: 43.9 us -> 0 us
  Pallas kernels: 0 us -> 32.1 us
  blocking collectives: 19.1 us -> 0 us
  between operations: 14.1 us -> 0.82 us
  other arithmetic: 2.94 us -> 5.33 us
    dot_general x12 -> x0, matrix products: 43.9 us -> none  [the longest x3 17.3 us: contract_cols(): lax.dot_general(left, right, (((1,), (1,)), ((), ())), preferred_element_...]
    reduce_scatter x1 -> x0, waiting for transfers between devices: 33.1 us -> none  [body(): lax.psum_scatter(contract_cols(gate_shard, grad_gate_pre) + contract_cols...]
    all_to_all x3 -> x0, waiting for transfers between devices: 32.8 us -> none  [the longest x1 17.3 us: body(): lax.all_to_all(slot_grad, 'expert', split_axis=0, concat_axis=0, tiled=True)]
    pallas_call x0 -> x4, Pallas kernels: none -> 32.1 us  [the longest x1 15.2 us: middle(): pl.pallas_call(middle_kernel, out_shape=(shape((rows, full), BF16), shape...]
    ppermute x0 -> x17, waiting for transfers between devices: none -> 21.2 us  [the longest x11 16.2 us: across(): return lax.ppermute(array, 'tensor', [(i, i ^ mask) for i in range(8)])]
    all_gather x2 -> x0, blocking collectives: 19.1 us -> none  [the longest x1 9.8 us: body(): lax.all_gather(acts, 'tensor', axis=1, tiled=True)]
    all_to_all x3 -> x0, starting transfers between devices: 18.1 us -> none  [the longest x1 7.63 us: body(): lax.all_to_all(slot_grad, 'expert', split_axis=0, concat_axis=0, tiled=True)]
    ppermute x0 -> x17, starting transfers between devices: none -> 17.5 us  [the longest x6 9.7 us: along(): lax.ppermute(array, 'expert', [(i, (i + distance) % count) for i in range...]
  transfers between devices with their start and end apart: 4 -> 17, of which waited for: 4 -> 8; matrix products, arithmetic and copies ran while one was open for 15% -> 0% of each run, Pallas kernels for 0% -> 22%
where the time goes in v1:
time: 78.3 us; the launch traced here: 77.7 us
  Pallas kernels  32.1 us (41%)
  waiting for transfers between devices  21.2 us (27%)
  starting transfers between devices  17.5 us (22%)
  other arithmetic  5.33 us (7%)
  between operations  0.82 us (1%)
    ppermute x11, waiting for transfers between devices, across(): return lax.ppermute(array, 'tensor', [(i, i ^ mask) for i in range(8)])  16.2 us
    pallas_call x1, Pallas kernels, middle(): pl.pallas_call(middle_kernel, out_shape=(shape((rows, full), BF16), shape...  15.2 us
    pallas_call x2, Pallas kernels, grad_in(): pl.pallas_call(rows_kernel, out_shape=jax.ShapeDtypeStruct((full, hidden_...  11.2 us
    ppermute x6, starting transfers between devices, along(): lax.ppermute(array, 'expert', [(i, (i + distance) % count) for i in range...  9.7 us
    ppermute x11, starting transfers between devices, across(): return lax.ppermute(array, 'tensor', [(i, i ^ mask) for i in range(8)])  7.81 us
    pallas_call x1, Pallas kernels, grad_out_of(): pl.pallas_call(rows_kernel, out_shape=jax.ShapeDtypeStruct((hidden_count,...  5.67 us
    ppermute x6, waiting for transfers between devices, along(): lax.ppermute(array, 'expert', [(i, (i + distance) % count) for i in range...  4.99 us
    another operation x2, other arithmetic, for_expert(): return jnp.stack([acts, (grad_wide * gate).astype(BF16)])  1.65 us
  transfers between devices with their start and end apart: 17, of which 8 were waited for; matrix products, arithmetic and copies ran while one was open for 0% of the time, Pallas kernels for 22%

profile of v1, /device:TPU:8, one launch (start us, length us, event | category | flops | bytes accessed | tf_op | source)
XLA Modules:
  0.0 77.7 jit_solution(7653703157305043269)
XLA Ops:
  0.7 0.7 fusion.14
  1.4 0.9 %fusion.13 = (bf16[1,48,384]{2,1,0:T(8,128)(2,1)S(1)}, bf16[1,48,384]{2,1,0:T(8,128)(2,1)S(1)}, bf16[1,48,384]{2,1,0:T(8,128)(2,1)S(1)}, bf16[1,48,384]{2,1,0:T(8,128)(2,1)S(1)}) fusion(bf16[48,384]{1,0:T(8,128)(2,1)} %param.8, f32[48]{0:T(128)S(1)} %get-tuple-element.18, f32[48]{0:T(128)S(1)} %get-tuple-element.19, f32[48]{0:T(128)S(1)} %get-tuple-element.21, ...), kind=kLoop, calls=%fused_computation.27 | loop fusion | flops 165888 | bytes 185088 | tf_op jit(solution)/shard_map/stack | solution.py:180
  2.3 0.8 %pad_maximum_fusion.3 = (bf16[2,48,384]{2,1,0:T(8,128)(2,1)S(1)}, bf16[2,48,384]{2,1,0:T(8,128)(2,1)S(1)}, bf16[2,48,384]{2,1,0:T(8,128)(2,1)S(1)}) fusion(bf16[1,48,384]{2,1,0:T(8,128)(2,1)} %bitcast.34, bf16[1,48,384]{2,1,0:T(8,128)(2,1)S(1)} %get-tuple-element.33, bf16[1,48,384]{2,1,0:T(8,128)(2,1)S(1)} %get-tuple-element.34, ...), kind=kLoop, calls=%fused_computation.15 | loop fusion | flops 110592 | bytes 368640 | tf_op jit(solution)/shard_map/stack | solution.py:180
  3.1 1.6 %collective-permute-start = (bf16[2,48,384]{2,1,0:T(8,128)(2,1)S(1)}, bf16[2,48,384]{2,1,0:T(8,128)(2,1)S(1)}, u32[]{:S(2)}, u32[]{:S(2)}) collective-permute-start(bf16[2,48,384]{2,1,0:T(8,128)(2,1)S(1)} %get-tuple-element.36), channel_id=1, source_target_pairs={{0,1},{1,2},{2,3},{3,0},{4,5},{5,6},{6,7},{7,4},{8,9},{9,10},{10,1... | collective-permute-start | bytes 221192 | tf_op jit(solution)/shard_map/ppermute | solution.py:168
  4.7 1.1 %collective-permute-start.1 = (bf16[2,48,384]{2,1,0:T(8,128)(2,1)S(1)}, bf16[2,48,384]{2,1,0:T(8,128)(2,1)S(1)}, u32[]{:S(2)}, u32[]{:S(2)}) collective-permute-start(bf16[2,48,384]{2,1,0:T(8,128)(2,1)S(1)} %get-tuple-element.37), channel_id=1, source_target_pairs={{0,2},{1,3},{2,0},{3,1},{4,6},{5,7},{6,4},{7,5},{8,10},{9,11},{10,... | collective-permute-start | bytes 221192 | tf_op jit(solution)/shard_map/ppermute | solution.py:168
  5.8 1.9 %collective-permute-start.2 = (bf16[2,48,384]{2,1,0:T(8,128)(2,1)S(1)}, bf16[2,48,384]{2,1,0:T(8,128)(2,1)S(1)}, u32[]{:S(2)}, u32[]{:S(2)}) collective-permute-start(bf16[2,48,384]{2,1,0:T(8,128)(2,1)S(1)} %get-tuple-element.38), channel_id=1, source_target_pairs={{0,3},{1,0},{2,1},{3,2},{4,7},{5,4},{6,5},{7,6},{8,11},{9,8},{10,9... | collective-permute-start | bytes 221192 | tf_op jit(solution)/shard_map/ppermute | solution.py:168
  7.7 2.0 %collective-permute-done = bf16[2,48,384]{2,1,0:T(8,128)(2,1)S(1)} collective-permute-done((bf16[2,48,384]{2,1,0:T(8,128)(2,1)S(1)}, bf16[2,48,384]{2,1,0:T(8,128)(2,1)S(1)}, u32[]{:S(2)}, u32[]{:S(2)}) %collective-permute-start) | collective-permute-done | bytes 73760 | tf_op jit(solution)/shard_map/ppermute | solution.py:168
  9.7 1.5 %collective-permute-done.1 = bf16[2,48,384]{2,1,0:T(8,128)(2,1)S(1)} collective-permute-done((bf16[2,48,384]{2,1,0:T(8,128)(2,1)S(1)}, bf16[2,48,384]{2,1,0:T(8,128)(2,1)S(1)}, u32[]{:S(2)}, u32[]{:S(2)}) %collective-permute-start.1) | collective-permute-done | bytes 73760 | tf_op jit(solution)/shard_map/ppermute | solution.py:168
  11.2 1.5 %collective-permute-done.2 = bf16[2,48,384]{2,1,0:T(8,128)(2,1)S(1)} collective-permute-done((bf16[2,48,384]{2,1,0:T(8,128)(2,1)S(1)}, bf16[2,48,384]{2,1,0:T(8,128)(2,1)S(1)}, u32[]{:S(2)}, u32[]{:S(2)}) %collective-permute-start.2) | collective-permute-done | bytes 73760 | tf_op jit(solution)/shard_map/ppermute | solution.py:168
  12.7 0.8 %pad_maximum_fusion.refs_0_ = bf16[2,192,384]{2,1,0:T(8,128)(2,1)S(1)} fusion(bf16[2,48,384]{2,1,0:T(8,128)(2,1)S(1)} %collective-permute-done.2, bf16[2,48,384]{2,1,0:T(8,128)(2,1)S(1)} %collective-permute-done.1, bf16[2,48,384]{2,1,0:T(8,128)(2,1)S(1)} %collective-permute-done, bf16[1,48,384]{2,1,0:T(8,128)(2,1)S(1)} %get-tuple-element.32, ...), kind=kLoop, calls=%fused_computation.5 | loop fusion | flops 1474560 | bytes 589824 | tf_op jit(solution)/shard_map/concatenate | solution.py:183
  13.5 2.5 %collective-permute-start.5 = (bf16[2,192,384]{2,1,0:T(8,128)(2,1)S(1)}, bf16[2,192,384]{2,1,0:T(8,128)(2,1)S(1)}, u32[]{:S(2)}, u32[]{:S(2)}) collective-permute-start(bf16[2,192,384]{2,1,0:T(8,128)(2,1)S(1)} %pad_maximum_fusion.refs_0_), channel_id=1, source_target_pairs={{0,24},{4,28},{8,16},{12,20},{16,8},{20,12},{24,0},{28,4},{1,25},{... | collective-permute-start | bytes 884744 | tf_op jit(solution)/shard_map/ppermute | solution.py:164
  16.0 0.5 collective-permute-start.4
  16.5 0.5 collective-permute-start.3
  17.1 7.3 %collective-permute-done.5.refs_3_ = bf16[2,192,384]{2,1,0:T(8,128)(2,1)S(1)} collective-permute-done((bf16[2,192,384]{2,1,0:T(8,128)(2,1)S(1)}, bf16[2,192,384]{2,1,0:T(8,128)(2,1)S(1)}, u32[]{:S(2)}, u32[]{:S(2)}) %collective-permute-start.5) | collective-permute-done | bytes 294944 | tf_op jit(solution)/shard_map/ppermute | solution.py:164
  24.4 5.3 %collective-permute-done.4.refs_2_ = bf16[2,192,384]{2,1,0:T(8,128)(2,1)S(1)} collective-permute-done((bf16[2,192,384]{2,1,0:T(8,128)(2,1)S(1)}, bf16[2,192,384]{2,1,0:T(8,128)(2,1)S(1)}, u32[]{:S(2)}, u32[]{:S(2)}) %collective-permute-start.4) | collective-permute-done | bytes 294944 | tf_op jit(solution)/shard_map/ppermute | solution.py:164
  29.8 0.5 collective-permute-start.7
  30.3 1.0 %collective-permute-done.8.refs_6_ = bf16[2,192,384]{2,1,0:T(8,128)(2,1)S(1)} collective-permute-done((bf16[2,192,384]{2,1,0:T(8,128)(2,1)S(1)}, bf16[2,192,384]{2,1,0:T(8,128)(2,1)S(1)}, u32[]{:S(2)}, u32[]{:S(2)}) %collective-permute-start.8) | collective-permute-done | bytes 294944 | tf_op jit(solution)/shard_map/ppermute | solution.py:164
  31.3 0.4 collective-permute-done.7.refs_5_
  31.8 0.3 copy-done.6
  32.0 0.4 copy-done.7
  32.4 15.2 %shard_map.102 = (bf16[192,3072]{1,0:T(8,128)(2,1)}, bf16[192,3072]{1,0:T(8,128)(2,1)}, bf16[192,1024]{1,0:T(8,128)(2,1)}, bf16[192,1024]{1,0:T(8,128)(2,1)}, bf...) custom-call(s32[1]{0:T(128)} %bitcast.place, bf16[2,192,384]{2,1,0:T(8,128)(2,1)} %copy-done, ...), custom_call_target="tpu_custom_call" | custom-call | flops 6039797760 | bytes 18874368 | tf_op jit(solution)/shard_map/pallas_call | solution.py:87
  47.8 2.1 %collective-permute-done.10 = bf16[4,192,384]{2,1,0:T(8,128)(2,1)S(1)} collective-permute-done((bf16[4,192,384]{2,1,0:T(8,128)(2,1)}, bf16[4,192,384]{2,1,0:T(8,128)(2,1)S(1)}, u32[]{:S(2)}, u32[]{:S(2)}) %collective-permute-start.10) | collective-permute-done | bytes 589856 | tf_op jit(solution)/shard_map/ppermute | solution.py:164
  49.9 1.5 %fusion.20 = (bf16[4,192,384]{2,1,0:T(8,128)(2,1)S(1)}, f32[4,192,384]{2,1,0:T(8,128)S(1)}) fusion(f32[4,192,384]{2,1,0:T(8,128)} %get-tuple-element.16, bf16[4,192,384]{2,1,0:T(8,128)(2,1)S(1)} %collective-permute-done.10), kind=kLoop, calls=%fused_computation.37 | loop fusion | flops 884736 | bytes 3538944 | tf_op jit(solution)/shard_map/convert
  51.5 1.4 %collective-permute-start.11 = (bf16[192,384]{1,0:T(8,128)(2,1)S(1)}, bf16[192,384]{1,0:T(8,128)(2,1)S(1)}, u32[]{:S(2)}, u32[]{:S(2)}) collective-permute-start(bf16[192,384]{1,0:T(8,128)(2,1)S(1)} %get-tuple-element.26), channel_id=1, source_target_pairs={{0,8},{4,12},{8,0},{12,4},{16,24},{20,28},{24,16},{28,20},{1,9},{5... | collective-permute-start | bytes 442376 | tf_op jit(solution)/shard_map/ppermute | solution.py:164
  52.8 1.5 %collective-permute-start.13 = (bf16[192,384]{1,0:T(8,128)(2,1)S(1)}, bf16[192,384]{1,0:T(8,128)(2,1)S(1)}, u32[]{:S(2)}, u32[]{:S(2)}) collective-permute-start(bf16[192,384]{1,0:T(8,128)(2,1)S(1)} %get-tuple-element.27), channel_id=1, source_target_pairs={{0,24},{4,28},{8,16},{12,20},{16,8},{20,12},{24,0},{28,4},{1,25},{... | collective-permute-start | bytes 442376 | tf_op jit(solution)/shard_map/ppermute | solution.py:164
  54.3 0.7 collective-permute-start.12
  55.0 5.6 %shard_map.103 = bf16[3072,1024]{1,0:T(8,128)(2,1)} custom-call(s32[1]{0:T(128)} %bitcast.place, bf16[192,3072]{1,0:T(8,128)(2,1)} %get-tuple-element.11.x, bf16[192,1024]{1,0:T(8,128)(2,1)} %get-tuple-element.12.d), custom_call_target="tpu_custom_call" | custom-call | flops 1207959552 | bytes 6291456 | tf_op jit(solution)/shard_map/pallas_call | solution.py:121
  60.6 5.6 %shard_map.104 = bf16[3072,1024]{1,0:T(8,128)(2,1)} custom-call(s32[1]{0:T(128)} %bitcast.place, bf16[192,3072]{1,0:T(8,128)(2,1)} %get-tuple-element.11.x, bf16[192,1024]{1,0:T(8,128)(2,1)} %get-tuple-element.13.d), custom_call_target="tpu_custom_call" | custom-call | flops 1207959552 | bytes 6291456 | tf_op jit(solution)/shard_map/pallas_call | solution.py:121
  66.4 2.0 %collective-permute-start.16 = (bf16[48,384]{1,0:T(8,128)(2,1)S(1)}, bf16[48,384]{1,0:T(8,128)(2,1)S(1)}, u32[]{:S(2)}, u32[]{:S(2)}) collective-permute-start(bf16[48,384]{1,0:T(8,128)(2,1)S(1)} %get-tuple-element.30), channel_id=1, source_target_pairs={{0,1},{1,2},{2,3},{3,0},{4,5},{5,6},{6,7},{7,4},{8,9},{9,10},{10,1... | collective-permute-start | bytes 110600 | tf_op jit(solution)/shard_map/ppermute | solution.py:168
  68.4 3.0 %collective-permute-start.15 = (bf16[48,384]{1,0:T(8,128)(2,1)S(1)}, bf16[48,384]{1,0:T(8,128)(2,1)S(1)}, u32[]{:S(2)}, u32[]{:S(2)}) collective-permute-start(bf16[48,384]{1,0:T(8,128)(2,1)S(1)} %get-tuple-element.31), channel_id=1, source_target_pairs={{0,2},{1,3},{2,0},{3,1},{4,6},{5,7},{6,4},{7,5},{8,10},{9,11},{10,... | collective-permute-start | bytes 110600 | tf_op jit(solution)/shard_map/ppermute | solution.py:168
  71.4 5.7 %shard_map.105 = bf16[1024,3072]{1,0:T(8,128)(2,1)} custom-call(s32[1]{0:T(128)} %bitcast.place, bf16[192,1024]{1,0:T(8,128)(2,1)} %get-tuple-element.14.x, bf16[192,3072]{1,0:T(8,128)(2,1)} %get-tuple-element.15.d), custom_call_target="tpu_custom_call" | custom-call | flops 1207959552 | bytes 6291456 | tf_op jit(solution)/shard_map/pallas_call | solution.py:144
  77.1 0.6 fusion.9
  (31 shorter events, 0.5 us)
Async XLA Ops:
  3.1 6.7 %collective-permute-start = (bf16[2,48,384]{2,1,0:T(8,128)(2,1)S(1)}, bf16[2,48,384]{2,1,0:T(8,128)(2,1)S(1)}, u32[]{:S(2)}, u32[]{:S(2)}) collective-permute-start(bf16[2,48,384]{2,1,0:T(8,128)(2,1)S(1)} %get-tuple-element.36), channel_id=1, source_target_pairs={{0,1},{1,2},{2,3},{3,0},{4,5},{5,6},{6,7},{7,4},{8,9},{9,10},{10,1... | collective-permute-start | bytes 221192 | tf_op jit(solution)/shard_map/ppermute | solution.py:168
  4.7 6.6 %collective-permute-start.1 = (bf16[2,48,384]{2,1,0:T(8,128)(2,1)S(1)}, bf16[2,48,384]{2,1,0:T(8,128)(2,1)S(1)}, u32[]{:S(2)}, u32[]{:S(2)}) collective-permute-start(bf16[2,48,384]{2,1,0:T(8,128)(2,1)S(1)} %get-tuple-element.37), channel_id=1, source_target_pairs={{0,2},{1,3},{2,0},{3,1},{4,6},{5,7},{6,4},{7,5},{8,10},{9,11},{10,... | collective-permute-start | bytes 221192 | tf_op jit(solution)/shard_map/ppermute | solution.py:168
  5.8 6.9 %collective-permute-start.2 = (bf16[2,48,384]{2,1,0:T(8,128)(2,1)S(1)}, bf16[2,48,384]{2,1,0:T(8,128)(2,1)S(1)}, u32[]{:S(2)}, u32[]{:S(2)}) collective-permute-start(bf16[2,48,384]{2,1,0:T(8,128)(2,1)S(1)} %get-tuple-element.38), channel_id=1, source_target_pairs={{0,3},{1,0},{2,1},{3,2},{4,7},{5,4},{6,5},{7,6},{8,11},{9,8},{10,9... | collective-permute-start | bytes 221192 | tf_op jit(solution)/shard_map/ppermute | solution.py:168
  13.5 18.2 %copy-start = (bf16[2,192,384]{2,1,0:T(8,128)(2,1)}, bf16[2,192,384]{2,1,0:T(8,128)(2,1)S(1)}, u32[]{:S(2)}) copy-start(bf16[2,192,384]{2,1,0:T(8,128)(2,1)S(1)} %pad_maximum_fusion.refs_0_) | copy-start | bytes 884740
  13.5 10.9 %collective-permute-start.5 = (bf16[2,192,384]{2,1,0:T(8,128)(2,1)S(1)}, bf16[2,192,384]{2,1,0:T(8,128)(2,1)S(1)}, u32[]{:S(2)}, u32[]{:S(2)}) collective-permute-start(bf16[2,192,384]{2,1,0:T(8,128)(2,1)S(1)} %pad_maximum_fusion.refs_0_), channel_id=1, source_target_pairs={{0,24},{4,28},{8,16},{12,20},{16,8},{20,12},{24,0},{28,4},{1,25},{... | collective-permute-start | bytes 884744 | tf_op jit(solution)/shard_map/ppermute | solution.py:164
  16.0 13.7 %collective-permute-start.4 = (bf16[2,192,384]{2,1,0:T(8,128)(2,1)S(1)}, bf16[2,192,384]{2,1,0:T(8,128)(2,1)S(1)}, u32[]{:S(2)}, u32[]{:S(2)}) collective-permute-start(bf16[2,192,384]{2,1,0:T(8,128)(2,1)S(1)} %pad_maximum_fusion.refs_0_), channel_id=1, source_target_pairs={{0,16},{4,20},{8,24},{12,28},{16,0},{20,4},{24,8},{28,12},{1,17},{... | collective-permute-start | bytes 884744 | tf_op jit(solution)/shard_map/ppermute | solution.py:164
  16.5 13.2 %collective-permute-start.3 = (bf16[2,192,384]{2,1,0:T(8,128)(2,1)S(1)}, bf16[2,192,384]{2,1,0:T(8,128)(2,1)S(1)}, u32[]{:S(2)}, u32[]{:S(2)}) collective-permute-start(bf16[2,192,384]{2,1,0:T(8,128)(2,1)S(1)} %pad_maximum_fusion.refs_0_), channel_id=1, source_target_pairs={{0,8},{4,12},{8,0},{12,4},{16,24},{20,28},{24,16},{28,20},{1,9},{5... | collective-permute-start | bytes 884744 | tf_op jit(solution)/shard_map/ppermute | solution.py:164
  17.1 13.2 %collective-permute-start.6 = (bf16[2,192,384]{2,1,0:T(8,128)(2,1)S(1)}, bf16[2,192,384]{2,1,0:T(8,128)(2,1)S(1)}, u32[]{:S(2)}, u32[]{:S(2)}) collective-permute-start(bf16[2,192,384]{2,1,0:T(8,128)(2,1)S(1)} %pad_maximum_fusion.refs_0_), channel_id=1, source_target_pairs={{0,4},{4,0},{8,12},{12,8},{16,20},{20,16},{24,28},{28,24},{1,5},{5... | collective-permute-start | bytes 884744 | tf_op jit(solution)/shard_map/ppermute | solution.py:164
  24.4 7.4 %copy-start.1 = (bf16[2,192,384]{2,1,0:T(8,128)(2,1)}, bf16[2,192,384]{2,1,0:T(8,128)(2,1)S(1)}, u32[]{:S(2)}) copy-start(bf16[2,192,384]{2,1,0:T(8,128)(2,1)S(1)} %collective-permute-done.5.refs_3_) | copy-start | bytes 884740
  24.4 5.9 %collective-permute-start.9 = (bf16[2,192,384]{2,1,0:T(8,128)(2,1)S(1)}, bf16[2,192,384]{2,1,0:T(8,128)(2,1)S(1)}, u32[]{:S(2)}, u32[]{:S(2)}) collective-permute-start(bf16[2,192,384]{2,1,0:T(8,128)(2,1)S(1)} %collective-permute-done.5.refs_3_), channel_id=1, source_target_pairs={{0,4},{4,0},{8,12},{12,8},{16,20},{20,16},{24,28},{28,24},{1,5},{5... | collective-permute-start | bytes 884744 | tf_op jit(solution)/shard_map/ppermute | solution.py:164
  29.7 2.0 %copy-start.2 = (bf16[2,192,384]{2,1,0:T(8,128)(2,1)}, bf16[2,192,384]{2,1,0:T(8,128)(2,1)S(1)}, u32[]{:S(2)}) copy-start(bf16[2,192,384]{2,1,0:T(8,128)(2,1)S(1)} %collective-permute-done.4.refs_2_) | copy-start | bytes 884740
  29.7 1.6 %collective-permute-start.8 = (bf16[2,192,384]{2,1,0:T(8,128)(2,1)S(1)}, bf16[2,192,384]{2,1,0:T(8,128)(2,1)S(1)}, u32[]{:S(2)}, u32[]{:S(2)}) collective-permute-start(bf16[2,192,384]{2,1,0:T(8,128)(2,1)S(1)} %collective-permute-done.4.refs_2_), channel_id=1, source_target_pairs={{0,4},{4,0},{8,12},{12,8},{16,20},{20,16},{24,28},{28,24},{1,5},{5... | collective-permute-start | bytes 884744 | tf_op jit(solution)/shard_map/ppermute | solution.py:164
  29.7 2.0 %copy-start.3 = (bf16[2,192,384]{2,1,0:T(8,128)(2,1)}, bf16[2,192,384]{2,1,0:T(8,128)(2,1)S(1)}, u32[]{:S(2)}) copy-start(bf16[2,192,384]{2,1,0:T(8,128)(2,1)S(1)} %collective-permute-done.3.refs_1_) | copy-start | bytes 884740
  29.8 2.0 %collective-permute-start.7 = (bf16[2,192,384]{2,1,0:T(8,128)(2,1)S(1)}, bf16[2,192,384]{2,1,0:T(8,128)(2,1)S(1)}, u32[]{:S(2)}, u32[]{:S(2)}) collective-permute-start(bf16[2,192,384]{2,1,0:T(8,128)(2,1)S(1)} %collective-permute-done.3.refs_1_), channel_id=1, source_target_pairs={{0,4},{4,0},{8,12},{12,8},{16,20},{20,16},{24,28},{28,24},{1,5},{5... | collective-permute-start | bytes 884744 | tf_op jit(solution)/shard_map/ppermute | solution.py:164
  30.2 1.5 %copy-start.4 = (bf16[2,192,384]{2,1,0:T(8,128)(2,1)}, bf16[2,192,384]{2,1,0:T(8,128)(2,1)S(1)}, u32[]{:S(2)}) copy-start(bf16[2,192,384]{2,1,0:T(8,128)(2,1)S(1)} %collective-permute-done.6.refs_4_) | copy-start | bytes 884740
  30.3 1.5 %copy-start.5 = (bf16[2,192,384]{2,1,0:T(8,128)(2,1)}, bf16[2,192,384]{2,1,0:T(8,128)(2,1)S(1)}, u32[]{:S(2)}) copy-start(bf16[2,192,384]{2,1,0:T(8,128)(2,1)S(1)} %collective-permute-done.9.refs_7_) | copy-start | bytes 884740
  31.3 0.7 copy-start.6
  31.7 0.7 copy-start.7
  47.7 2.3 %collective-permute-start.10 = (bf16[4,192,384]{2,1,0:T(8,128)(2,1)}, bf16[4,192,384]{2,1,0:T(8,128)(2,1)S(1)}, u32[]{:S(2)}, u32[]{:S(2)}) collective-permute-start(bf16[4,192,384]{2,1,0:T(8,128)(2,1)} %get-tuple-element.17), channel_id=1, source_target_pairs={{0,4},{4,0},{8,12},{12,8},{16,20},{20,16},{24,28},{28,24},{1,5},{5... | collective-permute-start | bytes 1769480 | tf_op jit(solution)/shard_map/ppermute | solution.py:164
  51.5 14.8 %collective-permute-start.11 = (bf16[192,384]{1,0:T(8,128)(2,1)S(1)}, bf16[192,384]{1,0:T(8,128)(2,1)S(1)}, u32[]{:S(2)}, u32[]{:S(2)}) collective-permute-start(bf16[192,384]{1,0:T(8,128)(2,1)S(1)} %get-tuple-element.26), channel_id=1, source_target_pairs={{0,8},{4,12},{8,0},{12,4},{16,24},{20,28},{24,16},{28,20},{1,9},{5... | collective-permute-start | bytes 442376 | tf_op jit(solution)/shard_map/ppermute | solution.py:164
  52.8 13.4 %collective-permute-start.13 = (bf16[192,384]{1,0:T(8,128)(2,1)S(1)}, bf16[192,384]{1,0:T(8,128)(2,1)S(1)}, u32[]{:S(2)}, u32[]{:S(2)}) collective-permute-start(bf16[192,384]{1,0:T(8,128)(2,1)S(1)} %get-tuple-element.27), channel_id=1, source_target_pairs={{0,24},{4,28},{8,16},{12,20},{16,8},{20,12},{24,0},{28,4},{1,25},{... | collective-permute-start | bytes 442376 | tf_op jit(solution)/shard_map/ppermute | solution.py:164
  54.3 11.9 %collective-permute-start.12 = (bf16[192,384]{1,0:T(8,128)(2,1)S(1)}, bf16[192,384]{1,0:T(8,128)(2,1)S(1)}, u32[]{:S(2)}, u32[]{:S(2)}) collective-permute-start(bf16[192,384]{1,0:T(8,128)(2,1)S(1)} %get-tuple-element.28), channel_id=1, source_target_pairs={{0,16},{4,20},{8,24},{12,28},{16,0},{20,4},{24,8},{28,12},{1,17},{... | collective-permute-start | bytes 442376 | tf_op jit(solution)/shard_map/ppermute | solution.py:164
  66.4 10.7 %collective-permute-start.14 = (bf16[48,384]{1,0:T(8,128)(2,1)S(1)}, bf16[48,384]{1,0:T(8,128)(2,1)S(1)}, u32[]{:S(2)}, u32[]{:S(2)}) collective-permute-start(bf16[48,384]{1,0:T(8,128)(2,1)S(1)} %get-tuple-element.29), channel_id=1, source_target_pairs={{0,3},{1,0},{2,1},{3,2},{4,7},{5,4},{6,5},{7,6},{8,11},{9,8},{10,9... | collective-permute-start | bytes 110600 | tf_op jit(solution)/shard_map/ppermute | solution.py:168
  66.4 10.6 %collective-permute-start.16 = (bf16[48,384]{1,0:T(8,128)(2,1)S(1)}, bf16[48,384]{1,0:T(8,128)(2,1)S(1)}, u32[]{:S(2)}, u32[]{:S(2)}) collective-permute-start(bf16[48,384]{1,0:T(8,128)(2,1)S(1)} %get-tuple-element.30), channel_id=1, source_target_pairs={{0,1},{1,2},{2,3},{3,0},{4,5},{5,6},{6,7},{7,4},{8,9},{9,10},{10,1... | collective-permute-start | bytes 110600 | tf_op jit(solution)/shard_map/ppermute | solution.py:168
  68.4 8.6 %collective-permute-start.15 = (bf16[48,384]{1,0:T(8,128)(2,1)S(1)}, bf16[48,384]{1,0:T(8,128)(2,1)S(1)}, u32[]{:S(2)}, u32[]{:S(2)}) collective-permute-start(bf16[48,384]{1,0:T(8,128)(2,1)S(1)} %get-tuple-element.31), channel_id=1, source_target_pairs={{0,2},{1,3},{2,0},{3,1},{4,6},{5,7},{6,4},{7,5},{8,10},{9,11},{10,... | collective-permute-start | bytes 110600 | tf_op jit(solution)/shard_map/ppermute | solution.py:168

commit v2 on v1

v2 whole, which is shorter than its diff:
```python
import functools

import jax
import jax.numpy as jnp
from jax import lax
from jax.experimental import pallas as pl
from jax.experimental.pallas import tpu as pltpu
from jax.sharding import PartitionSpec as P

F32 = jnp.float32
BF16 = jnp.bfloat16


def dot(left, right, left_dim, right_dim):
    return lax.dot_general(
        left, right, (((left_dim,), (right_dim,)), ((), ())), preferred_element_type=F32
    )


def gate_of(routing, gates, expert):
    return jnp.sum(jnp.where(routing == expert, gates, 0.0), axis=1, keepdims=True)


def hidden_grads(gate_pre, up_pre, grad_hidden):
    sig = jax.nn.sigmoid(gate_pre)
    act = gate_pre * sig
    hidden = (act * up_pre).astype(BF16)
    grad_up_pre = (grad_hidden * act).astype(BF16)
    grad_gate_pre = (grad_hidden * up_pre * sig * (1.0 + gate_pre * (1.0 - sig))).astype(BF16)
    return hidden, grad_gate_pre, grad_up_pre


VMEM = pl.BlockSpec(memory_space=pltpu.VMEM)
SMEM = pl.BlockSpec(memory_space=pltpu.SMEM)
HBM = pl.BlockSpec(memory_space=pl.ANY)


def shape(dims, dtype):
    return jax.ShapeDtypeStruct(dims, dtype)


def call(kernel, out_shape, in_specs, out_specs, flops, moved, scratch=(), limit=16, aliases={}):
    return pl.pallas_call(
        kernel,
        out_shape=out_shape,
        in_specs=in_specs,
        out_specs=out_specs,
        scratch_shapes=scratch,
        input_output_aliases=aliases,
        compiler_params=pltpu.CompilerParams(vmem_limit_bytes=limit * 1024 * 1024),
        cost_estimate=pl.CostEstimate(flops=flops, bytes_accessed=moved, transcendentals=0),
    )


def both_cores(core, mine, other):
    first = core == 0
    return jnp.concatenate([jnp.where(first, mine, other), jnp.where(first, other, mine)], axis=1)


def block_at(place, p, wide):
    return pl.ds(pl.multiple_of((place[0] // 2 ^ p) * wide, wide), wide)


STEP = 256
LOAD_LIMIT = 28


def half_at(place, m, width):
    return pl.ds(pl.multiple_of((place[0] ^ m) * width, width), width)


def pair(place, p, own, sib):
    core = place[0] % 2
    rows = block_at(place, p, 2 * own.shape[2])
    return rows, both_cores(core, own[0], sib[0]), both_cores(core, own[1], sib[1])


def half(place, m, ref):
    return half_at(place, m, ref.shape[2]), ref[0], ref[1]


def add_pieces(pieces, weights, acc_in, acc_out, finish, arrived=None):
    wg, wu, wd = weights
    for f in range(wg.shape[1] // STEP):
        cols = pl.ds(f * STEP, STEP)
        if arrived is not None:
            arrived(f)
        sums = [None if acc is None else acc[:, cols] for acc in acc_in]
        for rows, x, g in pieces:
            terms = (dot(x, wg[rows, cols], 1, 0), dot(x, wu[rows, cols], 1, 0), dot(g, wd[cols, rows], 1, 1))
            sums = [t if s is None else s + t for s, t in zip(sums, terms)]
        finish(cols, sums, acc_out)


def store(cols, sums, outs):
    for out, value in zip(outs, sums):
        out[:, cols] = value


def store_grads(cols, sums, outs):
    store(cols, hidden_grads(*sums), outs)


def load_kernel(place, own, wg, wu, wd, wg_here, wu_here, wd_here, gate, up, back, sems):
    copies = []
    for f in range(wg.shape[1] // STEP):
        cols = pl.ds(f * STEP, STEP)
        copies.append(
            [
                pltpu.make_async_copy(wg.at[:, cols], wg_here.at[:, cols], sems.at[f, 0]),
                pltpu.make_async_copy(wu.at[:, cols], wu_here.at[:, cols], sems.at[f, 1]),
                pltpu.make_async_copy(wd.at[cols, :], wd_here.at[cols, :], sems.at[f, 2]),
            ]
        )
        for copy in copies[f]:
            copy.start()

    def arrived(f):
        for copy in copies[f]:
            copy.wait()

    weights = (wg_here, wu_here, wd_here)
    add_pieces([half(place, 0, own)], weights, (None,) * 3, (gate, up, back), store, arrived)


def load_weights(place, own, weights):
    rows, hidden_count = own.shape[1], weights[0].shape[1]
    return call(
        load_kernel,
        tuple(shape(w.shape, BF16) for w in weights) + (shape((rows, hidden_count), F32),) * 3,
        [SMEM] + [VMEM] + [HBM] * 3,
        [VMEM] * 6,
        1,
        1,
        scratch=[pltpu.SemaphoreType.DMA((hidden_count // STEP, 3))],
        limit=LOAD_LIMIT,
    )(place, own, *weights)


def partial_kernel(place, near, own, sib, wg, wu, wd, *refs):
    pieces = [half(place, 1, near), pair(place, 3, own, sib)]
    add_pieces(pieces, (wg, wu, wd), refs[:3], refs[3:], store)


def partial_sums(place, near, own, sib, weights, acc):
    rows, hidden_count = own.shape[1], weights[0].shape[1]
    return call(
        partial_kernel,
        (shape((rows, hidden_count), F32),) * 3,
        [SMEM] + [VMEM] * 9,
        [VMEM] * 3,
        1,
        1,
        aliases={7: 0, 8: 1, 9: 2},
    )(place, near, own, sib, *weights, *acc)


def slot_rows(place, p, dg, du, wg, wu, wide):
    rows = block_at(place, p, wide)
    return dot(dg, wg[rows, :], 1, 1) + dot(du, wu[rows, :], 1, 1)


def middle_kernel(pieces, order, place, *refs):
    n = len(pieces)
    own, sib = refs[:n], refs[n : 2 * n]
    wg, wu, wd = refs[2 * n : 2 * n + 3]
    acc = refs[2 * n + 3 : 2 * n + 6]
    hid, dg, du, keep, send = refs[2 * n + 6 :]
    halves = [pair(place, p, o, s) for p, o, s in zip(pieces, own, sib)]
    add_pieces(halves, (wg, wu, wd), acc, (hid, dg, du), store_grads)
    width = own[0].shape[2]
    first = place[0] % 2 == 0
    for p in order:
        part = slot_rows(place, p, dg[...], du[...], wg, wu, 2 * width)
        low, high = part[:, :width], part[:, width:]
        keep[p - 1] = jnp.where(first, low, high)
        send[p - 1] = jnp.where(first, high, low).astype(BF16)


def middle(place, pieces, own, sib, weights, acc):
    rows, width = own[0].shape[1:]
    hidden_count = weights[0].shape[1]
    return call(
        functools.partial(middle_kernel, pieces, (3, 1, 2)),
        (shape((rows, hidden_count), BF16),) * 3
        + (shape((3, rows, width), F32), shape((3, rows, width), BF16)),
        [SMEM] + [VMEM] * (2 * len(pieces) + 6),
        [VMEM] * 5,
        24 * rows * width * hidden_count * 2,
        0,
    )(place, *own, *sib, *weights, *acc)


def own_slot_kernel(place, dg, du, wg, wu, keep, send):
    width = keep.shape[1]
    first = place[0] % 2 == 0
    part = slot_rows(place, 0, dg[...], du[...], wg, wu, 2 * width)
    low, high = part[:, :width], part[:, width:]
    keep[...] = jnp.where(first, low, high)
    send[...] = jnp.where(first, high, low).astype(BF16)


def own_slot(place, dg, du, wg, wu):
    rows, hidden_count = dg.shape
    width = wg.shape[0] // 8
    return call(
        own_slot_kernel,
        (shape((rows, width), F32), shape((rows, width), BF16)),
        [SMEM] + [VMEM] * 4,
        [VMEM] * 2,
        8 * rows * width * hidden_count,
        0,
    )(place, dg, du, wg, wu)


def weight_kernel(array, place, *refs):
    own, sib, d, out, buf, sems = refs[0:4], refs[4:8], refs[8], refs[9], refs[10], refs[11]
    core = place[0] % 2
    wide = 2 * own[0].shape[2]
    copies = []
    for p in range(4):
        rows = block_at(place, p, wide)
        piece = both_cores(core, own[p][array], sib[p][array])
        if array == 0:
            buf[p] = dot(piece, d[...], 0, 0).astype(BF16)
            target = out.at[rows, :]
        else:
            buf[p] = dot(d[...], piece, 0, 0).astype(BF16)
            target = out.at[:, rows]
        copies.append(pltpu.make_async_copy(buf.at[p], target, sems.at[p]))
        copies[p].start()
    for copy in copies:
        copy.wait()


def weight_grad(place, array, own, sib, d):
    rows, width = own[0].shape[1:]
    hidden_count = d.shape[1]
    block = (2 * width, hidden_count) if array == 0 else (hidden_count, 2 * width)
    out = (8 * width, hidden_count) if array == 0 else (hidden_count, 8 * width)
    return call(
        functools.partial(weight_kernel, array),
        shape(out, BF16),
        [SMEM] + [VMEM] * 9,
        HBM,
        16 * rows * width * hidden_count,
        16 * width * hidden_count,
        scratch=[pltpu.VMEM((4,) + block, BF16), pltpu.SemaphoreType.DMA((4,))],
    )(place, *own, *sib, d)


def across(array, mask):
    return lax.ppermute(array, "tensor", [(i, i ^ mask) for i in range(8)])


def along(array, distance, count):
    return lax.ppermute(array, "expert", [(i, (i + distance) % count) for i in range(count)])


def chips_body(acts, grad_out, routing, gates, w_gate, w_up, w_down):
    groups = lax.axis_size("expert")
    z = lax.axis_index("expert")
    place = lax.axis_index("tensor").astype(jnp.int32)[None]
    tok_count, width = acts.shape
    grad_wide = grad_out.astype(F32)

    def for_expert(distance):
        gate = gate_of(routing, gates, (z + distance) % groups)
        return jnp.stack([acts, (grad_wide * gate).astype(BF16)])

    blocks = [for_expert(0)] + [along(for_expert(k), k, groups) for k in range(1, groups)]
    own_piece = jnp.concatenate(blocks, axis=1)
    own = [own_piece] + [across(own_piece, 2 * p) for p in range(1, 4)]
    near = across(own[0], 1)
    weights = (w_gate[0], w_up[0], w_down[0])
    loaded = load_weights(place, own[0], weights)
    weights, acc = loaded[:3], loaded[3:]
    *own[1:], acc = lax.optimization_barrier((*own[1:], acc))
    sib = [near] + [across(piece, 1) for piece in own[1:]]
    acc = partial_sums(place, near, own[3], sib[3], weights, acc)
    hid, dg, du, keep, send = middle(place, (1, 2), own[1:3], sib[1:3], weights, acc)
    from_core = across(send, 1)
    keep_own, send_own = own_slot(place, dg, du, *weights[:2])
    own_from_core = across(send_own, 1)
    grad_gate = weight_grad(place, 0, own, sib, dg)
    grad_up = weight_grad(place, 0, own, sib, du)
    grad_down = weight_grad(place, 1, own, sib, hid)
    parts = (keep + from_core.astype(F32)).astype(BF16)
    mine = keep_own + own_from_core.astype(F32)
    for p in range(1, 4):
        mine = mine + across(parts[p - 1], 2 * p).astype(F32)
    mine = mine.reshape(groups, tok_count, width)
    back = mine[0]
    sent = mine.astype(BF16)
    for k in range(1, groups):
        back = back + along(sent[k], -k, groups).astype(F32)
    return (grad_gate[None], grad_up[None], grad_down[None], back.astype(BF16))


def any_body(acts, grad_out, routing, gates, w_gate, w_up, w_down):
    expert = lax.axis_index("expert")
    acts_all, grad_all = (
        lax.all_gather(
            lax.all_gather(array, "tensor", axis=1, tiled=True), "expert", axis=0, tiled=True
        )
        for array in (acts, grad_out)
    )
    routing_all = lax.all_gather(routing, "expert", axis=0, tiled=True)
    gates_all = lax.all_gather(gates, "expert", axis=0, tiled=True)
    grad_all = (grad_all.astype(F32) * gate_of(routing_all, gates_all, expert)).astype(BF16)
    wg, wu, wd = w_gate[0], w_up[0], w_down[0]
    hid, dg, du = hidden_grads(dot(acts_all, wg, 1, 0), dot(acts_all, wu, 1, 0), dot(grad_all, wd, 1, 1))
    partial = dot(dg, wg, 1, 1) + dot(du, wu, 1, 1)
    partial = lax.psum_scatter(partial, "tensor", scatter_dimension=1, tiled=True)
    back = lax.psum_scatter(partial, "expert", scatter_dimension=0, tiled=True)
    return (
        dot(acts_all, dg, 0, 0).astype(BF16)[None],
        dot(acts_all, du, 0, 0).astype(BF16)[None],
        dot(hid, grad_all, 0, 0).astype(BF16)[None],
        back.astype(BF16),
    )


def solution(mesh):
    chips = mesh.shape["tensor"] == 8
    return jax.shard_map(
        chips_body if chips else any_body,
        mesh=mesh,
        in_specs=(
            P("expert", "tensor"),
            P("expert", "tensor"),
            P("expert", None),
            P("expert", None),
            P("expert", None, "tensor"),
            P("expert", None, "tensor"),
            P("expert", "tensor", None),
        ),
        out_specs=(
            P("expert", None, "tensor"),
            P("expert", None, "tensor"),
            P("expert", "tensor", None),
            P("expert", "tensor"),
        ),
        check_vma=False,
    )
```

time: 78.3 us -> 64.1 us (0.82)
  waiting for transfers between devices: 21.2 us -> 12.7 us
  Pallas kernels: 32.1 us -> 27.2 us
  other arithmetic: 5.33 us -> 3.99 us
    ppermute x11 -> x12, waiting for transfers between devices: 16.2 us -> 7.69 us  [across(): return lax.ppermute(array, 'tensor', [(i, i ^ mask) for i in range(8)])]
    pallas_call x4 -> x7, Pallas kernels: 32.1 us -> 27.2 us  [the longest x3 10.2 us: weight_grad(): call(functools.partial(weight_kernel, array), shape(out, BF16), [SMEM] +...]
    another operation x1 -> x0, other arithmetic: 1.45 us -> none
    ppermute x11 -> x12, starting transfers between devices: 7.81 us -> 8.28 us  [across(): return lax.ppermute(array, 'tensor', [(i, i ^ mask) for i in range(8)])]
  transfers between devices with their start and end apart: 17 -> 18, of which waited for: 8 -> 7; matrix products, arithmetic and copies ran while one was open for 0% -> 0% of each run, Pallas kernels for 22% -> 33%
where the time goes in v2:
time: 64.1 us; the launch traced here: 63 us
  Pallas kernels  27.2 us (42%)
  starting transfers between devices  18.2 us (28%)
  waiting for transfers between devices  12.7 us (20%)
  other arithmetic  3.99 us (6%)
  between operations  0.84 us (1%)
    pallas_call x3, Pallas kernels, weight_grad(): call(functools.partial(weight_kernel, array), shape(out, BF16), [SMEM] +...  10.2 us
    ppermute x6, starting transfers between devices, along(): lax.ppermute(array, 'expert', [(i, (i + distance) % count) for i in range...  9.88 us
    ppermute x12, starting transfers between devices, across(): return lax.ppermute(array, 'tensor', [(i, i ^ mask) for i in range(8)])  8.28 us
    ppermute x12, waiting for transfers between devices, across(): return lax.ppermute(array, 'tensor', [(i, i ^ mask) for i in range(8)])  7.69 us
    pallas_call x1, Pallas kernels, load_weights(): call(load_kernel, tuple((shape(w.shape, BF16) for w in weights)) + (shape...  7.03 us
    pallas_call x1, Pallas kernels, middle(): call(functools.partial(middle_kernel, pieces, (3, 1, 2)), (shape((rows, h...  6.65 us
    ppermute x6, waiting for transfers between devices, along(): lax.ppermute(array, 'expert', [(i, (i + distance) % count) for i in range...  4.99 us
    pallas_call x1, Pallas kernels, partial_sums(): call(partial_kernel, (shape((rows, hidden_count), F32),) * 3, [SMEM] + [V...  2.12 us
  transfers between devices with their start and end apart: 18, of which 7 were waited for; matrix products, arithmetic and copies ran while one was open for 0% of the time, Pallas kernels for 33%

profile of v2, /device:TPU:8, one launch (start us, length us, event | category | flops | bytes accessed | tf_op | source)
XLA Modules:
  0.0 63.0 jit_solution(14797110282382364624)
XLA Ops:
  0.7 0.7 %fusion.11 = (f32[48]{0:T(128)S(1)}, f32[48]{0:T(128)S(1)}, f32[48]{0:T(128)S(1)}, f32[48]{0:T(128)S(1)}) fusion(f32[48,2]{0,1:T(2,128)} %param.10, s32[48,2]{0,1:T(2,128)} %param.9, s32[]{:T(128)S(6)} %select_n.32, s32[]{:T(128)S(6)} %select_n.34, s32[]{:T(128)S(6)} %select_n.38, s32[]{:T(128)S(6)} %select_n.36), kind=kLoop, calls=%fused_computation.29 | loop fusion | flops 960 | bytes 1552 | tf_op jit(solution)/shard_map/reduce_sum | solution.py:21
  1.4 0.9 %fusion.10 = (bf16[1,48,384]{2,1,0:T(8,128)(2,1)S(1)}, bf16[1,48,384]{2,1,0:T(8,128)(2,1)S(1)}, bf16[1,48,384]{2,1,0:T(8,128)(2,1)S(1)}, bf16[1,48,384]{2,1,0:T(8,128)(2,1)S(1)}) fusion(bf16[48,384]{1,0:T(8,128)(2,1)} %param.8, f32[48]{0:T(128)S(1)} %get-tuple-element.48, f32[48]{0:T(128)S(1)} %get-tuple-element.49, f32[48]{0:T(128)S(1)} %get-tuple-element.51, ...), kind=kLoop, calls=%fused_computation.24 | loop fusion | flops 165888 | bytes 185088 | tf_op jit(solution)/shard_map/stack | solution.py:269
  2.3 0.8 %pad_maximum_fusion.3 = (bf16[2,48,384]{2,1,0:T(8,128)(2,1)S(1)}, bf16[2,48,384]{2,1,0:T(8,128)(2,1)S(1)}, bf16[2,48,384]{2,1,0:T(8,128)(2,1)S(1)}) fusion(bf16[1,48,384]{2,1,0:T(8,128)(2,1)} %bitcast.28, bf16[1,48,384]{2,1,0:T(8,128)(2,1)S(1)} %get-tuple-element.61, bf16[1,48,384]{2,1,0:T(8,128)(2,1)S(1)} %get-tuple-element.62, ...), kind=kLoop, calls=%fused_computation.12 | loop fusion | flops 110592 | bytes 368640 | tf_op jit(solution)/shard_map/stack | solution.py:269
  3.1 1.6 %collective-permute-start = (bf16[2,48,384]{2,1,0:T(8,128)(2,1)S(1)}, bf16[2,48,384]{2,1,0:T(8,128)(2,1)S(1)}, u32[]{:S(2)}, u32[]{:S(2)}) collective-permute-start(bf16[2,48,384]{2,1,0:T(8,128)(2,1)S(1)} %get-tuple-element.64), channel_id=1, source_target_pairs={{0,1},{1,2},{2,3},{3,0},{4,5},{5,6},{6,7},{7,4},{8,9},{9,10},{10,1... | collective-permute-start | bytes 221192 | tf_op jit(solution)/shard_map/ppermute | solution.py:257
  4.7 1.1 %collective-permute-start.1 = (bf16[2,48,384]{2,1,0:T(8,128)(2,1)S(1)}, bf16[2,48,384]{2,1,0:T(8,128)(2,1)S(1)}, u32[]{:S(2)}, u32[]{:S(2)}) collective-permute-start(bf16[2,48,384]{2,1,0:T(8,128)(2,1)S(1)} %get-tuple-element.65), channel_id=1, source_target_pairs={{0,2},{1,3},{2,0},{3,1},{4,6},{5,7},{6,4},{7,5},{8,10},{9,11},{10,... | collective-permute-start | bytes 221192 | tf_op jit(solution)/shard_map/ppermute | solution.py:257
  5.8 1.9 %collective-permute-start.2 = (bf16[2,48,384]{2,1,0:T(8,128)(2,1)S(1)}, bf16[2,48,384]{2,1,0:T(8,128)(2,1)S(1)}, u32[]{:S(2)}, u32[]{:S(2)}) collective-permute-start(bf16[2,48,384]{2,1,0:T(8,128)(2,1)S(1)} %get-tuple-element.66), channel_id=1, source_target_pairs={{0,3},{1,0},{2,1},{3,2},{4,7},{5,4},{6,5},{7,6},{8,11},{9,8},{10,9... | collective-permute-start | bytes 221192 | tf_op jit(solution)/shard_map/ppermute | solution.py:257
  7.7 2.0 %collective-permute-done = bf16[2,48,384]{2,1,0:T(8,128)(2,1)S(1)} collective-permute-done((bf16[2,48,384]{2,1,0:T(8,128)(2,1)S(1)}, bf16[2,48,384]{2,1,0:T(8,128)(2,1)S(1)}, u32[]{:S(2)}, u32[]{:S(2)}) %collective-permute-start) | collective-permute-done | bytes 73760 | tf_op jit(solution)/shard_map/ppermute | solution.py:257
  9.7 1.5 %collective-permute-done.1 = bf16[2,48,384]{2,1,0:T(8,128)(2,1)S(1)} collective-permute-done((bf16[2,48,384]{2,1,0:T(8,128)(2,1)S(1)}, bf16[2,48,384]{2,1,0:T(8,128)(2,1)S(1)}, u32[]{:S(2)}, u32[]{:S(2)}) %collective-permute-start.1) | collective-permute-done | bytes 73760 | tf_op jit(solution)/shard_map/ppermute | solution.py:257
  11.2 1.5 %collective-permute-done.2 = bf16[2,48,384]{2,1,0:T(8,128)(2,1)S(1)} collective-permute-done((bf16[2,48,384]{2,1,0:T(8,128)(2,1)S(1)}, bf16[2,48,384]{2,1,0:T(8,128)(2,1)S(1)}, u32[]{:S(2)}, u32[]{:S(2)}) %collective-permute-start.2) | collective-permute-done | bytes 73760 | tf_op jit(solution)/shard_map/ppermute | solution.py:257
  12.7 0.8 %pad_maximum_fusion.own.refs_0_ = bf16[2,192,384]{2,1,0:T(8,128)(2,1)S(1)} fusion(bf16[2,48,384]{2,1,0:T(8,128)(2,1)S(1)} %collective-permute-done.2, bf16[2,48,384]{2,1,0:T(8,128)(2,1)S(1)} %collective-permute-done.1, bf16[2,48,384]{2,1,0:T(8,128)(2,1)S(1)} %collective-permute-done, bf16[1,48,384]{2,1,0:T(8,128)(2,1)S(1)} %get-tuple-element.60, ...), kind=kLoop, calls=%fused_computation.1 | loop fusion | flops 1474560 | bytes 589824 | tf_op jit(solution)/shard_map/concatenate | solution.py:272
  13.5 2.5 %collective-permute-start.5 = (bf16[2,192,384]{2,1,0:T(8,128)(2,1)S(1)}, bf16[2,192,384]{2,1,0:T(8,128)(2,1)S(1)}, u32[]{:S(2)}, u32[]{:S(2)}) collective-permute-start(bf16[2,192,384]{2,1,0:T(8,128)(2,1)S(1)} %pad_maximum_fusion.own.refs_0_), channel_id=1, source_target_pairs={{0,24},{4,28},{8,16},{12,20},{16,8},{20,12},{24,0},{28,4},{1,25},{... | collective-permute-start | bytes 884744 | tf_op jit(solution)/shard_map/ppermute | solution.py:253
  16.0 0.5 collective-permute-start.4
  16.5 0.5 collective-permute-start.3
  17.1 7.0 %shard_map.102 = (bf16[3072,1024]{1,0:T(8,128)(2,1)S(1)}, bf16[3072,1024]{1,0:T(8,128)(2,1)S(1)}, bf16[1024,3072]{1,0:T(8,128)(2,1)S(1)}, f32[192,1024]{1,0:T(8,...) custom-call(s32[1]{0:T(128)} %bitcast.place, bf16[2,192,384]{2,1,0:T(8,128)(2,1)S(1)} %pad_maximum_fusion.own.refs_0_, ...), custom_call_target="tpu_custom_call" | custom-call | flops 1 | bytes 1 | tf_op jit(solution)/shard_map/pallas_call | solution.py:128
  24.1 0.3 collective-permute-done.5.own.refs_3_
  24.4 5.3 %collective-permute-done.4.refs_1_.refs_2_ = bf16[2,192,384]{2,1,0:T(8,128)(2,1)S(1)} collective-permute-done((bf16[2,192,384]{2,1,0:T(8,128)(2,1)S(1)}, bf16[2,192,384]{2,1,0:T(8,128)(2,1)S(1)}, u32[]{:S(2)}, u32[]{:S(2)}) %collective-permute-start.4) | collective-permute-done | bytes 294944 | tf_op jit(solution)/shard_map/ppermute | solution.py:253
  29.7 0.5 collective-permute-start.7
  30.3 1.1 %collective-permute-done.9.sib.refs_7_ = bf16[2,192,384]{2,1,0:T(8,128)(2,1)S(1)} collective-permute-done((bf16[2,192,384]{2,1,0:T(8,128)(2,1)S(1)}, bf16[2,192,384]{2,1,0:T(8,128)(2,1)S(1)}, u32[]{:S(2)}, u32[]{:S(2)}) %collective-permute-start.9) | collective-permute-done | bytes 294944 | tf_op jit(solution)/shard_map/ppermute | solution.py:253
  31.3 2.1 %shard_map.103 = (f32[192,1024]{1,0:T(8,128)S(1)}, f32[192,1024]{1,0:T(8,128)S(1)}, f32[192,1024]{1,0:T(8,128)S(1)}) custom-call(s32[1]{0:T(128)} %bitcast.place, bf16[2,192,384]{2,1,0:T(8,128)(2,1)S(1)} %collective-permute-done.6.near.refs_4_, ...), custom_call_target="tpu_custom_call", output_to_operand_aliasing={{0}: (7, {}), {1}: (8, {}), {2}: (9, {})} | custom-call | flops 1 | bytes 1 | tf_op jit(solution)/shard_map/pallas_call | solution.py:147
  33.5 6.6 %shard_map.104 = (bf16[192,1024]{1,0:T(8,128)(2,1)S(1)}, bf16[192,1024]{1,0:T(8,128)(2,1)S(1)}, bf16[192,1024]{1,0:T(8,128)(2,1)S(1)}, f32[3,192,384]{2,1,0:T(8,128)S(1)}, bf16[3,192,384]{2,1,0:T(8,128)(2,1)S(1)}) custom-call(s32[1]{0:T(128)} %bitcast.place, bf16[2,192,384]{2,1,0:T(8,128)(2,1)S(1)} %collective-permute-done.3.refs_0_.refs_1_, ...), custom_call_target="tpu_custom_call" | custom-call | flops 3623878656 | tf_op jit(solution)/shard_map/pallas_call | solution.py:183
  40.3 1.2 %shard_map.108 = (f32[192,384]{1,0:T(8,128)S(1)}, bf16[192,384]{1,0:T(8,128)(2,1)S(1)}) custom-call(s32[1]{0:T(128)} %bitcast.place, bf16[192,1024]{1,0:T(8,128)(2,1)S(1)} %get-tuple-element.41.refs_8_.dg, bf16[192,1024]{1,0:T(8,128)(2,1)S(1)} %get-tuple-element.42.refs_8_.du, bf16[3072,1024]{1,0:T(8,128)(2,1)S(1)} %get-tuple-element.32.wg.refs_4_, ...), custom_call_target="tpu_custom_call" | custom-call | flops 603979776 | tf_op jit(solution)/shard_map/pallas_call | solution.py:206
  41.5 0.5 collective-permute-start.10
  42.1 1.4 %collective-permute-start.12 = (bf16[192,384]{1,0:T(8,128)(2,1)S(1)}, bf16[192,384]{1,0:T(8,128)(2,1)S(1)}, u32[]{:S(2)}, u32[]{:S(2)}) collective-permute-start(bf16[192,384]{1,0:T(8,128)(2,1)S(1)} %get-tuple-element.54), channel_id=1, source_target_pairs={{0,8},{4,12},{8,0},{12,4},{16,24},{20,28},{24,16},{28,20},{1,9},{5... | collective-permute-start | bytes 442376 | tf_op jit(solution)/shard_map/ppermute | solution.py:253
  43.6 1.4 %collective-permute-start.14 = (bf16[192,384]{1,0:T(8,128)(2,1)S(1)}, bf16[192,384]{1,0:T(8,128)(2,1)S(1)}, u32[]{:S(2)}, u32[]{:S(2)}) collective-permute-start(bf16[192,384]{1,0:T(8,128)(2,1)S(1)} %get-tuple-element.55), channel_id=1, source_target_pairs={{0,24},{4,28},{8,16},{12,20},{16,8},{20,12},{24,0},{28,4},{1,25},{... | collective-permute-start | bytes 442376 | tf_op jit(solution)/shard_map/ppermute | solution.py:253
  44.9 0.7 %collective-permute-start.13 = (bf16[192,384]{1,0:T(8,128)(2,1)S(1)}, bf16[192,384]{1,0:T(8,128)(2,1)S(1)}, u32[]{:S(2)}, u32[]{:S(2)}) collective-permute-start(bf16[192,384]{1,0:T(8,128)(2,1)S(1)} %get-tuple-element.56), channel_id=1, source_target_pairs={{0,16},{4,20},{8,24},{12,28},{16,0},{20,4},{24,8},{28,12},{1,17},{... | collective-permute-start | bytes 442376 | tf_op jit(solution)/shard_map/ppermute | solution.py:253
  45.7 3.4 %shard_map.105 = bf16[3072,1024]{1,0:T(8,128)(2,1)} custom-call(s32[1]{0:T(128)} %bitcast.place, bf16[2,192,384]{2,1,0:T(8,128)(2,1)S(1)} %pad_maximum_fusion.own.refs_0_, bf16[2,192,384]{2,1,0:T(8,128)(2,1)S(1)} %collective-permute-done.3.refs_0_.refs_1_, bf16[2,192,384]{2,1,0:T(8,128)(2,1)S(1)} %collective-permute-done.4.refs_1_.refs_2_, ...), custom_call_target="tpu_custom_call" | custom-call | flops 1207959552 | bytes 6291456 | tf_op jit(solution)/shard_map/pallas_call | solution.py:241
  49.0 3.4 %shard_map.106 = bf16[3072,1024]{1,0:T(8,128)(2,1)} custom-call(s32[1]{0:T(128)} %bitcast.place, bf16[2,192,384]{2,1,0:T(8,128)(2,1)S(1)} %pad_maximum_fusion.own.refs_0_, bf16[2,192,384]{2,1,0:T(8,128)(2,1)S(1)} %collective-permute-done.3.refs_0_.refs_1_, bf16[2,192,384]{2,1,0:T(8,128)(2,1)S(1)} %collective-permute-done.4.refs_1_.refs_2_, ...), custom_call_target="tpu_custom_call" | custom-call | flops 1207959552 | bytes 6291456 | tf_op jit(solution)/shard_map/pallas_call | solution.py:241
  52.5 1.0 %collective-permute-done.13 = bf16[192,384]{1,0:T(8,128)(2,1)S(1)} collective-permute-done((bf16[192,384]{1,0:T(8,128)(2,1)S(1)}, bf16[192,384]{1,0:T(8,128)(2,1)S(1)}, u32[]{:S(2)}, u32[]{:S(2)}) %collective-permute-start.13) | collective-permute-done | bytes 147488 | tf_op jit(solution)/shard_map/ppermute | solution.py:253
  53.6 2.0 %collective-permute-start.17 = (bf16[48,384]{1,0:T(8,128)(2,1)S(1)}, bf16[48,384]{1,0:T(8,128)(2,1)S(1)}, u32[]{:S(2)}, u32[]{:S(2)}) collective-permute-start(bf16[48,384]{1,0:T(8,128)(2,1)S(1)} %get-tuple-element.58), channel_id=1, source_target_pairs={{0,1},{1,2},{2,3},{3,0},{4,5},{5,6},{6,7},{7,4},{8,9},{9,10},{10,1... | collective-permute-start | bytes 110600 | tf_op jit(solution)/shard_map/ppermute | solution.py:257
  55.6 3.1 %collective-permute-start.16 = (bf16[48,384]{1,0:T(8,128)(2,1)S(1)}, bf16[48,384]{1,0:T(8,128)(2,1)S(1)}, u32[]{:S(2)}, u32[]{:S(2)}) collective-permute-start(bf16[48,384]{1,0:T(8,128)(2,1)S(1)} %get-tuple-element.59), channel_id=1, source_target_pairs={{0,2},{1,3},{2,0},{3,1},{4,6},{5,7},{6,4},{7,5},{8,10},{9,11},{10,... | collective-permute-start | bytes 110600 | tf_op jit(solution)/shard_map/ppermute | solution.py:257
  58.8 3.5 %shard_map.107 = bf16[1024,3072]{1,0:T(8,128)(2,1)} custom-call(s32[1]{0:T(128)} %bitcast.place, bf16[2,192,384]{2,1,0:T(8,128)(2,1)S(1)} %pad_maximum_fusion.own.refs_0_, bf16[2,192,384]{2,1,0:T(8,128)(2,1)S(1)} %collective-permute-done.3.refs_0_.refs_1_, bf16[2,192,384]{2,1,0:T(8,128)(2,1)S(1)} %collective-permute-done.4.refs_1_.refs_2_, ...), custom_call_target="tpu_custom_call" | custom-call | flops 1207959552 | bytes 6291456 | tf_op jit(solution)/shard_map/pallas_call | solution.py:241
  62.3 0.6 %fusion.6 = bf16[48,384]{1,0:T(8,128)(2,1)} fusion(f32[192,384]{1,0:T(8,128)S(1)} %get-tuple-element.53, bf16[48,384]{1,0:T(8,128)(2,1)S(1)} %collective-permute-done.17, bf16[48,384]{1,0:T(8,128)(2,1)S(1)} %collective-permute-done.16, bf16[48,384]{1,0:T(8,128)(2,1)S(1)} %collective-permute-done.15), kind=kLoop, calls=%fused_computation.20 | loop fusion | flops 129024 | bytes 221184 | tf_op jit(solution)/shard_map/convert_element_type | solution.py:297
  (20 shorter events, 0.5 us)
Async XLA Ops:
  3.1 6.7 %collective-permute-start = (bf16[2,48,384]{2,1,0:T(8,128)(2,1)S(1)}, bf16[2,48,384]{2,1,0:T(8,128)(2,1)S(1)}, u32[]{:S(2)}, u32[]{:S(2)}) collective-permute-start(bf16[2,48,384]{2,1,0:T(8,128)(2,1)S(1)} %get-tuple-element.64), channel_id=1, source_target_pairs={{0,1},{1,2},{2,3},{3,0},{4,5},{5,6},{6,7},{7,4},{8,9},{9,10},{10,1... | collective-permute-start | bytes 221192 | tf_op jit(solution)/shard_map/ppermute | solution.py:257
  4.7 6.6 %collective-permute-start.1 = (bf16[2,48,384]{2,1,0:T(8,128)(2,1)S(1)}, bf16[2,48,384]{2,1,0:T(8,128)(2,1)S(1)}, u32[]{:S(2)}, u32[]{:S(2)}) collective-permute-start(bf16[2,48,384]{2,1,0:T(8,128)(2,1)S(1)} %get-tuple-element.65), channel_id=1, source_target_pairs={{0,2},{1,3},{2,0},{3,1},{4,6},{5,7},{6,4},{7,5},{8,10},{9,11},{10,... | collective-permute-start | bytes 221192 | tf_op jit(solution)/shard_map/ppermute | solution.py:257
  5.8 6.9 %collective-permute-start.2 = (bf16[2,48,384]{2,1,0:T(8,128)(2,1)S(1)}, bf16[2,48,384]{2,1,0:T(8,128)(2,1)S(1)}, u32[]{:S(2)}, u32[]{:S(2)}) collective-permute-start(bf16[2,48,384]{2,1,0:T(8,128)(2,1)S(1)} %get-tuple-element.66), channel_id=1, source_target_pairs={{0,3},{1,0},{2,1},{3,2},{4,7},{5,4},{6,5},{7,6},{8,11},{9,8},{10,9... | collective-permute-start | bytes 221192 | tf_op jit(solution)/shard_map/ppermute | solution.py:257
  13.5 10.9 %collective-permute-start.5 = (bf16[2,192,384]{2,1,0:T(8,128)(2,1)S(1)}, bf16[2,192,384]{2,1,0:T(8,128)(2,1)S(1)}, u32[]{:S(2)}, u32[]{:S(2)}) collective-permute-start(bf16[2,192,384]{2,1,0:T(8,128)(2,1)S(1)} %pad_maximum_fusion.own.refs_0_), channel_id=1, source_target_pairs={{0,24},{4,28},{8,16},{12,20},{16,8},{20,12},{24,0},{28,4},{1,25},{... | collective-permute-start | bytes 884744 | tf_op jit(solution)/shard_map/ppermute | solution.py:253
  16.0 13.7 %collective-permute-start.4 = (bf16[2,192,384]{2,1,0:T(8,128)(2,1)S(1)}, bf16[2,192,384]{2,1,0:T(8,128)(2,1)S(1)}, u32[]{:S(2)}, u32[]{:S(2)}) collective-permute-start(bf16[2,192,384]{2,1,0:T(8,128)(2,1)S(1)} %pad_maximum_fusion.own.refs_0_), channel_id=1, source_target_pairs={{0,16},{4,20},{8,24},{12,28},{16,0},{20,4},{24,8},{28,12},{1,17},{... | collective-permute-start | bytes 884744 | tf_op jit(solution)/shard_map/ppermute | solution.py:253
  16.5 13.2 %collective-permute-start.3 = (bf16[2,192,384]{2,1,0:T(8,128)(2,1)S(1)}, bf16[2,192,384]{2,1,0:T(8,128)(2,1)S(1)}, u32[]{:S(2)}, u32[]{:S(2)}) collective-permute-start(bf16[2,192,384]{2,1,0:T(8,128)(2,1)S(1)} %pad_maximum_fusion.own.refs_0_), channel_id=1, source_target_pairs={{0,8},{4,12},{8,0},{12,4},{16,24},{20,28},{24,16},{28,20},{1,9},{5... | collective-permute-start | bytes 884744 | tf_op jit(solution)/shard_map/ppermute | solution.py:253
  17.1 13.2 %collective-permute-start.6 = (bf16[2,192,384]{2,1,0:T(8,128)(2,1)S(1)}, bf16[2,192,384]{2,1,0:T(8,128)(2,1)S(1)}, u32[]{:S(2)}, u32[]{:S(2)}) collective-permute-start(bf16[2,192,384]{2,1,0:T(8,128)(2,1)S(1)} %pad_maximum_fusion.own.refs_0_), channel_id=1, source_target_pairs={{0,4},{4,0},{8,12},{12,8},{16,20},{20,16},{24,28},{28,24},{1,5},{5... | collective-permute-start | bytes 884744 | tf_op jit(solution)/shard_map/ppermute | solution.py:253
  29.7 1.6 %collective-permute-start.9 = (bf16[2,192,384]{2,1,0:T(8,128)(2,1)S(1)}, bf16[2,192,384]{2,1,0:T(8,128)(2,1)S(1)}, u32[]{:S(2)}, u32[]{:S(2)}) collective-permute-start(bf16[2,192,384]{2,1,0:T(8,128)(2,1)S(1)} %collective-permute-done.5.own.refs_3_), channel_id=1, source_target_pairs={{0,4},{4,0},{8,12},{12,8},{16,20},{20,16},{24,28},{28,24},{1,5},{5... | collective-permute-start | bytes 884744 | tf_op jit(solution)/shard_map/ppermute | solution.py:253
  29.7 3.7 %collective-permute-start.7 = (bf16[2,192,384]{2,1,0:T(8,128)(2,1)S(1)}, bf16[2,192,384]{2,1,0:T(8,128)(2,1)S(1)}, u32[]{:S(2)}, u32[]{:S(2)}) collective-permute-start(bf16[2,192,384]{2,1,0:T(8,128)(2,1)S(1)} %collective-permute-done.3.refs_0_.refs_1_), channel_id=1, source_target_pairs={{0,4},{4,0},{8,12},{12,8},{16,20},{20,16},{24,28},{28,24},{1,5},{5... | collective-permute-start | bytes 884744 | tf_op jit(solution)/shard_map/ppermute | solution.py:253
  30.2 3.2 %collective-permute-start.8 = (bf16[2,192,384]{2,1,0:T(8,128)(2,1)S(1)}, bf16[2,192,384]{2,1,0:T(8,128)(2,1)S(1)}, u32[]{:S(2)}, u32[]{:S(2)}) collective-permute-start(bf16[2,192,384]{2,1,0:T(8,128)(2,1)S(1)} %collective-permute-done.4.refs_1_.refs_2_), channel_id=1, source_target_pairs={{0,4},{4,0},{8,12},{12,8},{16,20},{20,16},{24,28},{28,24},{1,5},{5... | collective-permute-start | bytes 884744 | tf_op jit(solution)/shard_map/ppermute | solution.py:253
  40.1 1.9 %collective-permute-start.11 = (bf16[3,192,384]{2,1,0:T(8,128)(2,1)S(1)}, bf16[3,192,384]{2,1,0:T(8,128)(2,1)S(1)}, u32[]{:S(2)}, u32[]{:S(2)}) collective-permute-start(bf16[3,192,384]{2,1,0:T(8,128)(2,1)S(1)} %get-tuple-element.47), channel_id=1, source_target_pairs={{0,4},{4,0},{8,12},{12,8},{16,20},{20,16},{24,28},{28,24},{1,5},{5... | collective-permute-start | bytes 1327112 | tf_op jit(solution)/shard_map/ppermute | solution.py:253
  41.5 11.0 %collective-permute-start.10 = (bf16[192,384]{1,0:T(8,128)(2,1)S(1)}, bf16[192,384]{1,0:T(8,128)(2,1)S(1)}, u32[]{:S(2)}, u32[]{:S(2)}) collective-permute-start(bf16[192,384]{1,0:T(8,128)(2,1)S(1)} %get-tuple-element.45), channel_id=1, source_target_pairs={{0,4},{4,0},{8,12},{12,8},{16,20},{20,16},{24,28},{28,24},{1,5},{5... | collective-permute-start | bytes 442376 | tf_op jit(solution)/shard_map/ppermute | solution.py:253
  42.1 10.3 %collective-permute-start.12 = (bf16[192,384]{1,0:T(8,128)(2,1)S(1)}, bf16[192,384]{1,0:T(8,128)(2,1)S(1)}, u32[]{:S(2)}, u32[]{:S(2)}) collective-permute-start(bf16[192,384]{1,0:T(8,128)(2,1)S(1)} %get-tuple-element.54), channel_id=1, source_target_pairs={{0,8},{4,12},{8,0},{12,4},{16,24},{20,28},{24,16},{28,20},{1,9},{5... | collective-permute-start | bytes 442376 | tf_op jit(solution)/shard_map/ppermute | solution.py:253
  43.6 8.9 %collective-permute-start.14 = (bf16[192,384]{1,0:T(8,128)(2,1)S(1)}, bf16[192,384]{1,0:T(8,128)(2,1)S(1)}, u32[]{:S(2)}, u32[]{:S(2)}) collective-permute-start(bf16[192,384]{1,0:T(8,128)(2,1)S(1)} %get-tuple-element.55), channel_id=1, source_target_pairs={{0,24},{4,28},{8,16},{12,20},{16,8},{20,12},{24,0},{28,4},{1,25},{... | collective-permute-start | bytes 442376 | tf_op jit(solution)/shard_map/ppermute | solution.py:253
  44.9 8.5 %collective-permute-start.13 = (bf16[192,384]{1,0:T(8,128)(2,1)S(1)}, bf16[192,384]{1,0:T(8,128)(2,1)S(1)}, u32[]{:S(2)}, u32[]{:S(2)}) collective-permute-start(bf16[192,384]{1,0:T(8,128)(2,1)S(1)} %get-tuple-element.56), channel_id=1, source_target_pairs={{0,16},{4,20},{8,24},{12,28},{16,0},{20,4},{24,8},{28,12},{1,17},{... | collective-permute-start | bytes 442376 | tf_op jit(solution)/shard_map/ppermute | solution.py:253
  53.6 8.7 %collective-permute-start.15 = (bf16[48,384]{1,0:T(8,128)(2,1)S(1)}, bf16[48,384]{1,0:T(8,128)(2,1)S(1)}, u32[]{:S(2)}, u32[]{:S(2)}) collective-permute-start(bf16[48,384]{1,0:T(8,128)(2,1)S(1)} %get-tuple-element.57), channel_id=1, source_target_pairs={{0,3},{1,0},{2,1},{3,2},{4,7},{5,4},{6,5},{7,6},{8,11},{9,8},{10,9... | collective-permute-start | bytes 110600 | tf_op jit(solution)/shard_map/ppermute | solution.py:257
  53.6 8.7 %collective-permute-start.17 = (bf16[48,384]{1,0:T(8,128)(2,1)S(1)}, bf16[48,384]{1,0:T(8,128)(2,1)S(1)}, u32[]{:S(2)}, u32[]{:S(2)}) collective-permute-start(bf16[48,384]{1,0:T(8,128)(2,1)S(1)} %get-tuple-element.58), channel_id=1, source_target_pairs={{0,1},{1,2},{2,3},{3,0},{4,5},{5,6},{6,7},{7,4},{8,9},{9,10},{10,1... | collective-permute-start | bytes 110600 | tf_op jit(solution)/shard_map/ppermute | solution.py:257
  55.6 6.7 %collective-permute-start.16 = (bf16[48,384]{1,0:T(8,128)(2,1)S(1)}, bf16[48,384]{1,0:T(8,128)(2,1)S(1)}, u32[]{:S(2)}, u32[]{:S(2)}) collective-permute-start(bf16[48,384]{1,0:T(8,128)(2,1)S(1)} %get-tuple-element.59), channel_id=1, source_target_pairs={{0,2},{1,3},{2,0},{3,1},{4,6},{5,7},{6,4},{7,5},{8,10},{9,11},{10,... | collective-permute-start | bytes 110600 | tf_op jit(solution)/shard_map/ppermute | solution.py:257

commit v3 on v2

v3 whole, which is shorter than its diff:
```python
import functools

import jax
import jax.numpy as jnp
from jax import lax
from jax.experimental import pallas as pl
from jax.experimental.pallas import tpu as pltpu
from jax.sharding import PartitionSpec as P

F32 = jnp.float32
BF16 = jnp.bfloat16


def dot(left, right, left_dim, right_dim):
    return lax.dot_general(
        left, right, (((left_dim,), (right_dim,)), ((), ())), preferred_element_type=F32
    )


def gate_of(routing, gates, expert):
    return jnp.sum(jnp.where(routing == expert, gates, 0.0), axis=1, keepdims=True)


def hidden_grads(gate_pre, up_pre, grad_hidden):
    sig = jax.nn.sigmoid(gate_pre)
    act = gate_pre * sig
    hidden = (act * up_pre).astype(BF16)
    grad_up_pre = (grad_hidden * act).astype(BF16)
    grad_gate_pre = (grad_hidden * up_pre * sig * (1.0 + gate_pre * (1.0 - sig))).astype(BF16)
    return hidden, grad_gate_pre, grad_up_pre


VMEM = pl.BlockSpec(memory_space=pltpu.VMEM)
SMEM = pl.BlockSpec(memory_space=pltpu.SMEM)
HBM = pl.BlockSpec(memory_space=pl.ANY)


def shape(dims, dtype):
    return jax.ShapeDtypeStruct(dims, dtype)


def call(kernel, out_shape, in_specs, out_specs, flops, moved, scratch=(), limit=16, aliases={}):
    return pl.pallas_call(
        kernel,
        out_shape=out_shape,
        in_specs=in_specs,
        out_specs=out_specs,
        scratch_shapes=scratch,
        input_output_aliases=aliases,
        compiler_params=pltpu.CompilerParams(vmem_limit_bytes=limit * 1024 * 1024),
        cost_estimate=pl.CostEstimate(flops=flops, bytes_accessed=moved, transcendentals=0),
    )


def both_cores(core, mine, other):
    first = core == 0
    return jnp.concatenate([jnp.where(first, mine, other), jnp.where(first, other, mine)], axis=1)


def block_at(place, p, wide):
    return pl.ds(pl.multiple_of((place[0] // 2 ^ p) * wide, wide), wide)


STEP = 256
LOAD_LIMIT = 28


def far(place):
    core = place[0] % 2
    return 0, 1 + core, 2 - core, 3


def pair(place, i, own, sib):
    core = place[0] % 2
    rows = block_at(place, far(place)[i], 2 * own.shape[2])
    return rows, both_cores(core, own[0], sib[0]), both_cores(core, own[1], sib[1])


def add_pieces(pieces, weights, acc_in, acc_out, finish, arrived=None):
    wg, wu, wd = weights
    for f in range(wg.shape[1] // STEP):
        cols = pl.ds(f * STEP, STEP)
        if arrived is not None:
            arrived(f)
        sums = [None if acc is None else acc[:, cols] for acc in acc_in]
        for rows, x, g in pieces:
            terms = (dot(x, wg[rows, cols], 1, 0), dot(x, wu[rows, cols], 1, 0), dot(g, wd[cols, rows], 1, 1))
            sums = [t if s is None else s + t for s, t in zip(sums, terms)]
        finish(cols, sums, acc_out)


def store(cols, sums, outs):
    for out, value in zip(outs, sums):
        out[:, cols] = value


def store_grads(cols, sums, outs):
    store(cols, hidden_grads(*sums), outs)


def load_kernel(place, own, near, wg, wu, wd, wg_here, wu_here, wd_here, gate, up, back, sems):
    copies = []
    for f in range(wg.shape[1] // STEP):
        cols = pl.ds(f * STEP, STEP)
        copies.append(
            [
                pltpu.make_async_copy(wg.at[:, cols], wg_here.at[:, cols], sems.at[f, 0]),
                pltpu.make_async_copy(wu.at[:, cols], wu_here.at[:, cols], sems.at[f, 1]),
                pltpu.make_async_copy(wd.at[cols, :], wd_here.at[cols, :], sems.at[f, 2]),
            ]
        )
        for copy in copies[f]:
            copy.start()

    def arrived(f):
        for copy in copies[f]:
            copy.wait()

    weights = (wg_here, wu_here, wd_here)
    add_pieces([pair(place, 0, own, near)], weights, (None,) * 3, (gate, up, back), store, arrived)


def load_weights(place, own, near, weights):
    rows, hidden_count = own.shape[1], weights[0].shape[1]
    return call(
        load_kernel,
        tuple(shape(w.shape, BF16) for w in weights) + (shape((rows, hidden_count), F32),) * 3,
        [SMEM] + [VMEM] * 2 + [HBM] * 3,
        [VMEM] * 6,
        1,
        1,
        scratch=[pltpu.SemaphoreType.DMA((hidden_count // STEP, 3))],
        limit=LOAD_LIMIT,
    )(place, own, near, *weights)


def partial_kernel(place, *refs):
    pieces = [pair(place, 1, *refs[0:2]), pair(place, 2, *refs[2:4])]
    add_pieces(pieces, refs[4:7], refs[7:10], refs[10:], store)


def partial_sums(place, halves, weights, acc):
    rows, hidden_count = acc[0].shape
    return call(
        partial_kernel,
        (shape((rows, hidden_count), F32),) * 3,
        [SMEM] + [VMEM] * 10,
        [VMEM] * 3,
        1,
        1,
        aliases={8: 0, 9: 1, 10: 2},
    )(place, *halves, *weights, *acc)


def slot_rows(place, p, dg, du, wg, wu, wide):
    rows = block_at(place, p, wide)
    return dot(dg, wg[rows, :], 1, 1) + dot(du, wu[rows, :], 1, 1)


def write_slots(place, p, dg, du, wg, wu, keep, send):
    width = keep.shape[1]
    first = place[0] % 2 == 0
    part = slot_rows(place, p, dg[...], du[...], wg, wu, 2 * width)
    low, high = part[:, :width], part[:, width:]
    keep[...] = jnp.where(first, low, high)
    send[...] = jnp.where(first, high, low).astype(BF16)


def middle_kernel(place, own, sib, wg, wu, wd, *refs):
    acc = refs[:3]
    hid, dg, du, keep, send = refs[3:]
    add_pieces([pair(place, 3, own, sib)], (wg, wu, wd), acc, (hid, dg, du), store_grads)
    write_slots(place, 3, dg, du, wg, wu, keep, send)


def middle(place, own, sib, weights, acc):
    rows, width = own.shape[1:]
    hidden_count = weights[0].shape[1]
    return call(
        middle_kernel,
        (shape((rows, hidden_count), BF16),) * 3 + (shape((rows, width), F32), shape((rows, width), BF16)),
        [SMEM] + [VMEM] * 8,
        [VMEM] * 5,
        20 * rows * width * hidden_count,
        0,
    )(place, own, sib, *weights, *acc)


def slot_kernel(p, place, *refs):
    write_slots(place, p, *refs)


def slots(place, p, dg, du, wg, wu):
    rows, hidden_count = dg.shape
    width = wg.shape[0] // 8
    return call(
        functools.partial(slot_kernel, p),
        (shape((rows, width), F32), shape((rows, width), BF16)),
        [SMEM] + [VMEM] * 4,
        [VMEM] * 2,
        8 * rows * width * hidden_count,
        0,
    )(place, dg, du, wg, wu)


def weight_kernel(arrays, place, *refs):
    n = len(arrays)
    own, sib, ds = refs[0:4], refs[4:8], refs[8 : 8 + n]
    outs, bufs, sems = refs[8 + n : 8 + 2 * n], refs[8 + 2 * n : 8 + 3 * n], refs[8 + 3 * n]
    core = place[0] % 2
    wide = 2 * own[0].shape[2]
    copies = []
    for i, (array, d, out, buf) in enumerate(zip(arrays, ds, outs, bufs)):
        for j, p in enumerate(far(place)):
            rows = block_at(place, p, wide)
            piece = both_cores(core, own[j][array], sib[j][array])
            if array == 0:
                buf[j] = dot(piece, d[...], 0, 0).astype(BF16)
                target = out.at[rows, :]
            else:
                buf[j] = dot(d[...], piece, 0, 0).astype(BF16)
                target = out.at[:, rows]
            copies.append(pltpu.make_async_copy(buf.at[j], target, sems.at[i, j]))
            copies[-1].start()
    for copy in copies:
        copy.wait()


def weight_grads(place, arrays, own, sib, ds):
    rows, width = own[0].shape[1:]
    hidden_count = ds[0].shape[1]
    blocks = [(2 * width, hidden_count) if array == 0 else (hidden_count, 2 * width) for array in arrays]
    outs = [(8 * width, hidden_count) if array == 0 else (hidden_count, 8 * width) for array in arrays]
    return call(
        functools.partial(weight_kernel, arrays),
        tuple(shape(out, BF16) for out in outs),
        [SMEM] + [VMEM] * (8 + len(ds)),
        [HBM] * len(ds),
        16 * rows * width * hidden_count * len(ds),
        16 * width * hidden_count * len(ds),
        scratch=[pltpu.VMEM((4,) + block, BF16) for block in blocks] + [pltpu.SemaphoreType.DMA((len(ds), 4))],
        limit=LOAD_LIMIT,
    )(place, *own, *sib, *ds)


def pack_kernel(groups, place, *refs):
    sources, outs, here, sems = refs[:4], refs[4 : 4 + groups], refs[4 + groups : 8 + groups], refs[8 + groups]
    copies = [pltpu.make_async_copy(s, d, sems.at[i]) for i, (s, d) in enumerate(zip(sources, here))]
    for copy in copies:
        copy.start()
    for copy in copies:
        copy.wait()
    acts, grad, routing, gates = here
    wide = grad[...].astype(F32)
    for distance, out in enumerate(outs):
        expert = lax.rem(place[0] + distance, groups)
        gate = jnp.sum(jnp.where(routing[...] == expert, gates[...], 0.0), axis=0, keepdims=True)
        out[0] = acts[...]
        out[1] = (wide * gate.T).astype(BF16)


def pack(place, acts, grad, routing, gates, groups):
    sources = (acts, grad, routing.T, gates.T)
    return call(
        functools.partial(pack_kernel, groups),
        (shape((2,) + acts.shape, BF16),) * groups,
        [SMEM] + [HBM] * 4,
        [VMEM] * groups,
        1,
        1,
        scratch=[pltpu.VMEM(s.shape, s.dtype) for s in sources] + [pltpu.SemaphoreType.DMA((4,))],
        limit=63,
    )(place, *sources)


def across(array, even, odd=None):
    masks = (even, even if odd is None else odd)
    return lax.ppermute(array, "tensor", [(i, i ^ masks[i % 2]) for i in range(8)])


def along(array, distance, count):
    return lax.ppermute(array, "expert", [(i, (i + distance) % count) for i in range(count)])


def chips_body(acts, grad_out, routing, gates, w_gate, w_up, w_down):
    groups = lax.axis_size("expert")
    place = lax.axis_index("tensor").astype(jnp.int32)[None]
    z = lax.axis_index("expert").astype(jnp.int32)[None]
    tok_count, width = acts.shape
    packed = pack(z, acts, grad_out, routing, gates, groups)
    blocks = [packed[0]] + [along(packed[k], k, groups) for k in range(1, groups)]
    own = jnp.concatenate(blocks, axis=1)
    near = across(own, 1)
    here = across(own, 2, 4), across(near, 2, 4)
    weights = (w_gate[0], w_up[0], w_down[0])
    loaded = load_weights(place, own, near, weights)
    weights, acc = loaded[:3], loaded[3:]
    here, acc = lax.optimization_barrier((here, acc))
    diag = across(here[0], 4, 2)
    there = across(here[1], 1), across(here[0], 1)
    acc = partial_sums(place, here + there, weights, acc)
    diag, acc = lax.optimization_barrier((diag, acc))
    diag_near = across(diag, 1)
    hid, dg, du, keep, send = middle(place, diag, diag_near, weights, acc)
    mine_of = own, here[0], there[0], diag
    other_of = near, here[1], there[1], diag_near
    wg, wu = weights[:2]

    def chip_sum(keep, send):
        return keep + across(send, 1).astype(F32)

    share = slots(place, 1, dg, du, wg, wu)
    diagonal, dg, du = lax.optimization_barrier((chip_sum(keep, send), dg, du))
    parts = [across(diagonal.astype(BF16), 6)]
    for p in (1, 2):
        later = slots(place, (p + 1) % 3, dg, du, wg, wu)
        total, dg, du = lax.optimization_barrier((chip_sum(*share), dg, du))
        parts.append(across(total.astype(BF16), 2 * p))
        share = later
    mine = chip_sum(*share)
    parts[0], dg = lax.optimization_barrier((parts[0], dg))
    (grad_gate,) = weight_grads(place, (0,), mine_of, other_of, (dg,))
    for part in parts:
        mine = mine + part.astype(F32)
    mine, du, hid = lax.optimization_barrier((mine, du, hid))
    grad_up, grad_down = weight_grads(place, (0, 1), mine_of, other_of, (du, hid))
    mine = mine.reshape(groups, tok_count, width)
    back = mine[0]
    sent = mine.astype(BF16)
    for k in range(1, groups):
        back = back + along(sent[k], -k, groups).astype(F32)
    return (grad_gate[None], grad_up[None], grad_down[None], back.astype(BF16))


def any_body(acts, grad_out, routing, gates, w_gate, w_up, w_down):
    expert = lax.axis_index("expert")
    acts_all, grad_all = (
        lax.all_gather(
            lax.all_gather(array, "tensor", axis=1, tiled=True), "expert", axis=0, tiled=True
        )
        for array in (acts, grad_out)
    )
    routing_all = lax.all_gather(routing, "expert", axis=0, tiled=True)
    gates_all = lax.all_gather(gates, "expert", axis=0, tiled=True)
    grad_all = (grad_all.astype(F32) * gate_of(routing_all, gates_all, expert)).astype(BF16)
    wg, wu, wd = w_gate[0], w_up[0], w_down[0]
    hid, dg, du = hidden_grads(dot(acts_all, wg, 1, 0), dot(acts_all, wu, 1, 0), dot(grad_all, wd, 1, 1))
    partial = dot(dg, wg, 1, 1) + dot(du, wu, 1, 1)
    partial = lax.psum_scatter(partial, "tensor", scatter_dimension=1, tiled=True)
    back = lax.psum_scatter(partial, "expert", scatter_dimension=0, tiled=True)
    return (
        dot(acts_all, dg, 0, 0).astype(BF16)[None],
        dot(acts_all, du, 0, 0).astype(BF16)[None],
        dot(hid, grad_all, 0, 0).astype(BF16)[None],
        back.astype(BF16),
    )


def solution(mesh):
    chips = mesh.shape["tensor"] == 8
    return jax.shard_map(
        chips_body if chips else any_body,
        mesh=mesh,
        in_specs=(
            P("expert", "tensor"),
            P("expert", "tensor"),
            P("expert", None),
            P("expert", None),
            P("expert", None, "tensor"),
            P("expert", None, "tensor"),
            P("expert", "tensor", None),
        ),
        out_specs=(
            P("expert", None, "tensor"),
            P("expert", None, "tensor"),
            P("expert", "tensor", None),
            P("expert", "tensor"),
        ),
        check_vma=False,
    )
```

time: 64.1 us -> 60 us (0.936); the launches traced: 63 us -> 59.8 us
  other arithmetic: 3.99 us -> 0.83 us
  waiting for transfers between devices: 12.7 us -> 10.1 us
  starting transfers between devices: 18.2 us -> 20.6 us
  local copies, waits for them, and re-layouts: 0.06 us -> 0.95 us
  Pallas kernels: 27.2 us -> 26.5 us
    ppermute x12 -> x14, waiting for transfers between devices: 7.69 us -> 5.81 us  [across(): lax.ppermute(array, 'tensor', [(i, i ^ masks[i % 2]) for i in range(8)])]
    ppermute x12 -> x14, starting transfers between devices: 8.28 us -> 10.1 us  [across(): lax.ppermute(array, 'tensor', [(i, i ^ masks[i % 2]) for i in range(8)])]
    another operation x2 -> x0, other arithmetic: 1.65 us -> none  [for_expert(): return jnp.stack([acts, (grad_wide * gate).astype(BF16)])]
    pallas_call x5 -> x7, Pallas kernels: 18.1 us -> 16.7 us  [the longest x2 8.7 us: weight_grads(): call(functools.partial(weight_kernel, arrays), tuple((shape(out, BF16) fo...]
    unnamed x0 -> x3, local copies, waits for them, and re-layouts: none -> 0.92 us
    concatenate x1 -> x0, other arithmetic: 0.8 us -> none  [chips_body(): own_piece = jnp.concatenate(blocks, axis=1)]
    reduce_sum x1 -> x0, other arithmetic: 0.72 us -> none  [gate_of(): jnp.sum(jnp.where(routing == expert, gates, 0.0), axis=1, keepdims=True)]
    ppermute x6, waiting for transfers between devices: 4.99 us -> 4.27 us  [along(): lax.ppermute(array, 'expert', [(i, (i + distance) % count) for i in range...]
  transfers between devices with their start and end apart: 18 -> 20, of which waited for: 7 -> 8; matrix products, arithmetic and copies ran while one was open for 0% -> 2% of each run, Pallas kernels for 33% -> 37%
where the time goes in v3:
time: 60 us; the launch traced here: 59.8 us
  Pallas kernels  26.5 us (44%)
  starting transfers between devices  20.6 us (34%)
  waiting for transfers between devices  10.1 us (17%)
  local copies, waits for them, and re-layouts  0.95 us (2%)
  other arithmetic  0.83 us (1%)
  between operations  0.83 us (1%)
    ppermute x6, starting transfers between devices, along(): lax.ppermute(array, 'expert', [(i, (i + distance) % count) for i in range...  10.5 us
    ppermute x14, starting transfers between devices, across(): lax.ppermute(array, 'tensor', [(i, i ^ masks[i % 2]) for i in range(8)])  10.1 us
    pallas_call x2, Pallas kernels, weight_grads(): call(functools.partial(weight_kernel, arrays), tuple((shape(out, BF16) fo...  8.7 us
    pallas_call x1, Pallas kernels, load_weights(): call(load_kernel, tuple((shape(w.shape, BF16) for w in weights)) + (shape...  7.19 us
    ppermute x14, waiting for transfers between devices, across(): lax.ppermute(array, 'tensor', [(i, i ^ masks[i % 2]) for i in range(8)])  5.81 us
    ppermute x6, waiting for transfers between devices, along(): lax.ppermute(array, 'expert', [(i, (i + distance) % count) for i in range...  4.27 us
    pallas_call x3, Pallas kernels, slots(): call(functools.partial(slot_kernel, p), (shape((rows, width), F32), shape...  3.58 us
    pallas_call x1, Pallas kernels, middle(): call(middle_kernel, (shape((rows, hidden_count), BF16),) * 3 + (shape((ro...  2.75 us
  transfers between devices with their start and end apart: 20, of which 8 were waited for; matrix products, arithmetic and copies ran while one was open for 2% of the time, Pallas kernels for 37%

profile of v3, /device:TPU:8, one launch (start us, length us, event | category | flops | bytes accessed | tf_op | source)
XLA Modules:
  0.0 59.8 jit_solution(10376063266736119242)
XLA Ops:
  0.6 1.7 %shard_map.102 = (bf16[2,48,384]{2,1,0:T(8,128)(2,1)}, bf16[2,48,384]{2,1,0:T(8,128)(2,1)}, bf16[2,48,384]{2,1,0:T(8,128)(2,1)}, bf16[2,48,384]{2,1,0:T(8,128)(2,1)}) custom-call(s32[1]{0:T(128)} %bitcast.1.place, bf16[48,384]{1,0:T(8,128)(2,1)} %refs_0_.1, bf16[48,384]{1,0:T(8,128)(2,1)} %refs_1_.1, s32[2,48]{1,0:T(2,128)} %bitcast.14, f32[2,48]{1,0:T(2,128)} %bitcast.15), custom_call_target="tpu_custom_call" | custom-call | flops 1 | bytes 1 | tf_op jit(solution)/shard_map/pallas_call | solution.py:264
  2.3 1.6 %collective-permute-start = (bf16[2,48,384]{2,1,0:T(8,128)(2,1)}, bf16[2,48,384]{2,1,0:T(8,128)(2,1)S(1)}, u32[]{:S(2)}, u32[]{:S(2)}) collective-permute-start(bf16[2,48,384]{2,1,0:T(8,128)(2,1)} %get-tuple-element.54), channel_id=1, source_target_pairs={{0,1},{1,2},{2,3},{3,0},{4,5},{5,6},{6,7},{7,4},{8,9},{9,10},{10,1... | collective-permute-start | bytes 221192 | tf_op jit(solution)/shard_map/ppermute | solution.py:282
  4.0 1.1 %collective-permute-start.1 = (bf16[2,48,384]{2,1,0:T(8,128)(2,1)}, bf16[2,48,384]{2,1,0:T(8,128)(2,1)S(1)}, u32[]{:S(2)}, u32[]{:S(2)}) collective-permute-start(bf16[2,48,384]{2,1,0:T(8,128)(2,1)} %get-tuple-element.55), channel_id=1, source_target_pairs={{0,2},{1,3},{2,0},{3,1},{4,6},{5,7},{6,4},{7,5},{8,10},{9,11},{10,... | collective-permute-start | bytes 221192 | tf_op jit(solution)/shard_map/ppermute | solution.py:282
  5.0 1.9 %collective-permute-start.2 = (bf16[2,48,384]{2,1,0:T(8,128)(2,1)}, bf16[2,48,384]{2,1,0:T(8,128)(2,1)S(1)}, u32[]{:S(2)}, u32[]{:S(2)}) collective-permute-start(bf16[2,48,384]{2,1,0:T(8,128)(2,1)} %get-tuple-element.56), channel_id=1, source_target_pairs={{0,3},{1,0},{2,1},{3,2},{4,7},{5,4},{6,5},{7,6},{8,11},{9,8},{10,9... | collective-permute-start | bytes 221192 | tf_op jit(solution)/shard_map/ppermute | solution.py:282
  7.0 0.9 %constant_dynamic-update-slice_fusion.3 = bf16[2,192,384]{2,1,0:T(8,128)(2,1)S(1)} fusion(bf16[2,48,384]{2,1,0:T(8,128)(2,1)} %get-tuple-element.53), kind=kLoop, calls=%fused_computation.8 | loop fusion | bytes 147456
  7.9 1.4 %collective-permute-done = bf16[2,48,384]{2,1,0:T(8,128)(2,1)S(1)} collective-permute-done((bf16[2,48,384]{2,1,0:T(8,128)(2,1)}, bf16[2,48,384]{2,1,0:T(8,128)(2,1)S(1)}, u32[]{:S(2)}, u32[]{:S(2)}) %collective-permute-start) | collective-permute-done | bytes 73760 | tf_op jit(solution)/shard_map/ppermute | solution.py:282
  9.3 1.5 %collective-permute-done.1 = bf16[2,48,384]{2,1,0:T(8,128)(2,1)S(1)} collective-permute-done((bf16[2,48,384]{2,1,0:T(8,128)(2,1)}, bf16[2,48,384]{2,1,0:T(8,128)(2,1)S(1)}, u32[]{:S(2)}, u32[]{:S(2)}) %collective-permute-start.1) | collective-permute-done | bytes 73760 | tf_op jit(solution)/shard_map/ppermute | solution.py:282
  10.9 1.3 %collective-permute-done.2 = bf16[2,48,384]{2,1,0:T(8,128)(2,1)S(1)} collective-permute-done((bf16[2,48,384]{2,1,0:T(8,128)(2,1)}, bf16[2,48,384]{2,1,0:T(8,128)(2,1)S(1)}, u32[]{:S(2)}, u32[]{:S(2)}) %collective-permute-start.2) | collective-permute-done | bytes 73760 | tf_op jit(solution)/shard_map/ppermute | solution.py:282
  12.3 1.6 %collective-permute-start.3 = (bf16[2,192,384]{2,1,0:T(8,128)(2,1)S(1)}, bf16[2,192,384]{2,1,0:T(8,128)(2,1)S(1)}, u32[]{:S(2)}, u32[]{:S(2)}) collective-permute-start(bf16[2,192,384]{2,1,0:T(8,128)(2,1)S(1)} %constant_dynamic-update-slice_fusion.own.refs_0_), channel_id=1, source_target_pairs={{0,8},{4,20},{8,0},{12,28},{16,24},{20,4},{24,16},{28,12},{1,9},{5... | collective-permute-start | bytes 884744 | tf_op jit(solution)/shard_map/ppermute | solution.py:278
  13.8 1.5 %collective-permute-start.5 = (bf16[2,192,384]{2,1,0:T(8,128)(2,1)S(1)}, bf16[2,192,384]{2,1,0:T(8,128)(2,1)S(1)}, u32[]{:S(2)}, u32[]{:S(2)}) collective-permute-start(bf16[2,192,384]{2,1,0:T(8,128)(2,1)S(1)} %collective-permute-done.4.near.refs_4_), channel_id=1, source_target_pairs={{0,8},{4,20},{8,0},{12,28},{16,24},{20,4},{24,16},{28,12},{1,9},{5... | collective-permute-start | bytes 884744 | tf_op jit(solution)/shard_map/ppermute | solution.py:278
  15.3 7.2 %shard_map.103 = (bf16[3072,1024]{1,0:T(8,128)(2,1)S(1)}, bf16[3072,1024]{1,0:T(8,128)(2,1)S(1)}, bf16[1024,3072]{1,0:T(8,128)(2,1)S(1)}, f32[192,1024]{1,0:T(8,...) custom-call(s32[1]{0:T(128)} %bitcast.place, ...), custom_call_target="tpu_custom_call" | custom-call | flops 1 | bytes 1 | tf_op jit(solution)/shard_map/pallas_call | solution.py:125
  22.6 0.5 collective-permute-start.8
  23.1 1.5 %collective-permute-start.7 = (bf16[2,192,384]{2,1,0:T(8,128)(2,1)S(1)}, bf16[2,192,384]{2,1,0:T(8,128)(2,1)S(1)}, u32[]{:S(2)}, u32[]{:S(2)}) collective-permute-start(bf16[2,192,384]{2,1,0:T(8,128)(2,1)S(1)} %collective-permute-done.3.refs_0_.refs_1_), channel_id=1, source_target_pairs={{0,16},{4,12},{8,24},{12,4},{16,0},{20,28},{24,8},{28,20},{1,17},{... | collective-permute-start | bytes 884744 | tf_op jit(solution)/shard_map/ppermute | solution.py:278
  24.7 2.6 %shard_map.104 = (f32[192,1024]{1,0:T(8,128)S(1)}, f32[192,1024]{1,0:T(8,128)S(1)}, f32[192,1024]{1,0:T(8,128)S(1)}) custom-call(s32[1]{0:T(128)} %bitcast.place, bf16[2,192,384]{2,1,0:T(8,128)(2,1)S(1)} %collective-permute-done.3.refs_0_.refs_1_, ...), custom_call_target="tpu_custom_call", output_to_operand_aliasing={{0}: (8, {}), {1}: (9, {}), {2}: (10, {})} | custom-call | flops 1 | bytes 1 | tf_op jit(solution)/shard_map/pallas_call | solution.py:144
  27.3 2.5 %collective-permute-done.7.own.refs_3_ = bf16[2,192,384]{2,1,0:T(8,128)(2,1)S(1)} collective-permute-done((bf16[2,192,384]{2,1,0:T(8,128)(2,1)S(1)}, bf16[2,192,384]{2,1,0:T(8,128)(2,1)S(1)}, u32[]{:S(2)}, u32[]{:S(2)}) %collective-permute-start.7) | collective-permute-done | bytes 294944 | tf_op jit(solution)/shard_map/ppermute | solution.py:278
  29.9 1.6 %collective-permute-done.9.sib.refs_7_ = bf16[2,192,384]{2,1,0:T(8,128)(2,1)S(1)} collective-permute-done((bf16[2,192,384]{2,1,0:T(8,128)(2,1)S(1)}, bf16[2,192,384]{2,1,0:T(8,128)(2,1)S(1)}, u32[]{:S(2)}, u32[]{:S(2)}) %collective-permute-start.9) | collective-permute-done | bytes 294944 | tf_op jit(solution)/shard_map/ppermute | solution.py:278
  31.4 2.7 %shard_map.105 = (bf16[192,1024]{1,0:T(8,128)(2,1)S(1)}, bf16[192,1024]{1,0:T(8,128)(2,1)S(1)}, bf16[192,1024]{1,0:T(8,128)(2,1)S(1)}, f32[192,384]{1,0:T(8,128)S(1)}, bf16[192,384]{1,0:T(8,128)(2,1)S(1)}) custom-call(s32[1]{0:T(128)} %bitcast.place, bf16[2,192,384]{2,1,0:T(8,128)(2,1)S(1)} %collective-permute-done.7.own.refs_3_, ...), custom_call_target="tpu_custom_call" | custom-call | flops 1509949440 | tf_op jit(solution)/shard_map/pallas_call | solution.py:179
  34.4 1.2 %shard_map.107 = (f32[192,384]{1,0:T(8,128)S(1)}, bf16[192,384]{1,0:T(8,128)(2,1)S(1)}) custom-call(s32[1]{0:T(128)} %bitcast.place, bf16[192,1024]{1,0:T(8,128)(2,1)S(1)} %get-tuple-element.89.refs_0_.refs_8_, bf16[192,1024]{1,0:T(8,128)(2,1)S(1)} %get-tuple-element.97.refs_1_.refs_8_, bf16[3072,1024]{1,0:T(8,128)(2,1)S(1)} %get-tuple-element.62.refs_4_.wg.refs_2_, ...), custom_call_target="tpu_custom_call" | custom-call | flops 603979776 | tf_op jit(solution)/shard_map/pallas_call | solution.py:196
  35.6 0.4 collective-permute-start.13
  36.1 2.1 %collective-permute-start.11 = (bf16[192,384]{1,0:T(8,128)(2,1)S(1)}, bf16[192,384]{1,0:T(8,128)(2,1)S(1)}, u32[]{:S(2)}, u32[]{:S(2)}) collective-permute-start(bf16[192,384]{1,0:T(8,128)(2,1)S(1)} %convert_add_fusion.3), channel_id=1, source_target_pairs={{0,24},{4,28},{8,16},{12,20},{16,8},{20,12},{24,0},{28,4},{1,25},{... | collective-permute-start | bytes 442376 | tf_op jit(solution)/shard_map/ppermute | solution.py:278
  38.2 1.2 %shard_map.106 = (f32[192,384]{1,0:T(8,128)S(1)}, bf16[192,384]{1,0:T(8,128)(2,1)S(1)}) custom-call(s32[1]{0:T(128)} %bitcast.place, bf16[192,1024]{1,0:T(8,128)(2,1)S(1)} %get-tuple-element.89.refs_0_.refs_8_, bf16[192,1024]{1,0:T(8,128)(2,1)S(1)} %get-tuple-element.97.refs_1_.refs_8_, bf16[3072,1024]{1,0:T(8,128)(2,1)S(1)} %get-tuple-element.62.refs_4_.wg.refs_2_, ...), custom_call_target="tpu_custom_call" | custom-call | flops 603979776 | tf_op jit(solution)/shard_map/pallas_call | solution.py:196
  39.5 1.2 %shard_map.109 = (f32[192,384]{1,0:T(8,128)S(1)}, bf16[192,384]{1,0:T(8,128)(2,1)S(1)}) custom-call(s32[1]{0:T(128)} %bitcast.place, bf16[192,1024]{1,0:T(8,128)(2,1)S(1)} %get-tuple-element.89.refs_0_.refs_8_, bf16[192,1024]{1,0:T(8,128)(2,1)S(1)} %get-tuple-element.97.refs_1_.refs_8_, bf16[3072,1024]{1,0:T(8,128)(2,1)S(1)} %get-tuple-element.62.refs_4_.wg.refs_2_, ...), custom_call_target="tpu_custom_call" | custom-call | flops 603979776 | tf_op jit(solution)/shard_map/pallas_call | solution.py:196
  40.7 0.6 collective-permute-start.14
  41.2 0.9 %collective-permute-start.15 = (bf16[192,384]{1,0:T(8,128)(2,1)S(1)}, bf16[192,384]{1,0:T(8,128)(2,1)S(1)}, u32[]{:S(2)}, u32[]{:S(2)}) collective-permute-start(bf16[192,384]{1,0:T(8,128)(2,1)S(1)} %convert_add_fusion.1), channel_id=1, source_target_pairs={{0,8},{4,12},{8,0},{12,4},{16,24},{20,28},{24,16},{28,20},{1,9},{5... | collective-permute-start | bytes 442376 | tf_op jit(solution)/shard_map/ppermute | solution.py:278
  42.2 0.6 collective-permute-start.16
  42.9 3.4 %shard_map.108 = bf16[3072,1024]{1,0:T(8,128)(2,1)} custom-call(s32[1]{0:T(128)} %bitcast.place, bf16[2,192,384]{2,1,0:T(8,128)(2,1)S(1)} %constant_dynamic-update-slice_fusion.own.refs_0_, bf16[2,192,384]{2,1,0:T(8,128)(2,1)S(1)} %collective-permute-done.3.refs_0_.refs_1_, bf16[2,192,384]{2,1,0:T(8,128)(2,1)S(1)} %collective-permute-done.6.refs_2_, ...), custom_call_target="tpu_custom_call" | custom-call | flops 1207959552 | bytes 6291456 | tf_op jit(solution)/shard_map/pallas_call | solution.py:234
  46.3 0.8 %collective-permute-done.15 = bf16[192,384]{1,0:T(8,128)(2,1)S(1)} collective-permute-done((bf16[192,384]{1,0:T(8,128)(2,1)S(1)}, bf16[192,384]{1,0:T(8,128)(2,1)S(1)}, u32[]{:S(2)}, u32[]{:S(2)}) %collective-permute-start.15) | collective-permute-done | bytes 147488 | tf_op jit(solution)/shard_map/ppermute | solution.py:278
  47.1 0.8 %collective-permute-done.16 = bf16[192,384]{1,0:T(8,128)(2,1)S(1)} collective-permute-done((bf16[192,384]{1,0:T(8,128)(2,1)S(1)}, bf16[192,384]{1,0:T(8,128)(2,1)S(1)}, u32[]{:S(2)}, u32[]{:S(2)}) %collective-permute-start.16) | collective-permute-done | bytes 147488 | tf_op jit(solution)/shard_map/ppermute | solution.py:278
  48.2 1.8 %collective-permute-start.19 = (bf16[48,384]{1,0:T(8,128)(2,1)S(1)}, bf16[48,384]{1,0:T(8,128)(2,1)S(1)}, u32[]{:S(2)}, u32[]{:S(2)}) collective-permute-start(bf16[48,384]{1,0:T(8,128)(2,1)S(1)} %get-tuple-element.103), channel_id=1, source_target_pairs={{0,1},{1,2},{2,3},{3,0},{4,5},{5,6},{6,7},{7,4},{8,9},{9,10},{10,1... | collective-permute-start | bytes 110600 | tf_op jit(solution)/shard_map/ppermute | solution.py:282
  50.1 3.7 %collective-permute-start.18 = (bf16[48,384]{1,0:T(8,128)(2,1)S(1)}, bf16[48,384]{1,0:T(8,128)(2,1)S(1)}, u32[]{:S(2)}, u32[]{:S(2)}) collective-permute-start(bf16[48,384]{1,0:T(8,128)(2,1)S(1)} %get-tuple-element.104), channel_id=1, source_target_pairs={{0,2},{1,3},{2,0},{3,1},{4,6},{5,7},{6,4},{7,5},{8,10},{9,11},{10,... | collective-permute-start | bytes 110600 | tf_op jit(solution)/shard_map/ppermute | solution.py:282
  53.8 5.3 %shard_map.110 = (bf16[3072,1024]{1,0:T(8,128)(2,1)}, bf16[1024,3072]{1,0:T(8,128)(2,1)}) custom-call(s32[1]{0:T(128)} %bitcast.place, bf16[2,192,384]{2,1,0:T(8,128)(2,1)S(1)} %constant_dynamic-update-slice_fusion.own.refs_0_, bf16[2,192,384]{2,1,0:T(8,128)(2,1)S(1)} %collective-permute-done.3.refs_0_.refs_1_, ...), custom_call_target="tpu_custom_call" | custom-call | flops 2415919104 | bytes 12582912 | tf_op jit(solution)/shard_map/pallas_call | solution.py:234
  59.2 0.6 %add_convert_fusion = bf16[48,384]{1,0:T(8,128)(2,1)} fusion(bf16[48,384]{1,0:T(8,128)(2,1)S(1)} %collective-permute-done.19, bf16[48,384]{1,0:T(8,128)(2,1)S(1)} %collective-permute-done.18, bf16[48,384]{1,0:T(8,128)(2,1)S(1)} %collective-permute-done.17, f32[192,384]{1,0:T(8,128)S(1)} %convert_add_fusion), kind=kLoop, calls=%fused_computation.4 | loop fusion | flops 129024 | bytes 221184 | tf_op jit(solution)/shard_map/convert_element_type | solution.py:332
  (28 shorter events, 1.1 us)
Async XLA Ops:
  2.3 7.0 %collective-permute-start = (bf16[2,48,384]{2,1,0:T(8,128)(2,1)}, bf16[2,48,384]{2,1,0:T(8,128)(2,1)S(1)}, u32[]{:S(2)}, u32[]{:S(2)}) collective-permute-start(bf16[2,48,384]{2,1,0:T(8,128)(2,1)} %get-tuple-element.54), channel_id=1, source_target_pairs={{0,1},{1,2},{2,3},{3,0},{4,5},{5,6},{6,7},{7,4},{8,9},{9,10},{10,1... | collective-permute-start | bytes 221192 | tf_op jit(solution)/shard_map/ppermute | solution.py:282
  4.0 6.9 %collective-permute-start.1 = (bf16[2,48,384]{2,1,0:T(8,128)(2,1)}, bf16[2,48,384]{2,1,0:T(8,128)(2,1)S(1)}, u32[]{:S(2)}, u32[]{:S(2)}) collective-permute-start(bf16[2,48,384]{2,1,0:T(8,128)(2,1)} %get-tuple-element.55), channel_id=1, source_target_pairs={{0,2},{1,3},{2,0},{3,1},{4,6},{5,7},{6,4},{7,5},{8,10},{9,11},{10,... | collective-permute-start | bytes 221192 | tf_op jit(solution)/shard_map/ppermute | solution.py:282
  5.0 7.1 %collective-permute-start.2 = (bf16[2,48,384]{2,1,0:T(8,128)(2,1)}, bf16[2,48,384]{2,1,0:T(8,128)(2,1)S(1)}, u32[]{:S(2)}, u32[]{:S(2)}) collective-permute-start(bf16[2,48,384]{2,1,0:T(8,128)(2,1)} %get-tuple-element.56), channel_id=1, source_target_pairs={{0,3},{1,0},{2,1},{3,2},{4,7},{5,4},{6,5},{7,6},{8,11},{9,8},{10,9... | collective-permute-start | bytes 221192 | tf_op jit(solution)/shard_map/ppermute | solution.py:282
  12.2 1.6 %collective-permute-start.4 = (bf16[2,192,384]{2,1,0:T(8,128)(2,1)S(1)}, bf16[2,192,384]{2,1,0:T(8,128)(2,1)S(1)}, u32[]{:S(2)}, u32[]{:S(2)}) collective-permute-start(bf16[2,192,384]{2,1,0:T(8,128)(2,1)S(1)} %constant_dynamic-update-slice_fusion.own.refs_0_), channel_id=1, source_target_pairs={{0,4},{4,0},{8,12},{12,8},{16,20},{20,16},{24,28},{28,24},{1,5},{5... | collective-permute-start | bytes 884744 | tf_op jit(solution)/shard_map/ppermute | solution.py:278
  12.3 10.3 %collective-permute-start.3 = (bf16[2,192,384]{2,1,0:T(8,128)(2,1)S(1)}, bf16[2,192,384]{2,1,0:T(8,128)(2,1)S(1)}, u32[]{:S(2)}, u32[]{:S(2)}) collective-permute-start(bf16[2,192,384]{2,1,0:T(8,128)(2,1)S(1)} %constant_dynamic-update-slice_fusion.own.refs_0_), channel_id=1, source_target_pairs={{0,8},{4,20},{8,0},{12,28},{16,24},{20,4},{24,16},{28,12},{1,9},{5... | collective-permute-start | bytes 884744 | tf_op jit(solution)/shard_map/ppermute | solution.py:278
  13.8 8.7 %collective-permute-start.5 = (bf16[2,192,384]{2,1,0:T(8,128)(2,1)S(1)}, bf16[2,192,384]{2,1,0:T(8,128)(2,1)S(1)}, u32[]{:S(2)}, u32[]{:S(2)}) collective-permute-start(bf16[2,192,384]{2,1,0:T(8,128)(2,1)S(1)} %collective-permute-done.4.near.refs_4_), channel_id=1, source_target_pairs={{0,8},{4,20},{8,0},{12,28},{16,24},{20,4},{24,16},{28,12},{1,9},{5... | collective-permute-start | bytes 884744 | tf_op jit(solution)/shard_map/ppermute | solution.py:278
  22.6 2.1 %collective-permute-start.6 = (bf16[2,192,384]{2,1,0:T(8,128)(2,1)S(1)}, bf16[2,192,384]{2,1,0:T(8,128)(2,1)S(1)}, u32[]{:S(2)}, u32[]{:S(2)}) collective-permute-start(bf16[2,192,384]{2,1,0:T(8,128)(2,1)S(1)} %collective-permute-done.5.refs_1_.refs_5_), channel_id=1, source_target_pairs={{0,4},{4,0},{8,12},{12,8},{16,20},{20,16},{24,28},{28,24},{1,5},{5... | collective-permute-start | bytes 884744 | tf_op jit(solution)/shard_map/ppermute | solution.py:278
  22.6 2.0 %collective-permute-start.8 = (bf16[2,192,384]{2,1,0:T(8,128)(2,1)S(1)}, bf16[2,192,384]{2,1,0:T(8,128)(2,1)S(1)}, u32[]{:S(2)}, u32[]{:S(2)}) collective-permute-start(bf16[2,192,384]{2,1,0:T(8,128)(2,1)S(1)} %collective-permute-done.3.refs_0_.refs_1_), channel_id=1, source_target_pairs={{0,4},{4,0},{8,12},{12,8},{16,20},{20,16},{24,28},{28,24},{1,5},{5... | collective-permute-start | bytes 884744 | tf_op jit(solution)/shard_map/ppermute | solution.py:278
  23.1 6.7 %collective-permute-start.7 = (bf16[2,192,384]{2,1,0:T(8,128)(2,1)S(1)}, bf16[2,192,384]{2,1,0:T(8,128)(2,1)S(1)}, u32[]{:S(2)}, u32[]{:S(2)}) collective-permute-start(bf16[2,192,384]{2,1,0:T(8,128)(2,1)S(1)} %collective-permute-done.3.refs_0_.refs_1_), channel_id=1, source_target_pairs={{0,16},{4,12},{8,24},{12,4},{16,0},{20,28},{24,8},{28,20},{1,17},{... | collective-permute-start | bytes 884744 | tf_op jit(solution)/shard_map/ppermute | solution.py:278
  29.9 1.6 %collective-permute-start.9 = (bf16[2,192,384]{2,1,0:T(8,128)(2,1)S(1)}, bf16[2,192,384]{2,1,0:T(8,128)(2,1)S(1)}, u32[]{:S(2)}, u32[]{:S(2)}) collective-permute-start(bf16[2,192,384]{2,1,0:T(8,128)(2,1)S(1)} %collective-permute-done.7.own.refs_3_), channel_id=1, source_target_pairs={{0,4},{4,0},{8,12},{12,8},{16,20},{20,16},{24,28},{28,24},{1,5},{5... | collective-permute-start | bytes 884744 | tf_op jit(solution)/shard_map/ppermute | solution.py:278
  34.2 1.8 %collective-permute-start.10 = (bf16[192,384]{1,0:T(8,128)(2,1)S(1)}, bf16[192,384]{1,0:T(8,128)(2,1)S(1)}, u32[]{:S(2)}, u32[]{:S(2)}) collective-permute-start(bf16[192,384]{1,0:T(8,128)(2,1)S(1)} %get-tuple-element.76), channel_id=1, source_target_pairs={{0,4},{4,0},{8,12},{12,8},{16,20},{20,16},{24,28},{28,24},{1,5},{5... | collective-permute-start | bytes 442376 | tf_op jit(solution)/shard_map/ppermute | solution.py:278
  35.6 3.8 %collective-permute-start.13 = (bf16[192,384]{1,0:T(8,128)(2,1)S(1)}, bf16[192,384]{1,0:T(8,128)(2,1)S(1)}, u32[]{:S(2)}, u32[]{:S(2)}) collective-permute-start(bf16[192,384]{1,0:T(8,128)(2,1)S(1)} %get-tuple-element.85), channel_id=1, source_target_pairs={{0,4},{4,0},{8,12},{12,8},{16,20},{20,16},{24,28},{28,24},{1,5},{5... | collective-permute-start | bytes 442376 | tf_op jit(solution)/shard_map/ppermute | solution.py:278
  36.1 6.9 %collective-permute-start.11 = (bf16[192,384]{1,0:T(8,128)(2,1)S(1)}, bf16[192,384]{1,0:T(8,128)(2,1)S(1)}, u32[]{:S(2)}, u32[]{:S(2)}) collective-permute-start(bf16[192,384]{1,0:T(8,128)(2,1)S(1)} %convert_add_fusion.3), channel_id=1, source_target_pairs={{0,24},{4,28},{8,16},{12,20},{16,8},{20,12},{24,0},{28,4},{1,25},{... | collective-permute-start | bytes 442376 | tf_op jit(solution)/shard_map/ppermute | solution.py:278
  39.4 2.8 %collective-permute-start.12 = (bf16[192,384]{1,0:T(8,128)(2,1)S(1)}, bf16[192,384]{1,0:T(8,128)(2,1)S(1)}, u32[]{:S(2)}, u32[]{:S(2)}) collective-permute-start(bf16[192,384]{1,0:T(8,128)(2,1)S(1)} %get-tuple-element.83), channel_id=1, source_target_pairs={{0,4},{4,0},{8,12},{12,8},{16,20},{20,16},{24,28},{28,24},{1,5},{5... | collective-permute-start | bytes 442376 | tf_op jit(solution)/shard_map/ppermute | solution.py:278
  40.7 5.6 %collective-permute-start.14 = (bf16[192,384]{1,0:T(8,128)(2,1)S(1)}, bf16[192,384]{1,0:T(8,128)(2,1)S(1)}, u32[]{:S(2)}, u32[]{:S(2)}) collective-permute-start(bf16[192,384]{1,0:T(8,128)(2,1)S(1)} %get-tuple-element.91), channel_id=1, source_target_pairs={{0,4},{4,0},{8,12},{12,8},{16,20},{20,16},{24,28},{28,24},{1,5},{5... | collective-permute-start | bytes 442376 | tf_op jit(solution)/shard_map/ppermute | solution.py:278
  41.2 5.8 %collective-permute-start.15 = (bf16[192,384]{1,0:T(8,128)(2,1)S(1)}, bf16[192,384]{1,0:T(8,128)(2,1)S(1)}, u32[]{:S(2)}, u32[]{:S(2)}) collective-permute-start(bf16[192,384]{1,0:T(8,128)(2,1)S(1)} %convert_add_fusion.1), channel_id=1, source_target_pairs={{0,8},{4,12},{8,0},{12,4},{16,24},{20,28},{24,16},{28,20},{1,9},{5... | collective-permute-start | bytes 442376 | tf_op jit(solution)/shard_map/ppermute | solution.py:278
  42.2 5.6 %collective-permute-start.16 = (bf16[192,384]{1,0:T(8,128)(2,1)S(1)}, bf16[192,384]{1,0:T(8,128)(2,1)S(1)}, u32[]{:S(2)}, u32[]{:S(2)}) collective-permute-start(bf16[192,384]{1,0:T(8,128)(2,1)S(1)} %convert_add_fusion.2), channel_id=1, source_target_pairs={{0,16},{4,20},{8,24},{12,28},{16,0},{20,4},{24,8},{28,12},{1,17},{... | collective-permute-start | bytes 442376 | tf_op jit(solution)/shard_map/ppermute | solution.py:278
  48.0 11.2 %collective-permute-start.17 = (bf16[48,384]{1,0:T(8,128)(2,1)S(1)}, bf16[48,384]{1,0:T(8,128)(2,1)S(1)}, u32[]{:S(2)}, u32[]{:S(2)}) collective-permute-start(bf16[48,384]{1,0:T(8,128)(2,1)S(1)} %get-tuple-element.102), channel_id=1, source_target_pairs={{0,3},{1,0},{2,1},{3,2},{4,7},{5,4},{6,5},{7,6},{8,11},{9,8},{10,9... | collective-permute-start | bytes 110600 | tf_op jit(solution)/shard_map/ppermute | solution.py:282
  48.2 10.9 %collective-permute-start.19 = (bf16[48,384]{1,0:T(8,128)(2,1)S(1)}, bf16[48,384]{1,0:T(8,128)(2,1)S(1)}, u32[]{:S(2)}, u32[]{:S(2)}) collective-permute-start(bf16[48,384]{1,0:T(8,128)(2,1)S(1)} %get-tuple-element.103), channel_id=1, source_target_pairs={{0,1},{1,2},{2,3},{3,0},{4,5},{5,6},{6,7},{7,4},{8,9},{9,10},{10,1... | collective-permute-start | bytes 110600 | tf_op jit(solution)/shard_map/ppermute | solution.py:282
  50.1 9.1 %collective-permute-start.18 = (bf16[48,384]{1,0:T(8,128)(2,1)S(1)}, bf16[48,384]{1,0:T(8,128)(2,1)S(1)}, u32[]{:S(2)}, u32[]{:S(2)}) collective-permute-start(bf16[48,384]{1,0:T(8,128)(2,1)S(1)} %get-tuple-element.104), channel_id=1, source_target_pairs={{0,2},{1,3},{2,0},{3,1},{4,6},{5,7},{6,4},{7,5},{8,10},{9,11},{10,... | collective-permute-start | bytes 110600 | tf_op jit(solution)/shard_map/ppermute | solution.py:282

commit v4 on v3

--- a/solution.py
+++ b/solution.py
@@ -63,6 +63,7 @@
 
 STEP = 256
 LOAD_LIMIT = 28
+UP_FIRST, UP_LAST = (0,), (1, 2, 3)
 
 
 def far(place):
@@ -76,12 +77,10 @@
     return rows, both_cores(core, own[0], sib[0]), both_cores(core, own[1], sib[1])
 
 
-def add_pieces(pieces, weights, acc_in, acc_out, finish, arrived=None):
+def add_pieces(pieces, weights, acc_in, acc_out, finish):
     wg, wu, wd = weights
     for f in range(wg.shape[1] // STEP):
         cols = pl.ds(f * STEP, STEP)
-        if arrived is not None:
-            arrived(f)
         sums = [None if acc is None else acc[:, cols] for acc in acc_in]
         for rows, x, g in pieces:
             terms = (dot(x, wg[rows, cols], 1, 0), dot(x, wu[rows, cols], 1, 0), dot(g, wd[cols, rows], 1, 1))
@@ -98,58 +97,68 @@
     store(cols, hidden_grads(*sums), outs)
 
 
-def load_kernel(place, own, near, wg, wu, wd, wg_here, wu_here, wd_here, gate, up, back, sems):
+def load_kernel(place, own, near, *refs):
+    sources, here, sums, sems = refs[:2], refs[2:4], refs[4:6], refs[6]
+    row, x, _ = pair(place, 0, own, near)
+    wide = x.shape[1]
     copies = []
-    for f in range(wg.shape[1] // STEP):
+    for p in range(4):
+        rows = block_at(place, p, wide)
+        for i, (s, h) in enumerate(zip(sources, here)):
+            copies.append(pltpu.make_async_copy(s.at[rows, :], h.at[rows, :], sems.at[i, p]))
+            copies[-1].start()
+    for copy, weight, total in zip(copies, here, sums):
+        copy.wait()
+        for f in range(weight.shape[1] // STEP):
+            cols = pl.ds(f * STEP, STEP)
+            total[:, cols] = dot(x, weight[row, cols], 1, 0)
+    for copy in copies[2:]:
+        copy.wait()
+
+
+def load(place, own, near, wg, wu):
+    rows, hidden_count = own.shape[1], wg.shape[1]
+    return call(
+        load_kernel,
+        (shape(wg.shape, BF16),) * 2 + (shape((rows, hidden_count), F32),) * 2,
+        [SMEM] + [VMEM] * 2 + [HBM] * 2,
+        [VMEM] * 4,
+        1,
+        1,
+        scratch=[pltpu.SemaphoreType.DMA((2, 4))],
+        limit=36,
+    )(place, own, near, wg, wu)
+
+
+def back_kernel(place, own, near, wd, back):
+    row, _, g = pair(place, 0, own, near)
+    for f in range(wd.shape[0] // STEP):
         cols = pl.ds(f * STEP, STEP)
-        copies.append(
-            [
-                pltpu.make_async_copy(wg.at[:, cols], wg_here.at[:, cols], sems.at[f, 0]),
-                pltpu.make_async_copy(wu.at[:, cols], wu_here.at[:, cols], sems.at[f, 1]),
-                pltpu.make_async_copy(wd.at[cols, :], wd_here.at[cols, :], sems.at[f, 2]),
-            ]
-        )
-        for copy in copies[f]:
-            copy.start()
-
-    def arrived(f):
-        for copy in copies[f]:
-            copy.wait()
-
-    weights = (wg_here, wu_here, wd_here)
-    add_pieces([pair(place, 0, own, near)], weights, (None,) * 3, (gate, up, back), store, arrived)
-
-
-def load_weights(place, own, near, weights):
-    rows, hidden_count = own.shape[1], weights[0].shape[1]
-    return call(
-        load_kernel,
-        tuple(shape(w.shape, BF16) for w in weights) + (shape((rows, hidden_count), F32),) * 3,
-        [SMEM] + [VMEM] * 2 + [HBM] * 3,
-        [VMEM] * 6,
-        1,
-        1,
-        scratch=[pltpu.SemaphoreType.DMA((hidden_count // STEP, 3))],
-        limit=LOAD_LIMIT,
-    )(place, own, near, *weights)
-
-
-def partial_kernel(place, *refs):
-    pieces = [pair(place, 1, *refs[0:2]), pair(place, 2, *refs[2:4])]
-    add_pieces(pieces, refs[4:7], refs[7:10], refs[10:], store)
-
-
-def partial_sums(place, halves, weights, acc):
+        back[:, cols] = dot(g, wd[cols, row], 1, 1)
+
+
+def own_back(place, own, near, wd):
+    rows, hidden_count = own.shape[1], wd.shape[0]
+    return call(
+        back_kernel, shape((rows, hidden_count), F32), [SMEM] + [VMEM] * 3, VMEM, 1, 1
+    )(place, own, near, wd)
+
+
+def partial_kernel(i, place, own, sib, wg, wu, wd, *refs):
+    add_pieces([pair(place, i, own, sib)], (wg, wu, wd), refs[:3], refs[3:], store)
+
+
+def partial_sums(place, i, own, sib, weights, acc):
     rows, hidden_count = acc[0].shape
     return call(
-        partial_kernel,
+        functools.partial(partial_kernel, i),
         (shape((rows, hidden_count), F32),) * 3,
-        [SMEM] + [VMEM] * 10,
+        [SMEM] + [VMEM] * 8,
         [VMEM] * 3,
         1,
         1,
-        aliases={8: 0, 9: 1, 10: 2},
-    )(place, *halves, *weights, *acc)
+        aliases={6: 0, 7: 1, 8: 2},
+    )(place, own, sib, *weights, *acc)
 
 
 def slot_rows(place, p, dg, du, wg, wu, wide):
@@ -203,17 +212,19 @@
     )(place, dg, du, wg, wu)
 
 
-def weight_kernel(arrays, place, *refs):
-    n = len(arrays)
+def weight_kernel(jobs, begun, place, *refs):
+    n = len(jobs)
     own, sib, ds = refs[0:4], refs[4:8], refs[8 : 8 + n]
-    outs, bufs, sems = refs[8 + n : 8 + 2 * n], refs[8 + 2 * n : 8 + 3 * n], refs[8 + 3 * n]
+    refs = refs[8 + n + begun :]
+    outs, bufs, sems = refs[:n], refs[n : 2 * n], refs[2 * n]
     core = place[0] % 2
     wide = 2 * own[0].shape[2]
+    chips = far(place)
     copies = []
-    for i, (array, d, out, buf) in enumerate(zip(arrays, ds, outs, bufs)):
-        for j, p in enumerate(far(place)):
-            rows = block_at(place, p, wide)
-            piece = both_cores(core, own[j][array], sib[j][array])
+    for i, ((array, pieces), d, out, buf) in enumerate(zip(jobs, ds, outs, bufs)):
+        for j, p in enumerate(pieces):
+            rows = block_at(place, chips[p], wide)
+            piece = both_cores(core, own[p][array], sib[p][array])
             if array == 0:
                 buf[j] = dot(piece, d[...], 0, 0).astype(BF16)
                 target = out.at[rows, :]
@@ -226,21 +237,25 @@
         copy.wait()
 
 
-def weight_grads(place, arrays, own, sib, ds):
+def weight_grads(place, jobs, own, sib, ds, begun=None):
     rows, width = own[0].shape[1:]
     hidden_count = ds[0].shape[1]
-    blocks = [(2 * width, hidden_count) if array == 0 else (hidden_count, 2 * width) for array in arrays]
-    outs = [(8 * width, hidden_count) if array == 0 else (hidden_count, 8 * width) for array in arrays]
-    return call(
-        functools.partial(weight_kernel, arrays),
+    blocks = [(2 * width, hidden_count) if array == 0 else (hidden_count, 2 * width) for array, _ in jobs]
+    outs = [(8 * width, hidden_count) if array == 0 else (hidden_count, 8 * width) for array, _ in jobs]
+    count = sum(len(pieces) for _, pieces in jobs)
+    more = [] if begun is None else [begun]
+    return call(
+        functools.partial(weight_kernel, jobs, len(more)),
         tuple(shape(out, BF16) for out in outs),
-        [SMEM] + [VMEM] * (8 + len(ds)),
+        [SMEM] + [VMEM] * (8 + len(ds)) + [HBM] * len(more),
         [HBM] * len(ds),
-        16 * rows * width * hidden_count * len(ds),
-        16 * width * hidden_count * len(ds),
-        scratch=[pltpu.VMEM((4,) + block, BF16) for block in blocks] + [pltpu.SemaphoreType.DMA((len(ds), 4))],
+        4 * rows * width * hidden_count * count,
+        4 * width * hidden_count * count,
+        scratch=[pltpu.VMEM((len(pieces),) + block, BF16) for block, (_, pieces) in zip(blocks, jobs)]
+        + [pltpu.SemaphoreType.DMA((len(ds), 4))],
         limit=LOAD_LIMIT,
-    )(place, *own, *sib, *ds)
+        aliases={9 + len(ds): 0} if more else {},
+    )(place, *own, *sib, *ds, *more)
 
 
 def pack_kernel(groups, place, *refs):
@@ -292,38 +307,47 @@
     own = jnp.concatenate(blocks, axis=1)
     near = across(own, 1)
     here = across(own, 2, 4), across(near, 2, 4)
-    weights = (w_gate[0], w_up[0], w_down[0])
-    loaded = load_weights(place, own, near, weights)
-    weights, acc = loaded[:3], loaded[3:]
-    here, acc = lax.optimization_barrier((here, acc))
-    diag = across(here[0], 4, 2)
-    there = across(here[1], 1), across(here[0], 1)
-    acc = partial_sums(place, here + there, weights, acc)
+    wg, wu, gate, up = load(place, own, near, w_gate[0], w_up[0])
+    first, gate, up = lax.optimization_barrier((here[0], gate, up))
+    diag = across(first, 4, 2)
+    there_second = across(first, 1)
+    wd = w_down[0]
+    back = own_back(place, own, near, wd)
+    second, back = lax.optimization_barrier((here[1], back))
+    there_first = across(second, 1)
+    weights, acc = (wg, wu, wd), (gate, up, back)
+    acc = partial_sums(place, 1, first, second, weights, acc)
     diag, acc = lax.optimization_barrier((diag, acc))
     diag_near = across(diag, 1)
+    acc = partial_sums(place, 2, there_first, there_second, weights, acc)
     hid, dg, du, keep, send = middle(place, diag, diag_near, weights, acc)
-    mine_of = own, here[0], there[0], diag
-    other_of = near, here[1], there[1], diag_near
-    wg, wu = weights[:2]
+    mine_of = own, first, there_first, diag
+    other_of = near, second, there_second, diag_near
 
     def chip_sum(keep, send):
         return keep + across(send, 1).astype(F32)
 
-    share = slots(place, 1, dg, du, wg, wu)
-    diagonal, dg, du = lax.optimization_barrier((chip_sum(keep, send), dg, du))
-    parts = [across(diagonal.astype(BF16), 6)]
-    for p in (1, 2):
-        later = slots(place, (p + 1) % 3, dg, du, wg, wu)
-        total, dg, du = lax.optimization_barrier((chip_sum(*share), dg, du))
-        parts.append(across(total.astype(BF16), 2 * p))
-        share = later
+    shares = {1: slots(place, 1, dg, du, wg, wu)}
+    total, dg, du = lax.optimization_barrier((chip_sum(keep, send), dg, du))
+    parts = [across(total.astype(BF16), 6)]
+    shares[2] = slots(place, 2, dg, du, wg, wu)
+    parts.append(across(chip_sum(*shares[1]).astype(BF16), 2))
+    total, dg, du = lax.optimization_barrier((chip_sum(*shares[2]), dg, du))
+    parts.append(across(total.astype(BF16), 4))
+    share = slots(place, 0, dg, du, wg, wu)
+    share, dg = lax.optimization_barrier((share, dg))
+    (grad_gate,) = weight_grads(place, [(0, (0, 1))], mine_of, other_of, (dg,))
     mine = chip_sum(*share)
-    parts[0], dg = lax.optimization_barrier((parts[0], dg))
-    (grad_gate,) = weight_grads(place, (0,), mine_of, other_of, (dg,))
+    parts[0], dg, grad_gate = lax.optimization_barrier((parts[0], dg, grad_gate))
+    grad_gate, grad_up = weight_grads(
+        place, [(0, (2, 3)), (0, UP_FIRST)], mine_of, other_of, (dg, du), grad_gate
+    )
     for part in parts:
         mine = mine + part.astype(F32)
-    mine, du, hid = lax.optimization_barrier((mine, du, hid))
-    grad_up, grad_down = weight_grads(place, (0, 1), mine_of, other_of, (du, hid))
+    mine, hid, grad_up = lax.optimization_barrier((mine, hid, grad_up))
+    grad_up, grad_down = weight_grads(
+        place, [(0, UP_LAST), (1, (0, 1, 2, 3))], mine_of, other_of, (du, hid), grad_up
+    )
     mine = mine.reshape(groups, tok_count, width)
     back = mine[0]
     sent = mine.astype(BF16)

time: 60 us -> 57 us (0.950)
  waiting for transfers between devices: 10.1 us -> 6.95 us
    ppermute x14, waiting for transfers between devices: 5.81 us -> 2.68 us  [across(): lax.ppermute(array, 'tensor', [(i, i ^ masks[i % 2]) for i in range(8)])]
    pallas_call x4 -> x7, Pallas kernels: 18.5 us -> 18.4 us  [the longest x3 10 us: weight_grads(): call(functools.partial(weight_kernel, jobs, len(more)), tuple((shape(out,...]
  transfers between devices with their start and end apart: 20 -> 20, of which waited for: 8 -> 5; matrix products, arithmetic and copies ran while one was open for 2% -> 2% of each run, Pallas kernels for 37% -> 39%
where the time goes in v4:
time: 57 us; the launch traced here: 56.6 us
  Pallas kernels  26.4 us (46%)
  starting transfers between devices  20.6 us (36%)
  waiting for transfers between devices  6.95 us (12%)
  local copies, waits for them, and re-layouts  0.96 us (2%)
  between operations  0.87 us (2%)
  other arithmetic  0.83 us (1%)
    ppermute x6, starting transfers between devices, along(): lax.ppermute(array, 'expert', [(i, (i + distance) % count) for i in range...  10.8 us
    pallas_call x3, Pallas kernels, weight_grads(): call(functools.partial(weight_kernel, jobs, len(more)), tuple((shape(out,...  10 us
    ppermute x14, starting transfers between devices, across(): lax.ppermute(array, 'tensor', [(i, i ^ masks[i % 2]) for i in range(8)])  9.82 us
    pallas_call x1, Pallas kernels, load(): call(load_kernel, (shape(wg.shape, BF16),) * 2 + (shape((rows, hidden_cou...  4.85 us
    ppermute x6, waiting for transfers between devices, along(): lax.ppermute(array, 'expert', [(i, (i + distance) % count) for i in range...  4.27 us
    pallas_call x3, Pallas kernels, slots(): call(functools.partial(slot_kernel, p), (shape((rows, width), F32), shape...  3.57 us
    pallas_call x2, Pallas kernels, partial_sums(): call(functools.partial(partial_kernel, i), (shape((rows, hidden_count), F...  2.85 us
    pallas_call x1, Pallas kernels, middle(): call(middle_kernel, (shape((rows, hidden_count), BF16),) * 3 + (shape((ro...  2.72 us
  transfers between devices with their start and end apart: 20, of which 5 were waited for; matrix products, arithmetic and copies ran while one was open for 2% of the time, Pallas kernels for 39%

profile of v4, /device:TPU:8, one launch (start us, length us, event | category | flops | bytes accessed | tf_op | source)
XLA Modules:
  0.0 56.6 jit_solution(3500428415917801997)
XLA Ops:
  0.6 1.7 %shard_map.102 = (bf16[2,48,384]{2,1,0:T(8,128)(2,1)}, bf16[2,48,384]{2,1,0:T(8,128)(2,1)}, bf16[2,48,384]{2,1,0:T(8,128)(2,1)}, bf16[2,48,384]{2,1,0:T(8,128)(2,1)}) custom-call(s32[1]{0:T(128)} %bitcast.1.place, bf16[48,384]{1,0:T(8,128)(2,1)} %refs_0_.1, bf16[48,384]{1,0:T(8,128)(2,1)} %refs_1_.1, s32[2,48]{1,0:T(2,128)} %bitcast.20, f32[2,48]{1,0:T(2,128)} %bitcast.21), custom_call_target="tpu_custom_call" | custom-call | flops 1 | bytes 1 | tf_op jit(solution)/shard_map/pallas_call | solution.py:279
  2.3 1.6 %collective-permute-start = (bf16[2,48,384]{2,1,0:T(8,128)(2,1)}, bf16[2,48,384]{2,1,0:T(8,128)(2,1)S(1)}, u32[]{:S(2)}, u32[]{:S(2)}) collective-permute-start(bf16[2,48,384]{2,1,0:T(8,128)(2,1)} %get-tuple-element.58), channel_id=1, source_target_pairs={{0,1},{1,2},{2,3},{3,0},{4,5},{5,6},{6,7},{7,4},{8,9},{9,10},{10,1... | collective-permute-start | bytes 221192 | tf_op jit(solution)/shard_map/ppermute | solution.py:297
  4.0 1.1 %collective-permute-start.1 = (bf16[2,48,384]{2,1,0:T(8,128)(2,1)}, bf16[2,48,384]{2,1,0:T(8,128)(2,1)S(1)}, u32[]{:S(2)}, u32[]{:S(2)}) collective-permute-start(bf16[2,48,384]{2,1,0:T(8,128)(2,1)} %get-tuple-element.59), channel_id=1, source_target_pairs={{0,2},{1,3},{2,0},{3,1},{4,6},{5,7},{6,4},{7,5},{8,10},{9,11},{10,... | collective-permute-start | bytes 221192 | tf_op jit(solution)/shard_map/ppermute | solution.py:297
  5.0 1.9 %collective-permute-start.2 = (bf16[2,48,384]{2,1,0:T(8,128)(2,1)}, bf16[2,48,384]{2,1,0:T(8,128)(2,1)S(1)}, u32[]{:S(2)}, u32[]{:S(2)}) collective-permute-start(bf16[2,48,384]{2,1,0:T(8,128)(2,1)} %get-tuple-element.60), channel_id=1, source_target_pairs={{0,3},{1,0},{2,1},{3,2},{4,7},{5,4},{6,5},{7,6},{8,11},{9,8},{10,9... | collective-permute-start | bytes 221192 | tf_op jit(solution)/shard_map/ppermute | solution.py:297
  7.0 0.9 %constant_dynamic-update-slice_fusion.3 = bf16[2,192,384]{2,1,0:T(8,128)(2,1)S(1)} fusion(bf16[2,48,384]{2,1,0:T(8,128)(2,1)} %get-tuple-element.57), kind=kLoop, calls=%fused_computation.8 | loop fusion | bytes 147456
  7.9 1.4 %collective-permute-done = bf16[2,48,384]{2,1,0:T(8,128)(2,1)S(1)} collective-permute-done((bf16[2,48,384]{2,1,0:T(8,128)(2,1)}, bf16[2,48,384]{2,1,0:T(8,128)(2,1)S(1)}, u32[]{:S(2)}, u32[]{:S(2)}) %collective-permute-start) | collective-permute-done | bytes 73760 | tf_op jit(solution)/shard_map/ppermute | solution.py:297
  9.3 1.5 %collective-permute-done.1 = bf16[2,48,384]{2,1,0:T(8,128)(2,1)S(1)} collective-permute-done((bf16[2,48,384]{2,1,0:T(8,128)(2,1)}, bf16[2,48,384]{2,1,0:T(8,128)(2,1)S(1)}, u32[]{:S(2)}, u32[]{:S(2)}) %collective-permute-start.1) | collective-permute-done | bytes 73760 | tf_op jit(solution)/shard_map/ppermute | solution.py:297
  10.9 1.3 %collective-permute-done.2 = bf16[2,48,384]{2,1,0:T(8,128)(2,1)S(1)} collective-permute-done((bf16[2,48,384]{2,1,0:T(8,128)(2,1)}, bf16[2,48,384]{2,1,0:T(8,128)(2,1)S(1)}, u32[]{:S(2)}, u32[]{:S(2)}) %collective-permute-start.2) | collective-permute-done | bytes 73760 | tf_op jit(solution)/shard_map/ppermute | solution.py:297
  12.3 1.6 %collective-permute-start.3 = (bf16[2,192,384]{2,1,0:T(8,128)(2,1)S(1)}, bf16[2,192,384]{2,1,0:T(8,128)(2,1)S(1)}, u32[]{:S(2)}, u32[]{:S(2)}) collective-permute-start(bf16[2,192,384]{2,1,0:T(8,128)(2,1)S(1)} %constant_dynamic-update-slice_fusion.own.refs_0_), channel_id=1, source_target_pairs={{0,8},{4,20},{8,0},{12,28},{16,24},{20,4},{24,16},{28,12},{1,9},{5... | collective-permute-start | bytes 884744 | tf_op jit(solution)/shard_map/ppermute | solution.py:293
  13.9 1.5 %collective-permute-start.5 = (bf16[2,192,384]{2,1,0:T(8,128)(2,1)S(1)}, bf16[2,192,384]{2,1,0:T(8,128)(2,1)S(1)}, u32[]{:S(2)}, u32[]{:S(2)}) collective-permute-start(bf16[2,192,384]{2,1,0:T(8,128)(2,1)S(1)} %collective-permute-done.4.near.refs_4_), channel_id=1, source_target_pairs={{0,8},{4,20},{8,0},{12,28},{16,24},{20,4},{24,16},{28,12},{1,9},{5... | collective-permute-start | bytes 884744 | tf_op jit(solution)/shard_map/ppermute | solution.py:293
  15.3 4.9 %shard_map.103 = (bf16[3072,1024]{1,0:T(8,128)(2,1)S(1)}, bf16[3072,1024]{1,0:T(8,128)(2,1)S(1)}, f32[192,1024]{1,0:T(8,128)S(1)}, f32[192,1024]{1,0:T(8,128)S(1)}) custom-call(s32[1]{0:T(128)} %bitcast.place, bf16[2,192,384]{2,1,0:T(8,128)(2,1)S(1)} %constant_dynamic-update-slice_fusion.own.refs_0_, ...), custom_call_target="tpu_custom_call" | custom-call | flops 1 | bytes 1 | tf_op jit(solution)/shard_map/pallas_call | solution.py:121
  20.2 1.6 %collective-permute-start.7 = (bf16[2,192,384]{2,1,0:T(8,128)(2,1)S(1)}, bf16[2,192,384]{2,1,0:T(8,128)(2,1)S(1)}, u32[]{:S(2)}, u32[]{:S(2)}) collective-permute-start(bf16[2,192,384]{2,1,0:T(8,128)(2,1)S(1)} %collective-permute-done.3.own.refs_1_), channel_id=1, source_target_pairs={{0,16},{4,12},{8,24},{12,4},{16,0},{20,28},{24,8},{28,20},{1,17},{... | collective-permute-start | bytes 884744 | tf_op jit(solution)/shard_map/ppermute | solution.py:293
  21.8 0.7 %shard_map.104.refs_2_ = f32[192,1024]{1,0:T(8,128)S(1)} custom-call(s32[1]{0:T(128)} %bitcast.place, bf16[2,192,384]{2,1,0:T(8,128)(2,1)S(1)} %constant_dynamic-update-slice_fusion.own.refs_0_, bf16[2,192,384]{2,1,0:T(8,128)(2,1)S(1)} %collective-permute-done.4.near.refs_4_, bf16[1024,3072]{1,0:T(8,128)(2,1)S(1)} %bitcast.12), custom_call_target="tpu_custom_call" | custom-call | flops 1 | bytes 1 | tf_op jit(solution)/shard_map/pallas_call | solution.py:142
  22.5 0.6 collective-permute-start.6
  23.1 1.4 %shard_map.105 = (f32[192,1024]{1,0:T(8,128)S(1)}, f32[192,1024]{1,0:T(8,128)S(1)}, f32[192,1024]{1,0:T(8,128)S(1)}) custom-call(s32[1]{0:T(128)} %bitcast.place, bf16[2,192,384]{2,1,0:T(8,128)(2,1)S(1)} %collective-permute-done.3.own.refs_1_, ...), custom_call_target="tpu_custom_call", output_to_operand_aliasing={{0}: (6, {}), {1}: (7, {}), {2}: (8, {})} | custom-call | flops 1 | bytes 1 | tf_op jit(solution)/shard_map/pallas_call | solution.py:153
  24.5 2.5 %collective-permute-done.7.own.refs_3_ = bf16[2,192,384]{2,1,0:T(8,128)(2,1)S(1)} collective-permute-done((bf16[2,192,384]{2,1,0:T(8,128)(2,1)S(1)}, bf16[2,192,384]{2,1,0:T(8,128)(2,1)S(1)}, u32[]{:S(2)}, u32[]{:S(2)}) %collective-permute-start.7) | collective-permute-done | bytes 294944 | tf_op jit(solution)/shard_map/ppermute | solution.py:293
  27.0 1.4 %shard_map.106 = (f32[192,1024]{1,0:T(8,128)S(1)}, f32[192,1024]{1,0:T(8,128)S(1)}, f32[192,1024]{1,0:T(8,128)S(1)}) custom-call(s32[1]{0:T(128)} %bitcast.place, bf16[2,192,384]{2,1,0:T(8,128)(2,1)S(1)} %collective-permute-done.6.own.refs_2_, ...), custom_call_target="tpu_custom_call", output_to_operand_aliasing={{0}: (6, {}), {1}: (7, {}), {2}: (8, {})} | custom-call | flops 1 | bytes 1 | tf_op jit(solution)/shard_map/pallas_call | solution.py:153
  28.6 2.7 %shard_map.107 = (bf16[192,1024]{1,0:T(8,128)(2,1)S(1)}, bf16[192,1024]{1,0:T(8,128)(2,1)S(1)}, bf16[192,1024]{1,0:T(8,128)(2,1)S(1)}, f32[192,384]{1,0:T(8,128)S(1)}, bf16[192,384]{1,0:T(8,128)(2,1)S(1)}) custom-call(s32[1]{0:T(128)} %bitcast.place, bf16[2,192,384]{2,1,0:T(8,128)(2,1)S(1)} %collective-permute-done.7.own.refs_3_, ...), custom_call_target="tpu_custom_call" | custom-call | flops 1509949440 | tf_op jit(solution)/shard_map/pallas_call | solution.py:188
  31.3 0.4 collective-permute-start.10
  31.8 1.2 %shard_map.112 = (f32[192,384]{1,0:T(8,128)S(1)}, bf16[192,384]{1,0:T(8,128)(2,1)S(1)}) custom-call(s32[1]{0:T(128)} %bitcast.place, bf16[192,1024]{1,0:T(8,128)(2,1)S(1)} %get-tuple-element.94.refs_0_.refs_8_, bf16[192,1024]{1,0:T(8,128)(2,1)S(1)} %get-tuple-element.90.refs_1_.refs_9_.refs_8_, bf16[3072,1024]{1,0:T(8,128)(2,1)S(1)} %get-tuple-element.65.wg.refs_2_, ...), custom_call_target="tpu_custom_call" | custom-call | flops 603979776 | tf_op jit(solution)/shard_map/pallas_call | solution.py:205
  33.2 1.6 %collective-permute-start.11 = (bf16[192,384]{1,0:T(8,128)(2,1)S(1)}, bf16[192,384]{1,0:T(8,128)(2,1)S(1)}, u32[]{:S(2)}, u32[]{:S(2)}) collective-permute-start(bf16[192,384]{1,0:T(8,128)(2,1)S(1)} %convert_add_fusion.2), channel_id=1, source_target_pairs={{0,24},{4,28},{8,16},{12,20},{16,8},{20,12},{24,0},{28,4},{1,25},{... | collective-permute-start | bytes 442376 | tf_op jit(solution)/shard_map/ppermute | solution.py:293
  34.8 1.2 %shard_map.108 = (f32[192,384]{1,0:T(8,128)S(1)}, bf16[192,384]{1,0:T(8,128)(2,1)S(1)}) custom-call(s32[1]{0:T(128)} %bitcast.place, bf16[192,1024]{1,0:T(8,128)(2,1)S(1)} %get-tuple-element.94.refs_0_.refs_8_, bf16[192,1024]{1,0:T(8,128)(2,1)S(1)} %get-tuple-element.90.refs_1_.refs_9_.refs_8_, bf16[3072,1024]{1,0:T(8,128)(2,1)S(1)} %get-tuple-element.65.wg.refs_2_, ...), custom_call_target="tpu_custom_call" | custom-call | flops 603979776 | tf_op jit(solution)/shard_map/pallas_call | solution.py:205
  36.2 1.5 %collective-permute-start.15 = (bf16[192,384]{1,0:T(8,128)(2,1)S(1)}, bf16[192,384]{1,0:T(8,128)(2,1)S(1)}, u32[]{:S(2)}, u32[]{:S(2)}) collective-permute-start(bf16[192,384]{1,0:T(8,128)(2,1)S(1)} %add_convert_fusion), channel_id=1, source_target_pairs={{0,8},{4,12},{8,0},{12,4},{16,24},{20,28},{24,16},{28,20},{1,9},{5... | collective-permute-start | bytes 442376 | tf_op jit(solution)/shard_map/ppermute | solution.py:293
  37.7 0.6 collective-permute-start.16
  38.3 1.2 %shard_map.109 = (f32[192,384]{1,0:T(8,128)S(1)}, bf16[192,384]{1,0:T(8,128)(2,1)S(1)}) custom-call(s32[1]{0:T(128)} %bitcast.place, bf16[192,1024]{1,0:T(8,128)(2,1)S(1)} %get-tuple-element.94.refs_0_.refs_8_, bf16[192,1024]{1,0:T(8,128)(2,1)S(1)} %get-tuple-element.90.refs_1_.refs_9_.refs_8_, bf16[3072,1024]{1,0:T(8,128)(2,1)S(1)} %get-tuple-element.65.wg.refs_2_, ...), custom_call_target="tpu_custom_call" | custom-call | flops 603979776 | tf_op jit(solution)/shard_map/pallas_call | solution.py:205
  39.6 2.3 %shard_map.110.refs_10_ = bf16[3072,1024]{1,0:T(8,128)(2,1)} custom-call(s32[1]{0:T(128)} %bitcast.place, bf16[2,192,384]{2,1,0:T(8,128)(2,1)S(1)} %constant_dynamic-update-slice_fusion.own.refs_0_, bf16[2,192,384]{2,1,0:T(8,128)(2,1)S(1)} %collective-permute-done.3.own.refs_1_, bf16[2,192,384]{2,1,0:T(8,128)(2,1)S(1)} %collective-permute-done.6.own.refs_2_, ...), custom_call_target="tpu_custom_call" | custom-call | flops 603979776 | bytes 3145728 | tf_op jit(solution)/shard_map/pallas_call | solution.py:247
  41.9 2.9 %shard_map.111 = (bf16[3072,1024]{1,0:T(8,128)(2,1)}, bf16[3072,1024]{1,0:T(8,128)(2,1)}) custom-call(s32[1]{0:T(128)} %bitcast.place, bf16[2,192,384]{2,1,0:T(8,128)(2,1)S(1)} %constant_dynamic-update-slice_fusion.own.refs_0_, bf16[2,192,384]{2,1,0:T(8,128)(2,1)S(1)} %collective-permute-done.3.own.refs_1_, ...), custom_call_target="tpu_custom_call", output_to_operand_aliasing={{0}: (11, {})} | custom-call | flops 905969664 | bytes 4718592 | tf_op jit(solution)/shard_map/pallas_call | solution.py:247
  45.0 0.4 collective-permute-start.17
  45.4 1.8 %collective-permute-start.19 = (bf16[48,384]{1,0:T(8,128)(2,1)S(1)}, bf16[48,384]{1,0:T(8,128)(2,1)S(1)}, u32[]{:S(2)}, u32[]{:S(2)}) collective-permute-start(bf16[48,384]{1,0:T(8,128)(2,1)S(1)} %get-tuple-element.111), channel_id=1, source_target_pairs={{0,1},{1,2},{2,3},{3,0},{4,5},{5,6},{6,7},{7,4},{8,9},{9,10},{10,1... | collective-permute-start | bytes 110600 | tf_op jit(solution)/shard_map/ppermute | solution.py:297
  47.3 3.8 %collective-permute-start.18 = (bf16[48,384]{1,0:T(8,128)(2,1)S(1)}, bf16[48,384]{1,0:T(8,128)(2,1)S(1)}, u32[]{:S(2)}, u32[]{:S(2)}) collective-permute-start(bf16[48,384]{1,0:T(8,128)(2,1)S(1)} %get-tuple-element.112), channel_id=1, source_target_pairs={{0,2},{1,3},{2,0},{3,1},{4,6},{5,7},{6,4},{7,5},{8,10},{9,11},{10,... | collective-permute-start | bytes 110600 | tf_op jit(solution)/shard_map/ppermute | solution.py:297
  51.1 4.8 %shard_map.113 = (bf16[3072,1024]{1,0:T(8,128)(2,1)}, bf16[1024,3072]{1,0:T(8,128)(2,1)}) custom-call(s32[1]{0:T(128)} %bitcast.place, bf16[2,192,384]{2,1,0:T(8,128)(2,1)S(1)} %constant_dynamic-update-slice_fusion.own.refs_0_, bf16[2,192,384]{2,1,0:T(8,128)(2,1)S(1)} %collective-permute-done.3.own.refs_1_, ...), custom_call_target="tpu_custom_call", output_to_operand_aliasing={{0}: (11, {})} | custom-call | flops 2113929216 | bytes 11010048 | tf_op jit(solution)/shard_map/pallas_call | solution.py:247
  56.0 0.6 %add_convert_fusion.1 = bf16[48,384]{1,0:T(8,128)(2,1)} fusion(bf16[48,384]{1,0:T(8,128)(2,1)S(1)} %collective-permute-done.19, bf16[48,384]{1,0:T(8,128)(2,1)S(1)} %collective-permute-done.18, bf16[48,384]{1,0:T(8,128)(2,1)S(1)} %collective-permute-done.17, f32[192,384]{1,0:T(8,128)S(1)} %convert_add_fusion), kind=kLoop, calls=%fused_computation.4 | loop fusion | flops 129024 | bytes 221184 | tf_op jit(solution)/shard_map/convert_element_type | solution.py:356
  (36 shorter events, 1.0 us)
Async XLA Ops:
  2.3 7.0 %collective-permute-start = (bf16[2,48,384]{2,1,0:T(8,128)(2,1)}, bf16[2,48,384]{2,1,0:T(8,128)(2,1)S(1)}, u32[]{:S(2)}, u32[]{:S(2)}) collective-permute-start(bf16[2,48,384]{2,1,0:T(8,128)(2,1)} %get-tuple-element.58), channel_id=1, source_target_pairs={{0,1},{1,2},{2,3},{3,0},{4,5},{5,6},{6,7},{7,4},{8,9},{9,10},{10,1... | collective-permute-start | bytes 221192 | tf_op jit(solution)/shard_map/ppermute | solution.py:297
  4.0 6.9 %collective-permute-start.1 = (bf16[2,48,384]{2,1,0:T(8,128)(2,1)}, bf16[2,48,384]{2,1,0:T(8,128)(2,1)S(1)}, u32[]{:S(2)}, u32[]{:S(2)}) collective-permute-start(bf16[2,48,384]{2,1,0:T(8,128)(2,1)} %get-tuple-element.59), channel_id=1, source_target_pairs={{0,2},{1,3},{2,0},{3,1},{4,6},{5,7},{6,4},{7,5},{8,10},{9,11},{10,... | collective-permute-start | bytes 221192 | tf_op jit(solution)/shard_map/ppermute | solution.py:297
  5.0 7.1 %collective-permute-start.2 = (bf16[2,48,384]{2,1,0:T(8,128)(2,1)}, bf16[2,48,384]{2,1,0:T(8,128)(2,1)S(1)}, u32[]{:S(2)}, u32[]{:S(2)}) collective-permute-start(bf16[2,48,384]{2,1,0:T(8,128)(2,1)} %get-tuple-element.60), channel_id=1, source_target_pairs={{0,3},{1,0},{2,1},{3,2},{4,7},{5,4},{6,5},{7,6},{8,11},{9,8},{10,9... | collective-permute-start | bytes 221192 | tf_op jit(solution)/shard_map/ppermute | solution.py:297
  12.2 9.6 %slice-start = ((s8[6291456]{0:T(1024)(128)(4,1)}), s8[2097152]{0:T(1024)(128)(4,1)S(1)}, s32[]{:S(2)}) async-start(s8[6291456]{0:T(1024)(128)(4,1)} %bitcast.10), calls=%async_computation | async-start | bytes 4194304
  12.2 1.6 %collective-permute-start.4 = (bf16[2,192,384]{2,1,0:T(8,128)(2,1)S(1)}, bf16[2,192,384]{2,1,0:T(8,128)(2,1)S(1)}, u32[]{:S(2)}, u32[]{:S(2)}) collective-permute-start(bf16[2,192,384]{2,1,0:T(8,128)(2,1)S(1)} %constant_dynamic-update-slice_fusion.own.refs_0_), channel_id=1, source_target_pairs={{0,4},{4,0},{8,12},{12,8},{16,20},{20,16},{24,28},{28,24},{1,5},{5... | collective-permute-start | bytes 884744 | tf_op jit(solution)/shard_map/ppermute | solution.py:293
  12.3 7.9 %collective-permute-start.3 = (bf16[2,192,384]{2,1,0:T(8,128)(2,1)S(1)}, bf16[2,192,384]{2,1,0:T(8,128)(2,1)S(1)}, u32[]{:S(2)}, u32[]{:S(2)}) collective-permute-start(bf16[2,192,384]{2,1,0:T(8,128)(2,1)S(1)} %constant_dynamic-update-slice_fusion.own.refs_0_), channel_id=1, source_target_pairs={{0,8},{4,20},{8,0},{12,28},{16,24},{20,4},{24,16},{28,12},{1,9},{5... | collective-permute-start | bytes 884744 | tf_op jit(solution)/shard_map/ppermute | solution.py:293
  13.9 8.7 %collective-permute-start.5 = (bf16[2,192,384]{2,1,0:T(8,128)(2,1)S(1)}, bf16[2,192,384]{2,1,0:T(8,128)(2,1)S(1)}, u32[]{:S(2)}, u32[]{:S(2)}) collective-permute-start(bf16[2,192,384]{2,1,0:T(8,128)(2,1)S(1)} %collective-permute-done.4.near.refs_4_), channel_id=1, source_target_pairs={{0,8},{4,20},{8,0},{12,28},{16,24},{20,4},{24,16},{28,12},{1,9},{5... | collective-permute-start | bytes 884744 | tf_op jit(solution)/shard_map/ppermute | solution.py:293
  15.3 6.5 %slice-start.1 = ((s8[6291456]{0:T(1024)(128)(4,1)}), s8[4194304]{0:T(1024)(128)(4,1)S(1)}, s32[]{:S(2)}) async-start(s8[6291456]{0:T(1024)(128)(4,1)} %bitcast.10), calls=%async_computation.1 | async-start | bytes 8388608
  20.2 6.8 %collective-permute-start.7 = (bf16[2,192,384]{2,1,0:T(8,128)(2,1)S(1)}, bf16[2,192,384]{2,1,0:T(8,128)(2,1)S(1)}, u32[]{:S(2)}, u32[]{:S(2)}) collective-permute-start(bf16[2,192,384]{2,1,0:T(8,128)(2,1)S(1)} %collective-permute-done.3.own.refs_1_), channel_id=1, source_target_pairs={{0,16},{4,12},{8,24},{12,4},{16,0},{20,28},{24,8},{28,20},{1,17},{... | collective-permute-start | bytes 884744 | tf_op jit(solution)/shard_map/ppermute | solution.py:293
  21.8 5.2 %collective-permute-start.8 = (bf16[2,192,384]{2,1,0:T(8,128)(2,1)S(1)}, bf16[2,192,384]{2,1,0:T(8,128)(2,1)S(1)}, u32[]{:S(2)}, u32[]{:S(2)}) collective-permute-start(bf16[2,192,384]{2,1,0:T(8,128)(2,1)S(1)} %collective-permute-done.3.own.refs_1_), channel_id=1, source_target_pairs={{0,4},{4,0},{8,12},{12,8},{16,20},{20,16},{24,28},{28,24},{1,5},{5... | collective-permute-start | bytes 884744 | tf_op jit(solution)/shard_map/ppermute | solution.py:293
  22.5 4.5 %collective-permute-start.6 = (bf16[2,192,384]{2,1,0:T(8,128)(2,1)S(1)}, bf16[2,192,384]{2,1,0:T(8,128)(2,1)S(1)}, u32[]{:S(2)}, u32[]{:S(2)}) collective-permute-start(bf16[2,192,384]{2,1,0:T(8,128)(2,1)S(1)} %collective-permute-done.5.sib.refs_5_), channel_id=1, source_target_pairs={{0,4},{4,0},{8,12},{12,8},{16,20},{20,16},{24,28},{28,24},{1,5},{5... | collective-permute-start | bytes 884744 | tf_op jit(solution)/shard_map/ppermute | solution.py:293
  27.0 1.6 %collective-permute-start.9 = (bf16[2,192,384]{2,1,0:T(8,128)(2,1)S(1)}, bf16[2,192,384]{2,1,0:T(8,128)(2,1)S(1)}, u32[]{:S(2)}, u32[]{:S(2)}) collective-permute-start(bf16[2,192,384]{2,1,0:T(8,128)(2,1)S(1)} %collective-permute-done.7.own.refs_3_), channel_id=1, source_target_pairs={{0,4},{4,0},{8,12},{12,8},{16,20},{20,16},{24,28},{28,24},{1,5},{5... | collective-permute-start | bytes 884744 | tf_op jit(solution)/shard_map/ppermute | solution.py:293
  31.3 1.8 %collective-permute-start.10 = (bf16[192,384]{1,0:T(8,128)(2,1)S(1)}, bf16[192,384]{1,0:T(8,128)(2,1)S(1)}, u32[]{:S(2)}, u32[]{:S(2)}) collective-permute-start(bf16[192,384]{1,0:T(8,128)(2,1)S(1)} %get-tuple-element.81), channel_id=1, source_target_pairs={{0,4},{4,0},{8,12},{12,8},{16,20},{20,16},{24,28},{28,24},{1,5},{5... | collective-permute-start | bytes 442376 | tf_op jit(solution)/shard_map/ppermute | solution.py:293
  32.9 3.2 %collective-permute-start.14 = (bf16[192,384]{1,0:T(8,128)(2,1)S(1)}, bf16[192,384]{1,0:T(8,128)(2,1)S(1)}, u32[]{:S(2)}, u32[]{:S(2)}) collective-permute-start(bf16[192,384]{1,0:T(8,128)(2,1)S(1)} %get-tuple-element.101), channel_id=1, source_target_pairs={{0,4},{4,0},{8,12},{12,8},{16,20},{20,16},{24,28},{28,24},{1,5},{5... | collective-permute-start | bytes 442376 | tf_op jit(solution)/shard_map/ppermute | solution.py:293
  33.2 8.7 %collective-permute-start.11 = (bf16[192,384]{1,0:T(8,128)(2,1)S(1)}, bf16[192,384]{1,0:T(8,128)(2,1)S(1)}, u32[]{:S(2)}, u32[]{:S(2)}) collective-permute-start(bf16[192,384]{1,0:T(8,128)(2,1)S(1)} %convert_add_fusion.2), channel_id=1, source_target_pairs={{0,24},{4,28},{8,16},{12,20},{16,8},{20,12},{24,0},{28,4},{1,25},{... | collective-permute-start | bytes 442376 | tf_op jit(solution)/shard_map/ppermute | solution.py:293
  36.0 1.7 %collective-permute-start.12 = (bf16[192,384]{1,0:T(8,128)(2,1)S(1)}, bf16[192,384]{1,0:T(8,128)(2,1)S(1)}, u32[]{:S(2)}, u32[]{:S(2)}) collective-permute-start(bf16[192,384]{1,0:T(8,128)(2,1)S(1)} %get-tuple-element.88), channel_id=1, source_target_pairs={{0,4},{4,0},{8,12},{12,8},{16,20},{20,16},{24,28},{28,24},{1,5},{5... | collective-permute-start | bytes 442376 | tf_op jit(solution)/shard_map/ppermute | solution.py:293
  36.2 8.7 %collective-permute-start.15 = (bf16[192,384]{1,0:T(8,128)(2,1)S(1)}, bf16[192,384]{1,0:T(8,128)(2,1)S(1)}, u32[]{:S(2)}, u32[]{:S(2)}) collective-permute-start(bf16[192,384]{1,0:T(8,128)(2,1)S(1)} %add_convert_fusion), channel_id=1, source_target_pairs={{0,8},{4,12},{8,0},{12,4},{16,24},{20,28},{24,16},{28,20},{1,9},{5... | collective-permute-start | bytes 442376 | tf_op jit(solution)/shard_map/ppermute | solution.py:293
  37.7 7.1 %collective-permute-start.16 = (bf16[192,384]{1,0:T(8,128)(2,1)S(1)}, bf16[192,384]{1,0:T(8,128)(2,1)S(1)}, u32[]{:S(2)}, u32[]{:S(2)}) collective-permute-start(bf16[192,384]{1,0:T(8,128)(2,1)S(1)} %convert_add_fusion.1), channel_id=1, source_target_pairs={{0,16},{4,20},{8,24},{12,28},{16,0},{20,4},{24,8},{28,12},{1,17},{... | collective-permute-start | bytes 442376 | tf_op jit(solution)/shard_map/ppermute | solution.py:293
  39.5 5.4 %collective-permute-start.13 = (bf16[192,384]{1,0:T(8,128)(2,1)S(1)}, bf16[192,384]{1,0:T(8,128)(2,1)S(1)}, u32[]{:S(2)}, u32[]{:S(2)}) collective-permute-start(bf16[192,384]{1,0:T(8,128)(2,1)S(1)} %get-tuple-element.98), channel_id=1, source_target_pairs={{0,4},{4,0},{8,12},{12,8},{16,20},{20,16},{24,28},{28,24},{1,5},{5... | collective-permute-start | bytes 442376 | tf_op jit(solution)/shard_map/ppermute | solution.py:293
  45.0 10.9 %collective-permute-start.17 = (bf16[48,384]{1,0:T(8,128)(2,1)S(1)}, bf16[48,384]{1,0:T(8,128)(2,1)S(1)}, u32[]{:S(2)}, u32[]{:S(2)}) collective-permute-start(bf16[48,384]{1,0:T(8,128)(2,1)S(1)} %get-tuple-element.110), channel_id=1, source_target_pairs={{0,3},{1,0},{2,1},{3,2},{4,7},{5,4},{6,5},{7,6},{8,11},{9,8},{10,9... | collective-permute-start | bytes 110600 | tf_op jit(solution)/shard_map/ppermute | solution.py:297
  45.4 10.5 %collective-permute-start.19 = (bf16[48,384]{1,0:T(8,128)(2,1)S(1)}, bf16[48,384]{1,0:T(8,128)(2,1)S(1)}, u32[]{:S(2)}, u32[]{:S(2)}) collective-permute-start(bf16[48,384]{1,0:T(8,128)(2,1)S(1)} %get-tuple-element.111), channel_id=1, source_target_pairs={{0,1},{1,2},{2,3},{3,0},{4,5},{5,6},{6,7},{7,4},{8,9},{9,10},{10,1... | collective-permute-start | bytes 110600 | tf_op jit(solution)/shard_map/ppermute | solution.py:297
  47.3 8.7 %collective-permute-start.18 = (bf16[48,384]{1,0:T(8,128)(2,1)S(1)}, bf16[48,384]{1,0:T(8,128)(2,1)S(1)}, u32[]{:S(2)}, u32[]{:S(2)}) collective-permute-start(bf16[48,384]{1,0:T(8,128)(2,1)S(1)} %get-tuple-element.112), channel_id=1, source_target_pairs={{0,2},{1,3},{2,0},{3,1},{4,6},{5,7},{6,4},{7,5},{8,10},{9,11},{10,... | collective-permute-start | bytes 110600 | tf_op jit(solution)/shard_map/ppermute | solution.py:297

commit v5 on v4

--- a/solution.py
+++ b/solution.py
@@ -63,7 +63,7 @@
 
 STEP = 256
 LOAD_LIMIT = 28
-UP_FIRST, UP_LAST = (0,), (1, 2, 3)
+PARTS = 2
 
 
 def far(place):
@@ -95,6 +95,11 @@
 
 def store_grads(cols, sums, outs):
     store(cols, hidden_grads(*sums), outs)
+
+
+def turn(block, out):
+    for c in range(0, block.shape[1], STEP):
+        out[c : c + STEP, :] = block[:, c : c + STEP].T
 
 
 def load_kernel(place, own, near, *refs):
@@ -145,46 +150,51 @@
 
 
 def partial_kernel(i, place, own, sib, wg, wu, wd, *refs):
-    add_pieces([pair(place, i, own, sib)], (wg, wu, wd), refs[:3], refs[3:], store)
-
-
-def partial_sums(place, i, own, sib, weights, acc):
+    add_pieces([pair(place, i, own, sib)], (wg, wu, wd), refs[:3], refs[3:6], store)
+    for weight, out in zip((wu,), refs[6:]):
+        for p in range(4):
+            turn(weight[block_at(place, p, out.shape[2]), :], out.at[p])
+
+
+def partial_sums(place, i, own, sib, weights, acc, turned=False):
     rows, hidden_count = acc[0].shape
+    more = (shape((4, hidden_count, weights[1].shape[0] // 4), BF16),) * 1 if turned else ()
     return call(
         functools.partial(partial_kernel, i),
-        (shape((rows, hidden_count), F32),) * 3,
+        (shape((rows, hidden_count), F32),) * 3 + more,
         [SMEM] + [VMEM] * 8,
-        [VMEM] * 3,
+        [VMEM] * (3 + len(more)),
         1,
         1,
         aliases={6: 0, 7: 1, 8: 2},
     )(place, own, sib, *weights, *acc)
-
-
-def slot_rows(place, p, dg, du, wg, wu, wide):
-    rows = block_at(place, p, wide)
-    return dot(dg, wg[rows, :], 1, 1) + dot(du, wu[rows, :], 1, 1)
 
 
 def write_slots(place, p, dg, du, wg, wu, keep, send):
     width = keep.shape[1]
     first = place[0] % 2 == 0
-    part = slot_rows(place, p, dg[...], du[...], wg, wu, 2 * width)
+    part = dot(dg[...], wg[block_at(place, p, 2 * width), :], 1, 1) + dot(du[...], wu[p], 1, 0)
     low, high = part[:, :width], part[:, width:]
     keep[...] = jnp.where(first, low, high)
     send[...] = jnp.where(first, high, low).astype(BF16)
 
 
-def middle_kernel(place, own, sib, wg, wu, wd, *refs):
-    acc = refs[:3]
-    hid, dg, du, keep, send = refs[3:]
-    add_pieces([pair(place, 3, own, sib)], (wg, wu, wd), acc, (hid, dg, du), store_grads)
+def middle_kernel(place, own, sib, wg, wu, wd, gate, up, back, hid, dg, du, keep, send):
+    rows, x, g = pair(place, 3, own, sib)
+    for f in range(wd.shape[0] // STEP):
+        cols = pl.ds(f * STEP, STEP)
+        sums = (
+            gate[:, cols] + dot(x, wg[rows, cols], 1, 0),
+            up[:, cols] + dot(x, wu[3, cols, :], 1, 1),
+            back[:, cols] + dot(g, wd[cols, rows], 1, 1),
+        )
+        store_grads(cols, sums, (hid, dg, du))
     write_slots(place, 3, dg, du, wg, wu, keep, send)
 
 
-def middle(place, own, sib, weights, acc):
+def middle(place, own, sib, turned, wd, acc):
     rows, width = own.shape[1:]
-    hidden_count = weights[0].shape[1]
+    hidden_count = wd.shape[0]
     return call(
         middle_kernel,
         (shape((rows, hidden_count), BF16),) * 3 + (shape((rows, width), F32), shape((rows, width), BF16)),
@@ -192,16 +202,16 @@
         [VMEM] * 5,
         20 * rows * width * hidden_count,
         0,
-    )(place, own, sib, *weights, *acc)
+    )(place, own, sib, *turned, wd, *acc)
 
 
 def slot_kernel(p, place, *refs):
     write_slots(place, p, *refs)
 
 
-def slots(place, p, dg, du, wg, wu):
+def slots(place, p, dg, du, turned):
     rows, hidden_count = dg.shape
-    width = wg.shape[0] // 8
+    width = turned[1].shape[2] // 2
     return call(
         functools.partial(slot_kernel, p),
         (shape((rows, width), F32), shape((rows, width), BF16)),
@@ -209,7 +219,7 @@
         [VMEM] * 2,
         8 * rows * width * hidden_count,
         0,
-    )(place, dg, du, wg, wu)
+    )(place, dg, du, *turned)
 
 
 def weight_kernel(jobs, begun, place, *refs):
@@ -225,14 +235,18 @@
         for j, p in enumerate(pieces):
             rows = block_at(place, chips[p], wide)
             piece = both_cores(core, own[p][array], sib[p][array])
-            if array == 0:
-                buf[j] = dot(piece, d[...], 0, 0).astype(BF16)
-                target = out.at[rows, :]
-            else:
-                buf[j] = dot(d[...], piece, 0, 0).astype(BF16)
-                target = out.at[:, rows]
-            copies.append(pltpu.make_async_copy(buf.at[j], target, sems.at[i, j]))
-            copies[-1].start()
+            left, right = (piece, d[...]) if array == 0 else (d[...], piece)
+            size = left.shape[1] // PARTS
+            for k in range(PARTS):
+                part = pl.ds(k * size, size)
+                buf[j, part, :] = dot(left[:, k * size : (k + 1) * size], right, 0, 0).astype(BF16)
+                if array == 0:
+                    start = pl.multiple_of((place[0] // 2 ^ chips[p]) * wide + k * size, size)
+                    target = out.at[pl.ds(start, size), :]
+                else:
+                    target = out.at[part, rows]
+                copies.append(pltpu.make_async_copy(buf.at[j, part, :], target, sems.at[i, j, k]))
+                copies[-1].start()
     for copy in copies:
         copy.wait()
 
@@ -252,7 +266,7 @@
         4 * rows * width * hidden_count * count,
         4 * width * hidden_count * count,
         scratch=[pltpu.VMEM((len(pieces),) + block, BF16) for block, (_, pieces) in zip(blocks, jobs)]
-        + [pltpu.SemaphoreType.DMA((len(ds), 4))],
+        + [pltpu.SemaphoreType.DMA((len(ds), 4, PARTS))],
         limit=LOAD_LIMIT,
         aliases={9 + len(ds): 0} if more else {},
     )(place, *own, *sib, *ds, *more)
@@ -316,38 +330,36 @@
     second, back = lax.optimization_barrier((here[1], back))
     there_first = across(second, 1)
     weights, acc = (wg, wu, wd), (gate, up, back)
-    acc = partial_sums(place, 1, first, second, weights, acc)
+    *acc, wu_turned = partial_sums(place, 1, first, second, weights, acc, True)
+    turned = wg, wu_turned
     diag, acc = lax.optimization_barrier((diag, acc))
     diag_near = across(diag, 1)
     acc = partial_sums(place, 2, there_first, there_second, weights, acc)
-    hid, dg, du, keep, send = middle(place, diag, diag_near, weights, acc)
+    hid, dg, du, keep, send = middle(place, diag, diag_near, turned, wd, acc)
     mine_of = own, first, there_first, diag
     other_of = near, second, there_second, diag_near
 
     def chip_sum(keep, send):
         return keep + across(send, 1).astype(F32)
 
-    shares = {1: slots(place, 1, dg, du, wg, wu)}
+    shares = {1: slots(place, 1, dg, du, turned)}
     total, dg, du = lax.optimization_barrier((chip_sum(keep, send), dg, du))
     parts = [across(total.astype(BF16), 6)]
-    shares[2] = slots(place, 2, dg, du, wg, wu)
+    shares[2] = slots(place, 2, dg, du, turned)
     parts.append(across(chip_sum(*shares[1]).astype(BF16), 2))
     total, dg, du = lax.optimization_barrier((chip_sum(*shares[2]), dg, du))
     parts.append(across(total.astype(BF16), 4))
-    share = slots(place, 0, dg, du, wg, wu)
+    share = slots(place, 0, dg, du, turned)
     share, dg = lax.optimization_barrier((share, dg))
     (grad_gate,) = weight_grads(place, [(0, (0, 1))], mine_of, other_of, (dg,))
     mine = chip_sum(*share)
     parts[0], dg, grad_gate = lax.optimization_barrier((parts[0], dg, grad_gate))
-    grad_gate, grad_up = weight_grads(
-        place, [(0, (2, 3)), (0, UP_FIRST)], mine_of, other_of, (dg, du), grad_gate
-    )
+    (grad_gate,) = weight_grads(place, [(0, (2, 3))], mine_of, other_of, (dg,), grad_gate)
     for part in parts:
         mine = mine + part.astype(F32)
-    mine, hid, grad_up = lax.optimization_barrier((mine, hid, grad_up))
-    grad_up, grad_down = weight_grads(
-        place, [(0, UP_LAST), (1, (0, 1, 2, 3))], mine_of, other_of, (du, hid), grad_up
-    )
+    mine, hid, grad_gate = lax.optimization_barrier((mine, hid, grad_gate))
+    whole = (0, 1, 2, 3)
+    grad_up, grad_down = weight_grads(place, [(0, whole), (1, whole)], mine_of, other_of, (du, hid))
     mine = mine.reshape(groups, tok_count, width)
     back = mine[0]
     sent = mine.astype(BF16)

time: 57 us -> 55.6 us (0.975)
  waiting for transfers between devices: 6.95 us -> 6.33 us
    pallas_call x2, Pallas kernels: 2.85 us -> 3.74 us  [partial_sums(): call(functools.partial(partial_kernel, i), (shape((rows, hidden_count), F...]
    pallas_call x3, Pallas kernels: 10 us -> 9.38 us  [weight_grads(): call(functools.partial(weight_kernel, jobs, len(more)), tuple((shape(out,...]
    ppermute x14, waiting for transfers between devices: 2.68 us -> 2.06 us  [across(): lax.ppermute(array, 'tensor', [(i, i ^ masks[i % 2]) for i in range(8)])]
    pallas_call x3, Pallas kernels: 3.57 us -> 2.96 us  [slots(): call(functools.partial(slot_kernel, p), (shape((rows, width), F32), shape...]
  transfers between devices with their start and end apart: 20 -> 20, of which waited for: 5 -> 6; matrix products, arithmetic and copies ran while one was open for 2% -> 2% of each run, Pallas kernels for 39% -> 39%
where the time goes in v5:
time: 55.6 us; the launch traced here: 55.3 us
  Pallas kernels  26 us (47%)
  starting transfers between devices  20.4 us (37%)
  waiting for transfers between devices  6.33 us (11%)
  local copies, waits for them, and re-layouts  0.96 us (2%)
  between operations  0.85 us (2%)
  other arithmetic  0.83 us (1%)
    ppermute x6, starting transfers between devices, along(): lax.ppermute(array, 'expert', [(i, (i + distance) % count) for i in range...  10.5 us
    ppermute x14, starting transfers between devices, across(): lax.ppermute(array, 'tensor', [(i, i ^ masks[i % 2]) for i in range(8)])  9.85 us
    pallas_call x3, Pallas kernels, weight_grads(): call(functools.partial(weight_kernel, jobs, len(more)), tuple((shape(out,...  9.38 us
    pallas_call x1, Pallas kernels, load(): call(load_kernel, (shape(wg.shape, BF16),) * 2 + (shape((rows, hidden_cou...  4.85 us
    ppermute x6, waiting for transfers between devices, along(): lax.ppermute(array, 'expert', [(i, (i + distance) % count) for i in range...  4.27 us
    pallas_call x2, Pallas kernels, partial_sums(): call(functools.partial(partial_kernel, i), (shape((rows, hidden_count), F...  3.74 us
    pallas_call x3, Pallas kernels, slots(): call(functools.partial(slot_kernel, p), (shape((rows, width), F32), shape...  2.96 us
    pallas_call x1, Pallas kernels, middle(): call(middle_kernel, (shape((rows, hidden_count), BF16),) * 3 + (shape((ro...  2.71 us
  transfers between devices with their start and end apart: 20, of which 6 were waited for; matrix products, arithmetic and copies ran while one was open for 2% of the time, Pallas kernels for 39%

profile of v5, /device:TPU:8, one launch (start us, length us, event | category | flops | bytes accessed | tf_op | source)
XLA Modules:
  0.0 55.3 jit_solution(5373071675390814217)
XLA Ops:
  0.6 1.7 %shard_map.102 = (bf16[2,48,384]{2,1,0:T(8,128)(2,1)}, bf16[2,48,384]{2,1,0:T(8,128)(2,1)}, bf16[2,48,384]{2,1,0:T(8,128)(2,1)}, bf16[2,48,384]{2,1,0:T(8,128)(2,1)}) custom-call(s32[1]{0:T(128)} %bitcast.1.place, bf16[48,384]{1,0:T(8,128)(2,1)} %refs_0_.1, bf16[48,384]{1,0:T(8,128)(2,1)} %refs_1_.1, s32[2,48]{1,0:T(2,128)} %bitcast.19, f32[2,48]{1,0:T(2,128)} %bitcast.20), custom_call_target="tpu_custom_call" | custom-call | flops 1 | bytes 1 | tf_op jit(solution)/shard_map/pallas_call | solution.py:293
  2.3 1.6 %collective-permute-start = (bf16[2,48,384]{2,1,0:T(8,128)(2,1)}, bf16[2,48,384]{2,1,0:T(8,128)(2,1)S(1)}, u32[]{:S(2)}, u32[]{:S(2)}) collective-permute-start(bf16[2,48,384]{2,1,0:T(8,128)(2,1)} %get-tuple-element.57), channel_id=1, source_target_pairs={{0,1},{1,2},{2,3},{3,0},{4,5},{5,6},{6,7},{7,4},{8,9},{9,10},{10,1... | collective-permute-start | bytes 221192 | tf_op jit(solution)/shard_map/ppermute | solution.py:311
  3.9 1.1 %collective-permute-start.1 = (bf16[2,48,384]{2,1,0:T(8,128)(2,1)}, bf16[2,48,384]{2,1,0:T(8,128)(2,1)S(1)}, u32[]{:S(2)}, u32[]{:S(2)}) collective-permute-start(bf16[2,48,384]{2,1,0:T(8,128)(2,1)} %get-tuple-element.58), channel_id=1, source_target_pairs={{0,2},{1,3},{2,0},{3,1},{4,6},{5,7},{6,4},{7,5},{8,10},{9,11},{10,... | collective-permute-start | bytes 221192 | tf_op jit(solution)/shard_map/ppermute | solution.py:311
  5.0 1.9 %collective-permute-start.2 = (bf16[2,48,384]{2,1,0:T(8,128)(2,1)}, bf16[2,48,384]{2,1,0:T(8,128)(2,1)S(1)}, u32[]{:S(2)}, u32[]{:S(2)}) collective-permute-start(bf16[2,48,384]{2,1,0:T(8,128)(2,1)} %get-tuple-element.59), channel_id=1, source_target_pairs={{0,3},{1,0},{2,1},{3,2},{4,7},{5,4},{6,5},{7,6},{8,11},{9,8},{10,9... | collective-permute-start | bytes 221192 | tf_op jit(solution)/shard_map/ppermute | solution.py:311
  7.0 0.9 %constant_dynamic-update-slice_fusion.3 = bf16[2,192,384]{2,1,0:T(8,128)(2,1)S(1)} fusion(bf16[2,48,384]{2,1,0:T(8,128)(2,1)} %get-tuple-element.56), kind=kLoop, calls=%fused_computation.8 | loop fusion | bytes 147456
  7.9 1.4 %collective-permute-done = bf16[2,48,384]{2,1,0:T(8,128)(2,1)S(1)} collective-permute-done((bf16[2,48,384]{2,1,0:T(8,128)(2,1)}, bf16[2,48,384]{2,1,0:T(8,128)(2,1)S(1)}, u32[]{:S(2)}, u32[]{:S(2)}) %collective-permute-start) | collective-permute-done | bytes 73760 | tf_op jit(solution)/shard_map/ppermute | solution.py:311
  9.3 1.5 %collective-permute-done.1 = bf16[2,48,384]{2,1,0:T(8,128)(2,1)S(1)} collective-permute-done((bf16[2,48,384]{2,1,0:T(8,128)(2,1)}, bf16[2,48,384]{2,1,0:T(8,128)(2,1)S(1)}, u32[]{:S(2)}, u32[]{:S(2)}) %collective-permute-start.1) | collective-permute-done | bytes 73760 | tf_op jit(solution)/shard_map/ppermute | solution.py:311
  10.8 1.3 %collective-permute-done.2 = bf16[2,48,384]{2,1,0:T(8,128)(2,1)S(1)} collective-permute-done((bf16[2,48,384]{2,1,0:T(8,128)(2,1)}, bf16[2,48,384]{2,1,0:T(8,128)(2,1)S(1)}, u32[]{:S(2)}, u32[]{:S(2)}) %collective-permute-start.2) | collective-permute-done | bytes 73760 | tf_op jit(solution)/shard_map/ppermute | solution.py:311
  12.3 1.6 %collective-permute-start.3 = (bf16[2,192,384]{2,1,0:T(8,128)(2,1)S(1)}, bf16[2,192,384]{2,1,0:T(8,128)(2,1)S(1)}, u32[]{:S(2)}, u32[]{:S(2)}) collective-permute-start(bf16[2,192,384]{2,1,0:T(8,128)(2,1)S(1)} %constant_dynamic-update-slice_fusion.own.refs_0_), channel_id=1, source_target_pairs={{0,8},{4,20},{8,0},{12,28},{16,24},{20,4},{24,16},{28,12},{1,9},{5... | collective-permute-start | bytes 884744 | tf_op jit(solution)/shard_map/ppermute | solution.py:307
  13.8 1.5 %collective-permute-start.6 = (bf16[2,192,384]{2,1,0:T(8,128)(2,1)S(1)}, bf16[2,192,384]{2,1,0:T(8,128)(2,1)S(1)}, u32[]{:S(2)}, u32[]{:S(2)}) collective-permute-start(bf16[2,192,384]{2,1,0:T(8,128)(2,1)S(1)} %collective-permute-done.4.near.refs_4_), channel_id=1, source_target_pairs={{0,8},{4,20},{8,0},{12,28},{16,24},{20,4},{24,16},{28,12},{1,9},{5... | collective-permute-start | bytes 884744 | tf_op jit(solution)/shard_map/ppermute | solution.py:307
  15.3 4.9 %shard_map.103 = (bf16[3072,1024]{1,0:T(8,128)(2,1)S(1)}, bf16[3072,1024]{1,0:T(8,128)(2,1)S(1)}, f32[192,1024]{1,0:T(8,128)S(1)}, f32[192,1024]{1,0:T(8,128)S(1)}) custom-call(s32[1]{0:T(128)} %bitcast.place, bf16[2,192,384]{2,1,0:T(8,128)(2,1)S(1)} %constant_dynamic-update-slice_fusion.own.refs_0_, ...), custom_call_target="tpu_custom_call" | custom-call | flops 1 | bytes 1 | tf_op jit(solution)/shard_map/pallas_call | solution.py:126
  20.2 1.6 %collective-permute-start.5 = (bf16[2,192,384]{2,1,0:T(8,128)(2,1)S(1)}, bf16[2,192,384]{2,1,0:T(8,128)(2,1)S(1)}, u32[]{:S(2)}, u32[]{:S(2)}) collective-permute-start(bf16[2,192,384]{2,1,0:T(8,128)(2,1)S(1)} %collective-permute-done.3.own.refs_1_), channel_id=1, source_target_pairs={{0,16},{4,12},{8,24},{12,4},{16,0},{20,28},{24,8},{28,20},{1,17},{... | collective-permute-start | bytes 884744 | tf_op jit(solution)/shard_map/ppermute | solution.py:307
  21.8 0.7 %shard_map.104.refs_2_ = f32[192,1024]{1,0:T(8,128)S(1)} custom-call(s32[1]{0:T(128)} %bitcast.place, bf16[2,192,384]{2,1,0:T(8,128)(2,1)S(1)} %constant_dynamic-update-slice_fusion.own.refs_0_, bf16[2,192,384]{2,1,0:T(8,128)(2,1)S(1)} %collective-permute-done.4.near.refs_4_, bf16[1024,3072]{1,0:T(8,128)(2,1)S(1)} %bitcast.12), custom_call_target="tpu_custom_call" | custom-call | flops 1 | bytes 1 | tf_op jit(solution)/shard_map/pallas_call | solution.py:147
  22.5 0.6 %collective-permute-start.8 = (bf16[2,192,384]{2,1,0:T(8,128)(2,1)S(1)}, bf16[2,192,384]{2,1,0:T(8,128)(2,1)S(1)}, u32[]{:S(2)}, u32[]{:S(2)}) collective-permute-start(bf16[2,192,384]{2,1,0:T(8,128)(2,1)S(1)} %collective-permute-done.6.sib.refs_5_), channel_id=1, source_target_pairs={{0,4},{4,0},{8,12},{12,8},{16,20},{20,16},{24,28},{28,24},{1,5},{5... | collective-permute-start | bytes 884744 | tf_op jit(solution)/shard_map/ppermute | solution.py:307
  23.1 2.3 %shard_map.105 = (f32[192,1024]{1,0:T(8,128)S(1)}, f32[192,1024]{1,0:T(8,128)S(1)}, f32[192,1024]{1,0:T(8,128)S(1)}, bf16[4,1024,768]{2,1,0:T(8,128)(2,1)S(1)}) custom-call(s32[1]{0:T(128)} %bitcast.place, bf16[2,192,384]{2,1,0:T(8,128)(2,1)S(1)} %collective-permute-done.3.own.refs_1_, ...), custom_call_target="tpu_custom_call", output_to_operand_aliasing={{0}: (6, {}), {1}: (7, {}), {2}: (8, {})} | custom-call | flops 1 | bytes 1 | tf_op jit(solution)/shard_map/pallas_call | solution.py:162
  25.4 1.6 %collective-permute-done.5.own.refs_3_ = bf16[2,192,384]{2,1,0:T(8,128)(2,1)S(1)} collective-permute-done((bf16[2,192,384]{2,1,0:T(8,128)(2,1)S(1)}, bf16[2,192,384]{2,1,0:T(8,128)(2,1)S(1)}, u32[]{:S(2)}, u32[]{:S(2)}) %collective-permute-start.5) | collective-permute-done | bytes 294944 | tf_op jit(solution)/shard_map/ppermute | solution.py:307
  27.0 1.4 %shard_map.106 = (f32[192,1024]{1,0:T(8,128)S(1)}, f32[192,1024]{1,0:T(8,128)S(1)}, f32[192,1024]{1,0:T(8,128)S(1)}) custom-call(s32[1]{0:T(128)} %bitcast.place, bf16[2,192,384]{2,1,0:T(8,128)(2,1)S(1)} %collective-permute-done.8.own.refs_2_, ...), custom_call_target="tpu_custom_call", output_to_operand_aliasing={{0}: (6, {}), {1}: (7, {}), {2}: (8, {})} | custom-call | flops 1 | bytes 1 | tf_op jit(solution)/shard_map/pallas_call | solution.py:162
  28.6 2.7 %shard_map.107 = (bf16[192,1024]{1,0:T(8,128)(2,1)S(1)}, bf16[192,1024]{1,0:T(8,128)(2,1)S(1)}, bf16[192,1024]{1,0:T(8,128)(2,1)S(1)}, f32[192,384]{1,0:T(8,128)S(1)}, bf16[192,384]{1,0:T(8,128)(2,1)S(1)}) custom-call(s32[1]{0:T(128)} %bitcast.place, bf16[2,192,384]{2,1,0:T(8,128)(2,1)S(1)} %collective-permute-done.5.own.refs_3_, ...), custom_call_target="tpu_custom_call" | custom-call | flops 1509949440 | tf_op jit(solution)/shard_map/pallas_call | solution.py:198
  31.3 0.5 collective-permute-start.10
  31.8 1.0 %shard_map.111 = (f32[192,384]{1,0:T(8,128)S(1)}, bf16[192,384]{1,0:T(8,128)(2,1)S(1)}) custom-call(s32[1]{0:T(128)} %bitcast.place, bf16[192,1024]{1,0:T(8,128)(2,1)S(1)} %get-tuple-element.101.refs_0_.refs_8_, bf16[192,1024]{1,0:T(8,128)(2,1)S(1)} %get-tuple-element.89.refs_1_.refs_8_, bf16[3072,1024]{1,0:T(8,128)(2,1)S(1)} %get-tuple-element.64.wg.refs_2_, ...), custom_call_target="tpu_custom_call" | custom-call | flops 603979776 | tf_op jit(solution)/shard_map/pallas_call | solution.py:215
  33.0 1.6 %collective-permute-start.13 = (bf16[192,384]{1,0:T(8,128)(2,1)S(1)}, bf16[192,384]{1,0:T(8,128)(2,1)S(1)}, u32[]{:S(2)}, u32[]{:S(2)}) collective-permute-start(bf16[192,384]{1,0:T(8,128)(2,1)S(1)} %convert_add_fusion.2), channel_id=1, source_target_pairs={{0,24},{4,28},{8,16},{12,20},{16,8},{20,12},{24,0},{28,4},{1,25},{... | collective-permute-start | bytes 442376 | tf_op jit(solution)/shard_map/ppermute | solution.py:307
  34.6 1.0 %shard_map.108 = (f32[192,384]{1,0:T(8,128)S(1)}, bf16[192,384]{1,0:T(8,128)(2,1)S(1)}) custom-call(s32[1]{0:T(128)} %bitcast.place, bf16[192,1024]{1,0:T(8,128)(2,1)S(1)} %get-tuple-element.101.refs_0_.refs_8_, bf16[192,1024]{1,0:T(8,128)(2,1)S(1)} %get-tuple-element.89.refs_1_.refs_8_, bf16[3072,1024]{1,0:T(8,128)(2,1)S(1)} %get-tuple-element.64.wg.refs_2_, ...), custom_call_target="tpu_custom_call" | custom-call | flops 603979776 | tf_op jit(solution)/shard_map/pallas_call | solution.py:215
  35.7 1.6 %collective-permute-start.15 = (bf16[192,384]{1,0:T(8,128)(2,1)S(1)}, bf16[192,384]{1,0:T(8,128)(2,1)S(1)}, u32[]{:S(2)}, u32[]{:S(2)}) collective-permute-start(bf16[192,384]{1,0:T(8,128)(2,1)S(1)} %add_convert_fusion), channel_id=1, source_target_pairs={{0,8},{4,12},{8,0},{12,4},{16,24},{20,28},{24,16},{28,20},{1,9},{5... | collective-permute-start | bytes 442376 | tf_op jit(solution)/shard_map/ppermute | solution.py:307
  37.3 0.6 %collective-permute-start.16 = (bf16[192,384]{1,0:T(8,128)(2,1)S(1)}, bf16[192,384]{1,0:T(8,128)(2,1)S(1)}, u32[]{:S(2)}, u32[]{:S(2)}) collective-permute-start(bf16[192,384]{1,0:T(8,128)(2,1)S(1)} %convert_add_fusion.1), channel_id=1, source_target_pairs={{0,16},{4,20},{8,24},{12,28},{16,0},{20,4},{24,8},{28,12},{1,17},{... | collective-permute-start | bytes 442376 | tf_op jit(solution)/shard_map/ppermute | solution.py:307
  37.9 1.0 %shard_map.109 = (f32[192,384]{1,0:T(8,128)S(1)}, bf16[192,384]{1,0:T(8,128)(2,1)S(1)}) custom-call(s32[1]{0:T(128)} %bitcast.place, bf16[192,1024]{1,0:T(8,128)(2,1)S(1)} %get-tuple-element.101.refs_0_.refs_8_, bf16[192,1024]{1,0:T(8,128)(2,1)S(1)} %get-tuple-element.89.refs_1_.refs_8_, bf16[3072,1024]{1,0:T(8,128)(2,1)S(1)} %get-tuple-element.64.wg.refs_2_, ...), custom_call_target="tpu_custom_call" | custom-call | flops 603979776 | tf_op jit(solution)/shard_map/pallas_call | solution.py:215
  39.0 2.1 %shard_map.110.refs_9_ = bf16[3072,1024]{1,0:T(8,128)(2,1)} custom-call(s32[1]{0:T(128)} %bitcast.place, bf16[2,192,384]{2,1,0:T(8,128)(2,1)S(1)} %constant_dynamic-update-slice_fusion.own.refs_0_, bf16[2,192,384]{2,1,0:T(8,128)(2,1)S(1)} %collective-permute-done.3.own.refs_1_, bf16[2,192,384]{2,1,0:T(8,128)(2,1)S(1)} %collective-permute-done.8.own.refs_2_, ...), custom_call_target="tpu_custom_call" | custom-call | flops 603979776 | bytes 3145728 | tf_op jit(solution)/shard_map/pallas_call | solution.py:261
  41.1 2.1 %shard_map.112 = bf16[3072,1024]{1,0:T(8,128)(2,1)} custom-call(s32[1]{0:T(128)} %bitcast.place, bf16[2,192,384]{2,1,0:T(8,128)(2,1)S(1)} %constant_dynamic-update-slice_fusion.own.refs_0_, bf16[2,192,384]{2,1,0:T(8,128)(2,1)S(1)} %collective-permute-done.3.own.refs_1_, ...), custom_call_target="tpu_custom_call", output_to_operand_aliasing={{}: (10, {})} | custom-call | flops 603979776 | bytes 3145728 | tf_op jit(solution)/shard_map/pallas_call | solution.py:261
  43.7 0.3 collective-permute-start.17
  44.0 1.8 %collective-permute-start.19 = (bf16[48,384]{1,0:T(8,128)(2,1)S(1)}, bf16[48,384]{1,0:T(8,128)(2,1)S(1)}, u32[]{:S(2)}, u32[]{:S(2)}) collective-permute-start(bf16[48,384]{1,0:T(8,128)(2,1)S(1)} %get-tuple-element.109), channel_id=1, source_target_pairs={{0,1},{1,2},{2,3},{3,0},{4,5},{5,6},{6,7},{7,4},{8,9},{9,10},{10,1... | collective-permute-start | bytes 110600 | tf_op jit(solution)/shard_map/ppermute | solution.py:311
  45.8 3.8 %collective-permute-start.18 = (bf16[48,384]{1,0:T(8,128)(2,1)S(1)}, bf16[48,384]{1,0:T(8,128)(2,1)S(1)}, u32[]{:S(2)}, u32[]{:S(2)}) collective-permute-start(bf16[48,384]{1,0:T(8,128)(2,1)S(1)} %get-tuple-element.110), channel_id=1, source_target_pairs={{0,2},{1,3},{2,0},{3,1},{4,6},{5,7},{6,4},{7,5},{8,10},{9,11},{10,... | collective-permute-start | bytes 110600 | tf_op jit(solution)/shard_map/ppermute | solution.py:311
  49.5 5.1 %shard_map.113 = (bf16[3072,1024]{1,0:T(8,128)(2,1)}, bf16[1024,3072]{1,0:T(8,128)(2,1)}) custom-call(s32[1]{0:T(128)} %bitcast.place, bf16[2,192,384]{2,1,0:T(8,128)(2,1)S(1)} %constant_dynamic-update-slice_fusion.own.refs_0_, bf16[2,192,384]{2,1,0:T(8,128)(2,1)S(1)} %collective-permute-done.3.own.refs_1_, ...), custom_call_target="tpu_custom_call" | custom-call | flops 2415919104 | bytes 12582912 | tf_op jit(solution)/shard_map/pallas_call | solution.py:261
  54.7 0.6 %add_convert_fusion.1 = bf16[48,384]{1,0:T(8,128)(2,1)} fusion(bf16[48,384]{1,0:T(8,128)(2,1)S(1)} %collective-permute-done.19, bf16[48,384]{1,0:T(8,128)(2,1)S(1)} %collective-permute-done.18, bf16[48,384]{1,0:T(8,128)(2,1)S(1)} %collective-permute-done.17, f32[192,384]{1,0:T(8,128)S(1)} %convert_add_fusion), kind=kLoop, calls=%fused_computation.4 | loop fusion | flops 129024 | bytes 221184 | tf_op jit(solution)/shard_map/convert_element_type | solution.py:368
  (36 shorter events, 1.2 us)
Async XLA Ops:
  2.3 7.0 %collective-permute-start = (bf16[2,48,384]{2,1,0:T(8,128)(2,1)}, bf16[2,48,384]{2,1,0:T(8,128)(2,1)S(1)}, u32[]{:S(2)}, u32[]{:S(2)}) collective-permute-start(bf16[2,48,384]{2,1,0:T(8,128)(2,1)} %get-tuple-element.57), channel_id=1, source_target_pairs={{0,1},{1,2},{2,3},{3,0},{4,5},{5,6},{6,7},{7,4},{8,9},{9,10},{10,1... | collective-permute-start | bytes 221192 | tf_op jit(solution)/shard_map/ppermute | solution.py:311
  3.9 6.9 %collective-permute-start.1 = (bf16[2,48,384]{2,1,0:T(8,128)(2,1)}, bf16[2,48,384]{2,1,0:T(8,128)(2,1)S(1)}, u32[]{:S(2)}, u32[]{:S(2)}) collective-permute-start(bf16[2,48,384]{2,1,0:T(8,128)(2,1)} %get-tuple-element.58), channel_id=1, source_target_pairs={{0,2},{1,3},{2,0},{3,1},{4,6},{5,7},{6,4},{7,5},{8,10},{9,11},{10,... | collective-permute-start | bytes 221192 | tf_op jit(solution)/shard_map/ppermute | solution.py:311
  5.0 7.1 %collective-permute-start.2 = (bf16[2,48,384]{2,1,0:T(8,128)(2,1)}, bf16[2,48,384]{2,1,0:T(8,128)(2,1)S(1)}, u32[]{:S(2)}, u32[]{:S(2)}) collective-permute-start(bf16[2,48,384]{2,1,0:T(8,128)(2,1)} %get-tuple-element.59), channel_id=1, source_target_pairs={{0,3},{1,0},{2,1},{3,2},{4,7},{5,4},{6,5},{7,6},{8,11},{9,8},{10,9... | collective-permute-start | bytes 221192 | tf_op jit(solution)/shard_map/ppermute | solution.py:311
  12.2 9.6 %slice-start = ((s8[6291456]{0:T(1024)(128)(4,1)}), s8[2097152]{0:T(1024)(128)(4,1)S(1)}, s32[]{:S(2)}) async-start(s8[6291456]{0:T(1024)(128)(4,1)} %bitcast.10), calls=%async_computation | async-start | bytes 4194304
  12.2 1.6 %collective-permute-start.4 = (bf16[2,192,384]{2,1,0:T(8,128)(2,1)S(1)}, bf16[2,192,384]{2,1,0:T(8,128)(2,1)S(1)}, u32[]{:S(2)}, u32[]{:S(2)}) collective-permute-start(bf16[2,192,384]{2,1,0:T(8,128)(2,1)S(1)} %constant_dynamic-update-slice_fusion.own.refs_0_), channel_id=1, source_target_pairs={{0,4},{4,0},{8,12},{12,8},{16,20},{20,16},{24,28},{28,24},{1,5},{5... | collective-permute-start | bytes 884744 | tf_op jit(solution)/shard_map/ppermute | solution.py:307
  12.3 7.9 %collective-permute-start.3 = (bf16[2,192,384]{2,1,0:T(8,128)(2,1)S(1)}, bf16[2,192,384]{2,1,0:T(8,128)(2,1)S(1)}, u32[]{:S(2)}, u32[]{:S(2)}) collective-permute-start(bf16[2,192,384]{2,1,0:T(8,128)(2,1)S(1)} %constant_dynamic-update-slice_fusion.own.refs_0_), channel_id=1, source_target_pairs={{0,8},{4,20},{8,0},{12,28},{16,24},{20,4},{24,16},{28,12},{1,9},{5... | collective-permute-start | bytes 884744 | tf_op jit(solution)/shard_map/ppermute | solution.py:307
  13.8 8.7 %collective-permute-start.6 = (bf16[2,192,384]{2,1,0:T(8,128)(2,1)S(1)}, bf16[2,192,384]{2,1,0:T(8,128)(2,1)S(1)}, u32[]{:S(2)}, u32[]{:S(2)}) collective-permute-start(bf16[2,192,384]{2,1,0:T(8,128)(2,1)S(1)} %collective-permute-done.4.near.refs_4_), channel_id=1, source_target_pairs={{0,8},{4,20},{8,0},{12,28},{16,24},{20,4},{24,16},{28,12},{1,9},{5... | collective-permute-start | bytes 884744 | tf_op jit(solution)/shard_map/ppermute | solution.py:307
  15.3 6.5 %slice-start.1 = ((s8[6291456]{0:T(1024)(128)(4,1)}), s8[4194304]{0:T(1024)(128)(4,1)S(1)}, s32[]{:S(2)}) async-start(s8[6291456]{0:T(1024)(128)(4,1)} %bitcast.10), calls=%async_computation.1 | async-start | bytes 8388608
  20.2 6.8 %collective-permute-start.5 = (bf16[2,192,384]{2,1,0:T(8,128)(2,1)S(1)}, bf16[2,192,384]{2,1,0:T(8,128)(2,1)S(1)}, u32[]{:S(2)}, u32[]{:S(2)}) collective-permute-start(bf16[2,192,384]{2,1,0:T(8,128)(2,1)S(1)} %collective-permute-done.3.own.refs_1_), channel_id=1, source_target_pairs={{0,16},{4,12},{8,24},{12,4},{16,0},{20,28},{24,8},{28,20},{1,17},{... | collective-permute-start | bytes 884744 | tf_op jit(solution)/shard_map/ppermute | solution.py:307
  21.8 5.2 %collective-permute-start.9 = (bf16[2,192,384]{2,1,0:T(8,128)(2,1)S(1)}, bf16[2,192,384]{2,1,0:T(8,128)(2,1)S(1)}, u32[]{:S(2)}, u32[]{:S(2)}) collective-permute-start(bf16[2,192,384]{2,1,0:T(8,128)(2,1)S(1)} %collective-permute-done.3.own.refs_1_), channel_id=1, source_target_pairs={{0,4},{4,0},{8,12},{12,8},{16,20},{20,16},{24,28},{28,24},{1,5},{5... | collective-permute-start | bytes 884744 | tf_op jit(solution)/shard_map/ppermute | solution.py:307
  22.5 4.5 %collective-permute-start.8 = (bf16[2,192,384]{2,1,0:T(8,128)(2,1)S(1)}, bf16[2,192,384]{2,1,0:T(8,128)(2,1)S(1)}, u32[]{:S(2)}, u32[]{:S(2)}) collective-permute-start(bf16[2,192,384]{2,1,0:T(8,128)(2,1)S(1)} %collective-permute-done.6.sib.refs_5_), channel_id=1, source_target_pairs={{0,4},{4,0},{8,12},{12,8},{16,20},{20,16},{24,28},{28,24},{1,5},{5... | collective-permute-start | bytes 884744 | tf_op jit(solution)/shard_map/ppermute | solution.py:307
  27.0 1.6 %collective-permute-start.7 = (bf16[2,192,384]{2,1,0:T(8,128)(2,1)S(1)}, bf16[2,192,384]{2,1,0:T(8,128)(2,1)S(1)}, u32[]{:S(2)}, u32[]{:S(2)}) collective-permute-start(bf16[2,192,384]{2,1,0:T(8,128)(2,1)S(1)} %collective-permute-done.5.own.refs_3_), channel_id=1, source_target_pairs={{0,4},{4,0},{8,12},{12,8},{16,20},{20,16},{24,28},{28,24},{1,5},{5... | collective-permute-start | bytes 884744 | tf_op jit(solution)/shard_map/ppermute | solution.py:307
  31.3 1.6 %collective-permute-start.10 = (bf16[192,384]{1,0:T(8,128)(2,1)S(1)}, bf16[192,384]{1,0:T(8,128)(2,1)S(1)}, u32[]{:S(2)}, u32[]{:S(2)}) collective-permute-start(bf16[192,384]{1,0:T(8,128)(2,1)S(1)} %get-tuple-element.81), channel_id=1, source_target_pairs={{0,4},{4,0},{8,12},{12,8},{16,20},{20,16},{24,28},{28,24},{1,5},{5... | collective-permute-start | bytes 442376 | tf_op jit(solution)/shard_map/ppermute | solution.py:307
  32.7 3.0 %collective-permute-start.14 = (bf16[192,384]{1,0:T(8,128)(2,1)S(1)}, bf16[192,384]{1,0:T(8,128)(2,1)S(1)}, u32[]{:S(2)}, u32[]{:S(2)}) collective-permute-start(bf16[192,384]{1,0:T(8,128)(2,1)S(1)} %get-tuple-element.98), channel_id=1, source_target_pairs={{0,4},{4,0},{8,12},{12,8},{16,20},{20,16},{24,28},{28,24},{1,5},{5... | collective-permute-start | bytes 442376 | tf_op jit(solution)/shard_map/ppermute | solution.py:307
  33.0 8.1 %collective-permute-start.13 = (bf16[192,384]{1,0:T(8,128)(2,1)S(1)}, bf16[192,384]{1,0:T(8,128)(2,1)S(1)}, u32[]{:S(2)}, u32[]{:S(2)}) collective-permute-start(bf16[192,384]{1,0:T(8,128)(2,1)S(1)} %convert_add_fusion.2), channel_id=1, source_target_pairs={{0,24},{4,28},{8,16},{12,20},{16,8},{20,12},{24,0},{28,4},{1,25},{... | collective-permute-start | bytes 442376 | tf_op jit(solution)/shard_map/ppermute | solution.py:307
  35.5 1.8 %collective-permute-start.11 = (bf16[192,384]{1,0:T(8,128)(2,1)S(1)}, bf16[192,384]{1,0:T(8,128)(2,1)S(1)}, u32[]{:S(2)}, u32[]{:S(2)}) collective-permute-start(bf16[192,384]{1,0:T(8,128)(2,1)S(1)} %get-tuple-element.87), channel_id=1, source_target_pairs={{0,4},{4,0},{8,12},{12,8},{16,20},{20,16},{24,28},{28,24},{1,5},{5... | collective-permute-start | bytes 442376 | tf_op jit(solution)/shard_map/ppermute | solution.py:307
  35.7 7.6 %collective-permute-start.15 = (bf16[192,384]{1,0:T(8,128)(2,1)S(1)}, bf16[192,384]{1,0:T(8,128)(2,1)S(1)}, u32[]{:S(2)}, u32[]{:S(2)}) collective-permute-start(bf16[192,384]{1,0:T(8,128)(2,1)S(1)} %add_convert_fusion), channel_id=1, source_target_pairs={{0,8},{4,12},{8,0},{12,4},{16,24},{20,28},{24,16},{28,20},{1,9},{5... | collective-permute-start | bytes 442376 | tf_op jit(solution)/shard_map/ppermute | solution.py:307
  37.3 6.2 %collective-permute-start.16 = (bf16[192,384]{1,0:T(8,128)(2,1)S(1)}, bf16[192,384]{1,0:T(8,128)(2,1)S(1)}, u32[]{:S(2)}, u32[]{:S(2)}) collective-permute-start(bf16[192,384]{1,0:T(8,128)(2,1)S(1)} %convert_add_fusion.1), channel_id=1, source_target_pairs={{0,16},{4,20},{8,24},{12,28},{16,0},{20,4},{24,8},{28,12},{1,17},{... | collective-permute-start | bytes 442376 | tf_op jit(solution)/shard_map/ppermute | solution.py:307
  38.9 4.7 %collective-permute-start.12 = (bf16[192,384]{1,0:T(8,128)(2,1)S(1)}, bf16[192,384]{1,0:T(8,128)(2,1)S(1)}, u32[]{:S(2)}, u32[]{:S(2)}) collective-permute-start(bf16[192,384]{1,0:T(8,128)(2,1)S(1)} %get-tuple-element.93), channel_id=1, source_target_pairs={{0,4},{4,0},{8,12},{12,8},{16,20},{20,16},{24,28},{28,24},{1,5},{5... | collective-permute-start | bytes 442376 | tf_op jit(solution)/shard_map/ppermute | solution.py:307
  43.7 11.0 %collective-permute-start.17 = (bf16[48,384]{1,0:T(8,128)(2,1)S(1)}, bf16[48,384]{1,0:T(8,128)(2,1)S(1)}, u32[]{:S(2)}, u32[]{:S(2)}) collective-permute-start(bf16[48,384]{1,0:T(8,128)(2,1)S(1)} %get-tuple-element.108), channel_id=1, source_target_pairs={{0,3},{1,0},{2,1},{3,2},{4,7},{5,4},{6,5},{7,6},{8,11},{9,8},{10,9... | collective-permute-start | bytes 110600 | tf_op jit(solution)/shard_map/ppermute | solution.py:311
  44.0 10.7 %collective-permute-start.19 = (bf16[48,384]{1,0:T(8,128)(2,1)S(1)}, bf16[48,384]{1,0:T(8,128)(2,1)S(1)}, u32[]{:S(2)}, u32[]{:S(2)}) collective-permute-start(bf16[48,384]{1,0:T(8,128)(2,1)S(1)} %get-tuple-element.109), channel_id=1, source_target_pairs={{0,1},{1,2},{2,3},{3,0},{4,5},{5,6},{6,7},{7,4},{8,9},{9,10},{10,1... | collective-permute-start | bytes 110600 | tf_op jit(solution)/shard_map/ppermute | solution.py:311
  45.8 8.9 %collective-permute-start.18 = (bf16[48,384]{1,0:T(8,128)(2,1)S(1)}, bf16[48,384]{1,0:T(8,128)(2,1)S(1)}, u32[]{:S(2)}, u32[]{:S(2)}) collective-permute-start(bf16[48,384]{1,0:T(8,128)(2,1)S(1)} %get-tuple-element.110), channel_id=1, source_target_pairs={{0,2},{1,3},{2,0},{3,1},{4,6},{5,7},{6,4},{7,5},{8,10},{9,11},{10,... | collective-permute-start | bytes 110600 | tf_op jit(solution)/shard_map/ppermute | solution.py:311

commit v6 on v5

--- a/solution.py
+++ b/solution.py
@@ -35,11 +35,15 @@
 HBM = pl.BlockSpec(memory_space=pl.ANY)
 
 
+def in_hbm(array):
+    return pltpu.with_memory_space_constraint(array, pltpu.HBM)
+
+
 def shape(dims, dtype):
     return jax.ShapeDtypeStruct(dims, dtype)
 
 
-def call(kernel, out_shape, in_specs, out_specs, flops, moved, scratch=(), limit=16, aliases={}):
+def call(kernel, out_shape, in_specs, out_specs, flops, moved, scratch=(), limit=8, aliases={}):
     return pl.pallas_call(
         kernel,
         out_shape=out_shape,
@@ -103,7 +107,7 @@
 
 
 def load_kernel(place, own, near, *refs):
-    sources, here, sums, sems = refs[:2], refs[2:4], refs[4:6], refs[6]
+    sources, here, sums, turned, sems = refs[:2], refs[2:4], refs[4:6], refs[6], refs[7]
     row, x, _ = pair(place, 0, own, near)
     wide = x.shape[1]
     copies = []
@@ -117,7 +121,11 @@
         for f in range(weight.shape[1] // STEP):
             cols = pl.ds(f * STEP, STEP)
             total[:, cols] = dot(x, weight[row, cols], 1, 0)
-    for copy in copies[2:]:
+    for p in range(4):
+        if p > 0:
+            copies[2 * p].wait()
+        turn(here[0][block_at(place, p, wide), :], turned.at[p])
+    for copy in copies[3::2]:
         copy.wait()
 
 
@@ -125,14 +133,16 @@
     rows, hidden_count = own.shape[1], wg.shape[1]
     return call(
         load_kernel,
-        (shape(wg.shape, BF16),) * 2 + (shape((rows, hidden_count), F32),) * 2,
+        (shape(wg.shape, BF16),) * 2
+        + (shape((rows, hidden_count), F32),) * 2
+        + (shape((4, hidden_count, wg.shape[0] // 4), BF16),),
         [SMEM] + [VMEM] * 2 + [HBM] * 2,
-        [VMEM] * 4,
+        [VMEM] * 5,
         1,
         1,
         scratch=[pltpu.SemaphoreType.DMA((2, 4))],
-        limit=36,
-    )(place, own, near, wg, wu)
+        limit=16,
+    )(place, own, near, in_hbm(wg), in_hbm(wu))
 
 
 def back_kernel(place, own, near, wd, back):
@@ -149,21 +159,48 @@
     )(place, own, near, wd)
 
 
-def partial_kernel(i, place, own, sib, wg, wu, wd, *refs):
-    add_pieces([pair(place, i, own, sib)], (wg, wu, wd), refs[:3], refs[3:6], store)
-    for weight, out in zip((wu,), refs[6:]):
-        for p in range(4):
-            turn(weight[block_at(place, p, out.shape[2]), :], out.at[p])
-
-
-def partial_sums(place, i, own, sib, weights, acc, turned=False):
+def partial_kernel(place, own, sib, wg, wu, wd, *refs):
+    add_pieces([pair(place, 1, own, sib)], (wg, wu, wd), refs[:3], refs[3:6], store)
+    up_turned, down_turned = refs[6:]
+    wide = up_turned.shape[2]
+    for i in range(2):
+        rows = block_at(place, far(place)[2 + i], wide)
+        for f in range(0, wd.shape[0], STEP):
+            down_turned[i, :, f : f + STEP] = wd[f : f + STEP, rows].T
+    for p in range(4):
+        turn(wu[block_at(place, p, wide), :], up_turned.at[p])
+
+
+def partial_sums(place, own, sib, weights, acc):
     rows, hidden_count = acc[0].shape
-    more = (shape((4, hidden_count, weights[1].shape[0] // 4), BF16),) * 1 if turned else ()
-    return call(
-        functools.partial(partial_kernel, i),
-        (shape((rows, hidden_count), F32),) * 3 + more,
+    wide = weights[1].shape[0] // 4
+    return call(
+        partial_kernel,
+        (shape((rows, hidden_count), F32),) * 3
+        + (shape((4, hidden_count, wide), BF16), shape((2, wide, hidden_count), BF16)),
         [SMEM] + [VMEM] * 8,
-        [VMEM] * (3 + len(more)),
+        [VMEM] * 5,
+        1,
+        1,
+        aliases={6: 0, 7: 1, 8: 2},
+    )(place, own, sib, *weights, *acc)
+
+
+def third_kernel(place, own, sib, wg, wu, wd, gate_in, up_in, back_in, gate, up, back):
+    rows, x, g = pair(place, 2, own, sib)
+    for f in range(wg.shape[1] // STEP):
+        cols = pl.ds(f * STEP, STEP)
+        gate[:, cols] = gate_in[:, cols] + dot(x, wg[rows, cols], 1, 0)
+        up[:, cols] = up_in[:, cols] + dot(x, wu[rows, cols], 1, 0)
+        back[:, cols] = back_in[:, cols] + dot(g, wd[0, :, cols], 1, 0)
+
+
+def third_sums(place, own, sib, weights, acc):
+    return call(
+        third_kernel,
+        (shape(acc[0].shape, F32),) * 3,
+        [SMEM] + [VMEM] * 8,
+        [VMEM] * 3,
         1,
         1,
         aliases={6: 0, 7: 1, 8: 2},
@@ -173,7 +210,7 @@
 def write_slots(place, p, dg, du, wg, wu, keep, send):
     width = keep.shape[1]
     first = place[0] % 2 == 0
-    part = dot(dg[...], wg[block_at(place, p, 2 * width), :], 1, 1) + dot(du[...], wu[p], 1, 0)
+    part = dot(dg[...], wg[p], 1, 0) + dot(du[...], wu[p], 1, 0)
     low, high = part[:, :width], part[:, width:]
     keep[...] = jnp.where(first, low, high)
     send[...] = jnp.where(first, high, low).astype(BF16)
@@ -181,12 +218,12 @@
 
 def middle_kernel(place, own, sib, wg, wu, wd, gate, up, back, hid, dg, du, keep, send):
     rows, x, g = pair(place, 3, own, sib)
-    for f in range(wd.shape[0] // STEP):
+    for f in range(wd.shape[2] // STEP):
         cols = pl.ds(f * STEP, STEP)
         sums = (
-            gate[:, cols] + dot(x, wg[rows, cols], 1, 0),
+            gate[:, cols] + dot(x, wg[3, cols, :], 1, 1),
             up[:, cols] + dot(x, wu[3, cols, :], 1, 1),
-            back[:, cols] + dot(g, wd[cols, rows], 1, 1),
+            back[:, cols] + dot(g, wd[1, :, cols], 1, 0),
         )
         store_grads(cols, sums, (hid, dg, du))
     write_slots(place, 3, dg, du, wg, wu, keep, send)
@@ -194,7 +231,7 @@
 
 def middle(place, own, sib, turned, wd, acc):
     rows, width = own.shape[1:]
-    hidden_count = wd.shape[0]
+    hidden_count = wd.shape[2]
     return call(
         middle_kernel,
         (shape((rows, hidden_count), BF16),) * 3 + (shape((rows, width), F32), shape((rows, width), BF16)),
@@ -289,7 +326,7 @@
 
 
 def pack(place, acts, grad, routing, gates, groups):
-    sources = (acts, grad, routing.T, gates.T)
+    sources = tuple(in_hbm(s) for s in (acts, grad, routing.T, gates.T))
     return call(
         functools.partial(pack_kernel, groups),
         (shape((2,) + acts.shape, BF16),) * groups,
@@ -298,7 +335,7 @@
         1,
         1,
         scratch=[pltpu.VMEM(s.shape, s.dtype) for s in sources] + [pltpu.SemaphoreType.DMA((4,))],
-        limit=63,
+        limit=16,
     )(place, *sources)
 
 
@@ -321,7 +358,7 @@
     own = jnp.concatenate(blocks, axis=1)
     near = across(own, 1)
     here = across(own, 2, 4), across(near, 2, 4)
-    wg, wu, gate, up = load(place, own, near, w_gate[0], w_up[0])
+    wg, wu, gate, up, wg_turned = load(place, own, near, w_gate[0], w_up[0])
     first, gate, up = lax.optimization_barrier((here[0], gate, up))
     diag = across(first, 4, 2)
     there_second = across(first, 1)
@@ -330,12 +367,12 @@
     second, back = lax.optimization_barrier((here[1], back))
     there_first = across(second, 1)
     weights, acc = (wg, wu, wd), (gate, up, back)
-    *acc, wu_turned = partial_sums(place, 1, first, second, weights, acc, True)
-    turned = wg, wu_turned
+    *acc, wu_turned, wd_turned = partial_sums(place, first, second, weights, acc)
+    turned = wg_turned, wu_turned
     diag, acc = lax.optimization_barrier((diag, acc))
     diag_near = across(diag, 1)
-    acc = partial_sums(place, 2, there_first, there_second, weights, acc)
-    hid, dg, du, keep, send = middle(place, diag, diag_near, turned, wd, acc)
+    acc = third_sums(place, there_first, there_second, (wg, wu, wd_turned), acc)
+    hid, dg, du, keep, send = middle(place, diag, diag_near, turned, wd_turned, acc)
     mine_of = own, first, there_first, diag
     other_of = near, second, there_second, diag_near
 

time: 55.6 us -> 54.2 us (0.975)
  local copies, waits for them, and re-layouts: 0.96 us -> 0.08 us
  Pallas kernels: 26 us -> 25.4 us
    unnamed x7, local copies, waits for them, and re-layouts: 0.93 us -> 0.05 us
    pallas_call x2, Pallas kernels: 3.74 us -> 4.49 us  [the longest x1 3.2 us: partial_sums(): call(partial_kernel, (shape((rows, hidden_count), F32),) * 3 + (shape((4,...]
    ppermute x6, waiting for transfers between devices: 4.27 us -> 4.94 us  [along(): lax.ppermute(array, 'expert', [(i, (i + distance) % count) for i in range...]
    pallas_call x1, Pallas kernels: 1.68 us -> 1.02 us  [pack(): call(functools.partial(pack_kernel, groups), (shape((2,) + acts.shape, BF...]
    pallas_call x3, Pallas kernels: 2.96 us -> 2.38 us  [slots(): call(functools.partial(slot_kernel, p), (shape((rows, width), F32), shape...]
  transfers between devices with their start and end apart: 20 -> 20, of which waited for: 6 -> 7; matrix products, arithmetic and copies ran while one was open for 2% -> 0% of each run, Pallas kernels for 39% -> 40%
where the time goes in v6:
time: 54.2 us; the launch traced here: 54 us
  Pallas kernels  25.4 us (47%)
  starting transfers between devices  20.3 us (37%)
  waiting for transfers between devices  6.58 us (12%)
  between operations  0.87 us (2%)
  other arithmetic  0.83 us (2%)
    ppermute x6, starting transfers between devices, along(): lax.ppermute(array, 'expert', [(i, (i + distance) % count) for i in range...  10.5 us
    ppermute x14, starting transfers between devices, across(): lax.ppermute(array, 'tensor', [(i, i ^ masks[i % 2]) for i in range(8)])  9.73 us
    pallas_call x3, Pallas kernels, weight_grads(): call(functools.partial(weight_kernel, jobs, len(more)), tuple((shape(out,...  9.4 us
    ppermute x6, waiting for transfers between devices, along(): lax.ppermute(array, 'expert', [(i, (i + distance) % count) for i in range...  4.94 us
    pallas_call x1, Pallas kernels, load(): call(load_kernel, (shape(wg.shape, BF16),) * 2 + (shape((rows, hidden_cou...  4.87 us
    pallas_call x1, Pallas kernels, partial_sums(): call(partial_kernel, (shape((rows, hidden_count), F32),) * 3 + (shape((4,...  3.2 us
    pallas_call x1, Pallas kernels, middle(): call(middle_kernel, (shape((rows, hidden_count), BF16),) * 3 + (shape((ro...  2.56 us
    pallas_call x3, Pallas kernels, slots(): call(functools.partial(slot_kernel, p), (shape((rows, width), F32), shape...  2.38 us
  transfers between devices with their start and end apart: 20, of which 7 were waited for; matrix products, arithmetic and copies ran while one was open for 0% of the time, Pallas kernels for 40%

profile of v6, /device:TPU:8, one launch (start us, length us, event | category | flops | bytes accessed | tf_op | source)
XLA Modules:
  0.0 54.0 jit_solution(9508495660292369012)
XLA Ops:
  0.6 1.0 %shard_map.102 = (bf16[2,48,384]{2,1,0:T(8,128)(2,1)S(1)}, bf16[2,48,384]{2,1,0:T(8,128)(2,1)S(1)}, bf16[2,48,384]{2,1,0:T(8,128)(2,1)S(1)}, bf16[2,48,384]{2,1,0:T(8,128)(2,1)S(1)}) custom-call(s32[1]{0:T(128)} %bitcast.1.place, bf16[48,384]{1,0:T(8,128)(2,1)} %refs_0_.1, bf16[48,384]{1,0:T(8,128)(2,1)} %refs_1_.1, s32[2,48]{1,0:T(2,128)} %bitcast.17, ...), custom_call_target="tpu_custom_call" | custom-call | flops 1 | bytes 1 | tf_op jit(solution)/shard_map/pallas_call | solution.py:330
  1.7 1.6 %collective-permute-start = (bf16[2,48,384]{2,1,0:T(8,128)(2,1)S(1)}, bf16[2,48,384]{2,1,0:T(8,128)(2,1)S(1)}, u32[]{:S(2)}, u32[]{:S(2)}) collective-permute-start(bf16[2,48,384]{2,1,0:T(8,128)(2,1)S(1)} %get-tuple-element.59), channel_id=1, source_target_pairs={{0,1},{1,2},{2,3},{3,0},{4,5},{5,6},{6,7},{7,4},{8,9},{9,10},{10,1... | collective-permute-start | bytes 221192 | tf_op jit(solution)/shard_map/ppermute | solution.py:348
  3.3 1.1 %collective-permute-start.1 = (bf16[2,48,384]{2,1,0:T(8,128)(2,1)S(1)}, bf16[2,48,384]{2,1,0:T(8,128)(2,1)S(1)}, u32[]{:S(2)}, u32[]{:S(2)}) collective-permute-start(bf16[2,48,384]{2,1,0:T(8,128)(2,1)S(1)} %get-tuple-element.60), channel_id=1, source_target_pairs={{0,2},{1,3},{2,0},{3,1},{4,6},{5,7},{6,4},{7,5},{8,10},{9,11},{10,... | collective-permute-start | bytes 221192 | tf_op jit(solution)/shard_map/ppermute | solution.py:348
  4.4 1.9 %collective-permute-start.2 = (bf16[2,48,384]{2,1,0:T(8,128)(2,1)S(1)}, bf16[2,48,384]{2,1,0:T(8,128)(2,1)S(1)}, u32[]{:S(2)}, u32[]{:S(2)}) collective-permute-start(bf16[2,48,384]{2,1,0:T(8,128)(2,1)S(1)} %get-tuple-element.61), channel_id=1, source_target_pairs={{0,3},{1,0},{2,1},{3,2},{4,7},{5,4},{6,5},{7,6},{8,11},{9,8},{10,9... | collective-permute-start | bytes 221192 | tf_op jit(solution)/shard_map/ppermute | solution.py:348
  6.3 2.0 %collective-permute-done = bf16[2,48,384]{2,1,0:T(8,128)(2,1)S(1)} collective-permute-done((bf16[2,48,384]{2,1,0:T(8,128)(2,1)S(1)}, bf16[2,48,384]{2,1,0:T(8,128)(2,1)S(1)}, u32[]{:S(2)}, u32[]{:S(2)}) %collective-permute-start) | collective-permute-done | bytes 73760 | tf_op jit(solution)/shard_map/ppermute | solution.py:348
  8.3 1.5 %collective-permute-done.1 = bf16[2,48,384]{2,1,0:T(8,128)(2,1)S(1)} collective-permute-done((bf16[2,48,384]{2,1,0:T(8,128)(2,1)S(1)}, bf16[2,48,384]{2,1,0:T(8,128)(2,1)S(1)}, u32[]{:S(2)}, u32[]{:S(2)}) %collective-permute-start.1) | collective-permute-done | bytes 73760 | tf_op jit(solution)/shard_map/ppermute | solution.py:348
  9.9 1.4 %collective-permute-done.2 = bf16[2,48,384]{2,1,0:T(8,128)(2,1)S(1)} collective-permute-done((bf16[2,48,384]{2,1,0:T(8,128)(2,1)S(1)}, bf16[2,48,384]{2,1,0:T(8,128)(2,1)S(1)}, u32[]{:S(2)}, u32[]{:S(2)}) %collective-permute-start.2) | collective-permute-done | bytes 73760 | tf_op jit(solution)/shard_map/ppermute | solution.py:348
  11.4 1.6 %collective-permute-start.3 = (bf16[2,192,384]{2,1,0:T(8,128)(2,1)S(1)}, bf16[2,192,384]{2,1,0:T(8,128)(2,1)S(1)}, u32[]{:S(2)}, u32[]{:S(2)}) collective-permute-start(bf16[2,192,384]{2,1,0:T(8,128)(2,1)S(1)} %constant_dynamic-update-slice_fusion.own.refs_0_), channel_id=1, source_target_pairs={{0,8},{4,20},{8,0},{12,28},{16,24},{20,4},{24,16},{28,12},{1,9},{5... | collective-permute-start | bytes 884744 | tf_op jit(solution)/shard_map/ppermute | solution.py:344
  13.0 1.5 %collective-permute-start.6 = (bf16[2,192,384]{2,1,0:T(8,128)(2,1)S(1)}, bf16[2,192,384]{2,1,0:T(8,128)(2,1)S(1)}, u32[]{:S(2)}, u32[]{:S(2)}) collective-permute-start(bf16[2,192,384]{2,1,0:T(8,128)(2,1)S(1)} %collective-permute-done.4.near.refs_4_), channel_id=1, source_target_pairs={{0,8},{4,20},{8,0},{12,28},{16,24},{20,4},{24,16},{28,12},{1,9},{5... | collective-permute-start | bytes 884744 | tf_op jit(solution)/shard_map/ppermute | solution.py:344
  14.5 4.9 %shard_map.103 = (bf16[3072,1024]{1,0:T(8,128)(2,1)S(1)}, bf16[3072,1024]{1,0:T(8,128)(2,1)S(1)}, f32[192,1024]{1,0:T(8,128)S(1)}, f32[192,1024]{1,0:T(8,128)S(1)}, bf16[4,1024,768]{2,1,0:T(8,128)(2,1)S(1)}) custom-call(s32[1]{0:T(128)} %bitcast.place, bf16[2,192,384]{2,1,0:T(8,128)(2,1)S(1)} %constant_dynamic-update-slice_fusion.own.refs_0_, ...), custom_call_target="tpu_custom_call" | custom-call | flops 1 | bytes 1 | tf_op jit(solution)/shard_map/pallas_call | solution.py:134
  19.4 1.6 %collective-permute-start.5 = (bf16[2,192,384]{2,1,0:T(8,128)(2,1)S(1)}, bf16[2,192,384]{2,1,0:T(8,128)(2,1)S(1)}, u32[]{:S(2)}, u32[]{:S(2)}) collective-permute-start(bf16[2,192,384]{2,1,0:T(8,128)(2,1)S(1)} %collective-permute-done.3.own.refs_1_), channel_id=1, source_target_pairs={{0,16},{4,12},{8,24},{12,4},{16,0},{20,28},{24,8},{28,20},{1,17},{... | collective-permute-start | bytes 884744 | tf_op jit(solution)/shard_map/ppermute | solution.py:344
  21.0 0.7 %shard_map.104.refs_2_ = f32[192,1024]{1,0:T(8,128)S(1)} custom-call(s32[1]{0:T(128)} %bitcast.place, bf16[2,192,384]{2,1,0:T(8,128)(2,1)S(1)} %constant_dynamic-update-slice_fusion.own.refs_0_, bf16[2,192,384]{2,1,0:T(8,128)(2,1)S(1)} %collective-permute-done.4.near.refs_4_, bf16[1024,3072]{1,0:T(8,128)(2,1)S(1)} %bitcast.12), custom_call_target="tpu_custom_call" | custom-call | flops 1 | bytes 1 | tf_op jit(solution)/shard_map/pallas_call | solution.py:157
  21.7 0.6 %collective-permute-start.8 = (bf16[2,192,384]{2,1,0:T(8,128)(2,1)S(1)}, bf16[2,192,384]{2,1,0:T(8,128)(2,1)S(1)}, u32[]{:S(2)}, u32[]{:S(2)}) collective-permute-start(bf16[2,192,384]{2,1,0:T(8,128)(2,1)S(1)} %collective-permute-done.6.sib.refs_5_), channel_id=1, source_target_pairs={{0,4},{4,0},{8,12},{12,8},{16,20},{20,16},{24,28},{28,24},{1,5},{5... | collective-permute-start | bytes 884744 | tf_op jit(solution)/shard_map/ppermute | solution.py:344
  22.2 3.2 %shard_map.105 = (f32[192,1024]{1,0:T(8,128)S(1)}, f32[192,1024]{1,0:T(8,128)S(1)}, f32[192,1024]{1,0:T(8,128)S(1)}, bf16[4,1024,768]{2,1,0:T(8,128)(2,1)S(1)}, bf16[2,768,1024]{2,1,0:T(8,128)(2,1)S(1)}) custom-call(s32[1]{0:T(128)} %bitcast.place, ...), custom_call_target="tpu_custom_call", output_to_operand_aliasing={{0}: (6, {}), {1}: (7, {}), {2}: (8, {})} | custom-call | flops 1 | bytes 1 | tf_op jit(solution)/shard_map/pallas_call | solution.py:177
  25.4 0.7 %collective-permute-done.5.own.refs_3_ = bf16[2,192,384]{2,1,0:T(8,128)(2,1)S(1)} collective-permute-done((bf16[2,192,384]{2,1,0:T(8,128)(2,1)S(1)}, bf16[2,192,384]{2,1,0:T(8,128)(2,1)S(1)}, u32[]{:S(2)}, u32[]{:S(2)}) %collective-permute-start.5) | collective-permute-done | bytes 294944 | tf_op jit(solution)/shard_map/ppermute | solution.py:344
  26.2 1.3 %shard_map.106 = (f32[192,1024]{1,0:T(8,128)S(1)}, f32[192,1024]{1,0:T(8,128)S(1)}, f32[192,1024]{1,0:T(8,128)S(1)}) custom-call(s32[1]{0:T(128)} %bitcast.place, bf16[2,192,384]{2,1,0:T(8,128)(2,1)S(1)} %collective-permute-done.8.own.refs_2_, ...), custom_call_target="tpu_custom_call", output_to_operand_aliasing={{0}: (6, {}), {1}: (7, {}), {2}: (8, {})} | custom-call | flops 1 | bytes 1 | tf_op jit(solution)/shard_map/pallas_call | solution.py:199
  27.7 2.6 %shard_map.107 = (bf16[192,1024]{1,0:T(8,128)(2,1)S(1)}, bf16[192,1024]{1,0:T(8,128)(2,1)S(1)}, bf16[192,1024]{1,0:T(8,128)(2,1)S(1)}, f32[192,384]{1,0:T(8,128)S(1)}, bf16[192,384]{1,0:T(8,128)(2,1)S(1)}) custom-call(s32[1]{0:T(128)} %bitcast.place, bf16[2,192,384]{2,1,0:T(8,128)(2,1)S(1)} %collective-permute-done.5.own.refs_3_, ...), custom_call_target="tpu_custom_call" | custom-call | flops 1509949440 | tf_op jit(solution)/shard_map/pallas_call | solution.py:235
  30.3 0.3 collective-permute-start.10
  30.6 0.8 %shard_map.111 = (f32[192,384]{1,0:T(8,128)S(1)}, bf16[192,384]{1,0:T(8,128)(2,1)S(1)}) custom-call(s32[1]{0:T(128)} %bitcast.place, bf16[192,1024]{1,0:T(8,128)(2,1)S(1)} %get-tuple-element.105.refs_0_.refs_8_, bf16[192,1024]{1,0:T(8,128)(2,1)S(1)} %get-tuple-element.93.refs_1_.refs_8_, bf16[4,1024,768]{2,1,0:T(8,128)(2,1)S(1)} %get-tuple-element.75.wg.refs_2_, ...), custom_call_target="tpu_custom_call" | custom-call | flops 603979776 | tf_op jit(solution)/shard_map/pallas_call | solution.py:252
  31.4 0.3 collective-permute-start.14
  31.8 1.6 %collective-permute-start.13 = (bf16[192,384]{1,0:T(8,128)(2,1)S(1)}, bf16[192,384]{1,0:T(8,128)(2,1)S(1)}, u32[]{:S(2)}, u32[]{:S(2)}) collective-permute-start(bf16[192,384]{1,0:T(8,128)(2,1)S(1)} %convert_add_fusion.2), channel_id=1, source_target_pairs={{0,24},{4,28},{8,16},{12,20},{16,8},{20,12},{24,0},{28,4},{1,25},{... | collective-permute-start | bytes 442376 | tf_op jit(solution)/shard_map/ppermute | solution.py:344
  33.4 0.8 %shard_map.108 = (f32[192,384]{1,0:T(8,128)S(1)}, bf16[192,384]{1,0:T(8,128)(2,1)S(1)}) custom-call(s32[1]{0:T(128)} %bitcast.place, bf16[192,1024]{1,0:T(8,128)(2,1)S(1)} %get-tuple-element.105.refs_0_.refs_8_, bf16[192,1024]{1,0:T(8,128)(2,1)S(1)} %get-tuple-element.93.refs_1_.refs_8_, bf16[4,1024,768]{2,1,0:T(8,128)(2,1)S(1)} %get-tuple-element.75.wg.refs_2_, ...), custom_call_target="tpu_custom_call" | custom-call | flops 603979776 | tf_op jit(solution)/shard_map/pallas_call | solution.py:252
  34.3 1.5 %collective-permute-start.15 = (bf16[192,384]{1,0:T(8,128)(2,1)S(1)}, bf16[192,384]{1,0:T(8,128)(2,1)S(1)}, u32[]{:S(2)}, u32[]{:S(2)}) collective-permute-start(bf16[192,384]{1,0:T(8,128)(2,1)S(1)} %add_convert_fusion), channel_id=1, source_target_pairs={{0,8},{4,12},{8,0},{12,4},{16,24},{20,28},{24,16},{28,20},{1,9},{5... | collective-permute-start | bytes 442376 | tf_op jit(solution)/shard_map/ppermute | solution.py:344
  35.9 0.6 %collective-permute-start.16 = (bf16[192,384]{1,0:T(8,128)(2,1)S(1)}, bf16[192,384]{1,0:T(8,128)(2,1)S(1)}, u32[]{:S(2)}, u32[]{:S(2)}) collective-permute-start(bf16[192,384]{1,0:T(8,128)(2,1)S(1)} %convert_add_fusion.1), channel_id=1, source_target_pairs={{0,16},{4,20},{8,24},{12,28},{16,0},{20,4},{24,8},{28,12},{1,17},{... | collective-permute-start | bytes 442376 | tf_op jit(solution)/shard_map/ppermute | solution.py:344
  36.4 0.8 %shard_map.109 = (f32[192,384]{1,0:T(8,128)S(1)}, bf16[192,384]{1,0:T(8,128)(2,1)S(1)}) custom-call(s32[1]{0:T(128)} %bitcast.place, bf16[192,1024]{1,0:T(8,128)(2,1)S(1)} %get-tuple-element.105.refs_0_.refs_8_, bf16[192,1024]{1,0:T(8,128)(2,1)S(1)} %get-tuple-element.93.refs_1_.refs_8_, bf16[4,1024,768]{2,1,0:T(8,128)(2,1)S(1)} %get-tuple-element.75.wg.refs_2_, ...), custom_call_target="tpu_custom_call" | custom-call | flops 603979776 | tf_op jit(solution)/shard_map/pallas_call | solution.py:252
  37.3 2.2 %shard_map.110.refs_9_ = bf16[3072,1024]{1,0:T(8,128)(2,1)} custom-call(s32[1]{0:T(128)} %bitcast.place, bf16[2,192,384]{2,1,0:T(8,128)(2,1)S(1)} %constant_dynamic-update-slice_fusion.own.refs_0_, bf16[2,192,384]{2,1,0:T(8,128)(2,1)S(1)} %collective-permute-done.3.own.refs_1_, bf16[2,192,384]{2,1,0:T(8,128)(2,1)S(1)} %collective-permute-done.8.own.refs_2_, ...), custom_call_target="tpu_custom_call" | custom-call | flops 603979776 | bytes 3145728 | tf_op jit(solution)/shard_map/pallas_call | solution.py:298
  39.5 2.1 %shard_map.112 = bf16[3072,1024]{1,0:T(8,128)(2,1)} custom-call(s32[1]{0:T(128)} %bitcast.place, bf16[2,192,384]{2,1,0:T(8,128)(2,1)S(1)} %constant_dynamic-update-slice_fusion.own.refs_0_, bf16[2,192,384]{2,1,0:T(8,128)(2,1)S(1)} %collective-permute-done.3.own.refs_1_, ...), custom_call_target="tpu_custom_call", output_to_operand_aliasing={{}: (10, {})} | custom-call | flops 603979776 | bytes 3145728 | tf_op jit(solution)/shard_map/pallas_call | solution.py:298
  41.6 0.3 collective-permute-done.15
  42.6 1.8 %collective-permute-start.19 = (bf16[48,384]{1,0:T(8,128)(2,1)S(1)}, bf16[48,384]{1,0:T(8,128)(2,1)S(1)}, u32[]{:S(2)}, u32[]{:S(2)}) collective-permute-start(bf16[48,384]{1,0:T(8,128)(2,1)S(1)} %get-tuple-element.113), channel_id=1, source_target_pairs={{0,1},{1,2},{2,3},{3,0},{4,5},{5,6},{6,7},{7,4},{8,9},{9,10},{10,1... | collective-permute-start | bytes 110600 | tf_op jit(solution)/shard_map/ppermute | solution.py:348
  44.5 3.8 %collective-permute-start.18 = (bf16[48,384]{1,0:T(8,128)(2,1)S(1)}, bf16[48,384]{1,0:T(8,128)(2,1)S(1)}, u32[]{:S(2)}, u32[]{:S(2)}) collective-permute-start(bf16[48,384]{1,0:T(8,128)(2,1)S(1)} %get-tuple-element.114), channel_id=1, source_target_pairs={{0,2},{1,3},{2,0},{3,1},{4,6},{5,7},{6,4},{7,5},{8,10},{9,11},{10,... | collective-permute-start | bytes 110600 | tf_op jit(solution)/shard_map/ppermute | solution.py:348
  48.2 5.1 %shard_map.113 = (bf16[3072,1024]{1,0:T(8,128)(2,1)}, bf16[1024,3072]{1,0:T(8,128)(2,1)}) custom-call(s32[1]{0:T(128)} %bitcast.place, bf16[2,192,384]{2,1,0:T(8,128)(2,1)S(1)} %constant_dynamic-update-slice_fusion.own.refs_0_, bf16[2,192,384]{2,1,0:T(8,128)(2,1)S(1)} %collective-permute-done.3.own.refs_1_, ...), custom_call_target="tpu_custom_call" | custom-call | flops 2415919104 | bytes 12582912 | tf_op jit(solution)/shard_map/pallas_call | solution.py:298
  53.4 0.6 %add_convert_fusion.1 = bf16[48,384]{1,0:T(8,128)(2,1)} fusion(bf16[48,384]{1,0:T(8,128)(2,1)S(1)} %collective-permute-done.19, bf16[48,384]{1,0:T(8,128)(2,1)S(1)} %collective-permute-done.18, bf16[48,384]{1,0:T(8,128)(2,1)S(1)} %collective-permute-done.17, f32[192,384]{1,0:T(8,128)S(1)} %convert_add_fusion), kind=kLoop, calls=%fused_computation.4 | loop fusion | flops 129024 | bytes 221184 | tf_op jit(solution)/shard_map/convert_element_type | solution.py:405
  (36 shorter events, 1.4 us)
Async XLA Ops:
  1.7 6.7 %collective-permute-start = (bf16[2,48,384]{2,1,0:T(8,128)(2,1)S(1)}, bf16[2,48,384]{2,1,0:T(8,128)(2,1)S(1)}, u32[]{:S(2)}, u32[]{:S(2)}) collective-permute-start(bf16[2,48,384]{2,1,0:T(8,128)(2,1)S(1)} %get-tuple-element.59), channel_id=1, source_target_pairs={{0,1},{1,2},{2,3},{3,0},{4,5},{5,6},{6,7},{7,4},{8,9},{9,10},{10,1... | collective-permute-start | bytes 221192 | tf_op jit(solution)/shard_map/ppermute | solution.py:348
  3.3 6.6 %collective-permute-start.1 = (bf16[2,48,384]{2,1,0:T(8,128)(2,1)S(1)}, bf16[2,48,384]{2,1,0:T(8,128)(2,1)S(1)}, u32[]{:S(2)}, u32[]{:S(2)}) collective-permute-start(bf16[2,48,384]{2,1,0:T(8,128)(2,1)S(1)} %get-tuple-element.60), channel_id=1, source_target_pairs={{0,2},{1,3},{2,0},{3,1},{4,6},{5,7},{6,4},{7,5},{8,10},{9,11},{10,... | collective-permute-start | bytes 221192 | tf_op jit(solution)/shard_map/ppermute | solution.py:348
  4.4 6.9 %collective-permute-start.2 = (bf16[2,48,384]{2,1,0:T(8,128)(2,1)S(1)}, bf16[2,48,384]{2,1,0:T(8,128)(2,1)S(1)}, u32[]{:S(2)}, u32[]{:S(2)}) collective-permute-start(bf16[2,48,384]{2,1,0:T(8,128)(2,1)S(1)} %get-tuple-element.61), channel_id=1, source_target_pairs={{0,3},{1,0},{2,1},{3,2},{4,7},{5,4},{6,5},{7,6},{8,11},{9,8},{10,9... | collective-permute-start | bytes 221192 | tf_op jit(solution)/shard_map/ppermute | solution.py:348
  11.3 9.6 %slice-start = ((s8[6291456]{0:T(1024)(128)(4,1)}), s8[2097152]{0:T(1024)(128)(4,1)S(1)}, s32[]{:S(2)}) async-start(s8[6291456]{0:T(1024)(128)(4,1)} %bitcast.10), calls=%async_computation | async-start | bytes 4194304
  11.3 1.6 %collective-permute-start.4 = (bf16[2,192,384]{2,1,0:T(8,128)(2,1)S(1)}, bf16[2,192,384]{2,1,0:T(8,128)(2,1)S(1)}, u32[]{:S(2)}, u32[]{:S(2)}) collective-permute-start(bf16[2,192,384]{2,1,0:T(8,128)(2,1)S(1)} %constant_dynamic-update-slice_fusion.own.refs_0_), channel_id=1, source_target_pairs={{0,4},{4,0},{8,12},{12,8},{16,20},{20,16},{24,28},{28,24},{1,5},{5... | collective-permute-start | bytes 884744 | tf_op jit(solution)/shard_map/ppermute | solution.py:344
  11.4 7.9 %collective-permute-start.3 = (bf16[2,192,384]{2,1,0:T(8,128)(2,1)S(1)}, bf16[2,192,384]{2,1,0:T(8,128)(2,1)S(1)}, u32[]{:S(2)}, u32[]{:S(2)}) collective-permute-start(bf16[2,192,384]{2,1,0:T(8,128)(2,1)S(1)} %constant_dynamic-update-slice_fusion.own.refs_0_), channel_id=1, source_target_pairs={{0,8},{4,20},{8,0},{12,28},{16,24},{20,4},{24,16},{28,12},{1,9},{5... | collective-permute-start | bytes 884744 | tf_op jit(solution)/shard_map/ppermute | solution.py:344
  13.0 8.7 %collective-permute-start.6 = (bf16[2,192,384]{2,1,0:T(8,128)(2,1)S(1)}, bf16[2,192,384]{2,1,0:T(8,128)(2,1)S(1)}, u32[]{:S(2)}, u32[]{:S(2)}) collective-permute-start(bf16[2,192,384]{2,1,0:T(8,128)(2,1)S(1)} %collective-permute-done.4.near.refs_4_), channel_id=1, source_target_pairs={{0,8},{4,20},{8,0},{12,28},{16,24},{20,4},{24,16},{28,12},{1,9},{5... | collective-permute-start | bytes 884744 | tf_op jit(solution)/shard_map/ppermute | solution.py:344
  14.5 6.5 %slice-start.1 = ((s8[6291456]{0:T(1024)(128)(4,1)}), s8[4194304]{0:T(1024)(128)(4,1)S(1)}, s32[]{:S(2)}) async-start(s8[6291456]{0:T(1024)(128)(4,1)} %bitcast.10), calls=%async_computation.1 | async-start | bytes 8388608
  19.4 6.8 %collective-permute-start.5 = (bf16[2,192,384]{2,1,0:T(8,128)(2,1)S(1)}, bf16[2,192,384]{2,1,0:T(8,128)(2,1)S(1)}, u32[]{:S(2)}, u32[]{:S(2)}) collective-permute-start(bf16[2,192,384]{2,1,0:T(8,128)(2,1)S(1)} %collective-permute-done.3.own.refs_1_), channel_id=1, source_target_pairs={{0,16},{4,12},{8,24},{12,4},{16,0},{20,28},{24,8},{28,20},{1,17},{... | collective-permute-start | bytes 884744 | tf_op jit(solution)/shard_map/ppermute | solution.py:344
  21.0 5.2 %collective-permute-start.9 = (bf16[2,192,384]{2,1,0:T(8,128)(2,1)S(1)}, bf16[2,192,384]{2,1,0:T(8,128)(2,1)S(1)}, u32[]{:S(2)}, u32[]{:S(2)}) collective-permute-start(bf16[2,192,384]{2,1,0:T(8,128)(2,1)S(1)} %collective-permute-done.3.own.refs_1_), channel_id=1, source_target_pairs={{0,4},{4,0},{8,12},{12,8},{16,20},{20,16},{24,28},{28,24},{1,5},{5... | collective-permute-start | bytes 884744 | tf_op jit(solution)/shard_map/ppermute | solution.py:344
  21.7 4.5 %collective-permute-start.8 = (bf16[2,192,384]{2,1,0:T(8,128)(2,1)S(1)}, bf16[2,192,384]{2,1,0:T(8,128)(2,1)S(1)}, u32[]{:S(2)}, u32[]{:S(2)}) collective-permute-start(bf16[2,192,384]{2,1,0:T(8,128)(2,1)S(1)} %collective-permute-done.6.sib.refs_5_), channel_id=1, source_target_pairs={{0,4},{4,0},{8,12},{12,8},{16,20},{20,16},{24,28},{28,24},{1,5},{5... | collective-permute-start | bytes 884744 | tf_op jit(solution)/shard_map/ppermute | solution.py:344
  26.2 1.6 %collective-permute-start.7 = (bf16[2,192,384]{2,1,0:T(8,128)(2,1)S(1)}, bf16[2,192,384]{2,1,0:T(8,128)(2,1)S(1)}, u32[]{:S(2)}, u32[]{:S(2)}) collective-permute-start(bf16[2,192,384]{2,1,0:T(8,128)(2,1)S(1)} %collective-permute-done.5.own.refs_3_), channel_id=1, source_target_pairs={{0,4},{4,0},{8,12},{12,8},{16,20},{20,16},{24,28},{28,24},{1,5},{5... | collective-permute-start | bytes 884744 | tf_op jit(solution)/shard_map/ppermute | solution.py:344
  30.3 1.4 %collective-permute-start.10 = (bf16[192,384]{1,0:T(8,128)(2,1)S(1)}, bf16[192,384]{1,0:T(8,128)(2,1)S(1)}, u32[]{:S(2)}, u32[]{:S(2)}) collective-permute-start(bf16[192,384]{1,0:T(8,128)(2,1)S(1)} %get-tuple-element.85), channel_id=1, source_target_pairs={{0,4},{4,0},{8,12},{12,8},{16,20},{20,16},{24,28},{28,24},{1,5},{5... | collective-permute-start | bytes 442376 | tf_op jit(solution)/shard_map/ppermute | solution.py:344
  31.4 2.9 %collective-permute-start.14 = (bf16[192,384]{1,0:T(8,128)(2,1)S(1)}, bf16[192,384]{1,0:T(8,128)(2,1)S(1)}, u32[]{:S(2)}, u32[]{:S(2)}) collective-permute-start(bf16[192,384]{1,0:T(8,128)(2,1)S(1)} %get-tuple-element.102), channel_id=1, source_target_pairs={{0,4},{4,0},{8,12},{12,8},{16,20},{20,16},{24,28},{28,24},{1,5},{5... | collective-permute-start | bytes 442376 | tf_op jit(solution)/shard_map/ppermute | solution.py:344
  31.8 7.7 %collective-permute-start.13 = (bf16[192,384]{1,0:T(8,128)(2,1)S(1)}, bf16[192,384]{1,0:T(8,128)(2,1)S(1)}, u32[]{:S(2)}, u32[]{:S(2)}) collective-permute-start(bf16[192,384]{1,0:T(8,128)(2,1)S(1)} %convert_add_fusion.2), channel_id=1, source_target_pairs={{0,24},{4,28},{8,16},{12,20},{16,8},{20,12},{24,0},{28,4},{1,25},{... | collective-permute-start | bytes 442376 | tf_op jit(solution)/shard_map/ppermute | solution.py:344
  34.2 1.6 %collective-permute-start.11 = (bf16[192,384]{1,0:T(8,128)(2,1)S(1)}, bf16[192,384]{1,0:T(8,128)(2,1)S(1)}, u32[]{:S(2)}, u32[]{:S(2)}) collective-permute-start(bf16[192,384]{1,0:T(8,128)(2,1)S(1)} %get-tuple-element.91), channel_id=1, source_target_pairs={{0,4},{4,0},{8,12},{12,8},{16,20},{20,16},{24,28},{28,24},{1,5},{5... | collective-permute-start | bytes 442376 | tf_op jit(solution)/shard_map/ppermute | solution.py:344
  34.3 7.6 %collective-permute-start.15 = (bf16[192,384]{1,0:T(8,128)(2,1)S(1)}, bf16[192,384]{1,0:T(8,128)(2,1)S(1)}, u32[]{:S(2)}, u32[]{:S(2)}) collective-permute-start(bf16[192,384]{1,0:T(8,128)(2,1)S(1)} %add_convert_fusion), channel_id=1, source_target_pairs={{0,8},{4,12},{8,0},{12,4},{16,24},{20,28},{24,16},{28,20},{1,9},{5... | collective-permute-start | bytes 442376 | tf_op jit(solution)/shard_map/ppermute | solution.py:344
  35.9 6.4 %collective-permute-start.16 = (bf16[192,384]{1,0:T(8,128)(2,1)S(1)}, bf16[192,384]{1,0:T(8,128)(2,1)S(1)}, u32[]{:S(2)}, u32[]{:S(2)}) collective-permute-start(bf16[192,384]{1,0:T(8,128)(2,1)S(1)} %convert_add_fusion.1), channel_id=1, source_target_pairs={{0,16},{4,20},{8,24},{12,28},{16,0},{20,4},{24,8},{28,12},{1,17},{... | collective-permute-start | bytes 442376 | tf_op jit(solution)/shard_map/ppermute | solution.py:344
  37.2 5.0 %collective-permute-start.12 = (bf16[192,384]{1,0:T(8,128)(2,1)S(1)}, bf16[192,384]{1,0:T(8,128)(2,1)S(1)}, u32[]{:S(2)}, u32[]{:S(2)}) collective-permute-start(bf16[192,384]{1,0:T(8,128)(2,1)S(1)} %get-tuple-element.97), channel_id=1, source_target_pairs={{0,4},{4,0},{8,12},{12,8},{16,20},{20,16},{24,28},{28,24},{1,5},{5... | collective-permute-start | bytes 442376 | tf_op jit(solution)/shard_map/ppermute | solution.py:344
  42.4 11.0 %collective-permute-start.17 = (bf16[48,384]{1,0:T(8,128)(2,1)S(1)}, bf16[48,384]{1,0:T(8,128)(2,1)S(1)}, u32[]{:S(2)}, u32[]{:S(2)}) collective-permute-start(bf16[48,384]{1,0:T(8,128)(2,1)S(1)} %get-tuple-element.112), channel_id=1, source_target_pairs={{0,3},{1,0},{2,1},{3,2},{4,7},{5,4},{6,5},{7,6},{8,11},{9,8},{10,9... | collective-permute-start | bytes 110600 | tf_op jit(solution)/shard_map/ppermute | solution.py:348
  42.6 10.7 %collective-permute-start.19 = (bf16[48,384]{1,0:T(8,128)(2,1)S(1)}, bf16[48,384]{1,0:T(8,128)(2,1)S(1)}, u32[]{:S(2)}, u32[]{:S(2)}) collective-permute-start(bf16[48,384]{1,0:T(8,128)(2,1)S(1)} %get-tuple-element.113), channel_id=1, source_target_pairs={{0,1},{1,2},{2,3},{3,0},{4,5},{5,6},{6,7},{7,4},{8,9},{9,10},{10,1... | collective-permute-start | bytes 110600 | tf_op jit(solution)/shard_map/ppermute | solution.py:348
  44.5 8.9 %collective-permute-start.18 = (bf16[48,384]{1,0:T(8,128)(2,1)S(1)}, bf16[48,384]{1,0:T(8,128)(2,1)S(1)}, u32[]{:S(2)}, u32[]{:S(2)}) collective-permute-start(bf16[48,384]{1,0:T(8,128)(2,1)S(1)} %get-tuple-element.114), channel_id=1, source_target_pairs={{0,2},{1,3},{2,0},{3,1},{4,6},{5,7},{6,4},{7,5},{8,10},{9,11},{10,... | collective-permute-start | bytes 110600 | tf_op jit(solution)/shard_map/ppermute | solution.py:348

commit v7 on v6

--- a/solution.py
+++ b/solution.py
@@ -106,80 +106,98 @@
         out[c : c + STEP, :] = block[:, c : c + STEP].T
 
 
-def load_kernel(place, own, near, *refs):
-    sources, here, sums, turned, sems = refs[:2], refs[2:4], refs[4:6], refs[6], refs[7]
+def load_gate_kernel(place, source, here, turned, sems):
+    wide = turned.shape[2]
+    blocks = [block_at(place, p, wide) for p in range(4)]
+    copies = [pltpu.make_async_copy(source.at[b, :], here.at[b, :], sems.at[p]) for p, b in enumerate(blocks)]
+    for copy in copies:
+        copy.start()
+    for p, block in enumerate(blocks):
+        copies[p].wait()
+        turn(here[block, :], turned.at[p])
+
+
+def load_gate(place, wg):
+    full, hidden_count = wg.shape
+    return call(
+        load_gate_kernel,
+        (shape(wg.shape, BF16), shape((4, hidden_count, full // 4), BF16)),
+        [SMEM, HBM],
+        [VMEM] * 2,
+        1,
+        1,
+        scratch=[pltpu.SemaphoreType.DMA((4,))],
+        limit=8,
+    )(place, in_hbm(wg))
+
+
+def load_up_kernel(place, own, near, source, wg, here, gate, up, turned, sems):
     row, x, _ = pair(place, 0, own, near)
     wide = x.shape[1]
     copies = []
     for p in range(4):
         rows = block_at(place, p, wide)
-        for i, (s, h) in enumerate(zip(sources, here)):
-            copies.append(pltpu.make_async_copy(s.at[rows, :], h.at[rows, :], sems.at[i, p]))
-            copies[-1].start()
-    for copy, weight, total in zip(copies, here, sums):
-        copy.wait()
+        copies.append(pltpu.make_async_copy(source.at[rows, :], here.at[rows, :], sems.at[p]))
+        copies[p].start()
+    for weight, total in ((wg, gate), (here, up)):
+        if weight is here:
+            copies[0].wait()
         for f in range(weight.shape[1] // STEP):
             cols = pl.ds(f * STEP, STEP)
             total[:, cols] = dot(x, weight[row, cols], 1, 0)
     for p in range(4):
         if p > 0:
-            copies[2 * p].wait()
-        turn(here[0][block_at(place, p, wide), :], turned.at[p])
-    for copy in copies[3::2]:
-        copy.wait()
-
-
-def load(place, own, near, wg, wu):
-    rows, hidden_count = own.shape[1], wg.shape[1]
-    return call(
-        load_kernel,
-        (shape(wg.shape, BF16),) * 2
+            copies[p].wait()
+        turn(here[block_at(place, p, wide), :], turned.at[p])
+
+
+def load_up(place, own, near, wu, wg):
+    rows, hidden_count = own.shape[1], wu.shape[1]
+    return call(
+        load_up_kernel,
+        (shape(wu.shape, BF16),)
         + (shape((rows, hidden_count), F32),) * 2
-        + (shape((4, hidden_count, wg.shape[0] // 4), BF16),),
-        [SMEM] + [VMEM] * 2 + [HBM] * 2,
-        [VMEM] * 5,
-        1,
-        1,
-        scratch=[pltpu.SemaphoreType.DMA((2, 4))],
-        limit=16,
-    )(place, own, near, in_hbm(wg), in_hbm(wu))
-
-
-def back_kernel(place, own, near, wd, back):
+        + (shape((4, hidden_count, wu.shape[0] // 4), BF16),),
+        [SMEM] + [VMEM] * 2 + [HBM] + [VMEM],
+        [VMEM] * 4,
+        1,
+        1,
+        scratch=[pltpu.SemaphoreType.DMA((4,))],
+        limit=8,
+    )(place, own, near, in_hbm(wu), wg)
+
+
+def back_kernel(place, own, near, wd, back, turned):
     row, _, g = pair(place, 0, own, near)
     for f in range(wd.shape[0] // STEP):
         cols = pl.ds(f * STEP, STEP)
         back[:, cols] = dot(g, wd[cols, row], 1, 1)
+        for i in range(2):
+            turned[i, :, cols] = wd[cols, block_at(place, far(place)[2 + i], g.shape[1])].T
 
 
 def own_back(place, own, near, wd):
-    rows, hidden_count = own.shape[1], wd.shape[0]
-    return call(
-        back_kernel, shape((rows, hidden_count), F32), [SMEM] + [VMEM] * 3, VMEM, 1, 1
+    rows, (hidden_count, full) = own.shape[1], wd.shape
+    return call(
+        back_kernel,
+        (shape((rows, hidden_count), F32), shape((2, full // 4, hidden_count), BF16)),
+        [SMEM] + [VMEM] * 3,
+        [VMEM] * 2,
+        1,
+        1,
     )(place, own, near, wd)
 
 
 def partial_kernel(place, own, sib, wg, wu, wd, *refs):
-    add_pieces([pair(place, 1, own, sib)], (wg, wu, wd), refs[:3], refs[3:6], store)
-    up_turned, down_turned = refs[6:]
-    wide = up_turned.shape[2]
-    for i in range(2):
-        rows = block_at(place, far(place)[2 + i], wide)
-        for f in range(0, wd.shape[0], STEP):
-            down_turned[i, :, f : f + STEP] = wd[f : f + STEP, rows].T
-    for p in range(4):
-        turn(wu[block_at(place, p, wide), :], up_turned.at[p])
+    add_pieces([pair(place, 1, own, sib)], (wg, wu, wd), refs[:3], refs[3:], store)
 
 
 def partial_sums(place, own, sib, weights, acc):
-    rows, hidden_count = acc[0].shape
-    wide = weights[1].shape[0] // 4
     return call(
         partial_kernel,
-        (shape((rows, hidden_count), F32),) * 3
-        + (shape((4, hidden_count, wide), BF16), shape((2, wide, hidden_count), BF16)),
+        (shape(acc[0].shape, F32),) * 3,
         [SMEM] + [VMEM] * 8,
-        [VMEM] * 5,
+        [VMEM] * 3,
         1,
         1,
         aliases={6: 0, 7: 1, 8: 2},
@@ -354,20 +372,22 @@
     z = lax.axis_index("expert").astype(jnp.int32)[None]
     tok_count, width = acts.shape
     packed = pack(z, acts, grad_out, routing, gates, groups)
-    blocks = [packed[0]] + [along(packed[k], k, groups) for k in range(1, groups)]
-    own = jnp.concatenate(blocks, axis=1)
+    blocks = [along(packed[k], k, groups) for k in range(1, groups)]
+    wg, wg_turned = load_gate(place, w_gate[0])
+    blocks, wg, wg_turned = lax.optimization_barrier((blocks, wg, wg_turned))
+    own = jnp.concatenate([packed[0]] + blocks, axis=1)
     near = across(own, 1)
     here = across(own, 2, 4), across(near, 2, 4)
-    wg, wu, gate, up, wg_turned = load(place, own, near, w_gate[0], w_up[0])
+    wu, gate, up, wu_turned = load_up(place, own, near, w_up[0], wg)
     first, gate, up = lax.optimization_barrier((here[0], gate, up))
     diag = across(first, 4, 2)
     there_second = across(first, 1)
     wd = w_down[0]
-    back = own_back(place, own, near, wd)
+    back, wd_turned = own_back(place, own, near, wd)
     second, back = lax.optimization_barrier((here[1], back))
     there_first = across(second, 1)
     weights, acc = (wg, wu, wd), (gate, up, back)
-    *acc, wu_turned, wd_turned = partial_sums(place, first, second, weights, acc)
+    acc = partial_sums(place, first, second, weights, acc)
     turned = wg_turned, wu_turned
     diag, acc = lax.optimization_barrier((diag, acc))
     diag_near = across(diag, 1)

time: 54.2 us -> 53.3 us (0.983)
  waiting for transfers between devices: 6.58 us -> 5.49 us
  Pallas kernels: 25.4 us -> 26.2 us
  starting transfers between devices: 20.3 us -> 19.6 us
    ppermute x6, waiting for transfers between devices: 4.94 us -> 1.63 us  [along(): lax.ppermute(array, 'expert', [(i, (i + distance) % count) for i in range...]
    ppermute x14, waiting for transfers between devices: 1.64 us -> 3.86 us  [across(): lax.ppermute(array, 'tensor', [(i, i ^ masks[i % 2]) for i in range(8)])]
    pallas_call x3 -> x4, Pallas kernels: 8.75 us -> 9.46 us  [the longest x1 3.63 us: load_up(): call(load_up_kernel, (shape(wu.shape, BF16),) + (shape((rows, hidden_coun...]
    ppermute x14, starting transfers between devices: 9.73 us -> 9.13 us  [across(): lax.ppermute(array, 'tensor', [(i, i ^ masks[i % 2]) for i in range(8)])]
  transfers between devices with their start and end apart: 20 -> 20, of which waited for: 7 -> 8; matrix products, arithmetic and copies ran while one was open for 0% -> 0% of each run, Pallas kernels for 40% -> 43%
where the time goes in v7:
time: 53.3 us; the launch traced here: 53.1 us
  Pallas kernels  26.2 us (49%)
  starting transfers between devices  19.6 us (37%)
  waiting for transfers between devices  5.49 us (10%)
  between operations  0.9 us (2%)
  other arithmetic  0.83 us (2%)
    ppermute x6, starting transfers between devices, along(): lax.ppermute(array, 'expert', [(i, (i + distance) % count) for i in range...  10.5 us
    pallas_call x3, Pallas kernels, weight_grads(): call(functools.partial(weight_kernel, jobs, len(more)), tuple((shape(out,...  9.47 us
    ppermute x14, starting transfers between devices, across(): lax.ppermute(array, 'tensor', [(i, i ^ masks[i % 2]) for i in range(8)])  9.13 us
    ppermute x14, waiting for transfers between devices, across(): lax.ppermute(array, 'tensor', [(i, i ^ masks[i % 2]) for i in range(8)])  3.86 us
    pallas_call x1, Pallas kernels, load_up(): call(load_up_kernel, (shape(wu.shape, BF16),) + (shape((rows, hidden_coun...  3.63 us
    pallas_call x1, Pallas kernels, load_gate(): call(load_gate_kernel, (shape(wg.shape, BF16), shape((4, hidden_count, fu...  3.33 us
    pallas_call x1, Pallas kernels, middle(): call(middle_kernel, (shape((rows, hidden_count), BF16),) * 3 + (shape((ro...  2.56 us
    pallas_call x3, Pallas kernels, slots(): call(functools.partial(slot_kernel, p), (shape((rows, width), F32), shape...  2.38 us
  transfers between devices with their start and end apart: 20, of which 8 were waited for; matrix products, arithmetic and copies ran while one was open for 0% of the time, Pallas kernels for 43%

profile of v7, /device:TPU:8, one launch (start us, length us, event | category | flops | bytes accessed | tf_op | source)
XLA Modules:
  0.0 53.1 jit_solution(7500693121965688119)
XLA Ops:
  0.6 1.0 %shard_map.102 = (bf16[2,48,384]{2,1,0:T(8,128)(2,1)S(1)}, bf16[2,48,384]{2,1,0:T(8,128)(2,1)S(1)}, bf16[2,48,384]{2,1,0:T(8,128)(2,1)S(1)}, bf16[2,48,384]{2,1,0:T(8,128)(2,1)S(1)}) custom-call(s32[1]{0:T(128)} %bitcast.1.place, bf16[48,384]{1,0:T(8,128)(2,1)} %refs_0_.1, bf16[48,384]{1,0:T(8,128)(2,1)} %refs_1_.1, s32[2,48]{1,0:T(2,128)} %bitcast.17, ...), custom_call_target="tpu_custom_call" | custom-call | flops 1 | bytes 1 | tf_op jit(solution)/shard_map/pallas_call | solution.py:348
  1.7 1.6 %collective-permute-start = (bf16[2,48,384]{2,1,0:T(8,128)(2,1)S(1)}, bf16[2,48,384]{2,1,0:T(8,128)(2,1)S(1)}, u32[]{:S(2)}, u32[]{:S(2)}) collective-permute-start(bf16[2,48,384]{2,1,0:T(8,128)(2,1)S(1)} %get-tuple-element.65), channel_id=1, source_target_pairs={{0,1},{1,2},{2,3},{3,0},{4,5},{5,6},{6,7},{7,4},{8,9},{9,10},{10,1... | collective-permute-start | bytes 221192 | tf_op jit(solution)/shard_map/ppermute | solution.py:366
  3.3 1.1 %collective-permute-start.1 = (bf16[2,48,384]{2,1,0:T(8,128)(2,1)S(1)}, bf16[2,48,384]{2,1,0:T(8,128)(2,1)S(1)}, u32[]{:S(2)}, u32[]{:S(2)}) collective-permute-start(bf16[2,48,384]{2,1,0:T(8,128)(2,1)S(1)} %get-tuple-element.66), channel_id=1, source_target_pairs={{0,2},{1,3},{2,0},{3,1},{4,6},{5,7},{6,4},{7,5},{8,10},{9,11},{10,... | collective-permute-start | bytes 221192 | tf_op jit(solution)/shard_map/ppermute | solution.py:366
  4.4 1.9 %collective-permute-start.2 = (bf16[2,48,384]{2,1,0:T(8,128)(2,1)S(1)}, bf16[2,48,384]{2,1,0:T(8,128)(2,1)S(1)}, u32[]{:S(2)}, u32[]{:S(2)}) collective-permute-start(bf16[2,48,384]{2,1,0:T(8,128)(2,1)S(1)} %get-tuple-element.67), channel_id=1, source_target_pairs={{0,3},{1,0},{2,1},{3,2},{4,7},{5,4},{6,5},{7,6},{8,11},{9,8},{10,9... | collective-permute-start | bytes 221192 | tf_op jit(solution)/shard_map/ppermute | solution.py:366
  6.3 3.3 %shard_map.103 = (bf16[3072,1024]{1,0:T(8,128)(2,1)S(1)}, bf16[4,1024,768]{2,1,0:T(8,128)(2,1)S(1)}) custom-call(s32[1]{0:T(128)} %bitcast.place, bf16[3072,1024]{1,0:T(8,128)(2,1)} %bitcast.15), custom_call_target="tpu_custom_call" | custom-call | flops 1 | bytes 1 | tf_op jit(solution)/shard_map/pallas_call | solution.py:122
  9.9 1.5 %collective-permute-done.2 = bf16[2,48,384]{2,1,0:T(8,128)(2,1)S(1)} collective-permute-done((bf16[2,48,384]{2,1,0:T(8,128)(2,1)S(1)}, bf16[2,48,384]{2,1,0:T(8,128)(2,1)S(1)}, u32[]{:S(2)}, u32[]{:S(2)}) %collective-permute-start.2) | collective-permute-done | bytes 73760 | tf_op jit(solution)/shard_map/ppermute | solution.py:366
  11.5 1.6 %collective-permute-start.3 = (bf16[2,192,384]{2,1,0:T(8,128)(2,1)S(1)}, bf16[2,192,384]{2,1,0:T(8,128)(2,1)S(1)}, u32[]{:S(2)}, u32[]{:S(2)}) collective-permute-start(bf16[2,192,384]{2,1,0:T(8,128)(2,1)S(1)} %constant_dynamic-update-slice_fusion.own.refs_0_), channel_id=1, source_target_pairs={{0,8},{4,20},{8,0},{12,28},{16,24},{20,4},{24,16},{28,12},{1,9},{5... | collective-permute-start | bytes 884744 | tf_op jit(solution)/shard_map/ppermute | solution.py:362
  13.0 1.5 %collective-permute-start.6 = (bf16[2,192,384]{2,1,0:T(8,128)(2,1)S(1)}, bf16[2,192,384]{2,1,0:T(8,128)(2,1)S(1)}, u32[]{:S(2)}, u32[]{:S(2)}) collective-permute-start(bf16[2,192,384]{2,1,0:T(8,128)(2,1)S(1)} %collective-permute-done.4.near.refs_4_), channel_id=1, source_target_pairs={{0,8},{4,20},{8,0},{12,28},{16,24},{20,4},{24,16},{28,12},{1,9},{5... | collective-permute-start | bytes 884744 | tf_op jit(solution)/shard_map/ppermute | solution.py:362
  14.5 3.6 %shard_map.104 = (bf16[3072,1024]{1,0:T(8,128)(2,1)S(1)}, f32[192,1024]{1,0:T(8,128)S(1)}, f32[192,1024]{1,0:T(8,128)S(1)}, bf16[4,1024,768]{2,1,0:T(8,128)(2,1)S(1)}) custom-call(s32[1]{0:T(128)} %bitcast.place, bf16[2,192,384]{2,1,0:T(8,128)(2,1)S(1)} %constant_dynamic-update-slice_fusion.own.refs_0_, ...), custom_call_target="tpu_custom_call" | custom-call | flops 1 | bytes 1 | tf_op jit(solution)/shard_map/pallas_call | solution.py:156
  18.3 1.5 %collective-permute-start.5 = (bf16[2,192,384]{2,1,0:T(8,128)(2,1)S(1)}, bf16[2,192,384]{2,1,0:T(8,128)(2,1)S(1)}, u32[]{:S(2)}, u32[]{:S(2)}) collective-permute-start(bf16[2,192,384]{2,1,0:T(8,128)(2,1)S(1)} %collective-permute-done.3.own.refs_1_), channel_id=1, source_target_pairs={{0,16},{4,12},{8,24},{12,4},{16,0},{20,28},{24,8},{28,20},{1,17},{... | collective-permute-start | bytes 884744 | tf_op jit(solution)/shard_map/ppermute | solution.py:362
  19.8 1.1 %shard_map.105 = (f32[192,1024]{1,0:T(8,128)S(1)}, bf16[2,768,1024]{2,1,0:T(8,128)(2,1)S(1)}) custom-call(s32[1]{0:T(128)} %bitcast.place, bf16[2,192,384]{2,1,0:T(8,128)(2,1)S(1)} %constant_dynamic-update-slice_fusion.own.refs_0_, bf16[2,192,384]{2,1,0:T(8,128)(2,1)S(1)} %collective-permute-done.4.near.refs_4_, bf16[1024,3072]{1,0:T(8,128)(2,1)S(1)} %bitcast.12), custom_call_target="tpu_custom_call" | custom-call | flops 1 | bytes 1 | tf_op jit(solution)/shard_map/pallas_call | solution.py:181
  20.9 1.2 %collective-permute-done.6.sib.refs_5_ = bf16[2,192,384]{2,1,0:T(8,128)(2,1)S(1)} collective-permute-done((bf16[2,192,384]{2,1,0:T(8,128)(2,1)S(1)}, bf16[2,192,384]{2,1,0:T(8,128)(2,1)S(1)}, u32[]{:S(2)}, u32[]{:S(2)}) %collective-permute-start.6) | collective-permute-done | bytes 294944 | tf_op jit(solution)/shard_map/ppermute | solution.py:362
  22.0 1.4 %shard_map.106 = (f32[192,1024]{1,0:T(8,128)S(1)}, f32[192,1024]{1,0:T(8,128)S(1)}, f32[192,1024]{1,0:T(8,128)S(1)}) custom-call(s32[1]{0:T(128)} %bitcast.place, bf16[2,192,384]{2,1,0:T(8,128)(2,1)S(1)} %collective-permute-done.3.own.refs_1_, ...), custom_call_target="tpu_custom_call", output_to_operand_aliasing={{0}: (6, {}), {1}: (7, {}), {2}: (8, {})} | custom-call | flops 1 | bytes 1 | tf_op jit(solution)/shard_map/pallas_call | solution.py:196
  23.5 1.5 %collective-permute-done.5.own.refs_3_ = bf16[2,192,384]{2,1,0:T(8,128)(2,1)S(1)} collective-permute-done((bf16[2,192,384]{2,1,0:T(8,128)(2,1)S(1)}, bf16[2,192,384]{2,1,0:T(8,128)(2,1)S(1)}, u32[]{:S(2)}, u32[]{:S(2)}) %collective-permute-start.5) | collective-permute-done | bytes 294944 | tf_op jit(solution)/shard_map/ppermute | solution.py:362
  25.0 1.3 %shard_map.107 = (f32[192,1024]{1,0:T(8,128)S(1)}, f32[192,1024]{1,0:T(8,128)S(1)}, f32[192,1024]{1,0:T(8,128)S(1)}) custom-call(s32[1]{0:T(128)} %bitcast.place, bf16[2,192,384]{2,1,0:T(8,128)(2,1)S(1)} %collective-permute-done.8.own.refs_2_, ...), custom_call_target="tpu_custom_call", output_to_operand_aliasing={{0}: (6, {}), {1}: (7, {}), {2}: (8, {})} | custom-call | flops 1 | bytes 1 | tf_op jit(solution)/shard_map/pallas_call | solution.py:217
  26.3 0.3 collective-permute-done.7.sib.refs_7_
  26.6 2.6 %shard_map.108 = (bf16[192,1024]{1,0:T(8,128)(2,1)S(1)}, bf16[192,1024]{1,0:T(8,128)(2,1)S(1)}, bf16[192,1024]{1,0:T(8,128)(2,1)S(1)}, f32[192,384]{1,0:T(8,128)S(1)}, bf16[192,384]{1,0:T(8,128)(2,1)S(1)}) custom-call(s32[1]{0:T(128)} %bitcast.place, bf16[2,192,384]{2,1,0:T(8,128)(2,1)S(1)} %collective-permute-done.5.own.refs_3_, ...), custom_call_target="tpu_custom_call" | custom-call | flops 1509949440 | tf_op jit(solution)/shard_map/pallas_call | solution.py:253
  29.1 0.3 collective-permute-start.10
  29.4 0.8 %shard_map.112 = (f32[192,384]{1,0:T(8,128)S(1)}, bf16[192,384]{1,0:T(8,128)(2,1)S(1)}) custom-call(s32[1]{0:T(128)} %bitcast.place, bf16[192,1024]{1,0:T(8,128)(2,1)S(1)} %get-tuple-element.117.refs_0_.refs_8_, bf16[192,1024]{1,0:T(8,128)(2,1)S(1)} %get-tuple-element.105.refs_1_.refs_8_, bf16[4,1024,768]{2,1,0:T(8,128)(2,1)S(1)} %get-tuple-element.87.wg.refs_2_, ...), custom_call_target="tpu_custom_call" | custom-call | flops 603979776 | tf_op jit(solution)/shard_map/pallas_call | solution.py:270
  30.2 0.4 collective-permute-start.14
  30.6 2.5 %collective-permute-start.13 = (bf16[192,384]{1,0:T(8,128)(2,1)S(1)}, bf16[192,384]{1,0:T(8,128)(2,1)S(1)}, u32[]{:S(2)}, u32[]{:S(2)}) collective-permute-start(bf16[192,384]{1,0:T(8,128)(2,1)S(1)} %convert_add_fusion.2), channel_id=1, source_target_pairs={{0,24},{4,28},{8,16},{12,20},{16,8},{20,12},{24,0},{28,4},{1,25},{... | collective-permute-start | bytes 442376 | tf_op jit(solution)/shard_map/ppermute | solution.py:362
  33.1 0.8 %shard_map.109 = (f32[192,384]{1,0:T(8,128)S(1)}, bf16[192,384]{1,0:T(8,128)(2,1)S(1)}) custom-call(s32[1]{0:T(128)} %bitcast.place, bf16[192,1024]{1,0:T(8,128)(2,1)S(1)} %get-tuple-element.117.refs_0_.refs_8_, bf16[192,1024]{1,0:T(8,128)(2,1)S(1)} %get-tuple-element.105.refs_1_.refs_8_, bf16[4,1024,768]{2,1,0:T(8,128)(2,1)S(1)} %get-tuple-element.87.wg.refs_2_, ...), custom_call_target="tpu_custom_call" | custom-call | flops 603979776 | tf_op jit(solution)/shard_map/pallas_call | solution.py:270
  34.1 0.6 %collective-permute-start.15 = (bf16[192,384]{1,0:T(8,128)(2,1)S(1)}, bf16[192,384]{1,0:T(8,128)(2,1)S(1)}, u32[]{:S(2)}, u32[]{:S(2)}) collective-permute-start(bf16[192,384]{1,0:T(8,128)(2,1)S(1)} %add_convert_fusion), channel_id=1, source_target_pairs={{0,8},{4,12},{8,0},{12,4},{16,24},{20,28},{24,16},{28,20},{1,9},{5... | collective-permute-start | bytes 442376 | tf_op jit(solution)/shard_map/ppermute | solution.py:362
  34.7 0.7 %collective-permute-done.11 = bf16[192,384]{1,0:T(8,128)(2,1)S(1)} collective-permute-done((bf16[192,384]{1,0:T(8,128)(2,1)S(1)}, bf16[192,384]{1,0:T(8,128)(2,1)S(1)}, u32[]{:S(2)}, u32[]{:S(2)}) %collective-permute-start.11) | collective-permute-done | bytes 147488 | tf_op jit(solution)/shard_map/ppermute | solution.py:362
  35.4 0.6 %collective-permute-start.16 = (bf16[192,384]{1,0:T(8,128)(2,1)S(1)}, bf16[192,384]{1,0:T(8,128)(2,1)S(1)}, u32[]{:S(2)}, u32[]{:S(2)}) collective-permute-start(bf16[192,384]{1,0:T(8,128)(2,1)S(1)} %convert_add_fusion.1), channel_id=1, source_target_pairs={{0,16},{4,20},{8,24},{12,28},{16,0},{20,4},{24,8},{28,12},{1,17},{... | collective-permute-start | bytes 442376 | tf_op jit(solution)/shard_map/ppermute | solution.py:362
  36.0 0.8 %shard_map.110 = (f32[192,384]{1,0:T(8,128)S(1)}, bf16[192,384]{1,0:T(8,128)(2,1)S(1)}) custom-call(s32[1]{0:T(128)} %bitcast.place, bf16[192,1024]{1,0:T(8,128)(2,1)S(1)} %get-tuple-element.117.refs_0_.refs_8_, bf16[192,1024]{1,0:T(8,128)(2,1)S(1)} %get-tuple-element.105.refs_1_.refs_8_, bf16[4,1024,768]{2,1,0:T(8,128)(2,1)S(1)} %get-tuple-element.87.wg.refs_2_, ...), custom_call_target="tpu_custom_call" | custom-call | flops 603979776 | tf_op jit(solution)/shard_map/pallas_call | solution.py:270
  36.9 2.2 %shard_map.111.refs_9_ = bf16[3072,1024]{1,0:T(8,128)(2,1)} custom-call(s32[1]{0:T(128)} %bitcast.place, bf16[2,192,384]{2,1,0:T(8,128)(2,1)S(1)} %constant_dynamic-update-slice_fusion.own.refs_0_, bf16[2,192,384]{2,1,0:T(8,128)(2,1)S(1)} %collective-permute-done.3.own.refs_1_, bf16[2,192,384]{2,1,0:T(8,128)(2,1)S(1)} %collective-permute-done.8.own.refs_2_, ...), custom_call_target="tpu_custom_call" | custom-call | flops 603979776 | bytes 3145728 | tf_op jit(solution)/shard_map/pallas_call | solution.py:316
  39.1 2.1 %shard_map.113 = bf16[3072,1024]{1,0:T(8,128)(2,1)} custom-call(s32[1]{0:T(128)} %bitcast.place, bf16[2,192,384]{2,1,0:T(8,128)(2,1)S(1)} %constant_dynamic-update-slice_fusion.own.refs_0_, bf16[2,192,384]{2,1,0:T(8,128)(2,1)S(1)} %collective-permute-done.3.own.refs_1_, ...), custom_call_target="tpu_custom_call", output_to_operand_aliasing={{}: (10, {})} | custom-call | flops 603979776 | bytes 3145728 | tf_op jit(solution)/shard_map/pallas_call | solution.py:316
  41.7 1.8 %collective-permute-start.19 = (bf16[48,384]{1,0:T(8,128)(2,1)S(1)}, bf16[48,384]{1,0:T(8,128)(2,1)S(1)}, u32[]{:S(2)}, u32[]{:S(2)}) collective-permute-start(bf16[48,384]{1,0:T(8,128)(2,1)S(1)} %get-tuple-element.125), channel_id=1, source_target_pairs={{0,1},{1,2},{2,3},{3,0},{4,5},{5,6},{6,7},{7,4},{8,9},{9,10},{10,1... | collective-permute-start | bytes 110600 | tf_op jit(solution)/shard_map/ppermute | solution.py:366
  43.6 3.7 %collective-permute-start.18 = (bf16[48,384]{1,0:T(8,128)(2,1)S(1)}, bf16[48,384]{1,0:T(8,128)(2,1)S(1)}, u32[]{:S(2)}, u32[]{:S(2)}) collective-permute-start(bf16[48,384]{1,0:T(8,128)(2,1)S(1)} %get-tuple-element.126), channel_id=1, source_target_pairs={{0,2},{1,3},{2,0},{3,1},{4,6},{5,7},{6,4},{7,5},{8,10},{9,11},{10,... | collective-permute-start | bytes 110600 | tf_op jit(solution)/shard_map/ppermute | solution.py:366
  47.3 5.1 %shard_map.114 = (bf16[3072,1024]{1,0:T(8,128)(2,1)}, bf16[1024,3072]{1,0:T(8,128)(2,1)}) custom-call(s32[1]{0:T(128)} %bitcast.place, bf16[2,192,384]{2,1,0:T(8,128)(2,1)S(1)} %constant_dynamic-update-slice_fusion.own.refs_0_, bf16[2,192,384]{2,1,0:T(8,128)(2,1)S(1)} %collective-permute-done.3.own.refs_1_, ...), custom_call_target="tpu_custom_call" | custom-call | flops 2415919104 | bytes 12582912 | tf_op jit(solution)/shard_map/pallas_call | solution.py:316
  52.4 0.6 %add_convert_fusion.1 = bf16[48,384]{1,0:T(8,128)(2,1)} fusion(bf16[48,384]{1,0:T(8,128)(2,1)S(1)} %collective-permute-done.19, bf16[48,384]{1,0:T(8,128)(2,1)S(1)} %collective-permute-done.18, bf16[48,384]{1,0:T(8,128)(2,1)S(1)} %collective-permute-done.17, f32[192,384]{1,0:T(8,128)S(1)} %convert_add_fusion), kind=kLoop, calls=%fused_computation.4 | loop fusion | flops 129024 | bytes 221184 | tf_op jit(solution)/shard_map/convert_element_type | solution.py:425
  (37 shorter events, 1.1 us)
Async XLA Ops:
  1.7 8.0 %collective-permute-start = (bf16[2,48,384]{2,1,0:T(8,128)(2,1)S(1)}, bf16[2,48,384]{2,1,0:T(8,128)(2,1)S(1)}, u32[]{:S(2)}, u32[]{:S(2)}) collective-permute-start(bf16[2,48,384]{2,1,0:T(8,128)(2,1)S(1)} %get-tuple-element.65), channel_id=1, source_target_pairs={{0,1},{1,2},{2,3},{3,0},{4,5},{5,6},{6,7},{7,4},{8,9},{9,10},{10,1... | collective-permute-start | bytes 221192 | tf_op jit(solution)/shard_map/ppermute | solution.py:366
  3.3 6.6 %collective-permute-start.1 = (bf16[2,48,384]{2,1,0:T(8,128)(2,1)S(1)}, bf16[2,48,384]{2,1,0:T(8,128)(2,1)S(1)}, u32[]{:S(2)}, u32[]{:S(2)}) collective-permute-start(bf16[2,48,384]{2,1,0:T(8,128)(2,1)S(1)} %get-tuple-element.66), channel_id=1, source_target_pairs={{0,2},{1,3},{2,0},{3,1},{4,6},{5,7},{6,4},{7,5},{8,10},{9,11},{10,... | collective-permute-start | bytes 221192 | tf_op jit(solution)/shard_map/ppermute | solution.py:366
  4.4 6.9 %collective-permute-start.2 = (bf16[2,48,384]{2,1,0:T(8,128)(2,1)S(1)}, bf16[2,48,384]{2,1,0:T(8,128)(2,1)S(1)}, u32[]{:S(2)}, u32[]{:S(2)}) collective-permute-start(bf16[2,48,384]{2,1,0:T(8,128)(2,1)S(1)} %get-tuple-element.67), channel_id=1, source_target_pairs={{0,3},{1,0},{2,1},{3,2},{4,7},{5,4},{6,5},{7,6},{8,11},{9,8},{10,9... | collective-permute-start | bytes 221192 | tf_op jit(solution)/shard_map/ppermute | solution.py:366
  11.3 8.5 %slice-start = ((s8[6291456]{0:T(1024)(128)(4,1)}), s8[4194304]{0:T(1024)(128)(4,1)S(1)}, s32[]{:S(2)}) async-start(s8[6291456]{0:T(1024)(128)(4,1)} %bitcast.10), calls=%async_computation | async-start | bytes 8388608
  11.4 1.6 %collective-permute-start.4 = (bf16[2,192,384]{2,1,0:T(8,128)(2,1)S(1)}, bf16[2,192,384]{2,1,0:T(8,128)(2,1)S(1)}, u32[]{:S(2)}, u32[]{:S(2)}) collective-permute-start(bf16[2,192,384]{2,1,0:T(8,128)(2,1)S(1)} %constant_dynamic-update-slice_fusion.own.refs_0_), channel_id=1, source_target_pairs={{0,4},{4,0},{8,12},{12,8},{16,20},{20,16},{24,28},{28,24},{1,5},{5... | collective-permute-start | bytes 884744 | tf_op jit(solution)/shard_map/ppermute | solution.py:362
  11.5 6.8 %collective-permute-start.3 = (bf16[2,192,384]{2,1,0:T(8,128)(2,1)S(1)}, bf16[2,192,384]{2,1,0:T(8,128)(2,1)S(1)}, u32[]{:S(2)}, u32[]{:S(2)}) collective-permute-start(bf16[2,192,384]{2,1,0:T(8,128)(2,1)S(1)} %constant_dynamic-update-slice_fusion.own.refs_0_), channel_id=1, source_target_pairs={{0,8},{4,20},{8,0},{12,28},{16,24},{20,4},{24,16},{28,12},{1,9},{5... | collective-permute-start | bytes 884744 | tf_op jit(solution)/shard_map/ppermute | solution.py:362
  13.0 9.0 %collective-permute-start.6 = (bf16[2,192,384]{2,1,0:T(8,128)(2,1)S(1)}, bf16[2,192,384]{2,1,0:T(8,128)(2,1)S(1)}, u32[]{:S(2)}, u32[]{:S(2)}) collective-permute-start(bf16[2,192,384]{2,1,0:T(8,128)(2,1)S(1)} %collective-permute-done.4.near.refs_4_), channel_id=1, source_target_pairs={{0,8},{4,20},{8,0},{12,28},{16,24},{20,4},{24,16},{28,12},{1,9},{5... | collective-permute-start | bytes 884744 | tf_op jit(solution)/shard_map/ppermute | solution.py:362
  14.5 5.3 %slice-start.1 = ((s8[6291456]{0:T(1024)(128)(4,1)}), s8[2097152]{0:T(1024)(128)(4,1)S(1)}, s32[]{:S(2)}) async-start(s8[6291456]{0:T(1024)(128)(4,1)} %bitcast.10), calls=%async_computation.1 | async-start | bytes 4194304
  18.3 6.7 %collective-permute-start.5 = (bf16[2,192,384]{2,1,0:T(8,128)(2,1)S(1)}, bf16[2,192,384]{2,1,0:T(8,128)(2,1)S(1)}, u32[]{:S(2)}, u32[]{:S(2)}) collective-permute-start(bf16[2,192,384]{2,1,0:T(8,128)(2,1)S(1)} %collective-permute-done.3.own.refs_1_), channel_id=1, source_target_pairs={{0,16},{4,12},{8,24},{12,4},{16,0},{20,28},{24,8},{28,20},{1,17},{... | collective-permute-start | bytes 884744 | tf_op jit(solution)/shard_map/ppermute | solution.py:362
  19.8 5.2 %collective-permute-start.9 = (bf16[2,192,384]{2,1,0:T(8,128)(2,1)S(1)}, bf16[2,192,384]{2,1,0:T(8,128)(2,1)S(1)}, u32[]{:S(2)}, u32[]{:S(2)}) collective-permute-start(bf16[2,192,384]{2,1,0:T(8,128)(2,1)S(1)} %collective-permute-done.3.own.refs_1_), channel_id=1, source_target_pairs={{0,4},{4,0},{8,12},{12,8},{16,20},{20,16},{24,28},{28,24},{1,5},{5... | collective-permute-start | bytes 884744 | tf_op jit(solution)/shard_map/ppermute | solution.py:362
  22.0 2.9 %collective-permute-start.8 = (bf16[2,192,384]{2,1,0:T(8,128)(2,1)S(1)}, bf16[2,192,384]{2,1,0:T(8,128)(2,1)S(1)}, u32[]{:S(2)}, u32[]{:S(2)}) collective-permute-start(bf16[2,192,384]{2,1,0:T(8,128)(2,1)S(1)} %collective-permute-done.6.sib.refs_5_), channel_id=1, source_target_pairs={{0,4},{4,0},{8,12},{12,8},{16,20},{20,16},{24,28},{28,24},{1,5},{5... | collective-permute-start | bytes 884744 | tf_op jit(solution)/shard_map/ppermute | solution.py:362
  25.0 1.6 %collective-permute-start.7 = (bf16[2,192,384]{2,1,0:T(8,128)(2,1)S(1)}, bf16[2,192,384]{2,1,0:T(8,128)(2,1)S(1)}, u32[]{:S(2)}, u32[]{:S(2)}) collective-permute-start(bf16[2,192,384]{2,1,0:T(8,128)(2,1)S(1)} %collective-permute-done.5.own.refs_3_), channel_id=1, source_target_pairs={{0,4},{4,0},{8,12},{12,8},{16,20},{20,16},{24,28},{28,24},{1,5},{5... | collective-permute-start | bytes 884744 | tf_op jit(solution)/shard_map/ppermute | solution.py:362
  29.1 1.4 %collective-permute-start.10 = (bf16[192,384]{1,0:T(8,128)(2,1)S(1)}, bf16[192,384]{1,0:T(8,128)(2,1)S(1)}, u32[]{:S(2)}, u32[]{:S(2)}) collective-permute-start(bf16[192,384]{1,0:T(8,128)(2,1)S(1)} %get-tuple-element.97), channel_id=1, source_target_pairs={{0,4},{4,0},{8,12},{12,8},{16,20},{20,16},{24,28},{28,24},{1,5},{5... | collective-permute-start | bytes 442376 | tf_op jit(solution)/shard_map/ppermute | solution.py:362
  30.2 3.8 %collective-permute-start.14 = (bf16[192,384]{1,0:T(8,128)(2,1)S(1)}, bf16[192,384]{1,0:T(8,128)(2,1)S(1)}, u32[]{:S(2)}, u32[]{:S(2)}) collective-permute-start(bf16[192,384]{1,0:T(8,128)(2,1)S(1)} %get-tuple-element.114), channel_id=1, source_target_pairs={{0,4},{4,0},{8,12},{12,8},{16,20},{20,16},{24,28},{28,24},{1,5},{5... | collective-permute-start | bytes 442376 | tf_op jit(solution)/shard_map/ppermute | solution.py:362
  30.6 8.5 %collective-permute-start.13 = (bf16[192,384]{1,0:T(8,128)(2,1)S(1)}, bf16[192,384]{1,0:T(8,128)(2,1)S(1)}, u32[]{:S(2)}, u32[]{:S(2)}) collective-permute-start(bf16[192,384]{1,0:T(8,128)(2,1)S(1)} %convert_add_fusion.2), channel_id=1, source_target_pairs={{0,24},{4,28},{8,16},{12,20},{16,8},{20,12},{24,0},{28,4},{1,25},{... | collective-permute-start | bytes 442376 | tf_op jit(solution)/shard_map/ppermute | solution.py:362
  33.9 1.4 %collective-permute-start.11 = (bf16[192,384]{1,0:T(8,128)(2,1)S(1)}, bf16[192,384]{1,0:T(8,128)(2,1)S(1)}, u32[]{:S(2)}, u32[]{:S(2)}) collective-permute-start(bf16[192,384]{1,0:T(8,128)(2,1)S(1)} %get-tuple-element.103), channel_id=1, source_target_pairs={{0,4},{4,0},{8,12},{12,8},{16,20},{20,16},{24,28},{28,24},{1,5},{5... | collective-permute-start | bytes 442376 | tf_op jit(solution)/shard_map/ppermute | solution.py:362
  34.1 7.2 %collective-permute-start.15 = (bf16[192,384]{1,0:T(8,128)(2,1)S(1)}, bf16[192,384]{1,0:T(8,128)(2,1)S(1)}, u32[]{:S(2)}, u32[]{:S(2)}) collective-permute-start(bf16[192,384]{1,0:T(8,128)(2,1)S(1)} %add_convert_fusion), channel_id=1, source_target_pairs={{0,8},{4,12},{8,0},{12,4},{16,24},{20,28},{24,16},{28,20},{1,9},{5... | collective-permute-start | bytes 442376 | tf_op jit(solution)/shard_map/ppermute | solution.py:362
  35.4 6.0 %collective-permute-start.16 = (bf16[192,384]{1,0:T(8,128)(2,1)S(1)}, bf16[192,384]{1,0:T(8,128)(2,1)S(1)}, u32[]{:S(2)}, u32[]{:S(2)}) collective-permute-start(bf16[192,384]{1,0:T(8,128)(2,1)S(1)} %convert_add_fusion.1), channel_id=1, source_target_pairs={{0,16},{4,20},{8,24},{12,28},{16,0},{20,4},{24,8},{28,12},{1,17},{... | collective-permute-start | bytes 442376 | tf_op jit(solution)/shard_map/ppermute | solution.py:362
  36.8 4.6 %collective-permute-start.12 = (bf16[192,384]{1,0:T(8,128)(2,1)S(1)}, bf16[192,384]{1,0:T(8,128)(2,1)S(1)}, u32[]{:S(2)}, u32[]{:S(2)}) collective-permute-start(bf16[192,384]{1,0:T(8,128)(2,1)S(1)} %get-tuple-element.109), channel_id=1, source_target_pairs={{0,4},{4,0},{8,12},{12,8},{16,20},{20,16},{24,28},{28,24},{1,5},{5... | collective-permute-start | bytes 442376 | tf_op jit(solution)/shard_map/ppermute | solution.py:362
  41.5 10.9 %collective-permute-start.17 = (bf16[48,384]{1,0:T(8,128)(2,1)S(1)}, bf16[48,384]{1,0:T(8,128)(2,1)S(1)}, u32[]{:S(2)}, u32[]{:S(2)}) collective-permute-start(bf16[48,384]{1,0:T(8,128)(2,1)S(1)} %get-tuple-element.124), channel_id=1, source_target_pairs={{0,3},{1,0},{2,1},{3,2},{4,7},{5,4},{6,5},{7,6},{8,11},{9,8},{10,9... | collective-permute-start | bytes 110600 | tf_op jit(solution)/shard_map/ppermute | solution.py:366
  41.7 10.7 %collective-permute-start.19 = (bf16[48,384]{1,0:T(8,128)(2,1)S(1)}, bf16[48,384]{1,0:T(8,128)(2,1)S(1)}, u32[]{:S(2)}, u32[]{:S(2)}) collective-permute-start(bf16[48,384]{1,0:T(8,128)(2,1)S(1)} %get-tuple-element.125), channel_id=1, source_target_pairs={{0,1},{1,2},{2,3},{3,0},{4,5},{5,6},{6,7},{7,4},{8,9},{9,10},{10,1... | collective-permute-start | bytes 110600 | tf_op jit(solution)/shard_map/ppermute | solution.py:366
  43.6 8.9 %collective-permute-start.18 = (bf16[48,384]{1,0:T(8,128)(2,1)S(1)}, bf16[48,384]{1,0:T(8,128)(2,1)S(1)}, u32[]{:S(2)}, u32[]{:S(2)}) collective-permute-start(bf16[48,384]{1,0:T(8,128)(2,1)S(1)} %get-tuple-element.126), channel_id=1, source_target_pairs={{0,2},{1,3},{2,0},{3,1},{4,6},{5,7},{6,4},{7,5},{8,10},{9,11},{10,... | collective-permute-start | bytes 110600 | tf_op jit(solution)/shard_map/ppermute | solution.py:366

commit v8 on v7

--- a/solution.py
+++ b/solution.py
@@ -234,30 +234,30 @@
     send[...] = jnp.where(first, high, low).astype(BF16)
 
 
-def middle_kernel(place, own, sib, wg, wu, wd, gate, up, back, hid, dg, du, keep, send):
+def middle_kernel(place, own, sib, wg, wu, wd, wg_turned, wu_turned, gate, up, back, hid, dg, du, keep, send):
     rows, x, g = pair(place, 3, own, sib)
     for f in range(wd.shape[2] // STEP):
         cols = pl.ds(f * STEP, STEP)
         sums = (
-            gate[:, cols] + dot(x, wg[3, cols, :], 1, 1),
-            up[:, cols] + dot(x, wu[3, cols, :], 1, 1),
+            gate[:, cols] + dot(x, wg[rows, cols], 1, 0),
+            up[:, cols] + dot(x, wu[rows, cols], 1, 0),
             back[:, cols] + dot(g, wd[1, :, cols], 1, 0),
         )
         store_grads(cols, sums, (hid, dg, du))
-    write_slots(place, 3, dg, du, wg, wu, keep, send)
-
-
-def middle(place, own, sib, turned, wd, acc):
+    write_slots(place, 3, dg, du, wg_turned, wu_turned, keep, send)
+
+
+def middle(place, own, sib, weights, turned, acc):
     rows, width = own.shape[1:]
-    hidden_count = wd.shape[2]
+    hidden_count = turned[0].shape[1]
     return call(
         middle_kernel,
         (shape((rows, hidden_count), BF16),) * 3 + (shape((rows, width), F32), shape((rows, width), BF16)),
-        [SMEM] + [VMEM] * 8,
+        [SMEM] + [VMEM] * 10,
         [VMEM] * 5,
         20 * rows * width * hidden_count,
         0,
-    )(place, own, sib, *turned, wd, *acc)
+    )(place, own, sib, *weights, *turned, *acc)
 
 
 def slot_kernel(p, place, *refs):
@@ -392,7 +392,7 @@
     diag, acc = lax.optimization_barrier((diag, acc))
     diag_near = across(diag, 1)
     acc = third_sums(place, there_first, there_second, (wg, wu, wd_turned), acc)
-    hid, dg, du, keep, send = middle(place, diag, diag_near, turned, wd_turned, acc)
+    hid, dg, du, keep, send = middle(place, diag, diag_near, (wg, wu, wd_turned), turned, acc)
     mine_of = own, first, there_first, diag
     other_of = near, second, there_second, diag_near
 

time: 53.3 us -> 53.1 us (level)
  no operation moved by 1% of the time
where the time goes in v8:
time: 53.1 us; the launch traced here: 52.9 us
  Pallas kernels  26 us (49%)
  starting transfers between devices  19.6 us (37%)
  waiting for transfers between devices  5.49 us (10%)
  between operations  0.9 us (2%)
  other arithmetic  0.83 us (2%)
    ppermute x6, starting transfers between devices, along(): lax.ppermute(array, 'expert', [(i, (i + distance) % count) for i in range...  10.5 us
    pallas_call x3, Pallas kernels, weight_grads(): call(functools.partial(weight_kernel, jobs, len(more)), tuple((shape(out,...  9.47 us
    ppermute x14, starting transfers between devices, across(): lax.ppermute(array, 'tensor', [(i, i ^ masks[i % 2]) for i in range(8)])  9.12 us
    ppermute x14, waiting for transfers between devices, across(): lax.ppermute(array, 'tensor', [(i, i ^ masks[i % 2]) for i in range(8)])  3.86 us
    pallas_call x1, Pallas kernels, load_up(): call(load_up_kernel, (shape(wu.shape, BF16),) + (shape((rows, hidden_coun...  3.63 us
    pallas_call x1, Pallas kernels, load_gate(): call(load_gate_kernel, (shape(wg.shape, BF16), shape((4, hidden_count, fu...  3.33 us
    pallas_call x3, Pallas kernels, slots(): call(functools.partial(slot_kernel, p), (shape((rows, width), F32), shape...  2.39 us
    pallas_call x1, Pallas kernels, middle(): call(middle_kernel, (shape((rows, hidden_count), BF16),) * 3 + (shape((ro...  2.34 us
  transfers between devices with their start and end apart: 20, of which 8 were waited for; matrix products, arithmetic and copies ran while one was open for 0% of the time, Pallas kernels for 43%

profile of v8, /device:TPU:8, one launch (start us, length us, event | category | flops | bytes accessed | tf_op | source)
XLA Modules:
  0.0 52.9 jit_solution(12437186681773856257)
XLA Ops:
  0.6 1.0 %shard_map.102 = (bf16[2,48,384]{2,1,0:T(8,128)(2,1)S(1)}, bf16[2,48,384]{2,1,0:T(8,128)(2,1)S(1)}, bf16[2,48,384]{2,1,0:T(8,128)(2,1)S(1)}, bf16[2,48,384]{2,1,0:T(8,128)(2,1)S(1)}) custom-call(s32[1]{0:T(128)} %bitcast.1.place, bf16[48,384]{1,0:T(8,128)(2,1)} %refs_0_.1, bf16[48,384]{1,0:T(8,128)(2,1)} %refs_1_.1, s32[2,48]{1,0:T(2,128)} %bitcast.17, ...), custom_call_target="tpu_custom_call" | custom-call | flops 1 | bytes 1 | tf_op jit(solution)/shard_map/pallas_call | solution.py:348
  1.7 1.6 %collective-permute-start = (bf16[2,48,384]{2,1,0:T(8,128)(2,1)S(1)}, bf16[2,48,384]{2,1,0:T(8,128)(2,1)S(1)}, u32[]{:S(2)}, u32[]{:S(2)}) collective-permute-start(bf16[2,48,384]{2,1,0:T(8,128)(2,1)S(1)} %get-tuple-element.65), channel_id=1, source_target_pairs={{0,1},{1,2},{2,3},{3,0},{4,5},{5,6},{6,7},{7,4},{8,9},{9,10},{10,1... | collective-permute-start | bytes 221192 | tf_op jit(solution)/shard_map/ppermute | solution.py:366
  3.3 1.1 %collective-permute-start.1 = (bf16[2,48,384]{2,1,0:T(8,128)(2,1)S(1)}, bf16[2,48,384]{2,1,0:T(8,128)(2,1)S(1)}, u32[]{:S(2)}, u32[]{:S(2)}) collective-permute-start(bf16[2,48,384]{2,1,0:T(8,128)(2,1)S(1)} %get-tuple-element.66), channel_id=1, source_target_pairs={{0,2},{1,3},{2,0},{3,1},{4,6},{5,7},{6,4},{7,5},{8,10},{9,11},{10,... | collective-permute-start | bytes 221192 | tf_op jit(solution)/shard_map/ppermute | solution.py:366
  4.4 1.9 %collective-permute-start.2 = (bf16[2,48,384]{2,1,0:T(8,128)(2,1)S(1)}, bf16[2,48,384]{2,1,0:T(8,128)(2,1)S(1)}, u32[]{:S(2)}, u32[]{:S(2)}) collective-permute-start(bf16[2,48,384]{2,1,0:T(8,128)(2,1)S(1)} %get-tuple-element.67), channel_id=1, source_target_pairs={{0,3},{1,0},{2,1},{3,2},{4,7},{5,4},{6,5},{7,6},{8,11},{9,8},{10,9... | collective-permute-start | bytes 221192 | tf_op jit(solution)/shard_map/ppermute | solution.py:366
  6.3 3.3 %shard_map.103 = (bf16[3072,1024]{1,0:T(8,128)(2,1)S(1)}, bf16[4,1024,768]{2,1,0:T(8,128)(2,1)S(1)}) custom-call(s32[1]{0:T(128)} %bitcast.place, bf16[3072,1024]{1,0:T(8,128)(2,1)} %bitcast.15), custom_call_target="tpu_custom_call" | custom-call | flops 1 | bytes 1 | tf_op jit(solution)/shard_map/pallas_call | solution.py:122
  9.9 1.5 %collective-permute-done.2 = bf16[2,48,384]{2,1,0:T(8,128)(2,1)S(1)} collective-permute-done((bf16[2,48,384]{2,1,0:T(8,128)(2,1)S(1)}, bf16[2,48,384]{2,1,0:T(8,128)(2,1)S(1)}, u32[]{:S(2)}, u32[]{:S(2)}) %collective-permute-start.2) | collective-permute-done | bytes 73760 | tf_op jit(solution)/shard_map/ppermute | solution.py:366
  11.5 1.6 %collective-permute-start.3 = (bf16[2,192,384]{2,1,0:T(8,128)(2,1)S(1)}, bf16[2,192,384]{2,1,0:T(8,128)(2,1)S(1)}, u32[]{:S(2)}, u32[]{:S(2)}) collective-permute-start(bf16[2,192,384]{2,1,0:T(8,128)(2,1)S(1)} %constant_dynamic-update-slice_fusion.own.refs_0_), channel_id=1, source_target_pairs={{0,8},{4,20},{8,0},{12,28},{16,24},{20,4},{24,16},{28,12},{1,9},{5... | collective-permute-start | bytes 884744 | tf_op jit(solution)/shard_map/ppermute | solution.py:362
  13.0 1.5 %collective-permute-start.6 = (bf16[2,192,384]{2,1,0:T(8,128)(2,1)S(1)}, bf16[2,192,384]{2,1,0:T(8,128)(2,1)S(1)}, u32[]{:S(2)}, u32[]{:S(2)}) collective-permute-start(bf16[2,192,384]{2,1,0:T(8,128)(2,1)S(1)} %collective-permute-done.4.near.refs_4_), channel_id=1, source_target_pairs={{0,8},{4,20},{8,0},{12,28},{16,24},{20,4},{24,16},{28,12},{1,9},{5... | collective-permute-start | bytes 884744 | tf_op jit(solution)/shard_map/ppermute | solution.py:362
  14.5 3.6 %shard_map.104 = (bf16[3072,1024]{1,0:T(8,128)(2,1)S(1)}, f32[192,1024]{1,0:T(8,128)S(1)}, f32[192,1024]{1,0:T(8,128)S(1)}, bf16[4,1024,768]{2,1,0:T(8,128)(2,1)S(1)}) custom-call(s32[1]{0:T(128)} %bitcast.place, bf16[2,192,384]{2,1,0:T(8,128)(2,1)S(1)} %constant_dynamic-update-slice_fusion.own.refs_0_, ...), custom_call_target="tpu_custom_call" | custom-call | flops 1 | bytes 1 | tf_op jit(solution)/shard_map/pallas_call | solution.py:156
  18.3 1.5 %collective-permute-start.5 = (bf16[2,192,384]{2,1,0:T(8,128)(2,1)S(1)}, bf16[2,192,384]{2,1,0:T(8,128)(2,1)S(1)}, u32[]{:S(2)}, u32[]{:S(2)}) collective-permute-start(bf16[2,192,384]{2,1,0:T(8,128)(2,1)S(1)} %collective-permute-done.3.own.refs_1_), channel_id=1, source_target_pairs={{0,16},{4,12},{8,24},{12,4},{16,0},{20,28},{24,8},{28,20},{1,17},{... | collective-permute-start | bytes 884744 | tf_op jit(solution)/shard_map/ppermute | solution.py:362
  19.8 1.1 %shard_map.105 = (f32[192,1024]{1,0:T(8,128)S(1)}, bf16[2,768,1024]{2,1,0:T(8,128)(2,1)S(1)}) custom-call(s32[1]{0:T(128)} %bitcast.place, bf16[2,192,384]{2,1,0:T(8,128)(2,1)S(1)} %constant_dynamic-update-slice_fusion.own.refs_0_, bf16[2,192,384]{2,1,0:T(8,128)(2,1)S(1)} %collective-permute-done.4.near.refs_4_, bf16[1024,3072]{1,0:T(8,128)(2,1)S(1)} %bitcast.12), custom_call_target="tpu_custom_call" | custom-call | flops 1 | bytes 1 | tf_op jit(solution)/shard_map/pallas_call | solution.py:181
  20.9 1.2 %collective-permute-done.6.sib.refs_5_ = bf16[2,192,384]{2,1,0:T(8,128)(2,1)S(1)} collective-permute-done((bf16[2,192,384]{2,1,0:T(8,128)(2,1)S(1)}, bf16[2,192,384]{2,1,0:T(8,128)(2,1)S(1)}, u32[]{:S(2)}, u32[]{:S(2)}) %collective-permute-start.6) | collective-permute-done | bytes 294944 | tf_op jit(solution)/shard_map/ppermute | solution.py:362
  22.0 1.4 %shard_map.106 = (f32[192,1024]{1,0:T(8,128)S(1)}, f32[192,1024]{1,0:T(8,128)S(1)}, f32[192,1024]{1,0:T(8,128)S(1)}) custom-call(s32[1]{0:T(128)} %bitcast.place, bf16[2,192,384]{2,1,0:T(8,128)(2,1)S(1)} %collective-permute-done.3.own.refs_1_, ...), custom_call_target="tpu_custom_call", output_to_operand_aliasing={{0}: (6, {}), {1}: (7, {}), {2}: (8, {})} | custom-call | flops 1 | bytes 1 | tf_op jit(solution)/shard_map/pallas_call | solution.py:196
  23.5 1.5 %collective-permute-done.5.own.refs_3_ = bf16[2,192,384]{2,1,0:T(8,128)(2,1)S(1)} collective-permute-done((bf16[2,192,384]{2,1,0:T(8,128)(2,1)S(1)}, bf16[2,192,384]{2,1,0:T(8,128)(2,1)S(1)}, u32[]{:S(2)}, u32[]{:S(2)}) %collective-permute-start.5) | collective-permute-done | bytes 294944 | tf_op jit(solution)/shard_map/ppermute | solution.py:362
  25.0 1.3 %shard_map.107 = (f32[192,1024]{1,0:T(8,128)S(1)}, f32[192,1024]{1,0:T(8,128)S(1)}, f32[192,1024]{1,0:T(8,128)S(1)}) custom-call(s32[1]{0:T(128)} %bitcast.place, bf16[2,192,384]{2,1,0:T(8,128)(2,1)S(1)} %collective-permute-done.8.own.refs_2_, ...), custom_call_target="tpu_custom_call", output_to_operand_aliasing={{0}: (6, {}), {1}: (7, {}), {2}: (8, {})} | custom-call | flops 1 | bytes 1 | tf_op jit(solution)/shard_map/pallas_call | solution.py:217
  26.3 0.3 collective-permute-done.7.sib.refs_7_
  26.6 2.3 %shard_map.108 = (bf16[192,1024]{1,0:T(8,128)(2,1)S(1)}, bf16[192,1024]{1,0:T(8,128)(2,1)S(1)}, bf16[192,1024]{1,0:T(8,128)(2,1)S(1)}, f32[192,384]{1,0:T(8,128)S(1)}, bf16[192,384]{1,0:T(8,128)(2,1)S(1)}) custom-call(s32[1]{0:T(128)} %bitcast.place, bf16[2,192,384]{2,1,0:T(8,128)(2,1)S(1)} %collective-permute-done.5.own.refs_3_, ...), custom_call_target="tpu_custom_call" | custom-call | flops 1509949440 | tf_op jit(solution)/shard_map/pallas_call | solution.py:253
  28.9 0.3 collective-permute-start.10
  29.2 0.8 %shard_map.112 = (f32[192,384]{1,0:T(8,128)S(1)}, bf16[192,384]{1,0:T(8,128)(2,1)S(1)}) custom-call(s32[1]{0:T(128)} %bitcast.place, bf16[192,1024]{1,0:T(8,128)(2,1)S(1)} %get-tuple-element.117.refs_0_.refs_8_, bf16[192,1024]{1,0:T(8,128)(2,1)S(1)} %get-tuple-element.105.refs_1_.refs_8_, bf16[4,1024,768]{2,1,0:T(8,128)(2,1)S(1)} %get-tuple-element.88.wg_turned.refs_2_, ...), custom_call_target="tpu_custom_call" | custom-call | flops 603979776 | tf_op jit(solution)/shard_map/pallas_call | solution.py:270
  30.0 0.4 collective-permute-start.14
  30.4 2.5 %collective-permute-start.13 = (bf16[192,384]{1,0:T(8,128)(2,1)S(1)}, bf16[192,384]{1,0:T(8,128)(2,1)S(1)}, u32[]{:S(2)}, u32[]{:S(2)}) collective-permute-start(bf16[192,384]{1,0:T(8,128)(2,1)S(1)} %convert_add_fusion.2), channel_id=1, source_target_pairs={{0,24},{4,28},{8,16},{12,20},{16,8},{20,12},{24,0},{28,4},{1,25},{... | collective-permute-start | bytes 442376 | tf_op jit(solution)/shard_map/ppermute | solution.py:362
  32.9 0.8 %shard_map.109 = (f32[192,384]{1,0:T(8,128)S(1)}, bf16[192,384]{1,0:T(8,128)(2,1)S(1)}) custom-call(s32[1]{0:T(128)} %bitcast.place, bf16[192,1024]{1,0:T(8,128)(2,1)S(1)} %get-tuple-element.117.refs_0_.refs_8_, bf16[192,1024]{1,0:T(8,128)(2,1)S(1)} %get-tuple-element.105.refs_1_.refs_8_, bf16[4,1024,768]{2,1,0:T(8,128)(2,1)S(1)} %get-tuple-element.88.wg_turned.refs_2_, ...), custom_call_target="tpu_custom_call" | custom-call | flops 603979776 | tf_op jit(solution)/shard_map/pallas_call | solution.py:270
  33.8 0.6 %collective-permute-start.15 = (bf16[192,384]{1,0:T(8,128)(2,1)S(1)}, bf16[192,384]{1,0:T(8,128)(2,1)S(1)}, u32[]{:S(2)}, u32[]{:S(2)}) collective-permute-start(bf16[192,384]{1,0:T(8,128)(2,1)S(1)} %add_convert_fusion), channel_id=1, source_target_pairs={{0,8},{4,12},{8,0},{12,4},{16,24},{20,28},{24,16},{28,20},{1,9},{5... | collective-permute-start | bytes 442376 | tf_op jit(solution)/shard_map/ppermute | solution.py:362
  34.4 0.7 %collective-permute-done.11 = bf16[192,384]{1,0:T(8,128)(2,1)S(1)} collective-permute-done((bf16[192,384]{1,0:T(8,128)(2,1)S(1)}, bf16[192,384]{1,0:T(8,128)(2,1)S(1)}, u32[]{:S(2)}, u32[]{:S(2)}) %collective-permute-start.11) | collective-permute-done | bytes 147488 | tf_op jit(solution)/shard_map/ppermute | solution.py:362
  35.2 0.6 %collective-permute-start.16 = (bf16[192,384]{1,0:T(8,128)(2,1)S(1)}, bf16[192,384]{1,0:T(8,128)(2,1)S(1)}, u32[]{:S(2)}, u32[]{:S(2)}) collective-permute-start(bf16[192,384]{1,0:T(8,128)(2,1)S(1)} %convert_add_fusion.1), channel_id=1, source_target_pairs={{0,16},{4,20},{8,24},{12,28},{16,0},{20,4},{24,8},{28,12},{1,17},{... | collective-permute-start | bytes 442376 | tf_op jit(solution)/shard_map/ppermute | solution.py:362
  35.8 0.8 %shard_map.110 = (f32[192,384]{1,0:T(8,128)S(1)}, bf16[192,384]{1,0:T(8,128)(2,1)S(1)}) custom-call(s32[1]{0:T(128)} %bitcast.place, bf16[192,1024]{1,0:T(8,128)(2,1)S(1)} %get-tuple-element.117.refs_0_.refs_8_, bf16[192,1024]{1,0:T(8,128)(2,1)S(1)} %get-tuple-element.105.refs_1_.refs_8_, bf16[4,1024,768]{2,1,0:T(8,128)(2,1)S(1)} %get-tuple-element.88.wg_turned.refs_2_, ...), custom_call_target="tpu_custom_call" | custom-call | flops 603979776 | tf_op jit(solution)/shard_map/pallas_call | solution.py:270
  36.6 2.2 %shard_map.111.refs_9_ = bf16[3072,1024]{1,0:T(8,128)(2,1)} custom-call(s32[1]{0:T(128)} %bitcast.place, bf16[2,192,384]{2,1,0:T(8,128)(2,1)S(1)} %constant_dynamic-update-slice_fusion.own.refs_0_, bf16[2,192,384]{2,1,0:T(8,128)(2,1)S(1)} %collective-permute-done.3.own.refs_1_, bf16[2,192,384]{2,1,0:T(8,128)(2,1)S(1)} %collective-permute-done.8.own.refs_2_, ...), custom_call_target="tpu_custom_call" | custom-call | flops 603979776 | bytes 3145728 | tf_op jit(solution)/shard_map/pallas_call | solution.py:316
  38.9 2.1 %shard_map.113 = bf16[3072,1024]{1,0:T(8,128)(2,1)} custom-call(s32[1]{0:T(128)} %bitcast.place, bf16[2,192,384]{2,1,0:T(8,128)(2,1)S(1)} %constant_dynamic-update-slice_fusion.own.refs_0_, bf16[2,192,384]{2,1,0:T(8,128)(2,1)S(1)} %collective-permute-done.3.own.refs_1_, ...), custom_call_target="tpu_custom_call", output_to_operand_aliasing={{}: (10, {})} | custom-call | flops 603979776 | bytes 3145728 | tf_op jit(solution)/shard_map/pallas_call | solution.py:316
  41.5 1.8 %collective-permute-start.19 = (bf16[48,384]{1,0:T(8,128)(2,1)S(1)}, bf16[48,384]{1,0:T(8,128)(2,1)S(1)}, u32[]{:S(2)}, u32[]{:S(2)}) collective-permute-start(bf16[48,384]{1,0:T(8,128)(2,1)S(1)} %get-tuple-element.125), channel_id=1, source_target_pairs={{0,1},{1,2},{2,3},{3,0},{4,5},{5,6},{6,7},{7,4},{8,9},{9,10},{10,1... | collective-permute-start | bytes 110600 | tf_op jit(solution)/shard_map/ppermute | solution.py:366
  43.4 3.7 %collective-permute-start.18 = (bf16[48,384]{1,0:T(8,128)(2,1)S(1)}, bf16[48,384]{1,0:T(8,128)(2,1)S(1)}, u32[]{:S(2)}, u32[]{:S(2)}) collective-permute-start(bf16[48,384]{1,0:T(8,128)(2,1)S(1)} %get-tuple-element.126), channel_id=1, source_target_pairs={{0,2},{1,3},{2,0},{3,1},{4,6},{5,7},{6,4},{7,5},{8,10},{9,11},{10,... | collective-permute-start | bytes 110600 | tf_op jit(solution)/shard_map/ppermute | solution.py:366
  47.1 5.1 %shard_map.114 = (bf16[3072,1024]{1,0:T(8,128)(2,1)}, bf16[1024,3072]{1,0:T(8,128)(2,1)}) custom-call(s32[1]{0:T(128)} %bitcast.place, bf16[2,192,384]{2,1,0:T(8,128)(2,1)S(1)} %constant_dynamic-update-slice_fusion.own.refs_0_, bf16[2,192,384]{2,1,0:T(8,128)(2,1)S(1)} %collective-permute-done.3.own.refs_1_, ...), custom_call_target="tpu_custom_call" | custom-call | flops 2415919104 | bytes 12582912 | tf_op jit(solution)/shard_map/pallas_call | solution.py:316
  52.2 0.6 %add_convert_fusion.1 = bf16[48,384]{1,0:T(8,128)(2,1)} fusion(bf16[48,384]{1,0:T(8,128)(2,1)S(1)} %collective-permute-done.19, bf16[48,384]{1,0:T(8,128)(2,1)S(1)} %collective-permute-done.18, bf16[48,384]{1,0:T(8,128)(2,1)S(1)} %collective-permute-done.17, f32[192,384]{1,0:T(8,128)S(1)} %convert_add_fusion), kind=kLoop, calls=%fused_computation.4 | loop fusion | flops 129024 | bytes 221184 | tf_op jit(solution)/shard_map/convert_element_type | solution.py:425
  (37 shorter events, 1.2 us)
Async XLA Ops:
  1.7 8.0 %collective-permute-start = (bf16[2,48,384]{2,1,0:T(8,128)(2,1)S(1)}, bf16[2,48,384]{2,1,0:T(8,128)(2,1)S(1)}, u32[]{:S(2)}, u32[]{:S(2)}) collective-permute-start(bf16[2,48,384]{2,1,0:T(8,128)(2,1)S(1)} %get-tuple-element.65), channel_id=1, source_target_pairs={{0,1},{1,2},{2,3},{3,0},{4,5},{5,6},{6,7},{7,4},{8,9},{9,10},{10,1... | collective-permute-start | bytes 221192 | tf_op jit(solution)/shard_map/ppermute | solution.py:366
  3.3 6.6 %collective-permute-start.1 = (bf16[2,48,384]{2,1,0:T(8,128)(2,1)S(1)}, bf16[2,48,384]{2,1,0:T(8,128)(2,1)S(1)}, u32[]{:S(2)}, u32[]{:S(2)}) collective-permute-start(bf16[2,48,384]{2,1,0:T(8,128)(2,1)S(1)} %get-tuple-element.66), channel_id=1, source_target_pairs={{0,2},{1,3},{2,0},{3,1},{4,6},{5,7},{6,4},{7,5},{8,10},{9,11},{10,... | collective-permute-start | bytes 221192 | tf_op jit(solution)/shard_map/ppermute | solution.py:366
  4.4 6.9 %collective-permute-start.2 = (bf16[2,48,384]{2,1,0:T(8,128)(2,1)S(1)}, bf16[2,48,384]{2,1,0:T(8,128)(2,1)S(1)}, u32[]{:S(2)}, u32[]{:S(2)}) collective-permute-start(bf16[2,48,384]{2,1,0:T(8,128)(2,1)S(1)} %get-tuple-element.67), channel_id=1, source_target_pairs={{0,3},{1,0},{2,1},{3,2},{4,7},{5,4},{6,5},{7,6},{8,11},{9,8},{10,9... | collective-permute-start | bytes 221192 | tf_op jit(solution)/shard_map/ppermute | solution.py:366
  11.3 8.5 %slice-start = ((s8[6291456]{0:T(1024)(128)(4,1)}), s8[4194304]{0:T(1024)(128)(4,1)S(1)}, s32[]{:S(2)}) async-start(s8[6291456]{0:T(1024)(128)(4,1)} %bitcast.10), calls=%async_computation | async-start | bytes 8388608
  11.4 1.6 %collective-permute-start.4 = (bf16[2,192,384]{2,1,0:T(8,128)(2,1)S(1)}, bf16[2,192,384]{2,1,0:T(8,128)(2,1)S(1)}, u32[]{:S(2)}, u32[]{:S(2)}) collective-permute-start(bf16[2,192,384]{2,1,0:T(8,128)(2,1)S(1)} %constant_dynamic-update-slice_fusion.own.refs_0_), channel_id=1, source_target_pairs={{0,4},{4,0},{8,12},{12,8},{16,20},{20,16},{24,28},{28,24},{1,5},{5... | collective-permute-start | bytes 884744 | tf_op jit(solution)/shard_map/ppermute | solution.py:362
  11.5 6.8 %collective-permute-start.3 = (bf16[2,192,384]{2,1,0:T(8,128)(2,1)S(1)}, bf16[2,192,384]{2,1,0:T(8,128)(2,1)S(1)}, u32[]{:S(2)}, u32[]{:S(2)}) collective-permute-start(bf16[2,192,384]{2,1,0:T(8,128)(2,1)S(1)} %constant_dynamic-update-slice_fusion.own.refs_0_), channel_id=1, source_target_pairs={{0,8},{4,20},{8,0},{12,28},{16,24},{20,4},{24,16},{28,12},{1,9},{5... | collective-permute-start | bytes 884744 | tf_op jit(solution)/shard_map/ppermute | solution.py:362
  13.0 9.0 %collective-permute-start.6 = (bf16[2,192,384]{2,1,0:T(8,128)(2,1)S(1)}, bf16[2,192,384]{2,1,0:T(8,128)(2,1)S(1)}, u32[]{:S(2)}, u32[]{:S(2)}) collective-permute-start(bf16[2,192,384]{2,1,0:T(8,128)(2,1)S(1)} %collective-permute-done.4.near.refs_4_), channel_id=1, source_target_pairs={{0,8},{4,20},{8,0},{12,28},{16,24},{20,4},{24,16},{28,12},{1,9},{5... | collective-permute-start | bytes 884744 | tf_op jit(solution)/shard_map/ppermute | solution.py:362
  14.5 5.3 %slice-start.1 = ((s8[6291456]{0:T(1024)(128)(4,1)}), s8[2097152]{0:T(1024)(128)(4,1)S(1)}, s32[]{:S(2)}) async-start(s8[6291456]{0:T(1024)(128)(4,1)} %bitcast.10), calls=%async_computation.1 | async-start | bytes 4194304
  18.3 6.7 %collective-permute-start.5 = (bf16[2,192,384]{2,1,0:T(8,128)(2,1)S(1)}, bf16[2,192,384]{2,1,0:T(8,128)(2,1)S(1)}, u32[]{:S(2)}, u32[]{:S(2)}) collective-permute-start(bf16[2,192,384]{2,1,0:T(8,128)(2,1)S(1)} %collective-permute-done.3.own.refs_1_), channel_id=1, source_target_pairs={{0,16},{4,12},{8,24},{12,4},{16,0},{20,28},{24,8},{28,20},{1,17},{... | collective-permute-start | bytes 884744 | tf_op jit(solution)/shard_map/ppermute | solution.py:362
  19.8 5.2 %collective-permute-start.9 = (bf16[2,192,384]{2,1,0:T(8,128)(2,1)S(1)}, bf16[2,192,384]{2,1,0:T(8,128)(2,1)S(1)}, u32[]{:S(2)}, u32[]{:S(2)}) collective-permute-start(bf16[2,192,384]{2,1,0:T(8,128)(2,1)S(1)} %collective-permute-done.3.own.refs_1_), channel_id=1, source_target_pairs={{0,4},{4,0},{8,12},{12,8},{16,20},{20,16},{24,28},{28,24},{1,5},{5... | collective-permute-start | bytes 884744 | tf_op jit(solution)/shard_map/ppermute | solution.py:362
  22.0 2.9 %collective-permute-start.8 = (bf16[2,192,384]{2,1,0:T(8,128)(2,1)S(1)}, bf16[2,192,384]{2,1,0:T(8,128)(2,1)S(1)}, u32[]{:S(2)}, u32[]{:S(2)}) collective-permute-start(bf16[2,192,384]{2,1,0:T(8,128)(2,1)S(1)} %collective-permute-done.6.sib.refs_5_), channel_id=1, source_target_pairs={{0,4},{4,0},{8,12},{12,8},{16,20},{20,16},{24,28},{28,24},{1,5},{5... | collective-permute-start | bytes 884744 | tf_op jit(solution)/shard_map/ppermute | solution.py:362
  25.0 1.6 %collective-permute-start.7 = (bf16[2,192,384]{2,1,0:T(8,128)(2,1)S(1)}, bf16[2,192,384]{2,1,0:T(8,128)(2,1)S(1)}, u32[]{:S(2)}, u32[]{:S(2)}) collective-permute-start(bf16[2,192,384]{2,1,0:T(8,128)(2,1)S(1)} %collective-permute-done.5.own.refs_3_), channel_id=1, source_target_pairs={{0,4},{4,0},{8,12},{12,8},{16,20},{20,16},{24,28},{28,24},{1,5},{5... | collective-permute-start | bytes 884744 | tf_op jit(solution)/shard_map/ppermute | solution.py:362
  28.9 1.4 %collective-permute-start.10 = (bf16[192,384]{1,0:T(8,128)(2,1)S(1)}, bf16[192,384]{1,0:T(8,128)(2,1)S(1)}, u32[]{:S(2)}, u32[]{:S(2)}) collective-permute-start(bf16[192,384]{1,0:T(8,128)(2,1)S(1)} %get-tuple-element.97), channel_id=1, source_target_pairs={{0,4},{4,0},{8,12},{12,8},{16,20},{20,16},{24,28},{28,24},{1,5},{5... | collective-permute-start | bytes 442376 | tf_op jit(solution)/shard_map/ppermute | solution.py:362
  30.0 3.8 %collective-permute-start.14 = (bf16[192,384]{1,0:T(8,128)(2,1)S(1)}, bf16[192,384]{1,0:T(8,128)(2,1)S(1)}, u32[]{:S(2)}, u32[]{:S(2)}) collective-permute-start(bf16[192,384]{1,0:T(8,128)(2,1)S(1)} %get-tuple-element.114), channel_id=1, source_target_pairs={{0,4},{4,0},{8,12},{12,8},{16,20},{20,16},{24,28},{28,24},{1,5},{5... | collective-permute-start | bytes 442376 | tf_op jit(solution)/shard_map/ppermute | solution.py:362
  30.4 8.5 %collective-permute-start.13 = (bf16[192,384]{1,0:T(8,128)(2,1)S(1)}, bf16[192,384]{1,0:T(8,128)(2,1)S(1)}, u32[]{:S(2)}, u32[]{:S(2)}) collective-permute-start(bf16[192,384]{1,0:T(8,128)(2,1)S(1)} %convert_add_fusion.2), channel_id=1, source_target_pairs={{0,24},{4,28},{8,16},{12,20},{16,8},{20,12},{24,0},{28,4},{1,25},{... | collective-permute-start | bytes 442376 | tf_op jit(solution)/shard_map/ppermute | solution.py:362
  33.7 1.4 %collective-permute-start.11 = (bf16[192,384]{1,0:T(8,128)(2,1)S(1)}, bf16[192,384]{1,0:T(8,128)(2,1)S(1)}, u32[]{:S(2)}, u32[]{:S(2)}) collective-permute-start(bf16[192,384]{1,0:T(8,128)(2,1)S(1)} %get-tuple-element.103), channel_id=1, source_target_pairs={{0,4},{4,0},{8,12},{12,8},{16,20},{20,16},{24,28},{28,24},{1,5},{5... | collective-permute-start | bytes 442376 | tf_op jit(solution)/shard_map/ppermute | solution.py:362
  33.8 7.2 %collective-permute-start.15 = (bf16[192,384]{1,0:T(8,128)(2,1)S(1)}, bf16[192,384]{1,0:T(8,128)(2,1)S(1)}, u32[]{:S(2)}, u32[]{:S(2)}) collective-permute-start(bf16[192,384]{1,0:T(8,128)(2,1)S(1)} %add_convert_fusion), channel_id=1, source_target_pairs={{0,8},{4,12},{8,0},{12,4},{16,24},{20,28},{24,16},{28,20},{1,9},{5... | collective-permute-start | bytes 442376 | tf_op jit(solution)/shard_map/ppermute | solution.py:362
  35.2 6.0 %collective-permute-start.16 = (bf16[192,384]{1,0:T(8,128)(2,1)S(1)}, bf16[192,384]{1,0:T(8,128)(2,1)S(1)}, u32[]{:S(2)}, u32[]{:S(2)}) collective-permute-start(bf16[192,384]{1,0:T(8,128)(2,1)S(1)} %convert_add_fusion.1), channel_id=1, source_target_pairs={{0,16},{4,20},{8,24},{12,28},{16,0},{20,4},{24,8},{28,12},{1,17},{... | collective-permute-start | bytes 442376 | tf_op jit(solution)/shard_map/ppermute | solution.py:362
  36.6 4.6 %collective-permute-start.12 = (bf16[192,384]{1,0:T(8,128)(2,1)S(1)}, bf16[192,384]{1,0:T(8,128)(2,1)S(1)}, u32[]{:S(2)}, u32[]{:S(2)}) collective-permute-start(bf16[192,384]{1,0:T(8,128)(2,1)S(1)} %get-tuple-element.109), channel_id=1, source_target_pairs={{0,4},{4,0},{8,12},{12,8},{16,20},{20,16},{24,28},{28,24},{1,5},{5... | collective-permute-start | bytes 442376 | tf_op jit(solution)/shard_map/ppermute | solution.py:362
  41.3 10.9 %collective-permute-start.17 = (bf16[48,384]{1,0:T(8,128)(2,1)S(1)}, bf16[48,384]{1,0:T(8,128)(2,1)S(1)}, u32[]{:S(2)}, u32[]{:S(2)}) collective-permute-start(bf16[48,384]{1,0:T(8,128)(2,1)S(1)} %get-tuple-element.124), channel_id=1, source_target_pairs={{0,3},{1,0},{2,1},{3,2},{4,7},{5,4},{6,5},{7,6},{8,11},{9,8},{10,9... | collective-permute-start | bytes 110600 | tf_op jit(solution)/shard_map/ppermute | solution.py:366
  41.5 10.7 %collective-permute-start.19 = (bf16[48,384]{1,0:T(8,128)(2,1)S(1)}, bf16[48,384]{1,0:T(8,128)(2,1)S(1)}, u32[]{:S(2)}, u32[]{:S(2)}) collective-permute-start(bf16[48,384]{1,0:T(8,128)(2,1)S(1)} %get-tuple-element.125), channel_id=1, source_target_pairs={{0,1},{1,2},{2,3},{3,0},{4,5},{5,6},{6,7},{7,4},{8,9},{9,10},{10,1... | collective-permute-start | bytes 110600 | tf_op jit(solution)/shard_map/ppermute | solution.py:366
  43.4 8.9 %collective-permute-start.18 = (bf16[48,384]{1,0:T(8,128)(2,1)S(1)}, bf16[48,384]{1,0:T(8,128)(2,1)S(1)}, u32[]{:S(2)}, u32[]{:S(2)}) collective-permute-start(bf16[48,384]{1,0:T(8,128)(2,1)S(1)} %get-tuple-element.126), channel_id=1, source_target_pairs={{0,2},{1,3},{2,0},{3,1},{4,6},{5,7},{6,4},{7,5},{8,10},{9,11},{10,... | collective-permute-start | bytes 110600 | tf_op jit(solution)/shard_map/ppermute | solution.py:366

commit v9 on v8

--- a/solution.py
+++ b/solution.py
@@ -188,32 +188,53 @@
     )(place, own, near, wd)
 
 
-def partial_kernel(place, own, sib, wg, wu, wd, *refs):
+def half_at(place, i, core, half, wg, wu, turned):
+    x, g = half[0], half[1]
+    width = x.shape[1]
+    rows = (place[0] // 2 ^ far(place)[i]) * 2 * width + core * width
+    rows = pl.ds(pl.multiple_of(rows, width), width)
+    down = pl.ds(pl.multiple_of(core * width, width), width)
+
+    def terms(cols):
+        return dot(x, wg[rows, cols], 1, 0), dot(x, wu[rows, cols], 1, 0), dot(g, turned[i - 2, down, cols], 1, 0)
+
+    return terms
+
+
+def add_halves(halves, count, acc_in, finish, acc_out):
+    for f in range(count // STEP):
+        cols = pl.ds(f * STEP, STEP)
+        sums = [acc[:, cols] for acc in acc_in]
+        for terms in halves:
+            sums = [s + t for s, t in zip(sums, terms(cols))]
+        finish(cols, sums, acc_out)
+
+
+def partial_kernel(place, own, sib, other, wg, wu, wd, turned, *refs):
     add_pieces([pair(place, 1, own, sib)], (wg, wu, wd), refs[:3], refs[3:], store)
-
-
-def partial_sums(place, own, sib, weights, acc):
+    terms = half_at(place, 2, 1 - place[0] % 2, other, wg, wu, turned)
+    add_halves([terms], wg.shape[1], refs[3:], store, refs[3:])
+
+
+def partial_sums(place, own, sib, other, weights, turned, acc):
     return call(
         partial_kernel,
         (shape(acc[0].shape, F32),) * 3,
-        [SMEM] + [VMEM] * 8,
+        [SMEM] + [VMEM] * 10,
         [VMEM] * 3,
         1,
         1,
-        aliases={6: 0, 7: 1, 8: 2},
-    )(place, own, sib, *weights, *acc)
-
-
-def third_kernel(place, own, sib, wg, wu, wd, gate_in, up_in, back_in, gate, up, back):
-    rows, x, g = pair(place, 2, own, sib)
-    for f in range(wg.shape[1] // STEP):
-        cols = pl.ds(f * STEP, STEP)
-        gate[:, cols] = gate_in[:, cols] + dot(x, wg[rows, cols], 1, 0)
-        up[:, cols] = up_in[:, cols] + dot(x, wu[rows, cols], 1, 0)
-        back[:, cols] = back_in[:, cols] + dot(g, wd[0, :, cols], 1, 0)
-
-
-def third_sums(place, own, sib, weights, acc):
+        aliases={8: 0, 9: 1, 10: 2},
+    )(place, own, sib, other, *weights, turned, *acc)
+
+
+def third_kernel(place, rest, diag, wg, wu, turned, *refs):
+    core = place[0] % 2
+    halves = [half_at(place, i, core, half, wg, wu, turned) for i, half in ((2, rest), (3, diag))]
+    add_halves(halves, wg.shape[1], refs[:3], store, refs[3:])
+
+
+def third_sums(place, rest, diag, weights, acc):
     return call(
         third_kernel,
         (shape(acc[0].shape, F32),) * 3,
@@ -222,7 +243,7 @@
         1,
         1,
         aliases={6: 0, 7: 1, 8: 2},
-    )(place, own, sib, *weights, *acc)
+    )(place, rest, diag, *weights, *acc)
 
 
 def write_slots(place, p, dg, du, wg, wu, keep, send):
@@ -234,30 +255,23 @@
     send[...] = jnp.where(first, high, low).astype(BF16)
 
 
-def middle_kernel(place, own, sib, wg, wu, wd, wg_turned, wu_turned, gate, up, back, hid, dg, du, keep, send):
-    rows, x, g = pair(place, 3, own, sib)
-    for f in range(wd.shape[2] // STEP):
-        cols = pl.ds(f * STEP, STEP)
-        sums = (
-            gate[:, cols] + dot(x, wg[rows, cols], 1, 0),
-            up[:, cols] + dot(x, wu[rows, cols], 1, 0),
-            back[:, cols] + dot(g, wd[1, :, cols], 1, 0),
-        )
-        store_grads(cols, sums, (hid, dg, du))
+def middle_kernel(place, sib, wg, wu, turned, wg_turned, wu_turned, gate, up, back, hid, dg, du, keep, send):
+    terms = half_at(place, 3, 1 - place[0] % 2, sib, wg, wu, turned)
+    add_halves([terms], wg.shape[1], (gate, up, back), store_grads, (hid, dg, du))
     write_slots(place, 3, dg, du, wg_turned, wu_turned, keep, send)
 
 
-def middle(place, own, sib, weights, turned, acc):
-    rows, width = own.shape[1:]
+def middle(place, sib, weights, turned, acc):
+    rows, width = sib.shape[1:]
     hidden_count = turned[0].shape[1]
     return call(
         middle_kernel,
         (shape((rows, hidden_count), BF16),) * 3 + (shape((rows, width), F32), shape((rows, width), BF16)),
-        [SMEM] + [VMEM] * 10,
+        [SMEM] + [VMEM] * 9,
         [VMEM] * 5,
         20 * rows * width * hidden_count,
         0,
-    )(place, own, sib, *weights, *turned, *acc)
+    )(place, sib, *weights, *turned, *acc)
 
 
 def slot_kernel(p, place, *refs):
@@ -387,12 +401,12 @@
     second, back = lax.optimization_barrier((here[1], back))
     there_first = across(second, 1)
     weights, acc = (wg, wu, wd), (gate, up, back)
-    acc = partial_sums(place, first, second, weights, acc)
+    acc = partial_sums(place, first, second, there_second, weights, wd_turned, acc)
     turned = wg_turned, wu_turned
     diag, acc = lax.optimization_barrier((diag, acc))
     diag_near = across(diag, 1)
-    acc = third_sums(place, there_first, there_second, (wg, wu, wd_turned), acc)
-    hid, dg, du, keep, send = middle(place, diag, diag_near, (wg, wu, wd_turned), turned, acc)
+    acc = third_sums(place, there_first, diag, (wg, wu, wd_turned), acc)
+    hid, dg, du, keep, send = middle(place, diag_near, (wg, wu, wd_turned), turned, acc)
     mine_of = own, first, there_first, diag
     other_of = near, second, there_second, diag_near
 

time: 53.1 us -> 52.8 us (level)
  waiting for transfers between devices: 5.49 us -> 4.55 us
    ppermute x14, waiting for transfers between devices: 3.86 us -> 2.92 us  [across(): lax.ppermute(array, 'tensor', [(i, i ^ masks[i % 2]) for i in range(8)])]
    pallas_call x1, Pallas kernels: 1.43 us -> 2.06 us  [partial_sums(): call(partial_kernel, (shape(acc[0].shape, F32),) * 3, [SMEM] + [VMEM] * 1...]
  transfers between devices with their start and end apart: 20 -> 20, of which waited for: 8 -> 8; matrix products, arithmetic and copies ran while one was open for 0% -> 0% of each run, Pallas kernels for 43% -> 45%
where the time goes in v9:
time: 52.8 us; the launch traced here: 52.6 us
  Pallas kernels  26.5 us (50%)
  starting transfers between devices  19.7 us (37%)
  waiting for transfers between devices  4.55 us (9%)
  between operations  0.93 us (2%)
  other arithmetic  0.83 us (2%)
    ppermute x6, starting transfers between devices, along(): lax.ppermute(array, 'expert', [(i, (i + distance) % count) for i in range...  10.5 us
    pallas_call x3, Pallas kernels, weight_grads(): call(functools.partial(weight_kernel, jobs, len(more)), tuple((shape(out,...  9.57 us
    ppermute x14, starting transfers between devices, across(): lax.ppermute(array, 'tensor', [(i, i ^ masks[i % 2]) for i in range(8)])  9.25 us
    pallas_call x1, Pallas kernels, load_up(): call(load_up_kernel, (shape(wu.shape, BF16),) + (shape((rows, hidden_coun...  3.63 us
    pallas_call x1, Pallas kernels, load_gate(): call(load_gate_kernel, (shape(wg.shape, BF16), shape((4, hidden_count, fu...  3.33 us
    ppermute x14, waiting for transfers between devices, across(): lax.ppermute(array, 'tensor', [(i, i ^ masks[i % 2]) for i in range(8)])  2.92 us
    pallas_call x3, Pallas kernels, slots(): call(functools.partial(slot_kernel, p), (shape((rows, width), F32), shape...  2.4 us
    pallas_call x1, Pallas kernels, partial_sums(): call(partial_kernel, (shape(acc[0].shape, F32),) * 3, [SMEM] + [VMEM] * 1...  2.06 us
  transfers between devices with their start and end apart: 20, of which 8 were waited for; matrix products, arithmetic and copies ran while one was open for 0% of the time, Pallas kernels for 45%

profile of v9, /device:TPU:8, one launch (start us, length us, event | category | flops | bytes accessed | tf_op | source)
XLA Modules:
  0.0 52.6 jit_solution(14103694288182822498)
XLA Ops:
  0.6 1.0 %shard_map.102 = (bf16[2,48,384]{2,1,0:T(8,128)(2,1)S(1)}, bf16[2,48,384]{2,1,0:T(8,128)(2,1)S(1)}, bf16[2,48,384]{2,1,0:T(8,128)(2,1)S(1)}, bf16[2,48,384]{2,1,0:T(8,128)(2,1)S(1)}) custom-call(s32[1]{0:T(128)} %bitcast.1.place, bf16[48,384]{1,0:T(8,128)(2,1)} %refs_0_.1, bf16[48,384]{1,0:T(8,128)(2,1)} %refs_1_.1, s32[2,48]{1,0:T(2,128)} %bitcast.17, ...), custom_call_target="tpu_custom_call" | custom-call | flops 1 | bytes 1 | tf_op jit(solution)/shard_map/pallas_call | solution.py:362
  1.7 1.6 %collective-permute-start = (bf16[2,48,384]{2,1,0:T(8,128)(2,1)S(1)}, bf16[2,48,384]{2,1,0:T(8,128)(2,1)S(1)}, u32[]{:S(2)}, u32[]{:S(2)}) collective-permute-start(bf16[2,48,384]{2,1,0:T(8,128)(2,1)S(1)} %get-tuple-element.65), channel_id=1, source_target_pairs={{0,1},{1,2},{2,3},{3,0},{4,5},{5,6},{6,7},{7,4},{8,9},{9,10},{10,1... | collective-permute-start | bytes 221192 | tf_op jit(solution)/shard_map/ppermute | solution.py:380
  3.3 1.1 %collective-permute-start.1 = (bf16[2,48,384]{2,1,0:T(8,128)(2,1)S(1)}, bf16[2,48,384]{2,1,0:T(8,128)(2,1)S(1)}, u32[]{:S(2)}, u32[]{:S(2)}) collective-permute-start(bf16[2,48,384]{2,1,0:T(8,128)(2,1)S(1)} %get-tuple-element.66), channel_id=1, source_target_pairs={{0,2},{1,3},{2,0},{3,1},{4,6},{5,7},{6,4},{7,5},{8,10},{9,11},{10,... | collective-permute-start | bytes 221192 | tf_op jit(solution)/shard_map/ppermute | solution.py:380
  4.4 1.9 %collective-permute-start.2 = (bf16[2,48,384]{2,1,0:T(8,128)(2,1)S(1)}, bf16[2,48,384]{2,1,0:T(8,128)(2,1)S(1)}, u32[]{:S(2)}, u32[]{:S(2)}) collective-permute-start(bf16[2,48,384]{2,1,0:T(8,128)(2,1)S(1)} %get-tuple-element.67), channel_id=1, source_target_pairs={{0,3},{1,0},{2,1},{3,2},{4,7},{5,4},{6,5},{7,6},{8,11},{9,8},{10,9... | collective-permute-start | bytes 221192 | tf_op jit(solution)/shard_map/ppermute | solution.py:380
  6.3 3.3 %shard_map.103 = (bf16[3072,1024]{1,0:T(8,128)(2,1)S(1)}, bf16[4,1024,768]{2,1,0:T(8,128)(2,1)S(1)}) custom-call(s32[1]{0:T(128)} %bitcast.place, bf16[3072,1024]{1,0:T(8,128)(2,1)} %bitcast.15), custom_call_target="tpu_custom_call" | custom-call | flops 1 | bytes 1 | tf_op jit(solution)/shard_map/pallas_call | solution.py:122
  9.7 0.2 collective-permute-done.1
  9.9 1.5 %collective-permute-done.2 = bf16[2,48,384]{2,1,0:T(8,128)(2,1)S(1)} collective-permute-done((bf16[2,48,384]{2,1,0:T(8,128)(2,1)S(1)}, bf16[2,48,384]{2,1,0:T(8,128)(2,1)S(1)}, u32[]{:S(2)}, u32[]{:S(2)}) %collective-permute-start.2) | collective-permute-done | bytes 73760 | tf_op jit(solution)/shard_map/ppermute | solution.py:380
  11.5 1.6 %collective-permute-start.3 = (bf16[2,192,384]{2,1,0:T(8,128)(2,1)S(1)}, bf16[2,192,384]{2,1,0:T(8,128)(2,1)S(1)}, u32[]{:S(2)}, u32[]{:S(2)}) collective-permute-start(bf16[2,192,384]{2,1,0:T(8,128)(2,1)S(1)} %constant_dynamic-update-slice_fusion.own.refs_0_), channel_id=1, source_target_pairs={{0,8},{4,20},{8,0},{12,28},{16,24},{20,4},{24,16},{28,12},{1,9},{5... | collective-permute-start | bytes 884744 | tf_op jit(solution)/shard_map/ppermute | solution.py:376
  13.0 1.5 %collective-permute-start.6 = (bf16[2,192,384]{2,1,0:T(8,128)(2,1)S(1)}, bf16[2,192,384]{2,1,0:T(8,128)(2,1)S(1)}, u32[]{:S(2)}, u32[]{:S(2)}) collective-permute-start(bf16[2,192,384]{2,1,0:T(8,128)(2,1)S(1)} %collective-permute-done.4.near.refs_4_), channel_id=1, source_target_pairs={{0,8},{4,20},{8,0},{12,28},{16,24},{20,4},{24,16},{28,12},{1,9},{5... | collective-permute-start | bytes 884744 | tf_op jit(solution)/shard_map/ppermute | solution.py:376
  14.5 3.6 %shard_map.104 = (bf16[3072,1024]{1,0:T(8,128)(2,1)S(1)}, f32[192,1024]{1,0:T(8,128)S(1)}, f32[192,1024]{1,0:T(8,128)S(1)}, bf16[4,1024,768]{2,1,0:T(8,128)(2,1)S(1)}) custom-call(s32[1]{0:T(128)} %bitcast.place, bf16[2,192,384]{2,1,0:T(8,128)(2,1)S(1)} %constant_dynamic-update-slice_fusion.own.refs_0_, ...), custom_call_target="tpu_custom_call" | custom-call | flops 1 | bytes 1 | tf_op jit(solution)/shard_map/pallas_call | solution.py:156
  18.3 1.6 %collective-permute-start.5 = (bf16[2,192,384]{2,1,0:T(8,128)(2,1)S(1)}, bf16[2,192,384]{2,1,0:T(8,128)(2,1)S(1)}, u32[]{:S(2)}, u32[]{:S(2)}) collective-permute-start(bf16[2,192,384]{2,1,0:T(8,128)(2,1)S(1)} %collective-permute-done.3.own.refs_1_), channel_id=1, source_target_pairs={{0,16},{4,12},{8,24},{12,4},{16,0},{20,28},{24,8},{28,20},{1,17},{... | collective-permute-start | bytes 884744 | tf_op jit(solution)/shard_map/ppermute | solution.py:376
  19.8 1.1 %shard_map.105 = (f32[192,1024]{1,0:T(8,128)S(1)}, bf16[2,768,1024]{2,1,0:T(8,128)(2,1)S(1)}) custom-call(s32[1]{0:T(128)} %bitcast.place, bf16[2,192,384]{2,1,0:T(8,128)(2,1)S(1)} %constant_dynamic-update-slice_fusion.own.refs_0_, bf16[2,192,384]{2,1,0:T(8,128)(2,1)S(1)} %collective-permute-done.4.near.refs_4_, bf16[1024,3072]{1,0:T(8,128)(2,1)S(1)} %bitcast.12), custom_call_target="tpu_custom_call" | custom-call | flops 1 | bytes 1 | tf_op jit(solution)/shard_map/pallas_call | solution.py:181
  20.9 0.5 collective-permute-done.6.sib.refs_5_
  21.4 2.1 %shard_map.106 = (f32[192,1024]{1,0:T(8,128)S(1)}, f32[192,1024]{1,0:T(8,128)S(1)}, f32[192,1024]{1,0:T(8,128)S(1)}) custom-call(s32[1]{0:T(128)} %bitcast.place, bf16[2,192,384]{2,1,0:T(8,128)(2,1)S(1)} %collective-permute-done.3.own.refs_1_, ...), custom_call_target="tpu_custom_call", output_to_operand_aliasing={{0}: (8, {}), {1}: (9, {}), {2}: (10, {})} | custom-call | flops 1 | bytes 1 | tf_op jit(solution)/shard_map/pallas_call | solution.py:220
  23.5 1.5 %collective-permute-done.5.diag.refs_3_ = bf16[2,192,384]{2,1,0:T(8,128)(2,1)S(1)} collective-permute-done((bf16[2,192,384]{2,1,0:T(8,128)(2,1)S(1)}, bf16[2,192,384]{2,1,0:T(8,128)(2,1)S(1)}, u32[]{:S(2)}, u32[]{:S(2)}) %collective-permute-start.5) | collective-permute-done | bytes 294944 | tf_op jit(solution)/shard_map/ppermute | solution.py:376
  25.1 1.5 %shard_map.107 = (f32[192,1024]{1,0:T(8,128)S(1)}, f32[192,1024]{1,0:T(8,128)S(1)}, f32[192,1024]{1,0:T(8,128)S(1)}) custom-call(s32[1]{0:T(128)} %bitcast.place, bf16[2,192,384]{2,1,0:T(8,128)(2,1)S(1)} %collective-permute-done.9.rest.refs_2_, ...), custom_call_target="tpu_custom_call", output_to_operand_aliasing={{0}: (6, {}), {1}: (7, {}), {2}: (8, {})} | custom-call | flops 1 | bytes 1 | tf_op jit(solution)/shard_map/pallas_call | solution.py:238
  26.6 1.9 %shard_map.108 = (bf16[192,1024]{1,0:T(8,128)(2,1)S(1)}, bf16[192,1024]{1,0:T(8,128)(2,1)S(1)}, bf16[192,1024]{1,0:T(8,128)(2,1)S(1)}, f32[192,384]{1,0:T(8,128)S(1)}, bf16[192,384]{1,0:T(8,128)(2,1)S(1)}) custom-call(s32[1]{0:T(128)} %bitcast.place, bf16[2,192,384]{2,1,0:T(8,128)(2,1)S(1)} %collective-permute-done.8.sib.refs_7_, ...), custom_call_target="tpu_custom_call" | custom-call | flops 1509949440 | tf_op jit(solution)/shard_map/pallas_call | solution.py:267
  28.5 0.5 collective-permute-start.10
  29.1 0.8 %shard_map.112 = (f32[192,384]{1,0:T(8,128)S(1)}, bf16[192,384]{1,0:T(8,128)(2,1)S(1)}) custom-call(s32[1]{0:T(128)} %bitcast.place, bf16[192,1024]{1,0:T(8,128)(2,1)S(1)} %get-tuple-element.117.refs_0_.refs_8_, bf16[192,1024]{1,0:T(8,128)(2,1)S(1)} %get-tuple-element.105.refs_1_.refs_8_, bf16[4,1024,768]{2,1,0:T(8,128)(2,1)S(1)} %get-tuple-element.88.wg_turned.refs_2_, ...), custom_call_target="tpu_custom_call" | custom-call | flops 603979776 | tf_op jit(solution)/shard_map/pallas_call | solution.py:284
  30.1 2.5 %collective-permute-start.13 = (bf16[192,384]{1,0:T(8,128)(2,1)S(1)}, bf16[192,384]{1,0:T(8,128)(2,1)S(1)}, u32[]{:S(2)}, u32[]{:S(2)}) collective-permute-start(bf16[192,384]{1,0:T(8,128)(2,1)S(1)} %convert_add_fusion.2), channel_id=1, source_target_pairs={{0,24},{4,28},{8,16},{12,20},{16,8},{20,12},{24,0},{28,4},{1,25},{... | collective-permute-start | bytes 442376 | tf_op jit(solution)/shard_map/ppermute | solution.py:376
  32.6 0.8 %shard_map.109 = (f32[192,384]{1,0:T(8,128)S(1)}, bf16[192,384]{1,0:T(8,128)(2,1)S(1)}) custom-call(s32[1]{0:T(128)} %bitcast.place, bf16[192,1024]{1,0:T(8,128)(2,1)S(1)} %get-tuple-element.117.refs_0_.refs_8_, bf16[192,1024]{1,0:T(8,128)(2,1)S(1)} %get-tuple-element.105.refs_1_.refs_8_, bf16[4,1024,768]{2,1,0:T(8,128)(2,1)S(1)} %get-tuple-element.88.wg_turned.refs_2_, ...), custom_call_target="tpu_custom_call" | custom-call | flops 603979776 | tf_op jit(solution)/shard_map/pallas_call | solution.py:284
  33.5 0.7 %collective-permute-start.15 = (bf16[192,384]{1,0:T(8,128)(2,1)S(1)}, bf16[192,384]{1,0:T(8,128)(2,1)S(1)}, u32[]{:S(2)}, u32[]{:S(2)}) collective-permute-start(bf16[192,384]{1,0:T(8,128)(2,1)S(1)} %add_convert_fusion), channel_id=1, source_target_pairs={{0,8},{4,12},{8,0},{12,4},{16,24},{20,28},{24,16},{28,20},{1,9},{5... | collective-permute-start | bytes 442376 | tf_op jit(solution)/shard_map/ppermute | solution.py:376
  34.2 0.6 %collective-permute-done.11 = bf16[192,384]{1,0:T(8,128)(2,1)S(1)} collective-permute-done((bf16[192,384]{1,0:T(8,128)(2,1)S(1)}, bf16[192,384]{1,0:T(8,128)(2,1)S(1)}, u32[]{:S(2)}, u32[]{:S(2)}) %collective-permute-start.11) | collective-permute-done | bytes 147488 | tf_op jit(solution)/shard_map/ppermute | solution.py:376
  34.9 0.6 %collective-permute-start.16 = (bf16[192,384]{1,0:T(8,128)(2,1)S(1)}, bf16[192,384]{1,0:T(8,128)(2,1)S(1)}, u32[]{:S(2)}, u32[]{:S(2)}) collective-permute-start(bf16[192,384]{1,0:T(8,128)(2,1)S(1)} %convert_add_fusion.1), channel_id=1, source_target_pairs={{0,16},{4,20},{8,24},{12,28},{16,0},{20,4},{24,8},{28,12},{1,17},{... | collective-permute-start | bytes 442376 | tf_op jit(solution)/shard_map/ppermute | solution.py:376
  35.4 0.8 %shard_map.110 = (f32[192,384]{1,0:T(8,128)S(1)}, bf16[192,384]{1,0:T(8,128)(2,1)S(1)}) custom-call(s32[1]{0:T(128)} %bitcast.place, bf16[192,1024]{1,0:T(8,128)(2,1)S(1)} %get-tuple-element.117.refs_0_.refs_8_, bf16[192,1024]{1,0:T(8,128)(2,1)S(1)} %get-tuple-element.105.refs_1_.refs_8_, bf16[4,1024,768]{2,1,0:T(8,128)(2,1)S(1)} %get-tuple-element.88.wg_turned.refs_2_, ...), custom_call_target="tpu_custom_call" | custom-call | flops 603979776 | tf_op jit(solution)/shard_map/pallas_call | solution.py:284
  36.3 2.3 %shard_map.111.refs_9_ = bf16[3072,1024]{1,0:T(8,128)(2,1)} custom-call(s32[1]{0:T(128)} %bitcast.place, bf16[2,192,384]{2,1,0:T(8,128)(2,1)S(1)} %constant_dynamic-update-slice_fusion.own.refs_0_, bf16[2,192,384]{2,1,0:T(8,128)(2,1)S(1)} %collective-permute-done.3.own.refs_1_, bf16[2,192,384]{2,1,0:T(8,128)(2,1)S(1)} %copy-done.3, ...), custom_call_target="tpu_custom_call" | custom-call | flops 603979776 | bytes 3145728 | tf_op jit(solution)/shard_map/pallas_call | solution.py:330
  38.7 2.1 %shard_map.113 = bf16[3072,1024]{1,0:T(8,128)(2,1)} custom-call(s32[1]{0:T(128)} %bitcast.place, bf16[2,192,384]{2,1,0:T(8,128)(2,1)S(1)} %constant_dynamic-update-slice_fusion.own.refs_0_, bf16[2,192,384]{2,1,0:T(8,128)(2,1)S(1)} %collective-permute-done.3.own.refs_1_, bf16[2,192,384]{2,1,0:T(8,128)(2,1)S(1)} %copy-done.3, ...), custom_call_target="tpu_custom_call", output_to_operand_aliasing={{}: (10, {})} | custom-call | flops 603979776 | bytes 3145728 | tf_op jit(solution)/shard_map/pallas_call | solution.py:330
  41.0 0.2 collective-permute-start.17
  41.3 1.8 %collective-permute-start.19 = (bf16[48,384]{1,0:T(8,128)(2,1)S(1)}, bf16[48,384]{1,0:T(8,128)(2,1)S(1)}, u32[]{:S(2)}, u32[]{:S(2)}) collective-permute-start(bf16[48,384]{1,0:T(8,128)(2,1)S(1)} %get-tuple-element.125), channel_id=1, source_target_pairs={{0,1},{1,2},{2,3},{3,0},{4,5},{5,6},{6,7},{7,4},{8,9},{9,10},{10,1... | collective-permute-start | bytes 110600 | tf_op jit(solution)/shard_map/ppermute | solution.py:380
  43.1 3.7 %collective-permute-start.18 = (bf16[48,384]{1,0:T(8,128)(2,1)S(1)}, bf16[48,384]{1,0:T(8,128)(2,1)S(1)}, u32[]{:S(2)}, u32[]{:S(2)}) collective-permute-start(bf16[48,384]{1,0:T(8,128)(2,1)S(1)} %get-tuple-element.126), channel_id=1, source_target_pairs={{0,2},{1,3},{2,0},{3,1},{4,6},{5,7},{6,4},{7,5},{8,10},{9,11},{10,... | collective-permute-start | bytes 110600 | tf_op jit(solution)/shard_map/ppermute | solution.py:380
  46.8 5.1 %shard_map.114 = (bf16[3072,1024]{1,0:T(8,128)(2,1)}, bf16[1024,3072]{1,0:T(8,128)(2,1)}) custom-call(s32[1]{0:T(128)} %bitcast.place, bf16[2,192,384]{2,1,0:T(8,128)(2,1)S(1)} %constant_dynamic-update-slice_fusion.own.refs_0_, bf16[2,192,384]{2,1,0:T(8,128)(2,1)S(1)} %collective-permute-done.3.own.refs_1_, bf16[2,192,384]{2,1,0:T(8,128)(2,1)S(1)} %copy-done.3, ...), custom_call_target="tpu_custom_call" | custom-call | flops 2415919104 | bytes 12582912 | tf_op jit(solution)/shard_map/pallas_call | solution.py:330
  52.0 0.6 %add_convert_fusion.1 = bf16[48,384]{1,0:T(8,128)(2,1)} fusion(bf16[48,384]{1,0:T(8,128)(2,1)S(1)} %collective-permute-done.19, bf16[48,384]{1,0:T(8,128)(2,1)S(1)} %collective-permute-done.18, bf16[48,384]{1,0:T(8,128)(2,1)S(1)} %collective-permute-done.17, f32[192,384]{1,0:T(8,128)S(1)} %convert_add_fusion), kind=kLoop, calls=%fused_computation.4 | loop fusion | flops 129024 | bytes 221184 | tf_op jit(solution)/shard_map/convert_element_type | solution.py:439
  (45 shorter events, 1.0 us)
Async XLA Ops:
  1.7 8.0 %collective-permute-start = (bf16[2,48,384]{2,1,0:T(8,128)(2,1)S(1)}, bf16[2,48,384]{2,1,0:T(8,128)(2,1)S(1)}, u32[]{:S(2)}, u32[]{:S(2)}) collective-permute-start(bf16[2,48,384]{2,1,0:T(8,128)(2,1)S(1)} %get-tuple-element.65), channel_id=1, source_target_pairs={{0,1},{1,2},{2,3},{3,0},{4,5},{5,6},{6,7},{7,4},{8,9},{9,10},{10,1... | collective-permute-start | bytes 221192 | tf_op jit(solution)/shard_map/ppermute | solution.py:380
  3.3 6.6 %collective-permute-start.1 = (bf16[2,48,384]{2,1,0:T(8,128)(2,1)S(1)}, bf16[2,48,384]{2,1,0:T(8,128)(2,1)S(1)}, u32[]{:S(2)}, u32[]{:S(2)}) collective-permute-start(bf16[2,48,384]{2,1,0:T(8,128)(2,1)S(1)} %get-tuple-element.66), channel_id=1, source_target_pairs={{0,2},{1,3},{2,0},{3,1},{4,6},{5,7},{6,4},{7,5},{8,10},{9,11},{10,... | collective-permute-start | bytes 221192 | tf_op jit(solution)/shard_map/ppermute | solution.py:380
  4.4 6.9 %collective-permute-start.2 = (bf16[2,48,384]{2,1,0:T(8,128)(2,1)S(1)}, bf16[2,48,384]{2,1,0:T(8,128)(2,1)S(1)}, u32[]{:S(2)}, u32[]{:S(2)}) collective-permute-start(bf16[2,48,384]{2,1,0:T(8,128)(2,1)S(1)} %get-tuple-element.67), channel_id=1, source_target_pairs={{0,3},{1,0},{2,1},{3,2},{4,7},{5,4},{6,5},{7,6},{8,11},{9,8},{10,9... | collective-permute-start | bytes 221192 | tf_op jit(solution)/shard_map/ppermute | solution.py:380
  11.3 8.5 %slice-start = ((s8[6291456]{0:T(1024)(128)(4,1)}), s8[4194304]{0:T(1024)(128)(4,1)S(1)}, s32[]{:S(2)}) async-start(s8[6291456]{0:T(1024)(128)(4,1)} %bitcast.10), calls=%async_computation | async-start | bytes 8388608
  11.4 1.6 %collective-permute-start.4 = (bf16[2,192,384]{2,1,0:T(8,128)(2,1)S(1)}, bf16[2,192,384]{2,1,0:T(8,128)(2,1)S(1)}, u32[]{:S(2)}, u32[]{:S(2)}) collective-permute-start(bf16[2,192,384]{2,1,0:T(8,128)(2,1)S(1)} %constant_dynamic-update-slice_fusion.own.refs_0_), channel_id=1, source_target_pairs={{0,4},{4,0},{8,12},{12,8},{16,20},{20,16},{24,28},{28,24},{1,5},{5... | collective-permute-start | bytes 884744 | tf_op jit(solution)/shard_map/ppermute | solution.py:376
  11.5 6.8 %collective-permute-start.3 = (bf16[2,192,384]{2,1,0:T(8,128)(2,1)S(1)}, bf16[2,192,384]{2,1,0:T(8,128)(2,1)S(1)}, u32[]{:S(2)}, u32[]{:S(2)}) collective-permute-start(bf16[2,192,384]{2,1,0:T(8,128)(2,1)S(1)} %constant_dynamic-update-slice_fusion.own.refs_0_), channel_id=1, source_target_pairs={{0,8},{4,20},{8,0},{12,28},{16,24},{20,4},{24,16},{28,12},{1,9},{5... | collective-permute-start | bytes 884744 | tf_op jit(solution)/shard_map/ppermute | solution.py:376
  13.0 8.4 %collective-permute-start.6 = (bf16[2,192,384]{2,1,0:T(8,128)(2,1)S(1)}, bf16[2,192,384]{2,1,0:T(8,128)(2,1)S(1)}, u32[]{:S(2)}, u32[]{:S(2)}) collective-permute-start(bf16[2,192,384]{2,1,0:T(8,128)(2,1)S(1)} %collective-permute-done.4.near.refs_4_), channel_id=1, source_target_pairs={{0,8},{4,20},{8,0},{12,28},{16,24},{20,4},{24,16},{28,12},{1,9},{5... | collective-permute-start | bytes 884744 | tf_op jit(solution)/shard_map/ppermute | solution.py:376
  14.5 5.3 %slice-start.1 = ((s8[6291456]{0:T(1024)(128)(4,1)}), s8[2097152]{0:T(1024)(128)(4,1)S(1)}, s32[]{:S(2)}) async-start(s8[6291456]{0:T(1024)(128)(4,1)} %bitcast.10), calls=%async_computation.1 | async-start | bytes 4194304
  18.3 3.2 %collective-permute-start.7 = (bf16[2,192,384]{2,1,0:T(8,128)(2,1)S(1)}, bf16[2,192,384]{2,1,0:T(8,128)(2,1)S(1)}, u32[]{:S(2)}, u32[]{:S(2)}) collective-permute-start(bf16[2,192,384]{2,1,0:T(8,128)(2,1)S(1)} %collective-permute-done.3.own.refs_1_), channel_id=1, source_target_pairs={{0,4},{4,0},{8,12},{12,8},{16,20},{20,16},{24,28},{28,24},{1,5},{5... | collective-permute-start | bytes 884744 | tf_op jit(solution)/shard_map/ppermute | solution.py:376
  18.3 6.8 %collective-permute-start.5 = (bf16[2,192,384]{2,1,0:T(8,128)(2,1)S(1)}, bf16[2,192,384]{2,1,0:T(8,128)(2,1)S(1)}, u32[]{:S(2)}, u32[]{:S(2)}) collective-permute-start(bf16[2,192,384]{2,1,0:T(8,128)(2,1)S(1)} %collective-permute-done.3.own.refs_1_), channel_id=1, source_target_pairs={{0,16},{4,12},{8,24},{12,4},{16,0},{20,28},{24,8},{28,20},{1,17},{... | collective-permute-start | bytes 884744 | tf_op jit(solution)/shard_map/ppermute | solution.py:376
  21.4 2.1 %copy-start = (bf16[2,192,384]{2,1,0:T(8,128)(2,1)}, bf16[2,192,384]{2,1,0:T(8,128)(2,1)S(1)}, u32[]{:S(2)}) copy-start(bf16[2,192,384]{2,1,0:T(8,128)(2,1)S(1)} %collective-permute-done.6.sib.refs_5_) | copy-start | bytes 884740
  21.4 3.6 %collective-permute-start.9 = (bf16[2,192,384]{2,1,0:T(8,128)(2,1)S(1)}, bf16[2,192,384]{2,1,0:T(8,128)(2,1)S(1)}, u32[]{:S(2)}, u32[]{:S(2)}) collective-permute-start(bf16[2,192,384]{2,1,0:T(8,128)(2,1)S(1)} %collective-permute-done.6.sib.refs_5_), channel_id=1, source_target_pairs={{0,4},{4,0},{8,12},{12,8},{16,20},{20,16},{24,28},{28,24},{1,5},{5... | collective-permute-start | bytes 884744 | tf_op jit(solution)/shard_map/ppermute | solution.py:376
  25.0 1.6 %collective-permute-start.8 = (bf16[2,192,384]{2,1,0:T(8,128)(2,1)S(1)}, bf16[2,192,384]{2,1,0:T(8,128)(2,1)S(1)}, u32[]{:S(2)}, u32[]{:S(2)}) collective-permute-start(bf16[2,192,384]{2,1,0:T(8,128)(2,1)S(1)} %collective-permute-done.5.diag.refs_3_), channel_id=1, source_target_pairs={{0,4},{4,0},{8,12},{12,8},{16,20},{20,16},{24,28},{28,24},{1,5},{5... | collective-permute-start | bytes 884744 | tf_op jit(solution)/shard_map/ppermute | solution.py:376
  25.1 1.5 %copy-start.2 = (bf16[2,192,384]{2,1,0:T(8,128)(2,1)}, bf16[2,192,384]{2,1,0:T(8,128)(2,1)S(1)}, u32[]{:S(2)}) copy-start(bf16[2,192,384]{2,1,0:T(8,128)(2,1)S(1)} %collective-permute-done.9.rest.refs_2_) | copy-start | bytes 884740
  28.5 1.5 %collective-permute-start.10 = (bf16[192,384]{1,0:T(8,128)(2,1)S(1)}, bf16[192,384]{1,0:T(8,128)(2,1)S(1)}, u32[]{:S(2)}, u32[]{:S(2)}) collective-permute-start(bf16[192,384]{1,0:T(8,128)(2,1)S(1)} %get-tuple-element.97), channel_id=1, source_target_pairs={{0,4},{4,0},{8,12},{12,8},{16,20},{20,16},{24,28},{28,24},{1,5},{5... | collective-permute-start | bytes 442376 | tf_op jit(solution)/shard_map/ppermute | solution.py:376
  29.9 3.7 %collective-permute-start.14 = (bf16[192,384]{1,0:T(8,128)(2,1)S(1)}, bf16[192,384]{1,0:T(8,128)(2,1)S(1)}, u32[]{:S(2)}, u32[]{:S(2)}) collective-permute-start(bf16[192,384]{1,0:T(8,128)(2,1)S(1)} %get-tuple-element.114), channel_id=1, source_target_pairs={{0,4},{4,0},{8,12},{12,8},{16,20},{20,16},{24,28},{28,24},{1,5},{5... | collective-permute-start | bytes 442376 | tf_op jit(solution)/shard_map/ppermute | solution.py:376
  30.1 8.6 %collective-permute-start.13 = (bf16[192,384]{1,0:T(8,128)(2,1)S(1)}, bf16[192,384]{1,0:T(8,128)(2,1)S(1)}, u32[]{:S(2)}, u32[]{:S(2)}) collective-permute-start(bf16[192,384]{1,0:T(8,128)(2,1)S(1)} %convert_add_fusion.2), channel_id=1, source_target_pairs={{0,24},{4,28},{8,16},{12,20},{16,8},{20,12},{24,0},{28,4},{1,25},{... | collective-permute-start | bytes 442376 | tf_op jit(solution)/shard_map/ppermute | solution.py:376
  33.4 1.4 %collective-permute-start.11 = (bf16[192,384]{1,0:T(8,128)(2,1)S(1)}, bf16[192,384]{1,0:T(8,128)(2,1)S(1)}, u32[]{:S(2)}, u32[]{:S(2)}) collective-permute-start(bf16[192,384]{1,0:T(8,128)(2,1)S(1)} %get-tuple-element.103), channel_id=1, source_target_pairs={{0,4},{4,0},{8,12},{12,8},{16,20},{20,16},{24,28},{28,24},{1,5},{5... | collective-permute-start | bytes 442376 | tf_op jit(solution)/shard_map/ppermute | solution.py:376
  33.5 7.3 %collective-permute-start.15 = (bf16[192,384]{1,0:T(8,128)(2,1)S(1)}, bf16[192,384]{1,0:T(8,128)(2,1)S(1)}, u32[]{:S(2)}, u32[]{:S(2)}) collective-permute-start(bf16[192,384]{1,0:T(8,128)(2,1)S(1)} %add_convert_fusion), channel_id=1, source_target_pairs={{0,8},{4,12},{8,0},{12,4},{16,24},{20,28},{24,16},{28,20},{1,9},{5... | collective-permute-start | bytes 442376 | tf_op jit(solution)/shard_map/ppermute | solution.py:376
  34.8 1.5 %copy-start.1 = (bf16[2,192,384]{2,1,0:T(8,128)(2,1)S(1)}, bf16[2,192,384]{2,1,0:T(8,128)(2,1)}, u32[]{:S(2)}) copy-start(bf16[2,192,384]{2,1,0:T(8,128)(2,1)} %copy-done) | copy-start | bytes 884740
  34.9 1.5 %copy-start.3 = (bf16[2,192,384]{2,1,0:T(8,128)(2,1)S(1)}, bf16[2,192,384]{2,1,0:T(8,128)(2,1)}, u32[]{:S(2)}) copy-start(bf16[2,192,384]{2,1,0:T(8,128)(2,1)} %copy-done.2) | copy-start | bytes 884740
  34.9 6.0 %collective-permute-start.16 = (bf16[192,384]{1,0:T(8,128)(2,1)S(1)}, bf16[192,384]{1,0:T(8,128)(2,1)S(1)}, u32[]{:S(2)}, u32[]{:S(2)}) collective-permute-start(bf16[192,384]{1,0:T(8,128)(2,1)S(1)} %convert_add_fusion.1), channel_id=1, source_target_pairs={{0,16},{4,20},{8,24},{12,28},{16,0},{20,4},{24,8},{28,12},{1,17},{... | collective-permute-start | bytes 442376 | tf_op jit(solution)/shard_map/ppermute | solution.py:376
  36.2 4.6 %collective-permute-start.12 = (bf16[192,384]{1,0:T(8,128)(2,1)S(1)}, bf16[192,384]{1,0:T(8,128)(2,1)S(1)}, u32[]{:S(2)}, u32[]{:S(2)}) collective-permute-start(bf16[192,384]{1,0:T(8,128)(2,1)S(1)} %get-tuple-element.109), channel_id=1, source_target_pairs={{0,4},{4,0},{8,12},{12,8},{16,20},{20,16},{24,28},{28,24},{1,5},{5... | collective-permute-start | bytes 442376 | tf_op jit(solution)/shard_map/ppermute | solution.py:376
  41.0 10.9 %collective-permute-start.17 = (bf16[48,384]{1,0:T(8,128)(2,1)S(1)}, bf16[48,384]{1,0:T(8,128)(2,1)S(1)}, u32[]{:S(2)}, u32[]{:S(2)}) collective-permute-start(bf16[48,384]{1,0:T(8,128)(2,1)S(1)} %get-tuple-element.124), channel_id=1, source_target_pairs={{0,3},{1,0},{2,1},{3,2},{4,7},{5,4},{6,5},{7,6},{8,11},{9,8},{10,9... | collective-permute-start | bytes 110600 | tf_op jit(solution)/shard_map/ppermute | solution.py:380
  41.3 10.7 %collective-permute-start.19 = (bf16[48,384]{1,0:T(8,128)(2,1)S(1)}, bf16[48,384]{1,0:T(8,128)(2,1)S(1)}, u32[]{:S(2)}, u32[]{:S(2)}) collective-permute-start(bf16[48,384]{1,0:T(8,128)(2,1)S(1)} %get-tuple-element.125), channel_id=1, source_target_pairs={{0,1},{1,2},{2,3},{3,0},{4,5},{5,6},{6,7},{7,4},{8,9},{9,10},{10,1... | collective-permute-start | bytes 110600 | tf_op jit(solution)/shard_map/ppermute | solution.py:380
  43.1 8.9 %collective-permute-start.18 = (bf16[48,384]{1,0:T(8,128)(2,1)S(1)}, bf16[48,384]{1,0:T(8,128)(2,1)S(1)}, u32[]{:S(2)}, u32[]{:S(2)}) collective-permute-start(bf16[48,384]{1,0:T(8,128)(2,1)S(1)} %get-tuple-element.126), channel_id=1, source_target_pairs={{0,2},{1,3},{2,0},{3,1},{4,6},{5,7},{6,4},{7,5},{8,10},{9,11},{10,... | collective-permute-start | bytes 110600 | tf_op jit(solution)/shard_map/ppermute | solution.py:380

commit v10 on v9

--- a/solution.py
+++ b/solution.py
@@ -66,7 +66,7 @@
 
 
 STEP = 256
-LOAD_LIMIT = 28
+LOAD_LIMIT = 18
 PARTS = 2
 
 
@@ -425,12 +425,13 @@
     (grad_gate,) = weight_grads(place, [(0, (0, 1))], mine_of, other_of, (dg,))
     mine = chip_sum(*share)
     parts[0], dg, grad_gate = lax.optimization_barrier((parts[0], dg, grad_gate))
-    (grad_gate,) = weight_grads(place, [(0, (2, 3))], mine_of, other_of, (dg,), grad_gate)
+    (grad_gate,) = weight_grads(place, [(0, (2,))], mine_of, other_of, (dg,), grad_gate)
     for part in parts:
         mine = mine + part.astype(F32)
     mine, hid, grad_gate = lax.optimization_barrier((mine, hid, grad_gate))
     whole = (0, 1, 2, 3)
-    grad_up, grad_down = weight_grads(place, [(0, whole), (1, whole)], mine_of, other_of, (du, hid))
+    jobs = [(0, (3,)), (0, whole), (1, whole)]
+    grad_gate, grad_up, grad_down = weight_grads(place, jobs, mine_of, other_of, (dg, du, hid), grad_gate)
     mine = mine.reshape(groups, tok_count, width)
     back = mine[0]
     sent = mine.astype(BF16)

time: 52.8 us -> 53.3 us (level)
  waiting for transfers between devices: 4.55 us -> 5.14 us
    ppermute x14, waiting for transfers between devices: 2.92 us -> 3.51 us  [across(): lax.ppermute(array, 'tensor', [(i, i ^ masks[i % 2]) for i in range(8)])]
  transfers between devices with their start and end apart: 20 -> 20, of which waited for: 8 -> 10; matrix products, arithmetic and copies ran while one was open for 0% -> 0% of each run, Pallas kernels for 45% -> 44%
where the time goes in v10:
time: 53.3 us; the launch traced here: 53.1 us
  Pallas kernels  26.4 us (50%)
  starting transfers between devices  19.8 us (37%)
  waiting for transfers between devices  5.14 us (10%)
  between operations  0.86 us (2%)
  other arithmetic  0.83 us (2%)
    ppermute x6, starting transfers between devices, along(): lax.ppermute(array, 'expert', [(i, (i + distance) % count) for i in range...  10.5 us
    pallas_call x3, Pallas kernels, weight_grads(): call(functools.partial(weight_kernel, jobs, len(more)), tuple((shape(out,...  9.59 us
    ppermute x14, starting transfers between devices, across(): lax.ppermute(array, 'tensor', [(i, i ^ masks[i % 2]) for i in range(8)])  9.28 us
    pallas_call x1, Pallas kernels, load_up(): call(load_up_kernel, (shape(wu.shape, BF16),) + (shape((rows, hidden_coun...  3.63 us
    ppermute x14, waiting for transfers between devices, across(): lax.ppermute(array, 'tensor', [(i, i ^ masks[i % 2]) for i in range(8)])  3.51 us
    pallas_call x1, Pallas kernels, load_gate(): call(load_gate_kernel, (shape(wg.shape, BF16), shape((4, hidden_count, fu...  3.33 us
    pallas_call x3, Pallas kernels, slots(): call(functools.partial(slot_kernel, p), (shape((rows, width), F32), shape...  2.37 us
    pallas_call x1, Pallas kernels, partial_sums(): call(partial_kernel, (shape(acc[0].shape, F32),) * 3, [SMEM] + [VMEM] * 1...  2.05 us
  transfers between devices with their start and end apart: 20, of which 10 were waited for; matrix products, arithmetic and copies ran while one was open for 0% of the time, Pallas kernels for 44%

profile of v10, /device:TPU:8, one launch (start us, length us, event | category | flops | bytes accessed | tf_op | source)
XLA Modules:
  0.0 53.1 jit_solution(6846260330540174126)
XLA Ops:
  0.6 1.0 %shard_map.102 = (bf16[2,48,384]{2,1,0:T(8,128)(2,1)S(1)}, bf16[2,48,384]{2,1,0:T(8,128)(2,1)S(1)}, bf16[2,48,384]{2,1,0:T(8,128)(2,1)S(1)}, bf16[2,48,384]{2,1,0:T(8,128)(2,1)S(1)}) custom-call(s32[1]{0:T(128)} %bitcast.1.place, bf16[48,384]{1,0:T(8,128)(2,1)} %refs_0_.1, bf16[48,384]{1,0:T(8,128)(2,1)} %refs_1_.1, s32[2,48]{1,0:T(2,128)} %bitcast.17, ...), custom_call_target="tpu_custom_call" | custom-call | flops 1 | bytes 1 | tf_op jit(solution)/shard_map/pallas_call | solution.py:362
  1.7 1.6 %collective-permute-start = (bf16[2,48,384]{2,1,0:T(8,128)(2,1)S(1)}, bf16[2,48,384]{2,1,0:T(8,128)(2,1)S(1)}, u32[]{:S(2)}, u32[]{:S(2)}) collective-permute-start(bf16[2,48,384]{2,1,0:T(8,128)(2,1)S(1)} %get-tuple-element.66), channel_id=1, source_target_pairs={{0,1},{1,2},{2,3},{3,0},{4,5},{5,6},{6,7},{7,4},{8,9},{9,10},{10,1... | collective-permute-start | bytes 221192 | tf_op jit(solution)/shard_map/ppermute | solution.py:380
  3.3 1.1 %collective-permute-start.1 = (bf16[2,48,384]{2,1,0:T(8,128)(2,1)S(1)}, bf16[2,48,384]{2,1,0:T(8,128)(2,1)S(1)}, u32[]{:S(2)}, u32[]{:S(2)}) collective-permute-start(bf16[2,48,384]{2,1,0:T(8,128)(2,1)S(1)} %get-tuple-element.67), channel_id=1, source_target_pairs={{0,2},{1,3},{2,0},{3,1},{4,6},{5,7},{6,4},{7,5},{8,10},{9,11},{10,... | collective-permute-start | bytes 221192 | tf_op jit(solution)/shard_map/ppermute | solution.py:380
  4.4 1.9 %collective-permute-start.2 = (bf16[2,48,384]{2,1,0:T(8,128)(2,1)S(1)}, bf16[2,48,384]{2,1,0:T(8,128)(2,1)S(1)}, u32[]{:S(2)}, u32[]{:S(2)}) collective-permute-start(bf16[2,48,384]{2,1,0:T(8,128)(2,1)S(1)} %get-tuple-element.68), channel_id=1, source_target_pairs={{0,3},{1,0},{2,1},{3,2},{4,7},{5,4},{6,5},{7,6},{8,11},{9,8},{10,9... | collective-permute-start | bytes 221192 | tf_op jit(solution)/shard_map/ppermute | solution.py:380
  6.3 3.3 %shard_map.103 = (bf16[3072,1024]{1,0:T(8,128)(2,1)S(1)}, bf16[4,1024,768]{2,1,0:T(8,128)(2,1)S(1)}) custom-call(s32[1]{0:T(128)} %bitcast.place, bf16[3072,1024]{1,0:T(8,128)(2,1)} %bitcast.15), custom_call_target="tpu_custom_call" | custom-call | flops 1 | bytes 1 | tf_op jit(solution)/shard_map/pallas_call | solution.py:122
  9.9 1.5 %collective-permute-done.2 = bf16[2,48,384]{2,1,0:T(8,128)(2,1)S(1)} collective-permute-done((bf16[2,48,384]{2,1,0:T(8,128)(2,1)S(1)}, bf16[2,48,384]{2,1,0:T(8,128)(2,1)S(1)}, u32[]{:S(2)}, u32[]{:S(2)}) %collective-permute-start.2) | collective-permute-done | bytes 73760 | tf_op jit(solution)/shard_map/ppermute | solution.py:380
  11.5 1.6 %collective-permute-start.3 = (bf16[2,192,384]{2,1,0:T(8,128)(2,1)S(1)}, bf16[2,192,384]{2,1,0:T(8,128)(2,1)S(1)}, u32[]{:S(2)}, u32[]{:S(2)}) collective-permute-start(bf16[2,192,384]{2,1,0:T(8,128)(2,1)S(1)} %constant_dynamic-update-slice_fusion.own.refs_0_), channel_id=1, source_target_pairs={{0,8},{4,20},{8,0},{12,28},{16,24},{20,4},{24,16},{28,12},{1,9},{5... | collective-permute-start | bytes 884744 | tf_op jit(solution)/shard_map/ppermute | solution.py:376
  13.0 1.5 %collective-permute-start.5 = (bf16[2,192,384]{2,1,0:T(8,128)(2,1)S(1)}, bf16[2,192,384]{2,1,0:T(8,128)(2,1)S(1)}, u32[]{:S(2)}, u32[]{:S(2)}) collective-permute-start(bf16[2,192,384]{2,1,0:T(8,128)(2,1)S(1)} %collective-permute-done.4.near.refs_4_), channel_id=1, source_target_pairs={{0,8},{4,20},{8,0},{12,28},{16,24},{20,4},{24,16},{28,12},{1,9},{5... | collective-permute-start | bytes 884744 | tf_op jit(solution)/shard_map/ppermute | solution.py:376
  14.5 3.6 %shard_map.104 = (bf16[3072,1024]{1,0:T(8,128)(2,1)S(1)}, f32[192,1024]{1,0:T(8,128)S(1)}, f32[192,1024]{1,0:T(8,128)S(1)}, bf16[4,1024,768]{2,1,0:T(8,128)(2,1)S(1)}) custom-call(s32[1]{0:T(128)} %bitcast.place, bf16[2,192,384]{2,1,0:T(8,128)(2,1)S(1)} %constant_dynamic-update-slice_fusion.own.refs_0_, ...), custom_call_target="tpu_custom_call" | custom-call | flops 1 | bytes 1 | tf_op jit(solution)/shard_map/pallas_call | solution.py:156
  18.3 1.6 %collective-permute-start.7 = (bf16[2,192,384]{2,1,0:T(8,128)(2,1)S(1)}, bf16[2,192,384]{2,1,0:T(8,128)(2,1)S(1)}, u32[]{:S(2)}, u32[]{:S(2)}) collective-permute-start(bf16[2,192,384]{2,1,0:T(8,128)(2,1)S(1)} %collective-permute-done.3.own.refs_1_), channel_id=1, source_target_pairs={{0,16},{4,12},{8,24},{12,4},{16,0},{20,28},{24,8},{28,20},{1,17},{... | collective-permute-start | bytes 884744 | tf_op jit(solution)/shard_map/ppermute | solution.py:376
  19.8 1.1 %shard_map.105 = (f32[192,1024]{1,0:T(8,128)S(1)}, bf16[2,768,1024]{2,1,0:T(8,128)(2,1)S(1)}) custom-call(s32[1]{0:T(128)} %bitcast.place, bf16[2,192,384]{2,1,0:T(8,128)(2,1)S(1)} %constant_dynamic-update-slice_fusion.own.refs_0_, bf16[2,192,384]{2,1,0:T(8,128)(2,1)S(1)} %collective-permute-done.4.near.refs_4_, bf16[1024,3072]{1,0:T(8,128)(2,1)S(1)} %bitcast.12), custom_call_target="tpu_custom_call" | custom-call | flops 1 | bytes 1 | tf_op jit(solution)/shard_map/pallas_call | solution.py:181
  20.9 0.5 collective-permute-done.5.sib.refs_5_
  21.4 2.0 %shard_map.106 = (f32[192,1024]{1,0:T(8,128)S(1)}, f32[192,1024]{1,0:T(8,128)S(1)}, f32[192,1024]{1,0:T(8,128)S(1)}) custom-call(s32[1]{0:T(128)} %bitcast.place, bf16[2,192,384]{2,1,0:T(8,128)(2,1)S(1)} %collective-permute-done.3.own.refs_1_, ...), custom_call_target="tpu_custom_call", output_to_operand_aliasing={{0}: (8, {}), {1}: (9, {}), {2}: (10, {})} | custom-call | flops 1 | bytes 1 | tf_op jit(solution)/shard_map/pallas_call | solution.py:220
  23.5 1.6 %collective-permute-done.7.diag.refs_3_ = bf16[2,192,384]{2,1,0:T(8,128)(2,1)S(1)} collective-permute-done((bf16[2,192,384]{2,1,0:T(8,128)(2,1)S(1)}, bf16[2,192,384]{2,1,0:T(8,128)(2,1)S(1)}, u32[]{:S(2)}, u32[]{:S(2)}) %collective-permute-start.7) | collective-permute-done | bytes 294944 | tf_op jit(solution)/shard_map/ppermute | solution.py:376
  25.1 1.5 %shard_map.107 = (f32[192,1024]{1,0:T(8,128)S(1)}, f32[192,1024]{1,0:T(8,128)S(1)}, f32[192,1024]{1,0:T(8,128)S(1)}) custom-call(s32[1]{0:T(128)} %bitcast.place, bf16[2,192,384]{2,1,0:T(8,128)(2,1)S(1)} %collective-permute-done.6.rest.refs_2_, ...), custom_call_target="tpu_custom_call", output_to_operand_aliasing={{0}: (6, {}), {1}: (7, {}), {2}: (8, {})} | custom-call | flops 1 | bytes 1 | tf_op jit(solution)/shard_map/pallas_call | solution.py:238
  26.6 1.9 %shard_map.108 = (bf16[192,1024]{1,0:T(8,128)(2,1)S(1)}, bf16[192,1024]{1,0:T(8,128)(2,1)S(1)}, bf16[192,1024]{1,0:T(8,128)(2,1)S(1)}, f32[192,384]{1,0:T(8,128)S(1)}, bf16[192,384]{1,0:T(8,128)(2,1)S(1)}) custom-call(s32[1]{0:T(128)} %bitcast.place, bf16[2,192,384]{2,1,0:T(8,128)(2,1)S(1)} %collective-permute-done.9.sib.refs_7_, ...), custom_call_target="tpu_custom_call" | custom-call | flops 1509949440 | tf_op jit(solution)/shard_map/pallas_call | solution.py:267
  28.5 0.5 collective-permute-start.10
  29.1 0.8 %shard_map.112 = (f32[192,384]{1,0:T(8,128)S(1)}, bf16[192,384]{1,0:T(8,128)(2,1)S(1)}) custom-call(s32[1]{0:T(128)} %bitcast.place, bf16[192,1024]{1,0:T(8,128)(2,1)S(1)} %get-tuple-element.111.refs_0_.refs_8_, bf16[192,1024]{1,0:T(8,128)(2,1)S(1)} %get-tuple-element.107.refs_1_.refs_9_, bf16[4,1024,768]{2,1,0:T(8,128)(2,1)S(1)} %get-tuple-element.89.wg_turned.refs_2_, ...), custom_call_target="tpu_custom_call" | custom-call | flops 603979776 | tf_op jit(solution)/shard_map/pallas_call | solution.py:284
  30.1 2.5 %collective-permute-start.11 = (bf16[192,384]{1,0:T(8,128)(2,1)S(1)}, bf16[192,384]{1,0:T(8,128)(2,1)S(1)}, u32[]{:S(2)}, u32[]{:S(2)}) collective-permute-start(bf16[192,384]{1,0:T(8,128)(2,1)S(1)} %convert_add_fusion.2), channel_id=1, source_target_pairs={{0,24},{4,28},{8,16},{12,20},{16,8},{20,12},{24,0},{28,4},{1,25},{... | collective-permute-start | bytes 442376 | tf_op jit(solution)/shard_map/ppermute | solution.py:376
  32.6 0.8 %shard_map.109 = (f32[192,384]{1,0:T(8,128)S(1)}, bf16[192,384]{1,0:T(8,128)(2,1)S(1)}) custom-call(s32[1]{0:T(128)} %bitcast.place, bf16[192,1024]{1,0:T(8,128)(2,1)S(1)} %get-tuple-element.111.refs_0_.refs_8_, bf16[192,1024]{1,0:T(8,128)(2,1)S(1)} %get-tuple-element.107.refs_1_.refs_9_, bf16[4,1024,768]{2,1,0:T(8,128)(2,1)S(1)} %get-tuple-element.89.wg_turned.refs_2_, ...), custom_call_target="tpu_custom_call" | custom-call | flops 603979776 | tf_op jit(solution)/shard_map/pallas_call | solution.py:284
  33.5 0.7 %collective-permute-start.15 = (bf16[192,384]{1,0:T(8,128)(2,1)S(1)}, bf16[192,384]{1,0:T(8,128)(2,1)S(1)}, u32[]{:S(2)}, u32[]{:S(2)}) collective-permute-start(bf16[192,384]{1,0:T(8,128)(2,1)S(1)} %add_convert_fusion), channel_id=1, source_target_pairs={{0,8},{4,12},{8,0},{12,4},{16,24},{20,28},{24,16},{28,20},{1,9},{5... | collective-permute-start | bytes 442376 | tf_op jit(solution)/shard_map/ppermute | solution.py:376
  34.2 0.6 %collective-permute-done.12 = bf16[192,384]{1,0:T(8,128)(2,1)S(1)} collective-permute-done((bf16[192,384]{1,0:T(8,128)(2,1)S(1)}, bf16[192,384]{1,0:T(8,128)(2,1)S(1)}, u32[]{:S(2)}, u32[]{:S(2)}) %collective-permute-start.12) | collective-permute-done | bytes 147488 | tf_op jit(solution)/shard_map/ppermute | solution.py:376
  34.8 0.6 %collective-permute-start.16 = (bf16[192,384]{1,0:T(8,128)(2,1)S(1)}, bf16[192,384]{1,0:T(8,128)(2,1)S(1)}, u32[]{:S(2)}, u32[]{:S(2)}) collective-permute-start(bf16[192,384]{1,0:T(8,128)(2,1)S(1)} %convert_add_fusion.1), channel_id=1, source_target_pairs={{0,16},{4,20},{8,24},{12,28},{16,0},{20,4},{24,8},{28,12},{1,17},{... | collective-permute-start | bytes 442376 | tf_op jit(solution)/shard_map/ppermute | solution.py:376
  35.4 0.8 %shard_map.110 = (f32[192,384]{1,0:T(8,128)S(1)}, bf16[192,384]{1,0:T(8,128)(2,1)S(1)}) custom-call(s32[1]{0:T(128)} %bitcast.place, bf16[192,1024]{1,0:T(8,128)(2,1)S(1)} %get-tuple-element.111.refs_0_.refs_8_, bf16[192,1024]{1,0:T(8,128)(2,1)S(1)} %get-tuple-element.107.refs_1_.refs_9_, bf16[4,1024,768]{2,1,0:T(8,128)(2,1)S(1)} %get-tuple-element.89.wg_turned.refs_2_, ...), custom_call_target="tpu_custom_call" | custom-call | flops 603979776 | tf_op jit(solution)/shard_map/pallas_call | solution.py:284
  36.3 2.3 %shard_map.111.refs_9_ = bf16[3072,1024]{1,0:T(8,128)(2,1)} custom-call(s32[1]{0:T(128)} %bitcast.place, bf16[2,192,384]{2,1,0:T(8,128)(2,1)S(1)} %constant_dynamic-update-slice_fusion.own.refs_0_, bf16[2,192,384]{2,1,0:T(8,128)(2,1)S(1)} %collective-permute-done.3.own.refs_1_, bf16[2,192,384]{2,1,0:T(8,128)(2,1)S(1)} %collective-permute-done.6.rest.refs_2_, ...), custom_call_target="tpu_custom_call" | custom-call | flops 603979776 | bytes 3145728 | tf_op jit(solution)/shard_map/pallas_call | solution.py:330
  38.6 1.6 %shard_map.113.refs_11_ = bf16[3072,1024]{1,0:T(8,128)(2,1)} custom-call(s32[1]{0:T(128)} %bitcast.place, bf16[2,192,384]{2,1,0:T(8,128)(2,1)S(1)} %constant_dynamic-update-slice_fusion.own.refs_0_, bf16[2,192,384]{2,1,0:T(8,128)(2,1)S(1)} %collective-permute-done.3.own.refs_1_, ...), custom_call_target="tpu_custom_call", output_to_operand_aliasing={{}: (10, {})} | custom-call | flops 301989888 | bytes 1572864 | tf_op jit(solution)/shard_map/pallas_call | solution.py:330
  40.4 0.4 collective-permute-done.16
  41.0 0.2 collective-permute-start.17
  41.2 1.8 %collective-permute-start.19 = (bf16[48,384]{1,0:T(8,128)(2,1)S(1)}, bf16[48,384]{1,0:T(8,128)(2,1)S(1)}, u32[]{:S(2)}, u32[]{:S(2)}) collective-permute-start(bf16[48,384]{1,0:T(8,128)(2,1)S(1)} %get-tuple-element.127), channel_id=1, source_target_pairs={{0,1},{1,2},{2,3},{3,0},{4,5},{5,6},{6,7},{7,4},{8,9},{9,10},{10,1... | collective-permute-start | bytes 110600 | tf_op jit(solution)/shard_map/ppermute | solution.py:380
  43.1 3.7 %collective-permute-start.18 = (bf16[48,384]{1,0:T(8,128)(2,1)S(1)}, bf16[48,384]{1,0:T(8,128)(2,1)S(1)}, u32[]{:S(2)}, u32[]{:S(2)}) collective-permute-start(bf16[48,384]{1,0:T(8,128)(2,1)S(1)} %get-tuple-element.128), channel_id=1, source_target_pairs={{0,2},{1,3},{2,0},{3,1},{4,6},{5,7},{6,4},{7,5},{8,10},{9,11},{10,... | collective-permute-start | bytes 110600 | tf_op jit(solution)/shard_map/ppermute | solution.py:380
  46.8 5.6 %shard_map.114 = (bf16[3072,1024]{1,0:T(8,128)(2,1)}, bf16[3072,1024]{1,0:T(8,128)(2,1)}, bf16[1024,3072]{1,0:T(8,128)(2,1)}) custom-call(s32[1]{0:T(128)} %bitcast.place, bf16[2,192,384]{2,1,0:T(8,128)(2,1)S(1)} %constant_dynamic-update-slice_fusion.own.refs_0_, ...), custom_call_target="tpu_custom_call", output_to_operand_aliasing={{0}: (12, {})} | custom-call | flops 2717908992 | bytes 14155776 | tf_op jit(solution)/shard_map/pallas_call | solution.py:330
  52.5 0.6 %add_convert_fusion.1 = bf16[48,384]{1,0:T(8,128)(2,1)} fusion(bf16[48,384]{1,0:T(8,128)(2,1)S(1)} %collective-permute-done.19, bf16[48,384]{1,0:T(8,128)(2,1)S(1)} %collective-permute-done.18, bf16[48,384]{1,0:T(8,128)(2,1)S(1)} %collective-permute-done.17, f32[192,384]{1,0:T(8,128)S(1)} %convert_add_fusion), kind=kLoop, calls=%fused_computation.4 | loop fusion | flops 129024 | bytes 221184 | tf_op jit(solution)/shard_map/convert_element_type | solution.py:440
  (37 shorter events, 1.3 us)
Async XLA Ops:
  1.7 8.0 %collective-permute-start = (bf16[2,48,384]{2,1,0:T(8,128)(2,1)S(1)}, bf16[2,48,384]{2,1,0:T(8,128)(2,1)S(1)}, u32[]{:S(2)}, u32[]{:S(2)}) collective-permute-start(bf16[2,48,384]{2,1,0:T(8,128)(2,1)S(1)} %get-tuple-element.66), channel_id=1, source_target_pairs={{0,1},{1,2},{2,3},{3,0},{4,5},{5,6},{6,7},{7,4},{8,9},{9,10},{10,1... | collective-permute-start | bytes 221192 | tf_op jit(solution)/shard_map/ppermute | solution.py:380
  3.3 6.6 %collective-permute-start.1 = (bf16[2,48,384]{2,1,0:T(8,128)(2,1)S(1)}, bf16[2,48,384]{2,1,0:T(8,128)(2,1)S(1)}, u32[]{:S(2)}, u32[]{:S(2)}) collective-permute-start(bf16[2,48,384]{2,1,0:T(8,128)(2,1)S(1)} %get-tuple-element.67), channel_id=1, source_target_pairs={{0,2},{1,3},{2,0},{3,1},{4,6},{5,7},{6,4},{7,5},{8,10},{9,11},{10,... | collective-permute-start | bytes 221192 | tf_op jit(solution)/shard_map/ppermute | solution.py:380
  4.4 6.9 %collective-permute-start.2 = (bf16[2,48,384]{2,1,0:T(8,128)(2,1)S(1)}, bf16[2,48,384]{2,1,0:T(8,128)(2,1)S(1)}, u32[]{:S(2)}, u32[]{:S(2)}) collective-permute-start(bf16[2,48,384]{2,1,0:T(8,128)(2,1)S(1)} %get-tuple-element.68), channel_id=1, source_target_pairs={{0,3},{1,0},{2,1},{3,2},{4,7},{5,4},{6,5},{7,6},{8,11},{9,8},{10,9... | collective-permute-start | bytes 221192 | tf_op jit(solution)/shard_map/ppermute | solution.py:380
  11.3 8.5 %slice-start = ((s8[6291456]{0:T(1024)(128)(4,1)}), s8[4194304]{0:T(1024)(128)(4,1)S(1)}, s32[]{:S(2)}) async-start(s8[6291456]{0:T(1024)(128)(4,1)} %bitcast.10), calls=%async_computation | async-start | bytes 8388608
  11.4 1.6 %collective-permute-start.4 = (bf16[2,192,384]{2,1,0:T(8,128)(2,1)S(1)}, bf16[2,192,384]{2,1,0:T(8,128)(2,1)S(1)}, u32[]{:S(2)}, u32[]{:S(2)}) collective-permute-start(bf16[2,192,384]{2,1,0:T(8,128)(2,1)S(1)} %constant_dynamic-update-slice_fusion.own.refs_0_), channel_id=1, source_target_pairs={{0,4},{4,0},{8,12},{12,8},{16,20},{20,16},{24,28},{28,24},{1,5},{5... | collective-permute-start | bytes 884744 | tf_op jit(solution)/shard_map/ppermute | solution.py:376
  11.5 6.8 %collective-permute-start.3 = (bf16[2,192,384]{2,1,0:T(8,128)(2,1)S(1)}, bf16[2,192,384]{2,1,0:T(8,128)(2,1)S(1)}, u32[]{:S(2)}, u32[]{:S(2)}) collective-permute-start(bf16[2,192,384]{2,1,0:T(8,128)(2,1)S(1)} %constant_dynamic-update-slice_fusion.own.refs_0_), channel_id=1, source_target_pairs={{0,8},{4,20},{8,0},{12,28},{16,24},{20,4},{24,16},{28,12},{1,9},{5... | collective-permute-start | bytes 884744 | tf_op jit(solution)/shard_map/ppermute | solution.py:376
  13.0 8.4 %collective-permute-start.5 = (bf16[2,192,384]{2,1,0:T(8,128)(2,1)S(1)}, bf16[2,192,384]{2,1,0:T(8,128)(2,1)S(1)}, u32[]{:S(2)}, u32[]{:S(2)}) collective-permute-start(bf16[2,192,384]{2,1,0:T(8,128)(2,1)S(1)} %collective-permute-done.4.near.refs_4_), channel_id=1, source_target_pairs={{0,8},{4,20},{8,0},{12,28},{16,24},{20,4},{24,16},{28,12},{1,9},{5... | collective-permute-start | bytes 884744 | tf_op jit(solution)/shard_map/ppermute | solution.py:376
  14.5 5.3 %slice-start.1 = ((s8[6291456]{0:T(1024)(128)(4,1)}), s8[2097152]{0:T(1024)(128)(4,1)S(1)}, s32[]{:S(2)}) async-start(s8[6291456]{0:T(1024)(128)(4,1)} %bitcast.10), calls=%async_computation.1 | async-start | bytes 4194304
  18.3 3.2 %collective-permute-start.8 = (bf16[2,192,384]{2,1,0:T(8,128)(2,1)S(1)}, bf16[2,192,384]{2,1,0:T(8,128)(2,1)S(1)}, u32[]{:S(2)}, u32[]{:S(2)}) collective-permute-start(bf16[2,192,384]{2,1,0:T(8,128)(2,1)S(1)} %collective-permute-done.3.own.refs_1_), channel_id=1, source_target_pairs={{0,4},{4,0},{8,12},{12,8},{16,20},{20,16},{24,28},{28,24},{1,5},{5... | collective-permute-start | bytes 884744 | tf_op jit(solution)/shard_map/ppermute | solution.py:376
  18.3 6.8 %collective-permute-start.7 = (bf16[2,192,384]{2,1,0:T(8,128)(2,1)S(1)}, bf16[2,192,384]{2,1,0:T(8,128)(2,1)S(1)}, u32[]{:S(2)}, u32[]{:S(2)}) collective-permute-start(bf16[2,192,384]{2,1,0:T(8,128)(2,1)S(1)} %collective-permute-done.3.own.refs_1_), channel_id=1, source_target_pairs={{0,16},{4,12},{8,24},{12,4},{16,0},{20,28},{24,8},{28,20},{1,17},{... | collective-permute-start | bytes 884744 | tf_op jit(solution)/shard_map/ppermute | solution.py:376
  21.4 3.6 %collective-permute-start.6 = (bf16[2,192,384]{2,1,0:T(8,128)(2,1)S(1)}, bf16[2,192,384]{2,1,0:T(8,128)(2,1)S(1)}, u32[]{:S(2)}, u32[]{:S(2)}) collective-permute-start(bf16[2,192,384]{2,1,0:T(8,128)(2,1)S(1)} %collective-permute-done.5.sib.refs_5_), channel_id=1, source_target_pairs={{0,4},{4,0},{8,12},{12,8},{16,20},{20,16},{24,28},{28,24},{1,5},{5... | collective-permute-start | bytes 884744 | tf_op jit(solution)/shard_map/ppermute | solution.py:376
  25.0 1.6 %collective-permute-start.9 = (bf16[2,192,384]{2,1,0:T(8,128)(2,1)S(1)}, bf16[2,192,384]{2,1,0:T(8,128)(2,1)S(1)}, u32[]{:S(2)}, u32[]{:S(2)}) collective-permute-start(bf16[2,192,384]{2,1,0:T(8,128)(2,1)S(1)} %collective-permute-done.7.diag.refs_3_), channel_id=1, source_target_pairs={{0,4},{4,0},{8,12},{12,8},{16,20},{20,16},{24,28},{28,24},{1,5},{5... | collective-permute-start | bytes 884744 | tf_op jit(solution)/shard_map/ppermute | solution.py:376
  28.5 1.5 %collective-permute-start.10 = (bf16[192,384]{1,0:T(8,128)(2,1)S(1)}, bf16[192,384]{1,0:T(8,128)(2,1)S(1)}, u32[]{:S(2)}, u32[]{:S(2)}) collective-permute-start(bf16[192,384]{1,0:T(8,128)(2,1)S(1)} %get-tuple-element.98), channel_id=1, source_target_pairs={{0,4},{4,0},{8,12},{12,8},{16,20},{20,16},{24,28},{28,24},{1,5},{5... | collective-permute-start | bytes 442376 | tf_op jit(solution)/shard_map/ppermute | solution.py:376
  29.8 3.7 %collective-permute-start.14 = (bf16[192,384]{1,0:T(8,128)(2,1)S(1)}, bf16[192,384]{1,0:T(8,128)(2,1)S(1)}, u32[]{:S(2)}, u32[]{:S(2)}) collective-permute-start(bf16[192,384]{1,0:T(8,128)(2,1)S(1)} %get-tuple-element.116), channel_id=1, source_target_pairs={{0,4},{4,0},{8,12},{12,8},{16,20},{20,16},{24,28},{28,24},{1,5},{5... | collective-permute-start | bytes 442376 | tf_op jit(solution)/shard_map/ppermute | solution.py:376
  30.1 8.5 %collective-permute-start.11 = (bf16[192,384]{1,0:T(8,128)(2,1)S(1)}, bf16[192,384]{1,0:T(8,128)(2,1)S(1)}, u32[]{:S(2)}, u32[]{:S(2)}) collective-permute-start(bf16[192,384]{1,0:T(8,128)(2,1)S(1)} %convert_add_fusion.2), channel_id=1, source_target_pairs={{0,24},{4,28},{8,16},{12,20},{16,8},{20,12},{24,0},{28,4},{1,25},{... | collective-permute-start | bytes 442376 | tf_op jit(solution)/shard_map/ppermute | solution.py:376
  33.4 1.4 %collective-permute-start.12 = (bf16[192,384]{1,0:T(8,128)(2,1)S(1)}, bf16[192,384]{1,0:T(8,128)(2,1)S(1)}, u32[]{:S(2)}, u32[]{:S(2)}) collective-permute-start(bf16[192,384]{1,0:T(8,128)(2,1)S(1)} %get-tuple-element.105), channel_id=1, source_target_pairs={{0,4},{4,0},{8,12},{12,8},{16,20},{20,16},{24,28},{28,24},{1,5},{5... | collective-permute-start | bytes 442376 | tf_op jit(solution)/shard_map/ppermute | solution.py:376
  33.5 6.9 %collective-permute-start.15 = (bf16[192,384]{1,0:T(8,128)(2,1)S(1)}, bf16[192,384]{1,0:T(8,128)(2,1)S(1)}, u32[]{:S(2)}, u32[]{:S(2)}) collective-permute-start(bf16[192,384]{1,0:T(8,128)(2,1)S(1)} %add_convert_fusion), channel_id=1, source_target_pairs={{0,8},{4,12},{8,0},{12,4},{16,24},{20,28},{24,16},{28,20},{1,9},{5... | collective-permute-start | bytes 442376 | tf_op jit(solution)/shard_map/ppermute | solution.py:376
  34.8 6.0 %collective-permute-start.16 = (bf16[192,384]{1,0:T(8,128)(2,1)S(1)}, bf16[192,384]{1,0:T(8,128)(2,1)S(1)}, u32[]{:S(2)}, u32[]{:S(2)}) collective-permute-start(bf16[192,384]{1,0:T(8,128)(2,1)S(1)} %convert_add_fusion.1), channel_id=1, source_target_pairs={{0,16},{4,20},{8,24},{12,28},{16,0},{20,4},{24,8},{28,12},{1,17},{... | collective-permute-start | bytes 442376 | tf_op jit(solution)/shard_map/ppermute | solution.py:376
  36.2 4.6 %collective-permute-start.13 = (bf16[192,384]{1,0:T(8,128)(2,1)S(1)}, bf16[192,384]{1,0:T(8,128)(2,1)S(1)}, u32[]{:S(2)}, u32[]{:S(2)}) collective-permute-start(bf16[192,384]{1,0:T(8,128)(2,1)S(1)} %get-tuple-element.113), channel_id=1, source_target_pairs={{0,4},{4,0},{8,12},{12,8},{16,20},{20,16},{24,28},{28,24},{1,5},{5... | collective-permute-start | bytes 442376 | tf_op jit(solution)/shard_map/ppermute | solution.py:376
  41.0 11.5 %collective-permute-start.17 = (bf16[48,384]{1,0:T(8,128)(2,1)S(1)}, bf16[48,384]{1,0:T(8,128)(2,1)S(1)}, u32[]{:S(2)}, u32[]{:S(2)}) collective-permute-start(bf16[48,384]{1,0:T(8,128)(2,1)S(1)} %get-tuple-element.126), channel_id=1, source_target_pairs={{0,3},{1,0},{2,1},{3,2},{4,7},{5,4},{6,5},{7,6},{8,11},{9,8},{10,9... | collective-permute-start | bytes 110600 | tf_op jit(solution)/shard_map/ppermute | solution.py:380
  41.2 11.2 %collective-permute-start.19 = (bf16[48,384]{1,0:T(8,128)(2,1)S(1)}, bf16[48,384]{1,0:T(8,128)(2,1)S(1)}, u32[]{:S(2)}, u32[]{:S(2)}) collective-permute-start(bf16[48,384]{1,0:T(8,128)(2,1)S(1)} %get-tuple-element.127), channel_id=1, source_target_pairs={{0,1},{1,2},{2,3},{3,0},{4,5},{5,6},{6,7},{7,4},{8,9},{9,10},{10,1... | collective-permute-start | bytes 110600 | tf_op jit(solution)/shard_map/ppermute | solution.py:380
  43.1 9.4 %collective-permute-start.18 = (bf16[48,384]{1,0:T(8,128)(2,1)S(1)}, bf16[48,384]{1,0:T(8,128)(2,1)S(1)}, u32[]{:S(2)}, u32[]{:S(2)}) collective-permute-start(bf16[48,384]{1,0:T(8,128)(2,1)S(1)} %get-tuple-element.128), channel_id=1, source_target_pairs={{0,2},{1,3},{2,0},{3,1},{4,6},{5,7},{6,4},{7,5},{8,10},{9,11},{10,... | collective-permute-start | bytes 110600 | tf_op jit(solution)/shard_map/ppermute | solution.py:380
